TPU v7x, 32 devices: a whole 2x2x4 slice. The times are simulated.
32 devices in a mesh: dp: 8 (over y, x, core), seq: 4 (over z).
Axes of the slice: x: 2, y: 2, z: 4, core: 2. Of those that a mesh axis runs over, the one named last changes fastest.
Arguments:
- tokens: bfloat16 [8192, 1536], P(('dp', 'seq')), may hold values from -6 to 6
- context: bfloat16 [8, 2, 128, 768], P('dp'), may hold values from -6 to 6
- item_lengths: int32 [8, 2], P('dp'), may hold values from 0 to 1024, as said below
- gain_self: bfloat16 [1536], replicated, may hold values from 0.25 to 1.75
- gain_cross: bfloat16 [1536], replicated, may hold values from 0.25 to 1.75
- gain_feed: bfloat16 [1536], replicated, may hold values from 0.25 to 1.75
- self_query: bfloat16 [1536, 1536], P(('dp', 'seq')), may hold values from -0.15625 to 0.15625
- self_key: bfloat16 [1536, 1536], P(('dp', 'seq')), may hold values from -0.15625 to 0.15625
- self_value: bfloat16 [1536, 1536], P(('dp', 'seq')), may hold values from -0.15625 to 0.15625
- self_out: bfloat16 [1536, 1536], P(('dp', 'seq')), may hold values from -3 to 3
- cross_query: bfloat16 [1536, 1536], P(('dp', 'seq')), may hold values from -0.15625 to 0.15625
- cross_key: bfloat16 [768, 1536], P(('dp', 'seq')), may hold values from -0.21875 to 0.21875
- cross_value: bfloat16 [768, 1536], P(('dp', 'seq')), may hold values from -0.21875 to 0.21875
- cross_out: bfloat16 [1536, 1536], P(('dp', 'seq')), may hold values from -1 to 1
- feed_gate: bfloat16 [6144, 1536], P(('dp', 'seq')), may hold values from -0.15625 to 0.15625
- feed_up: bfloat16 [6144, 1536], P(('dp', 'seq')), may hold values from -0.15625 to 0.15625
- feed_down: bfloat16 [6144, 1536], P(('dp', 'seq')), may hold values from -0.078125 to 0.078125
- cotangent: bfloat16 [8192, 1536], P(('dp', 'seq')), may hold values from -6 to 6
Outputs:
- output: bfloat16 [8192, 1536], P(('dp', 'seq'))
- grad_tokens: bfloat16 [8192, 1536], P(('dp', 'seq'))
- grad_gain_self: float32 [1536], P(('dp', 'seq'))
- grad_gain_cross: float32 [1536], P(('dp', 'seq'))
- grad_gain_feed: float32 [1536], P(('dp', 'seq'))
- grad_self_query: float32 [1536, 1536], P(('dp', 'seq'))
- grad_self_key: float32 [1536, 1536], P(('dp', 'seq'))
- grad_self_value: float32 [1536, 1536], P(('dp', 'seq'))
- grad_self_out: float32 [1536, 1536], P(('dp', 'seq'))
- grad_cross_query: float32 [1536, 1536], P(('dp', 'seq'))
- grad_cross_key: float32 [768, 1536], P(('dp', 'seq'))
- grad_cross_value: float32 [768, 1536], P(('dp', 'seq'))
- grad_cross_out: float32 [1536, 1536], P(('dp', 'seq'))
- grad_feed_gate: float32 [6144, 1536], P(('dp', 'seq'))
- grad_feed_up: float32 [6144, 1536], P(('dp', 'seq'))
- grad_feed_down: float32 [6144, 1536], P(('dp', 'seq'))
Inputs may be any that keep to these rules, and one draw needn't show every extreme that they name: Each sequence holds either one item (item_lengths[g, 1] = 0) followed by fewer than 256 padding rows, or two items, the first of 448 to 576 rows, the second filling the rest but for fewer than 256 padding rows. Some sequence is one item of all 1024 rows.
All inputs are finite; a program needn't handle non-finite values.
Results may differ from a plain program's by a relative error of at most 0.024.
Values may be sent and summed in bfloat16 or wider, within the bound.
No kernel may reach another device: no remote copies, remote signals or barrier semaphores. Data moves between devices by JAX's collectives and lax.ppermute only.
A program may use at most 448 MiB of HBM per device.

v0:
```python
import jax
import jax.numpy as jnp
from jax import lax
from jax.sharding import PartitionSpec as P

HEADS = 24
HDIM = 64
ROT = 32


EPSILON = 1e-05
NEG_FILL = -1e30
HIGHEST = lax.Precision.HIGHEST


def layer_norm(values, gain_vector):
    average = jnp.mean(values, axis=-1, keepdims=True)
    centered = values - average
    variance = jnp.mean(centered * centered, axis=-1, keepdims=True)
    return centered * lax.rsqrt(variance + EPSILON) * gain_vector


def layout(lengths, length):
    row_ids = jnp.arange(length, dtype=jnp.int32)
    first_end = lengths[0]
    second_end = lengths[0] + lengths[1]
    segment = jnp.where(row_ids < first_end, 0, jnp.where(row_ids < second_end, 1, 2)).astype(
        jnp.int32
    )
    seg_start = jnp.where(segment == 0, 0, jnp.where(segment == 1, first_end, second_end))
    return (segment, row_ids - seg_start)


def rotary_tables(position):
    half_rot = ROT // 2
    frequency = 10000.0 ** (-jnp.arange(half_rot, dtype=jnp.float32) / half_rot)
    angles = position.astype(jnp.float32)[:, None] * frequency[None, :]
    return (jnp.cos(angles), jnp.sin(angles))


def rotate(values, cosine, sine_table):
    half_rot = ROT // 2
    first_half = values[..., :half_rot]
    second_half = values[..., half_rot:ROT]
    remainder = values[..., ROT:]
    cos_heads = cosine[:, None, :]
    sin_heads = sine_table[:, None, :]
    return jnp.concatenate(
        [
            first_half * cos_heads - second_half * sin_heads,
            second_half * cos_heads + first_half * sin_heads,
            remainder,
        ],
        axis=-1,
    )


def matmul(left, right):
    return jnp.dot(left, right, preferred_element_type=jnp.float32)


def contract_rows(left, right):
    return lax.dot_general(
        left, right, (((0,), (0,)), ((), ())), preferred_element_type=jnp.float32
    )


def contract_cols(left, right):
    return lax.dot_general(
        left, right, (((1,), (1,)), ((), ())), preferred_element_type=jnp.float32
    )


def softmax_rows(scores):
    highest = jnp.max(scores, axis=-1, keepdims=True)
    raised = jnp.exp(scores - highest)
    denominator = jnp.sum(raised, axis=-1, keepdims=True)
    return (raised / denominator, highest + jnp.log(denominator))


def gate_backward(gate_proj, up_proj, grad_activation):
    unused, pullback = jax.vjp(
        lambda gate_in, up_in: jax.nn.silu(gate_in) * up_in, gate_proj, up_proj
    )
    grad_gate, grad_up = pullback(grad_activation)
    return (grad_gate.astype(jnp.bfloat16), grad_up.astype(jnp.bfloat16))


def heads_forward(queries, key_rows, value_rows, segment, block_rows):
    length, heads_dev, head_dim = queries.shape
    scaling = head_dim ** (-0.5)

    def attend(block_index):
        first_row = block_index * block_rows
        query_block = lax.dynamic_slice_in_dim(queries, first_row, block_rows, 0)
        query_segment = lax.dynamic_slice_in_dim(segment, first_row, block_rows, 0)
        scores = (
            jnp.einsum("qhd,khd->hqk", query_block, key_rows, preferred_element_type=jnp.float32)
            * scaling
        )
        scores = jnp.where(query_segment[None, :, None] == segment[None, None, :], scores, NEG_FILL)
        chance, log_total = softmax_rows(scores)
        attended = jnp.einsum(
            "hqk,khd->qhd",
            chance.astype(jnp.bfloat16),
            value_rows,
            preferred_element_type=jnp.float32,
        )
        return (attended, log_total[..., 0])

    attended, log_total = lax.map(attend, jnp.arange(length // block_rows))
    return (attended.reshape(length, heads_dev * head_dim), log_total)


def heads_backward(queries, key_rows, value_rows, grad_out, log_total, segment, block_rows):
    length, heads_dev, head_dim = queries.shape
    scaling = head_dim ** (-0.5)

    def backward_block(carried, block_index):
        grad_keys, grad_values = carried
        first_row = block_index * block_rows
        query_block = lax.dynamic_slice_in_dim(queries, first_row, block_rows, 0)
        grad_block = lax.dynamic_slice_in_dim(grad_out, first_row, block_rows, 0)
        query_segment = lax.dynamic_slice_in_dim(segment, first_row, block_rows, 0)
        scores = (
            jnp.einsum("qhd,khd->hqk", query_block, key_rows, preferred_element_type=jnp.float32)
            * scaling
        )
        scores = jnp.where(query_segment[None, :, None] == segment[None, None, :], scores, NEG_FILL)
        chance = jnp.exp(scores - log_total[block_index][:, :, None])
        grad_chance = jnp.einsum(
            "qhd,khd->hqk", grad_block, value_rows, preferred_element_type=jnp.float32
        )
        row_inner = jnp.sum(chance * grad_chance, axis=-1, keepdims=True)
        grad_scores = (chance * (grad_chance - row_inner)).astype(jnp.bfloat16)
        grad_query = (
            jnp.einsum("hqk,khd->qhd", grad_scores, key_rows, preferred_element_type=jnp.float32)
            * scaling
        )
        grad_keys = (
            grad_keys
            + jnp.einsum(
                "hqk,qhd->khd", grad_scores, query_block, preferred_element_type=jnp.float32
            )
            * scaling
        )
        grad_values = grad_values + jnp.einsum(
            "hqk,qhd->khd",
            chance.astype(jnp.bfloat16),
            grad_block,
            preferred_element_type=jnp.float32,
        )
        return ((grad_keys, grad_values), grad_query)

    initial = jnp.zeros((length, heads_dev, head_dim), jnp.float32)
    (grad_keys, grad_values), grad_query = lax.scan(
        backward_block, (initial, initial), jnp.arange(length // block_rows)
    )
    return (grad_query.reshape(length, heads_dev, head_dim), grad_keys, grad_values)


def local(
    tokens,
    context,
    item_lengths,
    gain_self,
    gain_cross,
    gain_feed,
    self_query,
    self_key,
    self_value,
    self_out,
    cross_query,
    cross_key,
    cross_value,
    cross_out,
    feed_gate,
    feed_up,
    feed_down,
    cotangent,
):
    rows_dev, width = tokens.shape
    seq_parts = lax.axis_size("seq")
    length = rows_dev * seq_parts
    heads_dev = HEADS // seq_parts
    head_width = heads_dev * HDIM
    block_rows = min(512, length)
    scaling = HDIM ** (-0.5)
    segment, position = layout(item_lengths[0], length)
    row_start = lax.axis_index("seq") * rows_dev
    col_start = lax.axis_index("seq") * head_width
    row_segment = lax.dynamic_slice_in_dim(segment, row_start, rows_dev, 0)
    cosine, sine_table = rotary_tables(position)
    (
        full_query,
        full_key,
        full_value,
        full_out,
        full_cross_query,
        full_cross_key,
        full_cross_value,
        full_cross_out,
    ) = (
        lax.all_gather(self_query, ("dp", "seq"), axis=0, tiled=True),
        lax.all_gather(self_key, ("dp", "seq"), axis=0, tiled=True),
        lax.all_gather(self_value, ("dp", "seq"), axis=0, tiled=True),
        lax.all_gather(self_out, ("dp", "seq"), axis=0, tiled=True),
        lax.all_gather(cross_query, ("dp", "seq"), axis=0, tiled=True),
        lax.all_gather(cross_key, ("dp", "seq"), axis=0, tiled=True),
        lax.all_gather(cross_value, ("dp", "seq"), axis=0, tiled=True),
        lax.all_gather(cross_out, ("dp", "seq"), axis=0, tiled=True),
    )
    token_values = tokens.astype(jnp.float32)
    norm_one, norm_one_back = jax.vjp(layer_norm, token_values, gain_self.astype(jnp.float32))
    norm_one = norm_one.astype(jnp.bfloat16)
    head_shape = (length, heads_dev, HDIM)
    all_norm_one = lax.all_gather(norm_one, "seq", axis=0, tiled=True)
    query_cols = lax.dynamic_slice_in_dim(full_query, col_start, head_width, 1)
    key_cols = lax.dynamic_slice_in_dim(full_key, col_start, head_width, 1)
    value_cols = lax.dynamic_slice_in_dim(full_value, col_start, head_width, 1)

    def project_heads(weight):
        projected = matmul(all_norm_one, weight).reshape(head_shape)
        return rotate(projected, cosine, sine_table).astype(jnp.bfloat16)

    head_queries = project_heads(query_cols)
    head_keys = project_heads(key_cols)
    head_values = matmul(all_norm_one, value_cols).astype(jnp.bfloat16).reshape(head_shape)
    head_attended, log_total = heads_forward(
        head_queries, head_keys, head_values, segment, block_rows
    )
    attended = lax.all_to_all(
        head_attended.astype(jnp.bfloat16), "seq", split_axis=0, concat_axis=1, tiled=True
    )
    first_sum = token_values + matmul(attended, full_out)
    norm_two, norm_two_back = jax.vjp(layer_norm, first_sum, gain_cross.astype(jnp.float32))
    norm_two = norm_two.astype(jnp.bfloat16)
    cross_queries = matmul(norm_two, full_cross_query).astype(jnp.bfloat16)
    memory = context[0].reshape(-1, context.shape[3])
    memory_rows = memory.shape[0]
    memory_keys = matmul(memory, full_cross_key).astype(jnp.bfloat16)
    memory_values = matmul(memory, full_cross_value).astype(jnp.bfloat16)
    item_index = jnp.where(row_segment == 1, 1, 0).astype(jnp.int32)
    key_item = jnp.arange(memory_rows, dtype=jnp.int32) // (memory_rows // 2)
    cross_mask = item_index[None, :, None] == key_item[None, None, :]
    query_heads = cross_queries.reshape(rows_dev, HEADS, HDIM)
    memory_key_heads = memory_keys.reshape(memory_rows, HEADS, HDIM)
    memory_value_heads = memory_values.reshape(memory_rows, HEADS, HDIM)
    cross_scores = (
        jnp.einsum(
            "qhd,khd->hqk", query_heads, memory_key_heads, preferred_element_type=jnp.float32
        )
        * scaling
    )
    cross_scores = jnp.where(cross_mask, cross_scores, NEG_FILL)
    cross_chance = softmax_rows(cross_scores)[0]
    cross_mixed = jnp.einsum(
        "hqk,khd->qhd",
        cross_chance.astype(jnp.bfloat16),
        memory_value_heads,
        preferred_element_type=jnp.float32,
    )
    cross_mixed = cross_mixed.reshape(rows_dev, width).astype(jnp.bfloat16)
    second_sum = first_sum + matmul(cross_mixed, full_cross_out)
    norm_three, norm_three_back = jax.vjp(layer_norm, second_sum, gain_feed.astype(jnp.float32))
    norm_three = norm_three.astype(jnp.bfloat16)
    valid_rows = (row_segment < 2).astype(jnp.float32)[:, None]
    grad_output = cotangent.astype(jnp.float32) * valid_rows
    grad_output_low = grad_output.astype(jnp.bfloat16)
    unit_gate, unit_up, unit_down = (
        lax.all_gather(feed_gate, "dp", axis=0, tiled=True),
        lax.all_gather(feed_up, "dp", axis=0, tiled=True),
        lax.all_gather(feed_down, "dp", axis=0, tiled=True),
    )
    all_norm = lax.all_gather(norm_three, "seq", axis=0, tiled=True)
    gate_proj = contract_cols(all_norm, unit_gate)
    up_proj = contract_cols(all_norm, unit_up)
    activation = (jax.nn.silu(gate_proj) * up_proj).astype(jnp.bfloat16)
    feed_result = lax.psum_scatter(
        matmul(activation, unit_down).astype(jnp.bfloat16), "seq", scatter_dimension=0, tiled=True
    ).astype(jnp.float32)
    output = (second_sum + feed_result).astype(jnp.bfloat16)
    all_grad = lax.all_gather(grad_output_low, "seq", axis=0, tiled=True)
    grad_activation = contract_cols(all_grad, unit_down)
    grad_gate, grad_up = gate_backward(gate_proj, up_proj, grad_activation)
    grad_norm_three = lax.psum_scatter(
        (matmul(grad_gate, unit_gate) + matmul(grad_up, unit_up)).astype(jnp.bfloat16),
        "seq",
        scatter_dimension=0,
        tiled=True,
    ).astype(jnp.float32)
    feed_grads = lax.psum_scatter(
        jnp.stack(
            [
                contract_rows(grad_gate, all_norm),
                contract_rows(grad_up, all_norm),
                contract_rows(activation, all_grad),
            ],
            axis=1,
        ).astype(jnp.bfloat16),
        "dp",
        scatter_dimension=0,
        tiled=True,
    ).astype(jnp.float32)
    grad_second, grad_gain_feed = norm_three_back(grad_norm_three)
    grad_second = grad_second + grad_output
    second_low = grad_second.astype(jnp.bfloat16)
    grad_cross_out_full = contract_rows(cross_mixed, second_low)
    grad_mixed = (
        contract_cols(second_low, full_cross_out)
        .astype(jnp.bfloat16)
        .reshape(rows_dev, HEADS, HDIM)
    )
    grad_chance = jnp.einsum(
        "qhd,khd->hqk", grad_mixed, memory_value_heads, preferred_element_type=jnp.float32
    )
    row_inner = jnp.sum(cross_chance * grad_chance, axis=-1, keepdims=True)
    grad_scores = (cross_chance * (grad_chance - row_inner)).astype(jnp.bfloat16)
    grad_cross_queries = (
        jnp.einsum(
            "hqk,khd->qhd", grad_scores, memory_key_heads, preferred_element_type=jnp.float32
        )
        * scaling
    )
    grad_cross_queries = grad_cross_queries.reshape(rows_dev, width).astype(jnp.bfloat16)
    grad_memory_keys = (
        jnp.einsum("hqk,qhd->khd", grad_scores, query_heads, preferred_element_type=jnp.float32)
        * scaling
    ).reshape(memory_rows, width)
    grad_memory_values = jnp.einsum(
        "hqk,qhd->khd",
        cross_chance.astype(jnp.bfloat16),
        grad_mixed,
        preferred_element_type=jnp.float32,
    ).reshape(memory_rows, width)
    memory_wide = memory.astype(jnp.float32)
    grad_cross_key_full = lax.dot_general(
        memory_wide, grad_memory_keys, (((0,), (0,)), ((), ())), precision=HIGHEST
    )
    grad_cross_value_full = lax.dot_general(
        memory_wide, grad_memory_values, (((0,), (0,)), ((), ())), precision=HIGHEST
    )
    grad_cross_query_full = contract_rows(norm_two, grad_cross_queries)
    grad_norm_two = contract_cols(grad_cross_queries, full_cross_query)
    grad_first, grad_gain_cross = norm_two_back(grad_norm_two)
    grad_first = grad_first + grad_second
    first_low = grad_first.astype(jnp.bfloat16)
    grad_self_out_full = contract_rows(attended, first_low)
    grad_attended = contract_cols(first_low, full_out).astype(jnp.bfloat16)
    head_grad = lax.all_to_all(
        grad_attended, "seq", split_axis=1, concat_axis=0, tiled=True
    ).reshape(head_shape)
    grad_head_queries, grad_head_keys, grad_head_values = heads_backward(
        head_queries, head_keys, head_values, head_grad, log_total, segment, block_rows
    )
    turned_queries = (
        rotate(grad_head_queries, cosine, -sine_table)
        .reshape(length, head_width)
        .astype(jnp.bfloat16)
    )
    turned_keys = (
        rotate(grad_head_keys, cosine, -sine_table).reshape(length, head_width).astype(jnp.bfloat16)
    )
    flat_values = grad_head_values.reshape(length, head_width).astype(jnp.bfloat16)
    grad_norm_one = lax.psum_scatter(
        (
            contract_cols(turned_queries, query_cols)
            + contract_cols(turned_keys, key_cols)
            + contract_cols(flat_values, value_cols)
        ).astype(jnp.bfloat16),
        "seq",
        scatter_dimension=0,
        tiled=True,
    ).astype(jnp.float32)
    column_sums = (
        lax.psum_scatter(
            contract_rows(all_norm_one, turned_queries).astype(jnp.bfloat16),
            "dp",
            scatter_dimension=0,
            tiled=True,
        ).astype(jnp.float32),
        lax.psum_scatter(
            contract_rows(all_norm_one, turned_keys).astype(jnp.bfloat16),
            "dp",
            scatter_dimension=0,
            tiled=True,
        ).astype(jnp.float32),
        lax.psum_scatter(
            contract_rows(all_norm_one, flat_values).astype(jnp.bfloat16),
            "dp",
            scatter_dimension=0,
            tiled=True,
        ).astype(jnp.float32),
    )
    placed = lax.all_to_all(
        jnp.stack([column_sums[0], column_sums[1], column_sums[2]]).astype(jnp.bfloat16),
        "seq",
        split_axis=1,
        concat_axis=2,
        tiled=True,
    ).astype(jnp.float32)
    grad_tokens_wide, grad_gain_self = norm_one_back(grad_norm_one)
    grad_tokens = (grad_tokens_wide + grad_first).astype(jnp.bfloat16)
    remaining = (
        lax.psum_scatter(grad_gain_self, ("dp", "seq"), scatter_dimension=0, tiled=True),
        lax.psum_scatter(grad_gain_cross, ("dp", "seq"), scatter_dimension=0, tiled=True),
        lax.psum_scatter(grad_gain_feed, ("dp", "seq"), scatter_dimension=0, tiled=True),
        lax.psum_scatter(grad_self_out_full, ("dp", "seq"), scatter_dimension=0, tiled=True),
        lax.psum_scatter(grad_cross_query_full, ("dp", "seq"), scatter_dimension=0, tiled=True),
        lax.psum_scatter(grad_cross_key_full, ("dp", "seq"), scatter_dimension=0, tiled=True),
        lax.psum_scatter(grad_cross_value_full, ("dp", "seq"), scatter_dimension=0, tiled=True),
        lax.psum_scatter(grad_cross_out_full, ("dp", "seq"), scatter_dimension=0, tiled=True),
    )
    projection_grads = (placed[0], placed[1], placed[2])
    return (
        output,
        grad_tokens,
        remaining[0],
        remaining[1],
        remaining[2],
        projection_grads[0],
        projection_grads[1],
        projection_grads[2],
        remaining[3],
        remaining[4],
        remaining[5],
        remaining[6],
        remaining[7],
        feed_grads[:, 0, :],
        feed_grads[:, 1, :],
        feed_grads[:, 2, :],
    )


def solution(mesh):
    placed = (
        P(("dp", "seq"), None),
        P("dp", None, None, None),
        P("dp", None),
        P(),
        P(),
        P(),
        P(("dp", "seq"), None),
        P(("dp", "seq"), None),
        P(("dp", "seq"), None),
        P(("dp", "seq"), None),
        P(("dp", "seq"), None),
        P(("dp", "seq"), None),
        P(("dp", "seq"), None),
        P(("dp", "seq"), None),
        P(("dp", "seq"), None),
        P(("dp", "seq"), None),
        P(("dp", "seq"), None),
        P(("dp", "seq"), None),
    )
    return jax.shard_map(
        local,
        mesh=mesh,
        in_specs=placed,
        out_specs=(
            P(("dp", "seq"), None),
            P(("dp", "seq"), None),
            P(("dp", "seq")),
            P(("dp", "seq")),
            P(("dp", "seq")),
            P(("dp", "seq"), None),
            P(("dp", "seq"), None),
            P(("dp", "seq"), None),
            P(("dp", "seq"), None),
            P(("dp", "seq"), None),
            P(("dp", "seq"), None),
            P(("dp", "seq"), None),
            P(("dp", "seq"), None),
            P(("dp", "seq"), None),
            P(("dp", "seq"), None),
            P(("dp", "seq"), None),
        ),
        check_vma=False,
    )
```

profile of v0, /device:TPU:0, one launch (start us, length us, event | category | flops | bytes accessed | tf_op | source)
XLA Modules:
  0.0 2133.0 jit_solution(10443503085510334469)
XLA Ops:
  24.5 56.1 %all-gather.15.cloned.1.call-done = bf16[1024,1536]{1,0:T(8,128)(2,1)} async-done(((bf16[256,1536]{1,0:T(8,128)(2,1)}), bf16[1024,1536]{1,0:T(8,128)(2,1)}) %all-gather.15.cloned.1.call-update) | async-done | bytes 3145744 | tf_op jit(solution)/shard_map/all_gather | solution.py:217
  80.7 65.0 %all-gather.17.cloned.1.call-done = bf16[1536,1536]{1,0:T(8,128)(2,1)} async-done(((bf16[48,1536]{1,0:T(8,128)(2,1)}), bf16[1536,1536]{1,0:T(8,128)(2,1)}) %all-gather.17.cloned.1.call-update) | async-done | bytes 4718608 | tf_op jit(solution)/shard_map/all_gather | solution.py:204
  149.4 61.5 %all-gather.19.cloned.1.call-done = bf16[1536,1536]{1,0:T(8,128)(2,1)} async-done(((bf16[48,1536]{1,0:T(8,128)(2,1)}), bf16[1536,1536]{1,0:T(8,128)(2,1)}) %all-gather.19.cloned.1.call-update) | async-done | bytes 4718608 | tf_op jit(solution)/shard_map/all_gather | solution.py:205
  215.9 60.0 %all-gather.21.cloned.1.call-done = bf16[1536,1536]{1,0:T(8,128)(2,1)} async-done(((bf16[48,1536]{1,0:T(8,128)(2,1)}), bf16[1536,1536]{1,0:T(8,128)(2,1)}) %all-gather.21.cloned.1.call-update) | async-done | bytes 4718608 | tf_op jit(solution)/shard_map/all_gather | solution.py:206
  279.6 26.4 %while.27 = (s32[]{:T(128)}, bf16[2,512,6,64]{1,3,2,0:T(8,128)(2,1)S(1)}, f32[2,6,512]{2,1,0:T(8,128)S(1)}, s32[2]{0:T(128)S(1)}, s32[1024]{0:T(1024)S(1)}, /*in...) while((s32[]{:T(128)}, ...), condition=%wide.region_5.6_spmd, body=%wide.region_2.5_spmd.sunk | while | flops 843576320 | bytes 42727620 | solution.py:111
  316.7 24.5 %all-gather.25.cloned.1.call-done = bf16[768,1536]{1,0:T(8,128)(2,1)} async-done(((bf16[24,1536]{1,0:T(8,128)(2,1)}), bf16[768,1536]{1,0:T(8,128)(2,1)}) %all-gather.25.cloned.1.call-update) | async-done | bytes 2359312 | tf_op jit(solution)/shard_map/all_gather | solution.py:210
  346.9 54.5 %all-gather.29.cloned.1.call-done = bf16[768,1536]{1,0:T(8,128)(2,1)} async-done(((bf16[24,1536]{1,0:T(8,128)(2,1)}), bf16[768,1536]{1,0:T(8,128)(2,1)}) %all-gather.29.cloned.1.call-update) | async-done | bytes 2359312 | tf_op jit(solution)/shard_map/all_gather | solution.py:209
  407.0 59.7 %all-gather.23.cloned.1.call-done = bf16[1536,1536]{1,0:T(8,128)(2,1)} async-done(((bf16[48,1536]{1,0:T(8,128)(2,1)}), bf16[1536,1536]{1,0:T(8,128)(2,1)}) %all-gather.23.cloned.1.call-update) | async-done | bytes 4718608 | tf_op jit(solution)/shard_map/all_gather | solution.py:207
  473.6 58.3 %all-gather.27.cloned.1.call-done = bf16[1536,1536]{1,0:T(8,128)(2,1)} async-done(((bf16[48,1536]{1,0:T(8,128)(2,1)}), bf16[1536,1536]{1,0:T(8,128)(2,1)}) %all-gather.27.cloned.1.call-update) | async-done | bytes 4718608 | tf_op jit(solution)/shard_map/all_gather | solution.py:208
  547.0 50.1 %all-gather.31.cloned.1.call-done = bf16[1536,1536]{1,0:T(8,128)(2,1)} async-done(((bf16[48,1536]{1,0:T(8,128)(2,1)}), bf16[1536,1536]{1,0:T(8,128)(2,1)}) %all-gather.31.cloned.1.call-update) | async-done | bytes 4718608 | tf_op jit(solution)/shard_map/all_gather | solution.py:211
  606.4 30.2 %all-gather.35.cloned.1.call-done = bf16[1536,1536]{1,0:T(8,128)(2,1)} async-done(((bf16[192,1536]{1,0:T(8,128)(2,1)}), bf16[1536,1536]{1,0:T(8,128)(2,1)}) %all-gather.35.cloned.1.call-update) | async-done | bytes 4718608 | tf_op jit(solution)/shard_map/all_gather | solution.py:271
  636.6 65.7 %all-gather.33.cloned.1.call-done = bf16[1024,1536]{1,0:T(8,128)(2,1)} async-done(((bf16[256,1536]{1,0:T(8,128)(2,1)}), bf16[1024,1536]{1,0:T(8,128)(2,1)}) %all-gather.33.cloned.1.call-update) | async-done | bytes 3145744 | tf_op jit(solution)/shard_map/all_gather | solution.py:275
  702.3 9.7 fusion.100
  712.0 29.6 %all-gather.37.cloned.1.call-done = bf16[1536,1536]{1,0:T(8,128)(2,1)} async-done(((bf16[192,1536]{1,0:T(8,128)(2,1)}), bf16[1536,1536]{1,0:T(8,128)(2,1)}) %all-gather.37.cloned.1.call-update) | async-done | bytes 4718608 | tf_op jit(solution)/shard_map/all_gather | solution.py:272
  741.6 9.8 fusion.101
  751.5 55.8 %all-gather.41.cloned.1.call-done = bf16[1024,1536]{1,0:T(8,128)(2,1)} async-done(((bf16[256,1536]{1,0:T(8,128)(2,1)}), bf16[1024,1536]{1,0:T(8,128)(2,1)}) %all-gather.41.cloned.1.call-update) | async-done | bytes 3145744 | tf_op jit(solution)/shard_map/all_gather | solution.py:283
  807.3 39.3 %all-gather.39.cloned.1.call-done = bf16[1536,1536]{1,0:T(8,128)(2,1)} async-done(((bf16[192,1536]{1,0:T(8,128)(2,1)}), bf16[1536,1536]{1,0:T(8,128)(2,1)}) %all-gather.39.cloned.1.call-update) | async-done | bytes 4718608 | tf_op jit(solution)/shard_map/all_gather | solution.py:273
  846.6 13.6 multiply_convert_fusion.2
  860.3 8.8 fusion.102
  869.1 6.5 add_convert_fusion.1
  875.9 9.2 convolution_convert_fusion.3
  885.1 50.9 %reduce-scatter.19.cloned.1.call-done = bf16[256,1536]{1,0:T(8,128)(2,1)} async-done(((bf16[1024,1536]{1,0:T(8,128)(2,1)}), bf16[256,1536]{1,0:T(8,128)(2,1)}) %reduce-scatter.19.cloned.1.call-update) | async-done | bytes 786448 | tf_op jit(solution)/shard_map/reduce_scatter | solution.py:286
  938.9 59.6 %reduce-scatter.17.cloned.1.call-done = bf16[256,1536]{1,0:T(8,128)(2,1)} async-done(((bf16[1024,1536]{1,0:T(8,128)(2,1)}), bf16[256,1536]{1,0:T(8,128)(2,1)}) %reduce-scatter.17.cloned.1.call-update) | async-done | bytes 786448 | tf_op jit(solution)/shard_map/reduce_scatter | solution.py:279
  1011.1 7.1 multiply_reduce_fusion.1
  1037.9 20.2 all-to-all-done.1
  1060.3 113.0 %while.28 = (s32[]{:T(128)}, f32[1024,6,64]{0,2,1:T(8,128)}, f32[1024,6,64]{0,2,1:T(8,128)}, f32[2,512,6,64]{1,0,3,2:T(2,128)}, s32[2]{0:T(128)S(1)}, /*index=5*...) while((s32[]{:T(128)}, f32[1024,6,64]{0,2,1:T(8,128)}, ...), condition=%wide.region_21.22_spmd.clone, body=%wide.region_19.21_spmd.clone.sunk | while | flops 2063135744 | bytes 217676240 | solution.py:156
  1062.0 7.4 fusion.205
  1071.9 7.7 multiply_reduce_fusion.7
  1101.5 15.0 dynamic_update_slice.19
  1117.7 7.4 fusion.205
  1127.5 7.7 multiply_reduce_fusion.7
  1148.8 6.5 bitcast_add_fusion.5
  1158.2 15.0 dynamic_update_slice.19
  1206.2 8.0 fusion.32
  1225.1 6.3 pad_maximum_fusion
  1239.8 6.2 copy.111
  1255.3 6.1 copy.113
  1269.2 6.7 fusion.92
  1282.3 15.6 reduce-scatter.23.cloned.1.call-done
  1304.8 30.5 %all-to-all-done.2 = bf16[3,192,384]{2,0,1:T(4,128)(2,1)S(1)} async-done(((bf16[3,192,384]{2,0,1:T(4,128)(2,1)}), bf16[3,192,384]{2,0,1:T(4,128)(2,1)S(1)}, u32[]{:S(2)}, u32[]{:S(2)}) %all-to-all-start.2) | async-done | bytes 442400 | tf_op jit(solution)/shard_map/all_to_all | solution.py:395
  1338.7 29.8 %reduce-scatter.21.cloned.1.call-done = bf16[256,1536]{1,0:T(8,128)(2,1)} async-done(((bf16[1024,1536]{1,0:T(8,128)(2,1)}), bf16[256,1536]{1,0:T(8,128)(2,1)}) %reduce-scatter.21.cloned.1.call-update) | async-done | bytes 786448 | tf_op jit(solution)/shard_map/reduce_scatter | solution.py:365
  1374.0 43.1 %all-reduce.3 = (f32[1536]{0:T(1024)}, f32[1536]{0:T(1024)}, f32[1536]{0:T(1024)}) all-reduce(f32[1536]{0:T(1024)} %get-tuple-element.238, f32[1536]{0:T(1024)} %get-tuple-element.234, f32[1536]{0:T(1024)} %get-tuple-element.236), channel_id=5, replica_groups=mesh['dp'=8,'seq'=4] {'dp','seq'}, use_global_device_ids=true, to_apply=%region_26.27.clone | all-reduce | flops 4608 | bytes 36864
  1423.7 51.4 %reduce-scatter.35.cloned.1.call-done = bf16[192,3,1536]{2,0,1:T(8,128)(2,1)} async-done(((bf16[1536,3,1536]{2,0,1:T(8,128)(2,1)}), bf16[192,3,1536]{2,0,1:T(8,128)(2,1)}) %reduce-scatter.35.cloned.1.call-update) | async-done | bytes 1769488 | tf_op jit(solution)/shard_map/reduce_scatter | solution.py:292
  1478.9 110.1 %reduce-scatter.37.cloned.1.call-done = f32[24,1536]{1,0:T(8,128)} async-done(((f32[768,1536]{1,0:T(8,128)}), f32[24,1536]{1,0:T(8,128)}) %reduce-scatter.37.cloned.1.call-update) | async-done | bytes 147472
  1589.0 112.1 %reduce-scatter.39.cloned.1.call-done = f32[24,1536]{1,0:T(8,128)} async-done(((f32[768,1536]{1,0:T(8,128)}), f32[24,1536]{1,0:T(8,128)}) %reduce-scatter.39.cloned.1.call-update) | async-done | bytes 147472
  1701.1 142.1 %reduce-scatter.29.cloned.1.call-done = f32[48,1536]{1,0:T(8,128)} async-done(((f32[1536,1536]{1,0:T(8,128)}), f32[48,1536]{1,0:T(8,128)}) %reduce-scatter.29.cloned.1.call-update) | async-done | bytes 294928 | tf_op jit(solution)/shard_map/reduce_scatter | solution.py:408
  1843.2 141.1 %reduce-scatter.31.cloned.1.call-done = f32[48,1536]{1,0:T(8,128)} async-done(((f32[1536,1536]{1,0:T(8,128)}), f32[48,1536]{1,0:T(8,128)}) %reduce-scatter.31.cloned.1.call-update) | async-done | bytes 294928 | tf_op jit(solution)/shard_map/reduce_scatter | solution.py:409
  1984.3 141.9 %reduce-scatter.33.cloned.1.call-done = f32[48,1536]{1,0:T(8,128)} async-done(((f32[1536,1536]{1,0:T(8,128)}), f32[48,1536]{1,0:T(8,128)}) %reduce-scatter.33.cloned.1.call-update) | async-done | bytes 294928 | tf_op jit(solution)/shard_map/reduce_scatter | solution.py:412
  (350 shorter events, 285.4 us)
Async XLA Ops:
  7.2 334.1 %copy-start = (bf16[1,2,128,768]{3,2,1,0:T(8,128)(2,1)S(1)}, bf16[1,2,128,768]{3,2,1,0:T(8,128)(2,1)}, u32[]{:S(2)}) copy-start(bf16[1,2,128,768]{3,2,1,0:T(8,128)(2,1)} %param.23) | copy-start | bytes 1179652
  7.2 13.2 copy-start.49
  7.2 73.5 %all-gather.15.cloned.1.call-start = ((), (), s32[]{:S(2)}) async-start(), calls=%async_computation.15 | async-start | bytes 3932160 | tf_op jit(solution)/shard_map/all_gather | solution.py:217
  14.3 131.4 %all-gather.17.cloned.1.call-start = ((), (), s32[]{:S(2)}) async-start(), calls=%async_computation.16 | async-start | bytes 4866048 | tf_op jit(solution)/shard_map/all_gather | solution.py:204
  15.0 195.8 %all-gather.19.cloned.1.call-start = ((), (), s32[]{:S(2)}) async-start(), calls=%async_computation.17 | async-start | bytes 4866048 | tf_op jit(solution)/shard_map/all_gather | solution.py:205
  15.8 260.2 %all-gather.21.cloned.1.call-start = ((), (), s32[]{:S(2)}) async-start(), calls=%async_computation.18 | async-start | bytes 4866048 | tf_op jit(solution)/shard_map/all_gather | solution.py:206
  16.4 324.9 %all-gather.25.cloned.1.call-start = ((), (), s32[]{:S(2)}) async-start(), calls=%async_computation.20 | async-start | bytes 2433024 | tf_op jit(solution)/shard_map/all_gather | solution.py:210
  16.9 384.5 %all-gather.29.cloned.1.call-start = ((), (), s32[]{:S(2)}) async-start(), calls=%async_computation.22 | async-start | bytes 2433024 | tf_op jit(solution)/shard_map/all_gather | solution.py:209
  17.5 449.2 %all-gather.23.cloned.1.call-start = ((), (), s32[]{:S(2)}) async-start(), calls=%async_computation.19 | async-start | bytes 4866048 | tf_op jit(solution)/shard_map/all_gather | solution.py:207
  18.3 513.6 %all-gather.27.cloned.1.call-start = ((), (), s32[]{:S(2)}) async-start(), calls=%async_computation.21 | async-start | bytes 4866048 | tf_op jit(solution)/shard_map/all_gather | solution.py:208
  19.0 578.1 %all-gather.31.cloned.1.call-start = ((), (), s32[]{:S(2)}) async-start(), calls=%async_computation.23 | async-start | bytes 4866048 | tf_op jit(solution)/shard_map/all_gather | solution.py:211
  19.8 616.8 %all-gather.35.cloned.1.call-start = ((), (), s32[]{:S(2)}) async-start(), calls=%async_computation.25 | async-start | bytes 5308416 | tf_op jit(solution)/shard_map/all_gather | solution.py:271
  24.5 190.0 %copy-start.30 = (f32[1024,16]{0,1:T(8,128)}, f32[1024,16]{0,1:T(8,128)S(1)}, u32[]{:S(2)}) copy-start(f32[1024,16]{0,1:T(8,128)S(1)} %get-tuple-element.313) | copy-start | bytes 196612
  215.9 63.7 %copy-start.28 = (bf16[2,512,6,64]{1,3,2,0:T(8,128)(2,1)S(1)}, bf16[2,512,6,64]{1,3,2,0:T(8,128)(2,1)}, u32[]{:S(2)}) copy-start(bf16[2,512,6,64]{1,3,2,0:T(8,128)(2,1)} %custom-call.2) | copy-start | bytes 2359300
  306.9 9.6 copy-start.48
  312.4 154.3 %all-to-all-start = ((bf16[4,256,384]{1,2,0:T(8,128)(2,1)}), bf16[4,256,384]{1,2,0:T(8,128)(2,1)S(1)}, u32[]{:S(2)}, u32[]{:S(2)}) async-start(bf16[4,256,384]{1,2,0:T(8,128)(2,1)} %copy.89), calls=%async_computation | async-start | bytes 1572864 | tf_op jit(solution)/shard_map/all_to_all | solution.py:232
  315.9 386.3 %all-gather.33.cloned.1.call-start = ((), (), s32[]{:S(2)}) async-start(), calls=%async_computation.24 | async-start | bytes 3932160 | tf_op jit(solution)/shard_map/all_gather | solution.py:275
  316.5 712.7 %copy-start.33 = (f32[1536]{0:T(1024)}, f32[1536]{0:T(1024)S(1)}, u32[]{:S(2)}) copy-start(f32[1536]{0:T(1024)S(1)} %convert_element_type.187) | copy-start | bytes 18436
  344.6 122.2 %copy-start.3 = (bf16[256,1536]{1,0:T(8,128)(2,1)S(1)}, bf16[256,1536]{1,0:T(8,128)(2,1)}, u32[]{:S(2)}) copy-start(bf16[256,1536]{1,0:T(8,128)(2,1)} %param.22) | copy-start | bytes 2359300
  471.9 557.3 %copy-start.37 = (f32[256]{0:T(256)}, f32[256]{0:T(256)S(1)}, u32[]{:S(2)}) copy-start(f32[256]{0:T(256)S(1)} %broadcast_multiply_fusion.1) | copy-start | bytes 3076
  473.6 555.6 %copy-start.43 = (f32[256]{0:T(256)}, f32[256]{0:T(256)S(1)}, u32[]{:S(2)}) copy-start(f32[256]{0:T(256)S(1)} %fusion.88) | copy-start | bytes 3076
  473.6 64.8 %copy-start.21 = (bf16[256,1536]{0,1:T(8,128)(2,1)S(1)}, bf16[256,1536]{0,1:T(8,128)(2,1)}, u32[]{:S(2)}) copy-start(bf16[256,1536]{0,1:T(8,128)(2,1)} %copy.92) | copy-start | bytes 2359300
  543.3 474.9 %copy-start.39 = (f32[24,256]{1,0:T(8,128)}, f32[24,256]{1,0:T(8,128)S(1)}, u32[]{:S(2)}) copy-start(f32[24,256]{1,0:T(8,128)S(1)} %get-tuple-element.318) | copy-start | bytes 73732
  547.0 50.1 %copy-start.25 = (bf16[24,64,256]{2,1,0:T(8,128)(2,1)}, bf16[24,64,256]{2,1,0:T(8,128)(2,1)S(1)}, u32[]{:S(2)}) copy-start(bf16[24,64,256]{2,1,0:T(8,128)(2,1)S(1)} %fusion.60) | copy-start | bytes 2359300
  603.8 137.8 %all-gather.37.cloned.1.call-start = ((), (), s32[]{:S(2)}) async-start(), calls=%async_computation.26 | async-start | bytes 5308416 | tf_op jit(solution)/shard_map/all_gather | solution.py:272
  604.4 202.9 %all-gather.41.cloned.1.call-start = ((), (), s32[]{:S(2)}) async-start(), calls=%async_computation.29 | async-start | bytes 3932160 | tf_op jit(solution)/shard_map/all_gather | solution.py:283
  605.6 241.0 %all-gather.39.cloned.1.call-start = ((), (), s32[]{:S(2)}) async-start(), calls=%async_computation.27 | async-start | bytes 5308416 | tf_op jit(solution)/shard_map/all_gather | solution.py:273
  606.2 329.8 %reduce-scatter.19.cloned.1.call-start = ((), (), s32[]{:S(2)}) async-start(), calls=%async_computation.30 | async-start | bytes 3932160 | tf_op jit(solution)/shard_map/reduce_scatter | solution.py:286
  875.6 122.9 %reduce-scatter.17.cloned.1.call-start = ((), (), s32[]{:S(2)}) async-start(), calls=%async_computation.28 | async-start | bytes 3932160 | tf_op jit(solution)/shard_map/reduce_scatter | solution.py:279
  1034.2 23.9 %all-to-all-start.1 = ((bf16[256,4,384]{2,0,1:T(8,128)(2,1)}), bf16[256,4,384]{2,0,1:T(8,128)(2,1)S(1)}, u32[]{:S(2)}, u32[]{:S(2)}) async-start(bf16[256,4,384]{2,0,1:T(8,128)(2,1)} %bitcast.163), calls=%async_computation.3 | async-start | bytes 1572864 | tf_op jit(solution)/shard_map/all_to_all | solution.py:350
  1037.9 244.3 %reduce-scatter.27.cloned.1.call-start = ((), (), s32[]{:S(2)}) async-start(), calls=%async_computation.34 | async-start | bytes 1327104 | tf_op jit(solution)/shard_map/reduce_scatter | solution.py:388
  1085.6 13.1 slice-start.3
  1141.3 14.0 slice-start.3
  1180.5 101.8 %reduce-scatter.25.cloned.1.call-start = ((), (), s32[]{:S(2)}) async-start(), calls=%async_computation.33 | async-start | bytes 1327104 | tf_op jit(solution)/shard_map/reduce_scatter | solution.py:382
  1188.3 109.5 %reduce-scatter.23.cloned.1.call-start = ((), (), s32[]{:S(2)}) async-start(), calls=%async_computation.32 | async-start | bytes 1327104 | tf_op jit(solution)/shard_map/reduce_scatter | solution.py:376
  1194.4 174.1 %reduce-scatter.21.cloned.1.call-start = ((), (), s32[]{:S(2)}) async-start(), calls=%async_computation.31 | async-start | bytes 3932160 | tf_op jit(solution)/shard_map/reduce_scatter | solution.py:365
  1205.8 269.3 %reduce-scatter.35.cloned.1.call-start = ((), (), s32[]{:S(2)}) async-start(), calls=%async_computation.38 | async-start | bytes 15925248 | tf_op jit(solution)/shard_map/reduce_scatter | solution.py:292
  1231.5 357.5 %reduce-scatter.37.cloned.1.call-start = ((), (), s32[]{:S(2)}) async-start(), calls=%async_computation.39 | async-start | bytes 4866048
  1246.1 455.1 %reduce-scatter.39.cloned.1.call-start = ((), (), s32[]{:S(2)}) async-start(), calls=%async_computation.40 | async-start | bytes 4866048
  1261.5 581.7 %reduce-scatter.29.cloned.1.call-start = ((), (), s32[]{:S(2)}) async-start(), calls=%async_computation.35 | async-start | bytes 9732096 | tf_op jit(solution)/shard_map/reduce_scatter | solution.py:408
  1268.1 716.3 %reduce-scatter.31.cloned.1.call-start = ((), (), s32[]{:S(2)}) async-start(), calls=%async_computation.36 | async-start | bytes 9732096 | tf_op jit(solution)/shard_map/reduce_scatter | solution.py:409
  1275.9 850.4 %reduce-scatter.33.cloned.1.call-start = ((), (), s32[]{:S(2)}) async-start(), calls=%async_computation.37 | async-start | bytes 9732096 | tf_op jit(solution)/shard_map/reduce_scatter | solution.py:412
  1300.2 35.1 %all-to-all-start.2 = ((bf16[3,192,384]{2,0,1:T(4,128)(2,1)}), bf16[3,192,384]{2,0,1:T(4,128)(2,1)S(1)}, u32[]{:S(2)}, u32[]{:S(2)}) async-start(bf16[3,192,384]{2,0,1:T(4,128)(2,1)} %copy.99), calls=%async_computation.8 | async-start | bytes 1179648 | tf_op jit(solution)/shard_map/all_to_all | solution.py:395
  1335.4 33.2 %copy-start.4 = (bf16[256,1536]{1,0:T(8,128)(2,1)S(1)}, bf16[256,1536]{1,0:T(8,128)(2,1)}, u32[]{:S(2)}) copy-start(bf16[256,1536]{1,0:T(8,128)(2,1)} %param.22) | copy-start | bytes 2359300
  1335.4 33.2 %copy-start.32 = (f32[1536]{0:T(1024)S(1)}, f32[1536]{0:T(1024)}, u32[]{:S(2)}) copy-start(f32[1536]{0:T(1024)} %copy-done.31) | copy-start | bytes 18436
  1335.4 33.2 %copy-start.36 = (f32[256]{0:T(256)S(1)}, f32[256]{0:T(256)}, u32[]{:S(2)}) copy-start(f32[256]{0:T(256)} %copy-done.35) | copy-start | bytes 3076
  1335.5 35.9 %copy-start.42 = (f32[256]{0:T(256)S(1)}, f32[256]{0:T(256)}, u32[]{:S(2)}) copy-start(f32[256]{0:T(256)} %copy-done.41) | copy-start | bytes 3076
  1368.6 53.0 %copy-start.15 = (bf16[256,1536]{1,0:T(8,128)(2,1)S(1)}, bf16[256,1536]{1,0:T(8,128)(2,1)}, u32[]{:S(2)}) copy-start(bf16[256,1536]{1,0:T(8,128)(2,1)} %reduce-scatter.21.cloned.1.call-done) | copy-start | bytes 2359300
  (53 other events, 228.5 us)
Sparse Core Ops, SparseCore 0:
  14.4 66.2 all-gather.14
  83.5 62.1 all-gather.16
  148.5 62.3 all-gather.18
  213.5 62.3 all-gather.20
  278.6 62.6 all-gather.24
  343.9 57.4 all-gather.28
  404.2 62.4 all-gather.22
  469.5 62.3 all-gather.26
  534.7 62.3 all-gather.30
  598.8 37.7 all-gather.34
  638.7 63.4 all-gather.32
  704.0 37.5 all-gather.36
  743.8 63.4 all-gather.40
  809.0 37.5 all-gather.38
  875.7 60.2 reduce-scatter.18
  938.2 60.2 reduce-scatter.16
  1180.6 35.8 reduce-scatter.26
  1220.5 36.7 reduce-scatter.24
  1261.1 36.7 reduce-scatter.22
  1300.2 68.3 reduce-scatter.20
  1372.6 102.4 reduce-scatter.34
  1482.0 106.9 reduce-scatter.36
  1595.0 106.0 reduce-scatter.38
  1708.5 134.7 reduce-scatter.28
  1849.7 134.5 reduce-scatter.30
  1991.7 134.5 reduce-scatter.32
where the time goes:
time: 2150 us; the launch traced here: 2130 us
  waiting for transfers between devices  1620 us (75%)
  matrix products  266 us (12%)
  local copies, waits for them, and re-layouts  95.5 us (4%)
  other arithmetic  68.1 us (3%)
  blocking collectives  43.1 us (2%)
    unnamed x28, waiting for transfers between devices  229 us
    reduce_scatter x1, waiting for transfers between devices, local(): lax.psum_scatter(grad_self_out_full, ('dp', 'seq'), scatter_dimension=0,...  142 us
    reduce_scatter x1, waiting for transfers between devices, local(): lax.psum_scatter(grad_cross_out_full, ('dp', 'seq'), scatter_dimension=0,...  142 us
    reduce_scatter x1, waiting for transfers between devices, local(): lax.psum_scatter(grad_cross_query_full, ('dp', 'seq'), scatter_dimension=...  141 us
    all_gather x1, waiting for transfers between devices, local(): all_norm = lax.all_gather(norm_three, 'seq', axis=0, tiled=True)  65.7 us
    all_gather x1, waiting for transfers between devices, local(): lax.all_gather(self_query, ('dp', 'seq'), axis=0, tiled=True)  65 us
    all_gather x1, waiting for transfers between devices, local(): lax.all_gather(self_key, ('dp', 'seq'), axis=0, tiled=True)  61.5 us
    all_gather x1, waiting for transfers between devices, local(): lax.all_gather(self_value, ('dp', 'seq'), axis=0, tiled=True)  60 us
  transfers between devices with their start and end apart: 29, of which 26 were waited for; matrix products, arithmetic and copies ran while one was open for 11% of the time, Pallas kernels for 0%

commit v1 on v0

--- a/solution.py
+++ b/solution.py
@@ -1,6 +1,8 @@
 import jax
 import jax.numpy as jnp
 from jax import lax
+from jax.experimental import pallas as pl
+from jax.experimental.pallas import tpu as pltpu
 from jax.sharding import PartitionSpec as P
 
 HEADS = 24
@@ -20,8 +22,7 @@
     return centered * lax.rsqrt(variance + EPSILON) * gain_vector
 
 
-def layout(lengths, length):
-    row_ids = jnp.arange(length, dtype=jnp.int32)
+def layout(lengths, row_ids):
     first_end = lengths[0]
     second_end = lengths[0] + lengths[1]
     segment = jnp.where(row_ids < first_end, 0, jnp.where(row_ids < second_end, 1, 2)).astype(
@@ -157,6 +158,131 @@
         backward_block, (initial, initial), jnp.arange(length // block_rows)
     )
     return (grad_query.reshape(length, heads_dev, head_dim), grad_keys, grad_values)
+
+
+def swap_core(values):
+    return lax.ppermute(values, "dp", [(d, d ^ 1) for d in range(lax.axis_size("dp"))])
+
+
+def swap_x(values):
+    return lax.ppermute(values, "dp", [(d, d ^ 2) for d in range(lax.axis_size("dp"))])
+
+
+def shift_y(values, step):
+    size = lax.axis_size("dp")
+    return lax.ppermute(values, "dp", [(d, (d + 4 * step) % size) for d in range(size)])
+
+
+def shift_seq(values, step):
+    size = lax.axis_size("seq")
+    return lax.ppermute(values, "seq", [(s, (s + step) % size) for s in range(size)])
+
+
+def gather_seq(values):
+    pieces = [values]
+    for _ in range(lax.axis_size("seq") - 1):
+        pieces.append(shift_seq(pieces[-1], 1))
+    return pieces
+
+
+def reduce_seq(blocks):
+    total = blocks[-1]
+    for block in blocks[-2::-1]:
+        total = add_low(shift_seq(total, -1), block)
+    return total
+
+
+def add_wide(left, right):
+    return left.astype(jnp.float32) + right.astype(jnp.float32)
+
+
+def add_low(left, right):
+    return add_wide(left, right).astype(jnp.bfloat16)
+
+
+def gather_dp(first, second):
+    y_size = lax.axis_size("dp") // 4
+    held = {(0, 0, 0, 0): first, (1, 0, 0, 0): second}
+    held[0, 0, 0, 1] = swap_x(first)
+    for y in range(1, y_size):
+        for x in range(2):
+            held[0, 0, y, x] = shift_y(held[0, 0, y - 1, x], 1)
+    for y in range(1, y_size):
+        held[1, 0, y, 0] = shift_y(held[1, 0, y - 1, 0], 1)
+    for y in range(y_size):
+        held[1, 0, y, 1] = swap_x(held[1, 0, y, 0])
+    for half, core, y, x in list(held):
+        held[half, 1, y, x] = swap_core(held[half, 0, y, x])
+    return held
+
+
+def pick(values, index, axis):
+    if isinstance(index, int):
+        return lax.index_in_dim(values, index, axis, keepdims=False)
+    return lax.dynamic_index_in_dim(values, index, axis, keepdims=False)
+
+
+def reduce_dp(first, second, y_place, x_place):
+    y_size = first.shape[0]
+    total = pick(first, y_place(y_size - 1), 0)
+    for y in range(y_size - 2, -1, -1):
+        total = add_low(shift_y(total, -1), pick(first, y_place(y), 0))
+    first_sum = add_wide(pick(total, x_place(0), 0), swap_x(pick(total, x_place(1), 0)))
+    rows = add_low(pick(second, x_place(0), 1), swap_x(pick(second, x_place(1), 1)))
+    total = pick(rows, y_place(y_size - 1), 0)
+    for y in range(y_size - 2, -1, -1):
+        total = add_wide(shift_y(total.astype(jnp.bfloat16), -1), pick(rows, y_place(y), 0))
+    return first_sum, total
+
+
+def assemble(pieces, out_shapes, copies):
+    count = len(pieces)
+
+    def body(*refs):
+        sources, targets = refs[:count], refs[count : count + len(out_shapes)]
+        held, loaded, stored = (
+            refs[count + len(out_shapes) : -2],
+            refs[-2],
+            refs[-1],
+        )
+        dp_place, seq_place = lax.axis_index("dp"), lax.axis_index("seq")
+        loads = [
+            pltpu.make_async_copy(sources[n], held[n], loaded.at[n]) for n in range(count)
+        ]
+        for load in loads:
+            load.start()
+        stores = []
+        for n in range(count):
+            loads[n].wait()
+            for number, (piece, source, out, target) in enumerate(copies):
+                if piece == n:
+                    stores.append(
+                        pltpu.make_async_copy(
+                            held[n].at[source],
+                            targets[out].at[target(dp_place, seq_place)],
+                            stored.at[number],
+                        )
+                    )
+                    stores[-1].start()
+        for store in stores:
+            store.wait()
+
+    moved = sum(2 * p.size * p.dtype.itemsize for p in pieces)
+    return pl.pallas_call(
+        body,
+        out_shape=[jax.ShapeDtypeStruct(s, jnp.bfloat16) for s in out_shapes],
+        in_specs=[pl.BlockSpec(memory_space=pl.ANY)] * len(pieces),
+        out_specs=[pl.BlockSpec(memory_space=pl.ANY)] * len(out_shapes),
+        scratch_shapes=[pltpu.VMEM(p.shape, p.dtype) for p in pieces]
+        + [pltpu.SemaphoreType.DMA((count,)), pltpu.SemaphoreType.DMA((len(copies),))],
+        compiler_params=pltpu.CompilerParams(vmem_limit_bytes=32 << 20),
+        cost_estimate=pl.CostEstimate(flops=0, bytes_accessed=moved, transcendentals=0),
+    )(*pieces)
+
+
+def dp_block(core, y, x, dp_place):
+    size = lax.axis_size("dp")
+    return ((dp_place + size - 4 * y) % size) ^ (core + 2 * x)
 
 
 def local(
@@ -180,57 +306,111 @@
     cotangent,
 ):
     rows_dev, width = tokens.shape
-    seq_parts = lax.axis_size("seq")
-    length = rows_dev * seq_parts
-    heads_dev = HEADS // seq_parts
+    dp_size, seq_size = lax.axis_size("dp"), lax.axis_size("seq")
+    dp_place, seq_place = lax.axis_index("dp"), lax.axis_index("seq")
+    y_size = dp_size // 4
+    y_own, x_own, core_own = dp_place // 4, (dp_place // 2) % 2, dp_place % 2
+    length = rows_dev * seq_size
+    heads_dev = HEADS // seq_size
     head_width = heads_dev * HDIM
     block_rows = min(512, length)
     scaling = HDIM ** (-0.5)
-    segment, position = layout(item_lengths[0], length)
-    row_start = lax.axis_index("seq") * rows_dev
-    col_start = lax.axis_index("seq") * head_width
-    row_segment = lax.dynamic_slice_in_dim(segment, row_start, rows_dev, 0)
+    part_rows = self_query.shape[0]
+    row_ids = jnp.concatenate(
+        [
+            (seq_place + seq_size - k) % seq_size * rows_dev + jnp.arange(rows_dev, dtype=jnp.int32)
+            for k in range(seq_size)
+        ]
+    )
+    segment, position = layout(item_lengths[0], row_ids)
+    row_segment = segment[:rows_dev]
     cosine, sine_table = rotary_tables(position)
-    (
-        full_query,
-        full_key,
-        full_value,
-        full_out,
-        full_cross_query,
-        full_cross_key,
-        full_cross_value,
-        full_cross_out,
-    ) = (
-        lax.all_gather(self_query, ("dp", "seq"), axis=0, tiled=True),
-        lax.all_gather(self_key, ("dp", "seq"), axis=0, tiled=True),
-        lax.all_gather(self_value, ("dp", "seq"), axis=0, tiled=True),
-        lax.all_gather(self_out, ("dp", "seq"), axis=0, tiled=True),
-        lax.all_gather(cross_query, ("dp", "seq"), axis=0, tiled=True),
-        lax.all_gather(cross_key, ("dp", "seq"), axis=0, tiled=True),
-        lax.all_gather(cross_value, ("dp", "seq"), axis=0, tiled=True),
-        lax.all_gather(cross_out, ("dp", "seq"), axis=0, tiled=True),
-    )
+
+    def seq_order(values):
+        blocks = values.reshape((seq_size, -1) + values.shape[1:])
+        return jnp.concatenate(
+            [pick(blocks, (seq_place + seq_size - k) % seq_size, 0) for k in range(seq_size)]
+        )
+
+    qkv_parts = jnp.stack([self_query, self_key, self_value]).reshape(
+        3, part_rows, seq_size, head_width
+    )
+    qkv_parts = lax.all_to_all(
+        qkv_parts.transpose(2, 1, 0, 3), "seq", split_axis=0, concat_axis=0, tiled=True
+    ).reshape(seq_size * part_rows, 3 * head_width)
+    half_rows = seq_size * part_rows // 2
+    held = gather_dp(qkv_parts[:half_rows], qkv_parts[half_rows:])
+    places = list(held)
+    qkv_cols = assemble(
+        [held[p] for p in places],
+        [(dp_size, 2, half_rows, 3 * head_width)],
+        [
+            (n, (), 0, lambda d, s, h=half, p=(core, y, x): (dp_block(*p, d), h))
+            for n, (half, core, y, x) in enumerate(places)
+        ],
+    )[0].reshape(width, 3 * head_width)
+
+    feed_parts = jnp.stack([feed_gate, feed_up, feed_down])
+    half_units = feed_parts.shape[1] // 2
+    held = gather_dp(feed_parts[:, :half_units], feed_parts[:, half_units:])
+    places = [
+        (half, core, y, x)
+        for core in range(2)
+        for half in range(2)
+        for y in range(y_size)
+        for x in range(2)
+    ]
+    unit_gate_up = jnp.concatenate(
+        [held[p][0] for p in places] + [held[p][1] for p in places], axis=0
+    )
+    unit_down = jnp.concatenate([held[p][2] for p in places], axis=0)
+    units = unit_down.shape[0]
+
+    part_groups = (
+        jnp.stack([self_out, cross_query]),
+        jnp.stack([cross_out, jnp.concatenate([cross_key, cross_value])]),
+    )
+    held = gather_dp(*(jnp.stack(gather_seq(group)) for group in part_groups))
+    whole = []
+    for group in range(2):
+        places = [p for p in held if p[0] == group]
+        whole += assemble(
+            [held[p] for p in places],
+            [(dp_size, seq_size, part_rows, width)] * 2,
+            [
+                (
+                    n,
+                    (k, weight),
+                    weight,
+                    lambda d, s, p=p[1:], k=k: (dp_block(*p, d), (s + seq_size - k) % seq_size),
+                )
+                for n, p in enumerate(places)
+                for k in range(seq_size)
+                for weight in range(2)
+            ],
+        )
+    full_out, full_cross_query, full_cross_out = (w.reshape(width, width) for w in whole[:3])
+    full_cross_kv = whole[3].reshape(dp_size * seq_size, 2, part_rows // 2, width)
+    full_cross_key = full_cross_kv[:, 0].reshape(-1, width)
+    full_cross_value = full_cross_kv[:, 1].reshape(-1, width)
+
     token_values = tokens.astype(jnp.float32)
     norm_one, norm_one_back = jax.vjp(layer_norm, token_values, gain_self.astype(jnp.float32))
     norm_one = norm_one.astype(jnp.bfloat16)
     head_shape = (length, heads_dev, HDIM)
-    all_norm_one = lax.all_gather(norm_one, "seq", axis=0, tiled=True)
-    query_cols = lax.dynamic_slice_in_dim(full_query, col_start, head_width, 1)
-    key_cols = lax.dynamic_slice_in_dim(full_key, col_start, head_width, 1)
-    value_cols = lax.dynamic_slice_in_dim(full_value, col_start, head_width, 1)
-
-    def project_heads(weight):
-        projected = matmul(all_norm_one, weight).reshape(head_shape)
-        return rotate(projected, cosine, sine_table).astype(jnp.bfloat16)
-
-    head_queries = project_heads(query_cols)
-    head_keys = project_heads(key_cols)
-    head_values = matmul(all_norm_one, value_cols).astype(jnp.bfloat16).reshape(head_shape)
+    all_norm_one = jnp.concatenate(gather_seq(norm_one))
+    projected = matmul(all_norm_one, qkv_cols)
+    head_queries = rotate(projected[:, :head_width].reshape(head_shape), cosine, sine_table)
+    head_queries = head_queries.astype(jnp.bfloat16)
+    head_keys = rotate(
+        projected[:, head_width : 2 * head_width].reshape(head_shape), cosine, sine_table
+    ).astype(jnp.bfloat16)
+    head_values = projected[:, 2 * head_width :].astype(jnp.bfloat16).reshape(head_shape)
     head_attended, log_total = heads_forward(
         head_queries, head_keys, head_values, segment, block_rows
     )
     attended = lax.all_to_all(
-        head_attended.astype(jnp.bfloat16), "seq", split_axis=0, concat_axis=1, tiled=True
+        seq_order(head_attended.astype(jnp.bfloat16)), "seq", split_axis=0, concat_axis=1, tiled=True
     )
     first_sum = token_values + matmul(attended, full_out)
     norm_two, norm_two_back = jax.vjp(layer_norm, first_sum, gain_cross.astype(jnp.float32))
@@ -267,45 +447,57 @@
     valid_rows = (row_segment < 2).astype(jnp.float32)[:, None]
     grad_output = cotangent.astype(jnp.float32) * valid_rows
     grad_output_low = grad_output.astype(jnp.bfloat16)
-    unit_gate, unit_up, unit_down = (
-        lax.all_gather(feed_gate, "dp", axis=0, tiled=True),
-        lax.all_gather(feed_up, "dp", axis=0, tiled=True),
-        lax.all_gather(feed_down, "dp", axis=0, tiled=True),
-    )
-    all_norm = lax.all_gather(norm_three, "seq", axis=0, tiled=True)
-    gate_proj = contract_cols(all_norm, unit_gate)
-    up_proj = contract_cols(all_norm, unit_up)
+    all_norm = jnp.concatenate(gather_seq(norm_three))
+    all_grad = jnp.concatenate(gather_seq(grad_output_low))
+    gate_up = contract_cols(all_norm, unit_gate_up)
+    gate_proj, up_proj = gate_up[:, :units], gate_up[:, units:]
     activation = (jax.nn.silu(gate_proj) * up_proj).astype(jnp.bfloat16)
-    feed_result = lax.psum_scatter(
-        matmul(activation, unit_down).astype(jnp.bfloat16), "seq", scatter_dimension=0, tiled=True
-    ).astype(jnp.float32)
+    feed_partial = matmul(activation, unit_down).astype(jnp.bfloat16)
+    grad_activation = contract_cols(all_grad, unit_down)
+    grad_gate_up = jnp.concatenate(gate_backward(gate_proj, up_proj, grad_activation), axis=1)
+    norm_partial = matmul(grad_gate_up, unit_gate_up).astype(jnp.bfloat16)
+
+    def seq_blocks(values):
+        return [values[k * rows_dev : (k + 1) * rows_dev] for k in range(seq_size)]
+
+    grad_norm_three = reduce_seq(seq_blocks(norm_partial)).astype(jnp.float32)
+    feed_result = reduce_seq(seq_blocks(feed_partial)).astype(jnp.float32)
     output = (second_sum + feed_result).astype(jnp.bfloat16)
-    all_grad = lax.all_gather(grad_output_low, "seq", axis=0, tiled=True)
-    grad_activation = contract_cols(all_grad, unit_down)
-    grad_gate, grad_up = gate_backward(gate_proj, up_proj, grad_activation)
-    grad_norm_three = lax.psum_scatter(
-        (matmul(grad_gate, unit_gate) + matmul(grad_up, unit_up)).astype(jnp.bfloat16),
-        "seq",
-        scatter_dimension=0,
-        tiled=True,
-    ).astype(jnp.float32)
-    feed_grads = lax.psum_scatter(
-        jnp.stack(
-            [
-                contract_rows(grad_gate, all_norm),
-                contract_rows(grad_up, all_norm),
-                contract_rows(activation, all_grad),
-            ],
-            axis=1,
-        ).astype(jnp.bfloat16),
-        "dp",
-        scatter_dimension=0,
-        tiled=True,
-    ).astype(jnp.float32)
+
+    def unit_grad(terms):
+        terms = terms.astype(jnp.bfloat16).reshape(2, 2, y_size, 2, half_units, width)
+        chip = add_low(terms[0], swap_core(terms[1]))
+        return jnp.concatenate(reduce_dp(chip[0], chip[1], lambda y: y, lambda x: x))
+
+    grad_feed_down = unit_grad(contract_rows(activation, all_grad))
+    grad_feed_gate = unit_grad(contract_rows(grad_gate_up[:, :units], all_norm))
+    grad_feed_up = unit_grad(contract_rows(grad_gate_up[:, units:], all_norm))
+
+    def own_blocks(terms):
+        terms = terms.astype(jnp.bfloat16).reshape(y_size, 2, 2, 2, -1, terms.shape[1])
+        sent = swap_core(pick(terms, 1 - core_own, 2))
+        chip = add_low(pick(terms, core_own, 2), sent)
+        halves = reduce_dp(
+            chip[:, :, 0],
+            chip[:, :, 1],
+            lambda y: (y_own + y_size - y) % y_size,
+            lambda x: x_own if x == 0 else 1 - x_own,
+        )
+        return jnp.concatenate([h.astype(jnp.bfloat16) for h in halves])
+
+    def own_rows(terms):
+        blocks = own_blocks(terms).reshape(seq_size, -1, terms.shape[1])
+        return jnp.sum(
+            lax.all_to_all(blocks, "seq", split_axis=0, concat_axis=0, tiled=True).astype(
+                jnp.float32
+            ),
+            axis=0,
+        )
+
     grad_second, grad_gain_feed = norm_three_back(grad_norm_three)
     grad_second = grad_second + grad_output
     second_low = grad_second.astype(jnp.bfloat16)
-    grad_cross_out_full = contract_rows(cross_mixed, second_low)
+    grad_cross_out = own_rows(contract_rows(cross_mixed, second_low))
     grad_mixed = (
         contract_cols(second_low, full_cross_out)
         .astype(jnp.bfloat16)
@@ -333,102 +525,66 @@
         grad_mixed,
         preferred_element_type=jnp.float32,
     ).reshape(memory_rows, width)
-    memory_wide = memory.astype(jnp.float32)
-    grad_cross_key_full = lax.dot_general(
-        memory_wide, grad_memory_keys, (((0,), (0,)), ((), ())), precision=HIGHEST
-    )
-    grad_cross_value_full = lax.dot_general(
-        memory_wide, grad_memory_values, (((0,), (0,)), ((), ())), precision=HIGHEST
-    )
-    grad_cross_query_full = contract_rows(norm_two, grad_cross_queries)
+    grad_cross_key = own_rows(contract_rows(memory, grad_memory_keys.astype(jnp.bfloat16)))
+    grad_cross_value = own_rows(contract_rows(memory, grad_memory_values.astype(jnp.bfloat16)))
+    grad_cross_query = own_rows(contract_rows(norm_two, grad_cross_queries))
     grad_norm_two = contract_cols(grad_cross_queries, full_cross_query)
     grad_first, grad_gain_cross = norm_two_back(grad_norm_two)
     grad_first = grad_first + grad_second
     first_low = grad_first.astype(jnp.bfloat16)
-    grad_self_out_full = contract_rows(attended, first_low)
+    grad_self_out = own_rows(contract_rows(attended, first_low))
     grad_attended = contract_cols(first_low, full_out).astype(jnp.bfloat16)
-    head_grad = lax.all_to_all(
-        grad_attended, "seq", split_axis=1, concat_axis=0, tiled=True
+    head_grad = seq_order(
+        lax.all_to_all(grad_attended, "seq", split_axis=1, concat_axis=0, tiled=True)
     ).reshape(head_shape)
     grad_head_queries, grad_head_keys, grad_head_values = heads_backward(
         head_queries, head_keys, head_values, head_grad, log_total, segment, block_rows
     )
-    turned_queries = (
-        rotate(grad_head_queries, cosine, -sine_table)
-        .reshape(length, head_width)
-        .astype(jnp.bfloat16)
-    )
-    turned_keys = (
-        rotate(grad_head_keys, cosine, -sine_table).reshape(length, head_width).astype(jnp.bfloat16)
-    )
-    flat_values = grad_head_values.reshape(length, head_width).astype(jnp.bfloat16)
-    grad_norm_one = lax.psum_scatter(
-        (
-            contract_cols(turned_queries, query_cols)
-            + contract_cols(turned_keys, key_cols)
-            + contract_cols(flat_values, value_cols)
-        ).astype(jnp.bfloat16),
-        "seq",
-        scatter_dimension=0,
-        tiled=True,
+    turned = jnp.concatenate(
+        [
+            rotate(grad_head_queries, cosine, -sine_table).reshape(length, head_width),
+            rotate(grad_head_keys, cosine, -sine_table).reshape(length, head_width),
+            grad_head_values.reshape(length, head_width),
+        ],
+        axis=1,
+    ).astype(jnp.bfloat16)
+    grad_norm_one = reduce_seq(
+        seq_blocks(contract_cols(turned, qkv_cols).astype(jnp.bfloat16))
     ).astype(jnp.float32)
-    column_sums = (
-        lax.psum_scatter(
-            contract_rows(all_norm_one, turned_queries).astype(jnp.bfloat16),
-            "dp",
-            scatter_dimension=0,
-            tiled=True,
-        ).astype(jnp.float32),
-        lax.psum_scatter(
-            contract_rows(all_norm_one, turned_keys).astype(jnp.bfloat16),
-            "dp",
-            scatter_dimension=0,
-            tiled=True,
-        ).astype(jnp.float32),
-        lax.psum_scatter(
-            contract_rows(all_norm_one, flat_values).astype(jnp.bfloat16),
-            "dp",
-            scatter_dimension=0,
-            tiled=True,
-        ).astype(jnp.float32),
-    )
-    placed = lax.all_to_all(
-        jnp.stack([column_sums[0], column_sums[1], column_sums[2]]).astype(jnp.bfloat16),
-        "seq",
-        split_axis=1,
-        concat_axis=2,
-        tiled=True,
-    ).astype(jnp.float32)
+    qkv_sums = own_blocks(contract_rows(all_norm_one, turned)).reshape(
+        seq_size, part_rows, 3, head_width
+    )
+    placed = lax.all_to_all(qkv_sums, "seq", split_axis=0, concat_axis=0, tiled=True)
+    placed = placed.transpose(2, 1, 0, 3).reshape(3, part_rows, width).astype(jnp.float32)
     grad_tokens_wide, grad_gain_self = norm_one_back(grad_norm_one)
     grad_tokens = (grad_tokens_wide + grad_first).astype(jnp.bfloat16)
-    remaining = (
-        lax.psum_scatter(grad_gain_self, ("dp", "seq"), scatter_dimension=0, tiled=True),
-        lax.psum_scatter(grad_gain_cross, ("dp", "seq"), scatter_dimension=0, tiled=True),
-        lax.psum_scatter(grad_gain_feed, ("dp", "seq"), scatter_dimension=0, tiled=True),
-        lax.psum_scatter(grad_self_out_full, ("dp", "seq"), scatter_dimension=0, tiled=True),
-        lax.psum_scatter(grad_cross_query_full, ("dp", "seq"), scatter_dimension=0, tiled=True),
-        lax.psum_scatter(grad_cross_key_full, ("dp", "seq"), scatter_dimension=0, tiled=True),
-        lax.psum_scatter(grad_cross_value_full, ("dp", "seq"), scatter_dimension=0, tiled=True),
-        lax.psum_scatter(grad_cross_out_full, ("dp", "seq"), scatter_dimension=0, tiled=True),
-    )
-    projection_grads = (placed[0], placed[1], placed[2])
+
+    def own_gain(terms):
+        terms = terms.reshape(dp_size * seq_size, -1)
+        return jnp.sum(
+            lax.all_to_all(terms, ("dp", "seq"), split_axis=0, concat_axis=0, tiled=True), axis=0
+        )
+
+    later = own_gain(jnp.stack([grad_gain_cross, grad_gain_feed]).reshape(
+        2, dp_size * seq_size, -1).transpose(1, 0, 2))
+    gain_rows = later.shape[0] // 2
     return (
         output,
         grad_tokens,
-        remaining[0],
-        remaining[1],
-        remaining[2],
-        projection_grads[0],
-        projection_grads[1],
-        projection_grads[2],
-        remaining[3],
-        remaining[4],
-        remaining[5],
-        remaining[6],
-        remaining[7],
-        feed_grads[:, 0, :],
-        feed_grads[:, 1, :],
-        feed_grads[:, 2, :],
+        own_gain(grad_gain_self),
+        later[:gain_rows],
+        later[gain_rows:],
+        placed[0],
+        placed[1],
+        placed[2],
+        grad_self_out,
+        grad_cross_query,
+        grad_cross_key,
+        grad_cross_value,
+        grad_cross_out,
+        grad_feed_gate,
+        grad_feed_up,
+        grad_feed_down,
     )
 
 

time: 2150 us -> 1130 us (0.53)
  waiting for transfers between devices: 1620 us -> 416 us
  starting transfers between devices: 14.2 us -> 150 us
  local copies, waits for them, and re-layouts: 95.5 us -> 182 us
  matrix products: 266 us -> 212 us
  blocking collectives: 43.1 us -> 0 us
  other arithmetic: 68.1 us -> 110 us
  Pallas kernels: 0 us -> 36.2 us
    all_gather x14 -> x0, waiting for transfers between devices: 710 us -> none  [the longest x1 65.7 us: local(): all_norm = lax.all_gather(norm_three, 'seq', axis=0, tiled=True)]
    reduce_scatter x10 -> x0, waiting for transfers between devices: 633 us -> none  [the longest x1 142 us: local(): lax.psum_scatter(grad_self_out_full, ('dp', 'seq'), scatter_dimension=0,...]
    ppermute x0 -> x111, waiting for transfers between devices: none -> 353 us  [the longest x24 182 us: shift_seq(): lax.ppermute(values, 'seq', [(s, (s + step) % size) for s in range(size)])]
    unnamed x28 -> x0, waiting for transfers between devices: 229 us -> none
    ppermute x0 -> x111, starting transfers between devices: none -> 96.7 us  [the longest x24 40.6 us: shift_seq(): lax.ppermute(values, 'seq', [(s, (s + step) % size) for s in range(size)])]
    unnamed x1 -> x0, blocking collectives: 43.1 us -> none
    all_to_all x2 -> x10, starting transfers between devices: 8.1 us -> 49.6 us  [the longest x5 20.1 us: own_rows(): lax.all_to_all(blocks, 'seq', split_axis=0, concat_axis=0, tiled=True)]
    pallas_call x0 -> x3, Pallas kernels: none -> 36.2 us  [assemble(): pl.pallas_call(body, out_shape=[jax.ShapeDtypeStruct(s, jnp.bfloat16) for...]
  transfers between devices with their start and end apart: 29 -> 122, of which waited for: 26 -> 51; matrix products, arithmetic and copies ran while one was open for 11% -> 39% of each run, Pallas kernels for 0% -> 3%
where the time goes in v1:
time: 1130 us; the launch traced here: 1120 us
  waiting for transfers between devices  416 us (37%)
  matrix products  212 us (19%)
  local copies, waits for them, and re-layouts  182 us (16%)
  starting transfers between devices  150 us (13%)
  other arithmetic  110 us (10%)
  Pallas kernels  36.2 us (3%)
    ppermute x24, waiting for transfers between devices, shift_seq(): lax.ppermute(values, 'seq', [(s, (s + step) % size) for s in range(size)])  182 us
    ppermute x27, waiting for transfers between devices, shift_y(): lax.ppermute(values, 'dp', [(d, (d + 4 * step) % size) for d in range(siz...  92.9 us
    ppermute x27, waiting for transfers between devices, swap_x(): lax.ppermute(values, 'dp', [(d, d ^ 2) for d in range(lax.axis_size('dp'))])  77.7 us
    unnamed x369, local copies, waits for them, and re-layouts  60.3 us
    dot_general x6, matrix products, contract_cols(): lax.dot_general(left, right, (((1,), (1,)), ((), ())), preferred_element_...  41.4 us
    ppermute x24, starting transfers between devices, shift_seq(): lax.ppermute(values, 'seq', [(s, (s + step) % size) for s in range(size)])  40.6 us
    all_to_all x5, waiting for transfers between devices, own_rows(): lax.all_to_all(blocks, 'seq', split_axis=0, concat_axis=0, tiled=True)  36.8 us
    pallas_call x3, Pallas kernels, assemble(): pl.pallas_call(body, out_shape=[jax.ShapeDtypeStruct(s, jnp.bfloat16) for...  36.2 us
  transfers between devices with their start and end apart: 122, of which 51 were waited for; matrix products, arithmetic and copies ran while one was open for 39% of the time, Pallas kernels for 3%

profile of v1, /device:TPU:0, one launch (start us, length us, event | category | flops | bytes accessed | tf_op | source)
XLA Modules:
  0.0 1119.3 jit_solution(16035892937896996269)
XLA Ops:
  33.9 6.3 collective-permute-done.27
  42.2 10.1 all-to-all-done
  75.8 16.5 %collective-permute-done.5.refs_4_ = bf16[96,1152]{1,0:T(8,128)(2,1)S(1)} collective-permute-done((bf16[96,1152]{1,0:T(8,128)(2,1)S(1)}, bf16[96,1152]{1,0:T(8,128)(2,1)S(1)}, u32[]{:S(2)}, u32[]{:S(2)}) %collective-permute-start.5) | collective-permute-done | bytes 221216 | tf_op jit(solution)/shard_map/ppermute | solution.py:173
  96.7 9.6 shard_map.297
  109.1 9.8 collective-permute-done
  118.9 16.5 %collective-permute-done.57 = bf16[256,1536]{1,0:T(8,128)(2,1)} collective-permute-done((bf16[256,1536]{1,0:T(8,128)(2,1)S(1)}, bf16[256,1536]{1,0:T(8,128)(2,1)}, u32[]{:S(2)}, u32[]{:S(2)}) %collective-permute-start.57) | collective-permute-done | bytes 786464 | tf_op jit(solution)/shard_map/ppermute | solution.py:178
  137.6 19.2 %collective-permute-done.45 = bf16[3,96,1536]{2,1,0:T(8,128)(2,1)S(1)} collective-permute-done((bf16[3,96,1536]{2,1,0:T(8,128)(2,1)S(1)}, bf16[3,96,1536]{2,1,0:T(8,128)(2,1)S(1)}, u32[]{:S(2)}, u32[]{:S(2)}) %collective-permute-start.45) | collective-permute-done | bytes 884768 | tf_op jit(solution)/shard_map/ppermute | solution.py:168
  162.9 27.1 %collective-permute-done.2 = bf16[256,1536]{1,0:T(8,128)(2,1)S(1)} collective-permute-done((bf16[256,1536]{1,0:T(8,128)(2,1)S(1)}, bf16[256,1536]{1,0:T(8,128)(2,1)S(1)}, u32[]{:S(2)}, u32[]{:S(2)}) %collective-permute-start.2) | collective-permute-done | bytes 786464 | tf_op jit(solution)/shard_map/ppermute | solution.py:178
  210.1 28.8 %while.27 = (s32[]{:T(128)}, bf16[2,512,6,64]{1,3,2,0:T(8,128)(2,1)}, f32[2,6,512]{2,1,0:T(8,128)}, s32[2]{0:T(128)S(1)}, s32[1024]{0:T(1024)S(1)}, /*index=5*/b...) while((s32[]{:T(128)}, ...), condition=%wide.region_5.6_spmd, body=%wide.region_2.5_spmd.sunk | while | flops 843576320 | bytes 45858000 | solution.py:112
  280.3 14.7 %collective-permute-done.30.refs_1_ = bf16[4,2,48,1536]{3,2,1,0:T(8,128)(2,1)} collective-permute-done((bf16[4,2,48,1536]{3,2,1,0:T(8,128)(2,1)S(1)}, bf16[4,2,48,1536]{3,2,1,0:T(8,128)(2,1)}, u32[]{:S(2)}, u32[]{:S(2)}) %collective-permute-start.30) | collective-permute-done | bytes 1179680 | tf_op jit(solution)/shard_map/ppermute | solution.py:173
  295.5 24.1 %collective-permute-done.22.refs_3_ = bf16[4,2,48,1536]{3,2,1,0:T(8,128)(2,1)} collective-permute-done((bf16[4,2,48,1536]{3,2,1,0:T(8,128)(2,1)}, bf16[4,2,48,1536]{3,2,1,0:T(8,128)(2,1)}, u32[]{:S(2)}, u32[]{:S(2)}) %collective-permute-start.22) | collective-permute-done | bytes 1179680 | tf_op jit(solution)/shard_map/ppermute | solution.py:173
  333.3 13.4 %shard_map.298 = (bf16[8,4,48,1536]{3,2,1,0:T(8,128)(2,1)S(1)}, bf16[8,4,48,1536]{3,2,1,0:T(8,128)(2,1)S(1)}) custom-call(bf16[4,2,48,1536]{3,2,1,0:T(8,128)(2,1)S(1)} %pad_maximum_fusion.5.refs_0_, bf16[4,2,48,1536]{3,2,1,0:T(8,128)(2,1)} %collective-permute-done.20.refs_1_, bf16[4,2,48,1536]{3,2,1,0:T(8,128)(2,1)} %collective-permute-done.21.refs_2_, ...), custom_call_target="tpu_custom_call" | custom-call | bytes 18874368 | tf_op jit(solution)/shard_map/pallas_call | solution.py:271
  352.6 13.2 %shard_map.299 = (bf16[8,4,48,1536]{3,2,1,0:T(8,128)(2,1)S(1)}, bf16[8,4,48,1536]{3,2,1,0:T(8,128)(2,1)S(1)}) custom-call(bf16[4,2,48,1536]{3,2,1,0:T(8,128)(2,1)S(1)} %pad_maximum_fusion.6.refs_0_, bf16[4,2,48,1536]{3,2,1,0:T(8,128)(2,1)} %collective-permute-done.30.refs_1_, bf16[4,2,48,1536]{3,2,1,0:T(8,128)(2,1)} %collective-permute-done.31.refs_2_, ...), custom_call_target="tpu_custom_call" | custom-call | bytes 18874368 | tf_op jit(solution)/shard_map/pallas_call | solution.py:271
  386.8 16.7 %collective-permute-done.37 = bf16[256,1536]{1,0:T(8,128)(2,1)S(1)} collective-permute-done((bf16[256,1536]{1,0:T(8,128)(2,1)S(1)}, bf16[256,1536]{1,0:T(8,128)(2,1)S(1)}, u32[]{:S(2)}, u32[]{:S(2)}) %collective-permute-start.37) | collective-permute-done | bytes 786464 | tf_op jit(solution)/shard_map/ppermute | solution.py:178
  406.6 17.3 %collective-permute-done.38 = bf16[256,1536]{1,0:T(8,128)(2,1)S(1)} collective-permute-done((bf16[256,1536]{1,0:T(8,128)(2,1)S(1)}, bf16[256,1536]{1,0:T(8,128)(2,1)S(1)}, u32[]{:S(2)}, u32[]{:S(2)}) %collective-permute-start.38) | collective-permute-done | bytes 786464 | tf_op jit(solution)/shard_map/ppermute | solution.py:178
  425.9 17.6 %collective-permute-done.39 = bf16[256,1536]{1,0:T(8,128)(2,1)S(1)} collective-permute-done((bf16[256,1536]{1,0:T(8,128)(2,1)S(1)}, bf16[256,1536]{1,0:T(8,128)(2,1)S(1)}, u32[]{:S(2)}, u32[]{:S(2)}) %collective-permute-start.39) | collective-permute-done | bytes 786464 | tf_op jit(solution)/shard_map/ppermute | solution.py:178
  443.6 15.4 %fusion.179 = f32[1024,3072]{1,0:T(8,128)} fusion(bf16[3072,1536]{1,0:T(8,128)(2,1)} %get-tuple-element.282, bf16[256,1536]{1,0:T(8,128)(2,1)S(1)} %collective-permute-done.39, bf16[256,1536]{1,0:T(8,128)(2,1)S(1)} %collective-permute-done.38, bf16[256,1536]{1,0:T(8,128)(2,1)S(1)} %collective-permute-done.37, bf16[256,1536]{1,0:T(8,128)(2,1)S(1)} %multiply_convert_fusion.6), kind=kOutput, calls=%fused_computation.477 | convolution fusion | flops 9676259328 | bytes 25165824 | tf_op jit(solution)/shard_map/dot_general | solution.py:70
  459.0 15.1 %fusion.32 = (bf16[1024,1536]{1,0:T(8,128)(2,1)}, bf16[1024,1536]{1,0:T(8,128)(2,1)}, bf16[1024,1536]{1,0:T(8,128)(2,1)}) fusion(f32[1024,3072]{1,0:T(8,128)} %fusion.179, bf16[1536,1536]{1,0:T(8,128)(2,1)} %get-tuple-element.281, bf16[256,1536]{1,0:T(8,128)(2,1)} %collective-permute-done.59, bf16[256,1536]{1,0:T(8,128)(2,1)} %collective-permute-done.58, ...), kind=kOutput, calls=%fused_computation.50 | convolution fusion | flops 4869586944 | bytes 29884416 | tf_op jit(solution)/shard_map/dot_general | solution.py:70
  474.1 8.2 convolution_convert_fusion.7
  482.4 7.0 convolution_convert_fusion
  501.8 13.1 %fusion.45 = bf16[1024,1536]{1,0:T(8,128)(2,1)S(1)} fusion(bf16[3072,1536]{1,0:T(8,128)(2,1)} %get-tuple-element.282, bf16[1024,1536]{1,0:T(8,128)(2,1)} %get-tuple-element.241, bf16[1024,1536]{1,0:T(8,128)(2,1)S(1)} %copy-done.150), kind=kOutput, calls=%fused_computation.78 | convolution fusion | flops 9677832192 | bytes 18874368 | tf_op jit(solution)/shard_map/dot_general | solution.py:60
  515.1 7.8 convolution_convert_fusion.2
  525.5 13.5 %collective-permute-done.60 = bf16[256,1536]{1,0:T(8,128)(2,1)S(1)} collective-permute-done((bf16[256,1536]{1,0:T(8,128)(2,1)S(1)}, bf16[256,1536]{1,0:T(8,128)(2,1)S(1)}, u32[]{:S(2)}, u32[]{:S(2)}) %collective-permute-start.60) | collective-permute-done | bytes 786464 | tf_op jit(solution)/shard_map/ppermute | solution.py:178
  541.8 14.1 %collective-permute-done.55 = bf16[256,1536]{1,0:T(8,128)(2,1)S(1)} collective-permute-done((bf16[256,1536]{1,0:T(8,128)(2,1)S(1)}, bf16[256,1536]{1,0:T(8,128)(2,1)S(1)}, u32[]{:S(2)}, u32[]{:S(2)}) %collective-permute-start.55) | collective-permute-done | bytes 786464 | tf_op jit(solution)/shard_map/ppermute | solution.py:178
  558.0 14.8 %collective-permute-done.61 = bf16[256,1536]{1,0:T(8,128)(2,1)} collective-permute-done((bf16[256,1536]{1,0:T(8,128)(2,1)S(1)}, bf16[256,1536]{1,0:T(8,128)(2,1)}, u32[]{:S(2)}, u32[]{:S(2)}) %collective-permute-start.61) | collective-permute-done | bytes 786464 | tf_op jit(solution)/shard_map/ppermute | solution.py:178
  589.0 17.0 %collective-permute-done.62 = bf16[256,1536]{1,0:T(8,128)(2,1)S(1)} collective-permute-done((bf16[256,1536]{1,0:T(8,128)(2,1)S(1)}, bf16[256,1536]{1,0:T(8,128)(2,1)S(1)}, u32[]{:S(2)}, u32[]{:S(2)}) %collective-permute-start.62) | collective-permute-done | bytes 786464 | tf_op jit(solution)/shard_map/ppermute | solution.py:178
  680.2 6.4 collective-permute-done.99
  687.4 7.2 collective-permute-done.108
  695.2 6.3 collective-permute-done.110
  738.8 126.4 %while.28 = (s32[]{:T(128)}, f32[1024,6,64]{0,2,1:T(8,128)S(1)}, f32[1024,6,64]{0,2,1:T(8,128)}, f32[2,512,6,64]{1,0,3,2:T(2,128)}, s32[2]{0:T(128)S(1)}, /*inde...) while((s32[]{:T(128)}, f32[1024,6,64]{0,2,1:T(8,128)S(1)}, ...), condition=%wide.region_19.20_spmd.clone, body=%wide.region_17.19_spmd.clone.sunk | while | flops 2063135744 | bytes 176785808 | solution.py:157
  740.3 7.3 fusion.285
  750.7 11.6 %multiply_reduce_fusion.7 = (f32[6,512]{1,0:T(8,128)S(1)}, f32[6,512,1024]{2,1,0:T(8,128)}) fusion(f32[6,512,1024]{2,1,0:T(8,128)} %fusion.285, f32[6,512]{1,0:T(8,128)S(1)} %dynamic-slice_bitcast_fusion.31, pred[512,1024]{1,0:T(8,128)(4,1)S(1)} %broadcast_compare_fusion.6, bf16[1024,6,64]{0,2,1:T(8,128)(2,1)} %get-tuple-element.553, ...), kind=kOutput, calls=%fused_computation.16.clone.1 | convolution fusion | flops 418378752 | bytes 26894340 | tf_op jit(solution)/shard_map/while/body/eval_jaxpr/qhd,khd->hqk/dot_general | solution.py:132
  763.7 6.9 multiply_convert_fusion.11
  775.0 15.0 %dynamic_update_slice.19 = f32[2,512,6,64]{1,0,3,2:T(2,128)} dynamic-update-slice(f32[2,512,6,64]{1,0,3,2:T(2,128)} %get-tuple-element.530, f32[1,512,6,64]{1,0,3,2:T(1,128)} %copy.401, s32[]{:T(128)} %get-tuple-element.527, s32[]{:T(128)} %constant.418.clone.1..sunk.1, s32[]{:T(128)} %constant.418.clone.1..sunk.1, s32[]{:T(128)} %constant.418.clone.1..sunk.1) | dynamic-update-slice | bytes 1572868 | tf_op jit(solution)/shard_map/while/body/jit(dynamic_update_index_in_dim)/dynamic_update_slice | solution.py:112
  794.3 7.7 bitcast_add_fusion.5
  803.2 7.3 fusion.285
  813.6 11.6 %multiply_reduce_fusion.7 = (f32[6,512]{1,0:T(8,128)S(1)}, f32[6,512,1024]{2,1,0:T(8,128)}) fusion(f32[6,512,1024]{2,1,0:T(8,128)} %fusion.285, f32[6,512]{1,0:T(8,128)S(1)} %dynamic-slice_bitcast_fusion.31, pred[512,1024]{1,0:T(8,128)(4,1)S(1)} %broadcast_compare_fusion.6, bf16[1024,6,64]{0,2,1:T(8,128)(2,1)} %get-tuple-element.553, ...), kind=kOutput, calls=%fused_computation.16.clone.1 | convolution fusion | flops 418378752 | bytes 26894340 | tf_op jit(solution)/shard_map/while/body/eval_jaxpr/qhd,khd->hqk/dot_general | solution.py:132
  826.6 6.9 multiply_convert_fusion.11
  837.8 15.0 %dynamic_update_slice.19 = f32[2,512,6,64]{1,0,3,2:T(2,128)} dynamic-update-slice(f32[2,512,6,64]{1,0,3,2:T(2,128)} %get-tuple-element.530, f32[1,512,6,64]{1,0,3,2:T(1,128)} %copy.401, s32[]{:T(128)} %get-tuple-element.527, s32[]{:T(128)} %constant.418.clone.1..sunk.1, s32[]{:T(128)} %constant.418.clone.1..sunk.1, s32[]{:T(128)} %constant.418.clone.1..sunk.1) | dynamic-update-slice | bytes 1572868 | tf_op jit(solution)/shard_map/while/body/jit(dynamic_update_index_in_dim)/dynamic_update_slice | solution.py:112
  857.1 8.1 bitcast_add_fusion.5
  888.3 6.3 collective-permute-done.82
  963.1 18.3 %collective-permute-start.65 = (bf16[256,1536]{1,0:T(8,128)(2,1)S(1)}, bf16[256,1536]{1,0:T(8,128)(2,1)S(1)}, u32[]{:S(2)}, u32[]{:S(2)}) collective-permute-start(bf16[256,1536]{1,0:T(8,128)(2,1)S(1)} %add_convert_fusion.2), channel_id=1, source_target_pairs={{0,3},{1,0},{2,1},{3,2},{4,7},{5,4},{6,5},{7,6},{8,11},{9,8},{10,9... | collective-permute-start | bytes 2359304 | tf_op jit(solution)/shard_map/ppermute | solution.py:178
  989.9 11.4 %collective-permute-done.93 = bf16[96,1536]{1,0:T(8,128)(2,1)S(1)} collective-permute-done((bf16[96,1536]{1,0:T(8,128)(2,1)S(1)}, bf16[96,1536]{1,0:T(8,128)(2,1)S(1)}, u32[]{:S(2)}, u32[]{:S(2)}) %collective-permute-start.93) | collective-permute-done | bytes 294944 | tf_op jit(solution)/shard_map/ppermute | solution.py:168
  1019.8 13.3 %all-to-all-start.3 = ((f32[32,1,48]{2,1,0:T(1,128)}), f32[32,1,48]{2,1,0:T(1,128)S(1)}, u32[]{:S(2)}, u32[]{:S(2)}) async-start(f32[32,1,48]{2,1,0:T(1,128)} %all_to_all.64), calls=%async_computation.3 | async-start | bytes 32768 | tf_op jit(solution)/shard_map/all_to_all | solution.py:565
  1033.9 6.2 all-to-all-done.3
  1048.2 11.6 %all-to-all-done.10 = bf16[4,48,1536]{2,1,0:T(8,128)(2,1)S(1)} async-done(((bf16[4,48,1536]{2,1,0:T(8,128)(2,1)}), bf16[4,48,1536]{2,1,0:T(8,128)(2,1)S(1)}, u32[]{:S(2)}, u32[]{:S(2)}) %all-to-all-start.10) | async-done | bytes 589856 | tf_op jit(solution)/shard_map/all_to_all | solution.py:491
  1067.1 12.2 %all-to-all-done.7 = bf16[4,48,1536]{2,1,0:T(8,128)(2,1)} async-done(((bf16[4,48,1536]{2,1,0:T(8,128)(2,1)}), bf16[4,48,1536]{2,1,0:T(8,128)(2,1)}, u32[]{:S(2)}, u32[]{:S(2)}) %all-to-all-start.7) | async-done | bytes 589856 | tf_op jit(solution)/shard_map/all_to_all | solution.py:491
  1090.7 8.3 all-to-all-done.6
  (907 shorter events, 544.4 us)
Async XLA Ops:
  3.8 52.6 %collective-permute-start.40 = (bf16[3,96,1536]{2,1,0:T(8,128)(2,1)}, bf16[3,96,1536]{2,1,0:T(8,128)(2,1)}, u32[]{:S(2)}, u32[]{:S(2)}) collective-permute-start(bf16[3,96,1536]{2,1,0:T(8,128)(2,1)} %get-tuple-element.264), channel_id=1, source_target_pairs={{0,8},{4,12},{8,0},{12,4},{16,24},{20,28},{24,16},{28,20},{1,9},{5... | collective-permute-start | bytes 2654216 | tf_op jit(solution)/shard_map/ppermute | solution.py:168
  6.8 52.8 %collective-permute-start.41 = (bf16[3,96,1536]{2,1,0:T(8,128)(2,1)}, bf16[3,96,1536]{2,1,0:T(8,128)(2,1)}, u32[]{:S(2)}, u32[]{:S(2)}) collective-permute-start(bf16[3,96,1536]{2,1,0:T(8,128)(2,1)} %get-tuple-element.264), channel_id=1, source_target_pairs={{0,16},{4,20},{8,24},{12,28},{16,0},{20,4},{24,8},{28,12},{1,17},{... | collective-permute-start | bytes 2654216 | tf_op jit(solution)/shard_map/ppermute | solution.py:173
  9.7 42.6 %all-to-all-start = ((bf16[4,48,3,384]{3,1,2,0:T(8,128)(2,1)}), bf16[4,48,3,384]{3,1,2,0:T(8,128)(2,1)}, u32[]{:S(2)}, u32[]{:S(2)}) async-start(bf16[4,48,3,384]{3,1,2,0:T(8,128)(2,1)} %copy.279), calls=%async_computation | async-start | bytes 884736 | tf_op jit(solution)/shard_map/all_to_all | solution.py:338
  65.7 40.6 %collective-permute-start.42 = (bf16[3,96,1536]{2,1,0:T(8,128)(2,1)}, bf16[3,96,1536]{2,1,0:T(8,128)(2,1)}, u32[]{:S(2)}, u32[]{:S(2)}) collective-permute-start(bf16[3,96,1536]{2,1,0:T(8,128)(2,1)} %collective-permute-done.40), channel_id=1, source_target_pairs={{0,16},{4,20},{8,24},{12,28},{16,0},{20,4},{24,8},{28,12},{1,17},{... | collective-permute-start | bytes 2654216 | tf_op jit(solution)/shard_map/ppermute | solution.py:173
  94.6 40.8 %collective-permute-start.43 = (bf16[3,96,1536]{2,1,0:T(8,128)(2,1)}, bf16[3,96,1536]{2,1,0:T(8,128)(2,1)S(1)}, u32[]{:S(2)}, u32[]{:S(2)}) collective-permute-start(bf16[3,96,1536]{2,1,0:T(8,128)(2,1)} %get-tuple-element.263), channel_id=1, source_target_pairs={{0,8},{4,12},{8,0},{12,4},{16,24},{20,28},{24,16},{28,20},{1,9},{5... | collective-permute-start | bytes 2654216 | tf_op jit(solution)/shard_map/ppermute | solution.py:168
  96.1 39.3 %collective-permute-start.44 = (bf16[3,96,1536]{2,1,0:T(8,128)(2,1)}, bf16[3,96,1536]{2,1,0:T(8,128)(2,1)S(1)}, u32[]{:S(2)}, u32[]{:S(2)}) collective-permute-start(bf16[3,96,1536]{2,1,0:T(8,128)(2,1)} %get-tuple-element.263), channel_id=1, source_target_pairs={{0,16},{4,20},{8,24},{12,28},{16,0},{20,4},{24,8},{28,12},{1,17},{... | collective-permute-start | bytes 2654216 | tf_op jit(solution)/shard_map/ppermute | solution.py:173
  96.6 60.9 %collective-permute-start.46 = (bf16[3,96,1536]{2,1,0:T(8,128)(2,1)}, bf16[3,96,1536]{2,1,0:T(8,128)(2,1)S(1)}, u32[]{:S(2)}, u32[]{:S(2)}) collective-permute-start(bf16[3,96,1536]{2,1,0:T(8,128)(2,1)} %get-tuple-element.264), channel_id=1, source_target_pairs={{0,4},{4,0},{8,12},{12,8},{16,20},{20,16},{24,28},{28,24},{1,5},{5... | collective-permute-start | bytes 2654216 | tf_op jit(solution)/shard_map/ppermute | solution.py:164
  118.8 143.2 %collective-permute-start.50 = (bf16[3,96,1536]{2,1,0:T(8,128)(2,1)}, bf16[3,96,1536]{2,1,0:T(8,128)(2,1)}, u32[]{:S(2)}, u32[]{:S(2)}) collective-permute-start(bf16[3,96,1536]{2,1,0:T(8,128)(2,1)} %get-tuple-element.263), channel_id=1, source_target_pairs={{0,4},{4,0},{8,12},{12,8},{16,20},{20,16},{24,28},{28,24},{1,5},{5... | collective-permute-start | bytes 2654216 | tf_op jit(solution)/shard_map/ppermute | solution.py:164
  135.4 142.8 %collective-permute-start.58 = (bf16[256,1536]{1,0:T(8,128)(2,1)}, bf16[256,1536]{1,0:T(8,128)(2,1)}, u32[]{:S(2)}, u32[]{:S(2)}) collective-permute-start(bf16[256,1536]{1,0:T(8,128)(2,1)} %collective-permute-done.57), channel_id=1, source_target_pairs={{0,1},{1,2},{2,3},{3,0},{4,5},{5,6},{6,7},{7,4},{8,9},{9,10},{10,1... | collective-permute-start | bytes 2359304 | tf_op jit(solution)/shard_map/ppermute | solution.py:178
  158.7 107.3 %collective-permute-start.20 = (bf16[4,2,48,1536]{3,2,1,0:T(8,128)(2,1)S(1)}, bf16[4,2,48,1536]{3,2,1,0:T(8,128)(2,1)}, u32[]{:S(2)}, u32[]{:S(2)}) collective-permute-start(bf16[4,2,48,1536]{3,2,1,0:T(8,128)(2,1)S(1)} %pad_maximum_fusion.5.refs_0_), channel_id=1, source_target_pairs={{0,8},{4,12},{8,0},{12,4},{16,24},{20,28},{24,16},{28,20},{1,9},{5... | collective-permute-start | bytes 3538952 | tf_op jit(solution)/shard_map/ppermute | solution.py:168
  159.4 30.6 %collective-permute-start.2 = (bf16[256,1536]{1,0:T(8,128)(2,1)S(1)}, bf16[256,1536]{1,0:T(8,128)(2,1)S(1)}, u32[]{:S(2)}, u32[]{:S(2)}) collective-permute-start(bf16[256,1536]{1,0:T(8,128)(2,1)S(1)} %collective-permute-done.1), channel_id=1, source_target_pairs={{0,1},{1,2},{2,3},{3,0},{4,5},{5,6},{6,7},{7,4},{8,9},{9,10},{10,1... | collective-permute-start | bytes 2359304 | tf_op jit(solution)/shard_map/ppermute | solution.py:178
  160.6 118.1 %collective-permute-start.21 = (bf16[4,2,48,1536]{3,2,1,0:T(8,128)(2,1)S(1)}, bf16[4,2,48,1536]{3,2,1,0:T(8,128)(2,1)}, u32[]{:S(2)}, u32[]{:S(2)}) collective-permute-start(bf16[4,2,48,1536]{3,2,1,0:T(8,128)(2,1)S(1)} %pad_maximum_fusion.5.refs_0_), channel_id=1, source_target_pairs={{0,16},{4,20},{8,24},{12,28},{16,0},{20,4},{24,8},{28,12},{1,17},{... | collective-permute-start | bytes 3538952 | tf_op jit(solution)/shard_map/ppermute | solution.py:173
  190.0 69.8 %collective-permute-start.49 = (bf16[3,96,1536]{2,1,0:T(8,128)(2,1)}, bf16[3,96,1536]{2,1,0:T(8,128)(2,1)}, u32[]{:S(2)}, u32[]{:S(2)}) collective-permute-start(bf16[3,96,1536]{2,1,0:T(8,128)(2,1)} %collective-permute-done.42), channel_id=1, source_target_pairs={{0,4},{4,0},{8,12},{12,8},{16,20},{20,16},{24,28},{28,24},{1,5},{5... | collective-permute-start | bytes 2654216 | tf_op jit(solution)/shard_map/ppermute | solution.py:164
  256.3 65.9 %all-to-all-start.1 = ((bf16[4,256,384]{2,1,0:T(8,128)(2,1)}), bf16[4,256,384]{2,1,0:T(8,128)(2,1)S(1)}, u32[]{:S(2)}, u32[]{:S(2)}) async-start(bf16[4,256,384]{2,1,0:T(8,128)(2,1)} %bitcast.754), calls=%async_computation.1 | async-start | bytes 1572864 | tf_op jit(solution)/shard_map/all_to_all | solution.py:412
  267.6 52.0 %collective-permute-start.22 = (bf16[4,2,48,1536]{3,2,1,0:T(8,128)(2,1)}, bf16[4,2,48,1536]{3,2,1,0:T(8,128)(2,1)}, u32[]{:S(2)}, u32[]{:S(2)}) collective-permute-start(bf16[4,2,48,1536]{3,2,1,0:T(8,128)(2,1)} %collective-permute-done.20.refs_1_), channel_id=1, source_target_pairs={{0,16},{4,20},{8,24},{12,28},{16,0},{20,4},{24,8},{28,12},{1,17},{... | collective-permute-start | bytes 3538952 | tf_op jit(solution)/shard_map/ppermute | solution.py:173
  278.2 47.2 %collective-permute-start.31 = (bf16[4,2,48,1536]{3,2,1,0:T(8,128)(2,1)S(1)}, bf16[4,2,48,1536]{3,2,1,0:T(8,128)(2,1)}, u32[]{:S(2)}, u32[]{:S(2)}) collective-permute-start(bf16[4,2,48,1536]{3,2,1,0:T(8,128)(2,1)S(1)} %pad_maximum_fusion.6.refs_0_), channel_id=1, source_target_pairs={{0,8},{4,12},{8,0},{12,4},{16,24},{20,28},{24,16},{28,20},{1,9},{5... | collective-permute-start | bytes 3538952 | tf_op jit(solution)/shard_map/ppermute | solution.py:168
  278.7 47.2 %collective-permute-start.24 = (bf16[4,2,48,1536]{3,2,1,0:T(8,128)(2,1)}, bf16[4,2,48,1536]{3,2,1,0:T(8,128)(2,1)}, u32[]{:S(2)}, u32[]{:S(2)}) collective-permute-start(bf16[4,2,48,1536]{3,2,1,0:T(8,128)(2,1)} %collective-permute-done.20.refs_1_), channel_id=1, source_target_pairs={{0,4},{4,0},{8,12},{12,8},{16,20},{20,16},{24,28},{28,24},{1,5},{5... | collective-permute-start | bytes 3538952 | tf_op jit(solution)/shard_map/ppermute | solution.py:164
  279.8 48.3 %collective-permute-start.25 = (bf16[4,2,48,1536]{3,2,1,0:T(8,128)(2,1)}, bf16[4,2,48,1536]{3,2,1,0:T(8,128)(2,1)}, u32[]{:S(2)}, u32[]{:S(2)}) collective-permute-start(bf16[4,2,48,1536]{3,2,1,0:T(8,128)(2,1)} %collective-permute-done.21.refs_2_), channel_id=1, source_target_pairs={{0,4},{4,0},{8,12},{12,8},{16,20},{20,16},{24,28},{28,24},{1,5},{5... | collective-permute-start | bytes 3538952 | tf_op jit(solution)/shard_map/ppermute | solution.py:164
  295.0 36.5 %collective-permute-start.32 = (bf16[4,2,48,1536]{3,2,1,0:T(8,128)(2,1)}, bf16[4,2,48,1536]{3,2,1,0:T(8,128)(2,1)}, u32[]{:S(2)}, u32[]{:S(2)}) collective-permute-start(bf16[4,2,48,1536]{3,2,1,0:T(8,128)(2,1)} %collective-permute-done.30.refs_1_), channel_id=1, source_target_pairs={{0,8},{4,12},{8,0},{12,4},{16,24},{20,28},{24,16},{28,20},{1,9},{5... | collective-permute-start | bytes 3538952 | tf_op jit(solution)/shard_map/ppermute | solution.py:168
  325.9 133.1 %collective-permute-start.59 = (bf16[256,1536]{1,0:T(8,128)(2,1)}, bf16[256,1536]{1,0:T(8,128)(2,1)}, u32[]{:S(2)}, u32[]{:S(2)}) collective-permute-start(bf16[256,1536]{1,0:T(8,128)(2,1)} %collective-permute-done.58), channel_id=1, source_target_pairs={{0,1},{1,2},{2,3},{3,0},{4,5},{5,6},{6,7},{7,4},{8,9},{9,10},{10,1... | collective-permute-start | bytes 2359304 | tf_op jit(solution)/shard_map/ppermute | solution.py:178
  491.4 85.1 %collective-permute-start.106 = (bf16[2,2,2,96,1536]{4,3,1,2,0:T(8,128)(2,1)}, bf16[2,2,2,96,1536]{4,3,1,2,0:T(8,128)(2,1)S(1)}, u32[]{:S(2)}, u32[]{:S(2)}) collective-permute-start(bf16[2,2,2,96,1536]{4,3,1,2,0:T(8,128)(2,1)} %copy.322), channel_id=1, source_target_pairs={{0,4},{4,0},{8,12},{12,8},{16,20},{20,16},{24,28},{28,24},{1,5},{5... | collective-permute-start | bytes 7077896 | tf_op jit(solution)/shard_map/ppermute | solution.py:164
  500.7 77.4 %collective-permute-start.101 = (bf16[2,2,2,96,1536]{4,3,1,2,0:T(8,128)(2,1)}, bf16[2,2,2,96,1536]{4,3,1,2,0:T(8,128)(2,1)}, u32[]{:S(2)}, u32[]{:S(2)}) collective-permute-start(bf16[2,2,2,96,1536]{4,3,1,2,0:T(8,128)(2,1)} %copy.319), channel_id=1, source_target_pairs={{0,4},{4,0},{8,12},{12,8},{16,20},{20,16},{24,28},{28,24},{1,5},{5... | collective-permute-start | bytes 7077896 | tf_op jit(solution)/shard_map/ppermute | solution.py:164
  524.2 31.7 %collective-permute-start.55 = (bf16[256,1536]{1,0:T(8,128)(2,1)S(1)}, bf16[256,1536]{1,0:T(8,128)(2,1)S(1)}, u32[]{:S(2)}, u32[]{:S(2)}) collective-permute-start(bf16[256,1536]{1,0:T(8,128)(2,1)S(1)} %add_convert_fusion.10), channel_id=1, source_target_pairs={{0,3},{1,0},{2,1},{3,2},{4,7},{5,4},{6,5},{7,6},{8,11},{9,8},{10,9... | collective-permute-start | bytes 2359304 | tf_op jit(solution)/shard_map/ppermute | solution.py:178
  539.2 33.6 %collective-permute-start.61 = (bf16[256,1536]{1,0:T(8,128)(2,1)S(1)}, bf16[256,1536]{1,0:T(8,128)(2,1)}, u32[]{:S(2)}, u32[]{:S(2)}) collective-permute-start(bf16[256,1536]{1,0:T(8,128)(2,1)S(1)} %add_convert_fusion.6), channel_id=1, source_target_pairs={{0,3},{1,0},{2,1},{3,2},{4,7},{5,4},{6,5},{7,6},{8,11},{9,8},{10,9... | collective-permute-start | bytes 2359304 | tf_op jit(solution)/shard_map/ppermute | solution.py:178
  541.7 40.3 %collective-permute-start.96 = (bf16[2,2,2,96,1536]{4,3,1,2,0:T(8,128)(2,1)S(1)}, bf16[2,2,2,96,1536]{4,3,1,2,0:T(8,128)(2,1)S(1)}, u32[]{:S(2)}, u32[]{:S(2)}) collective-permute-start(bf16[2,2,2,96,1536]{4,3,1,2,0:T(8,128)(2,1)S(1)} %copy.316), channel_id=1, source_target_pairs={{0,4},{4,0},{8,12},{12,8},{16,20},{20,16},{24,28},{28,24},{1,5},{5... | collective-permute-start | bytes 7077896 | tf_op jit(solution)/shard_map/ppermute | solution.py:164
  556.1 51.2 %collective-permute-start.56 = (bf16[256,1536]{1,0:T(8,128)(2,1)S(1)}, bf16[256,1536]{1,0:T(8,128)(2,1)S(1)}, u32[]{:S(2)}, u32[]{:S(2)}) collective-permute-start(bf16[256,1536]{1,0:T(8,128)(2,1)S(1)} %add_convert_fusion.9), channel_id=1, source_target_pairs={{0,3},{1,0},{2,1},{3,2},{4,7},{5,4},{6,5},{7,6},{8,11},{9,8},{10,9... | collective-permute-start | bytes 2359304 | tf_op jit(solution)/shard_map/ppermute | solution.py:178
  574.2 31.9 %collective-permute-start.62 = (bf16[256,1536]{1,0:T(8,128)(2,1)S(1)}, bf16[256,1536]{1,0:T(8,128)(2,1)S(1)}, u32[]{:S(2)}, u32[]{:S(2)}) collective-permute-start(bf16[256,1536]{1,0:T(8,128)(2,1)S(1)} %add_convert_fusion.5), channel_id=1, source_target_pairs={{0,3},{1,0},{2,1},{3,2},{4,7},{5,4},{6,5},{7,6},{8,11},{9,8},{10,9... | collective-permute-start | bytes 2359304 | tf_op jit(solution)/shard_map/ppermute | solution.py:178
  583.8 87.6 %collective-permute-start.107 = (bf16[2,96,1536]{2,1,0:T(8,128)(2,1)}, bf16[2,96,1536]{2,1,0:T(8,128)(2,1)}, u32[]{:S(2)}, u32[]{:S(2)}) collective-permute-start(bf16[2,96,1536]{2,1,0:T(8,128)(2,1)} %slice_bitcast_fusion.6), channel_id=1, source_target_pairs={{0,16},{4,20},{8,24},{12,28},{16,0},{20,4},{24,8},{28,12},{1,17},{... | collective-permute-start | bytes 1769480 | tf_op jit(solution)/shard_map/ppermute | solution.py:173
  585.9 87.5 %collective-permute-start.109 = (bf16[2,96,1536]{2,1,0:T(8,128)(2,1)}, bf16[2,96,1536]{2,1,0:T(8,128)(2,1)}, u32[]{:S(2)}, u32[]{:S(2)}) collective-permute-start(bf16[2,96,1536]{2,1,0:T(8,128)(2,1)} %slice_bitcast_fusion.3), channel_id=1, source_target_pairs={{0,8},{4,12},{8,0},{12,4},{16,24},{20,28},{24,16},{28,20},{1,9},{5... | collective-permute-start | bytes 1769480 | tf_op jit(solution)/shard_map/ppermute | solution.py:168
  586.5 88.6 %collective-permute-start.102 = (bf16[2,96,1536]{2,1,0:T(8,128)(2,1)}, bf16[2,96,1536]{2,1,0:T(8,128)(2,1)}, u32[]{:S(2)}, u32[]{:S(2)}) collective-permute-start(bf16[2,96,1536]{2,1,0:T(8,128)(2,1)} %slice_bitcast_fusion.10), channel_id=1, source_target_pairs={{0,16},{4,20},{8,24},{12,28},{16,0},{20,4},{24,8},{28,12},{1,17},{... | collective-permute-start | bytes 1769480 | tf_op jit(solution)/shard_map/ppermute | solution.py:173
  606.1 70.9 %collective-permute-start.104 = (bf16[2,96,1536]{2,1,0:T(8,128)(2,1)}, bf16[2,96,1536]{2,1,0:T(8,128)(2,1)}, u32[]{:S(2)}, u32[]{:S(2)}) collective-permute-start(bf16[2,96,1536]{2,1,0:T(8,128)(2,1)} %slice_bitcast_fusion.7), channel_id=1, source_target_pairs={{0,8},{4,12},{8,0},{12,4},{16,24},{20,28},{24,16},{28,20},{1,9},{5... | collective-permute-start | bytes 1769480 | tf_op jit(solution)/shard_map/ppermute | solution.py:168
  607.3 71.2 %collective-permute-start.97 = (bf16[2,96,1536]{2,1,0:T(8,128)(2,1)}, bf16[2,96,1536]{2,1,0:T(8,128)(2,1)}, u32[]{:S(2)}, u32[]{:S(2)}) collective-permute-start(bf16[2,96,1536]{2,1,0:T(8,128)(2,1)} %slice_bitcast_fusion.14), channel_id=1, source_target_pairs={{0,16},{4,20},{8,24},{12,28},{16,0},{20,4},{24,8},{28,12},{1,17},{... | collective-permute-start | bytes 1769480 | tf_op jit(solution)/shard_map/ppermute | solution.py:173
  666.6 67.6 %all-to-all-start.2 = ((bf16[256,4,384]{2,0,1:T(8,128)(2,1)}), bf16[256,4,384]{2,0,1:T(8,128)(2,1)}, u32[]{:S(2)}, u32[]{:S(2)}) async-start(bf16[256,4,384]{2,0,1:T(8,128)(2,1)} %bitcast.656), calls=%async_computation.2 | async-start | bytes 1572864 | tf_op jit(solution)/shard_map/all_to_all | solution.py:538
  673.4 268.8 %collective-permute-start.91 = (bf16[2,2,2,96,1536]{4,3,2,1,0:T(8,128)(2,1)}, bf16[2,2,2,96,1536]{4,3,2,1,0:T(8,128)(2,1)}, u32[]{:S(2)}, u32[]{:S(2)}) collective-permute-start(bf16[2,2,2,96,1536]{4,3,2,1,0:T(8,128)(2,1)} %dynamic-slice_bitcast_fusion.1), channel_id=1, source_target_pairs={{0,4},{4,0},{8,12},{12,8},{16,20},{20,16},{24,28},{28,24},{1,5},{5... | collective-permute-start | bytes 7077896 | tf_op jit(solution)/shard_map/ppermute | solution.py:164
  675.1 54.5 %collective-permute-start.86 = (bf16[2,2,2,48,1536]{4,3,2,1,0:T(8,128)(2,1)S(1)}, bf16[2,2,2,48,1536]{4,3,2,1,0:T(8,128)(2,1)S(1)}, u32[]{:S(2)}, u32[]{:S(2)}) collective-permute-start(bf16[2,2,2,48,1536]{4,3,2,1,0:T(8,128)(2,1)S(1)} %copy-done.67), channel_id=1, source_target_pairs={{0,4},{4,0},{8,12},{12,8},{16,20},{20,16},{24,28},{28,24},{1,5},{5... | collective-permute-start | bytes 3538952 | tf_op jit(solution)/shard_map/ppermute | solution.py:164
  676.9 55.2 %collective-permute-start.81 = (bf16[2,2,2,48,1536]{4,3,2,1,0:T(8,128)(2,1)S(1)}, bf16[2,2,2,48,1536]{4,3,2,1,0:T(8,128)(2,1)S(1)}, u32[]{:S(2)}, u32[]{:S(2)}) collective-permute-start(bf16[2,2,2,48,1536]{4,3,2,1,0:T(8,128)(2,1)S(1)} %copy-done.68), channel_id=1, source_target_pairs={{0,4},{4,0},{8,12},{12,8},{16,20},{20,16},{24,28},{28,24},{1,5},{5... | collective-permute-start | bytes 3538952 | tf_op jit(solution)/shard_map/ppermute | solution.py:164
  678.5 268.9 %collective-permute-start.76 = (bf16[2,2,2,96,1536]{4,3,2,1,0:T(8,128)(2,1)}, bf16[2,2,2,96,1536]{4,3,2,1,0:T(8,128)(2,1)}, u32[]{:S(2)}, u32[]{:S(2)}) collective-permute-start(bf16[2,2,2,96,1536]{4,3,2,1,0:T(8,128)(2,1)} %dynamic-slice_bitcast_fusion.2), channel_id=1, source_target_pairs={{0,4},{4,0},{8,12},{12,8},{16,20},{20,16},{24,28},{28,24},{1,5},{5... | collective-permute-start | bytes 7077896 | tf_op jit(solution)/shard_map/ppermute | solution.py:164
  728.4 222.3 %collective-permute-start.71 = (bf16[2,2,2,96,1536]{4,3,2,1,0:T(8,128)(2,1)}, bf16[2,2,2,96,1536]{4,3,2,1,0:T(8,128)(2,1)}, u32[]{:S(2)}, u32[]{:S(2)}) collective-permute-start(bf16[2,2,2,96,1536]{4,3,2,1,0:T(8,128)(2,1)} %dynamic-slice_bitcast_fusion.3), channel_id=1, source_target_pairs={{0,4},{4,0},{8,12},{12,8},{16,20},{20,16},{24,28},{28,24},{1,5},{5... | collective-permute-start | bytes 7077896 | tf_op jit(solution)/shard_map/ppermute | solution.py:164
  730.8 154.9 %collective-permute-start.87 = (bf16[2,48,1536]{2,1,0:T(8,128)(2,1)}, bf16[2,48,1536]{2,1,0:T(8,128)(2,1)}, u32[]{:S(2)}, u32[]{:S(2)}) collective-permute-start(bf16[2,48,1536]{2,1,0:T(8,128)(2,1)} %dynamic-slice_bitcast_fusion.17), channel_id=1, source_target_pairs={{0,16},{4,20},{8,24},{12,28},{16,0},{20,4},{24,8},{28,12},{1,17},{... | collective-permute-start | bytes 884744 | tf_op jit(solution)/shard_map/ppermute | solution.py:173
  732.1 164.1 %collective-permute-start.89 = (bf16[2,48,1536]{2,1,0:T(8,128)(2,1)}, bf16[2,48,1536]{2,1,0:T(8,128)(2,1)}, u32[]{:S(2)}, u32[]{:S(2)}) collective-permute-start(bf16[2,48,1536]{2,1,0:T(8,128)(2,1)} %dynamic-slice_bitcast_fusion.16), channel_id=1, source_target_pairs={{0,8},{4,12},{8,0},{12,4},{16,24},{20,28},{24,16},{28,20},{1,9},{5... | collective-permute-start | bytes 884744 | tf_op jit(solution)/shard_map/ppermute | solution.py:168
  896.2 34.3 %collective-permute-start.63 = (bf16[256,1536]{1,0:T(8,128)(2,1)S(1)}, bf16[256,1536]{1,0:T(8,128)(2,1)}, u32[]{:S(2)}, u32[]{:S(2)}) collective-permute-start(bf16[256,1536]{1,0:T(8,128)(2,1)S(1)} %slice.673), channel_id=1, source_target_pairs={{0,3},{1,0},{2,1},{3,2},{4,7},{5,4},{6,5},{7,6},{8,11},{9,8},{10,9... | collective-permute-start | bytes 2359304 | tf_op jit(solution)/shard_map/ppermute | solution.py:178
  924.6 31.5 %collective-permute-start.66 = (bf16[2,2,2,96,1152]{4,3,0,2,1:T(8,128)(2,1)}, bf16[2,2,2,96,1152]{4,3,0,2,1:T(8,128)(2,1)}, u32[]{:S(2)}, u32[]{:S(2)}) collective-permute-start(bf16[2,2,2,96,1152]{4,3,0,2,1:T(8,128)(2,1)} %bitcast.771), channel_id=1, source_target_pairs={{0,4},{4,0},{8,12},{12,8},{16,20},{20,16},{24,28},{28,24},{1,5},{5... | collective-permute-start | bytes 5308424 | tf_op jit(solution)/shard_map/ppermute | solution.py:164
  950.6 30.9 %collective-permute-start.77 = (bf16[2,96,1536]{2,1,0:T(8,128)(2,1)S(1)}, bf16[2,96,1536]{2,1,0:T(8,128)(2,1)S(1)}, u32[]{:S(2)}, u32[]{:S(2)}) collective-permute-start(bf16[2,96,1536]{2,1,0:T(8,128)(2,1)S(1)} %dynamic-slice_bitcast_fusion.9), channel_id=1, source_target_pairs={{0,16},{4,20},{8,24},{12,28},{16,0},{20,4},{24,8},{28,12},{1,17},{... | collective-permute-start | bytes 1769480 | tf_op jit(solution)/shard_map/ppermute | solution.py:173
  956.1 31.3 %collective-permute-start.72 = (bf16[2,96,1536]{2,1,0:T(8,128)(2,1)S(1)}, bf16[2,96,1536]{2,1,0:T(8,128)(2,1)S(1)}, u32[]{:S(2)}, u32[]{:S(2)}) collective-permute-start(bf16[2,96,1536]{2,1,0:T(8,128)(2,1)S(1)} %dynamic-slice_bitcast_fusion.11), channel_id=1, source_target_pairs={{0,16},{4,20},{8,24},{12,28},{16,0},{20,4},{24,8},{28,12},{1,17},{... | collective-permute-start | bytes 1769480 | tf_op jit(solution)/shard_map/ppermute | solution.py:173
  963.1 54.6 %collective-permute-start.65 = (bf16[256,1536]{1,0:T(8,128)(2,1)S(1)}, bf16[256,1536]{1,0:T(8,128)(2,1)S(1)}, u32[]{:S(2)}, u32[]{:S(2)}) collective-permute-start(bf16[256,1536]{1,0:T(8,128)(2,1)S(1)} %add_convert_fusion.2), channel_id=1, source_target_pairs={{0,3},{1,0},{2,1},{3,2},{4,7},{5,4},{6,5},{7,6},{8,11},{9,8},{10,9... | collective-permute-start | bytes 2359304 | tf_op jit(solution)/shard_map/ppermute | solution.py:178
  981.6 64.0 %collective-permute-start.67 = (bf16[2,96,1152]{2,1,0:T(8,128)(2,1)}, bf16[2,96,1152]{2,1,0:T(8,128)(2,1)}, u32[]{:S(2)}, u32[]{:S(2)}) collective-permute-start(bf16[2,96,1152]{2,1,0:T(8,128)(2,1)} %dynamic-slice_bitcast_fusion.13), channel_id=1, source_target_pairs={{0,16},{4,20},{8,24},{12,28},{16,0},{20,4},{24,8},{28,12},{1,17},{... | collective-permute-start | bytes 1327112 | tf_op jit(solution)/shard_map/ppermute | solution.py:173
  982.4 81.5 %collective-permute-start.69 = (bf16[2,96,1152]{2,1,0:T(8,128)(2,1)}, bf16[2,96,1152]{2,1,0:T(8,128)(2,1)}, u32[]{:S(2)}, u32[]{:S(2)}) collective-permute-start(bf16[2,96,1152]{2,1,0:T(8,128)(2,1)} %dynamic-slice_bitcast_fusion.12), channel_id=1, source_target_pairs={{0,8},{4,12},{8,0},{12,4},{16,24},{20,28},{24,16},{28,20},{1,9},{5... | collective-permute-start | bytes 1327112 | tf_op jit(solution)/shard_map/ppermute | solution.py:168
  1047.6 36.0 %collective-permute-start.68 = (bf16[96,1152]{1,0:T(8,128)(2,1)S(1)}, bf16[96,1152]{1,0:T(8,128)(2,1)}, u32[]{:S(2)}, u32[]{:S(2)}) collective-permute-start(bf16[96,1152]{1,0:T(8,128)(2,1)S(1)} %dynamic-slice_bitcast_fusion.25), channel_id=1, source_target_pairs={{0,8},{4,12},{8,0},{12,4},{16,24},{20,28},{24,16},{28,20},{1,9},{5... | collective-permute-start | bytes 663560 | tf_op jit(solution)/shard_map/ppermute | solution.py:168
  (250 other events, 3416.7 us)

commit v2 on v0

v2 whole, which is shorter than its diff:
```python
import jax
import jax.numpy as jnp
from jax import lax
from jax.experimental import pallas as pl
from jax.experimental.pallas import tpu as pltpu
from jax.sharding import PartitionSpec as P

HEADS = 24
HDIM = 64
ROT = 32


EPSILON = 1e-05
NEG_FILL = -1e30


def layer_norm(values, gain_vector):
    average = jnp.mean(values, axis=-1, keepdims=True)
    centered = values - average
    variance = jnp.mean(centered * centered, axis=-1, keepdims=True)
    return centered * lax.rsqrt(variance + EPSILON) * gain_vector


def layout(lengths, row_ids):
    first_end = lengths[0]
    second_end = lengths[0] + lengths[1]
    segment = jnp.where(row_ids < first_end, 0, jnp.where(row_ids < second_end, 1, 2)).astype(
        jnp.int32
    )
    seg_start = jnp.where(segment == 0, 0, jnp.where(segment == 1, first_end, second_end))
    return (segment, row_ids - seg_start)


def matmul(left, right):
    return jnp.dot(left, right, preferred_element_type=jnp.float32)


def contract_rows(left, right):
    return lax.dot_general(
        left, right, (((0,), (0,)), ((), ())), preferred_element_type=jnp.float32
    )


def contract_cols(left, right):
    return lax.dot_general(
        left, right, (((1,), (1,)), ((), ())), preferred_element_type=jnp.float32
    )


LANES = 128
PAIR = LANES // HDIM
LOG2E = 1.4426950408889634


def turn(values, cosine, sine_low, sine_high, sign):
    half_rot = ROT // 2
    ahead = pltpu.roll(values, LANES - half_rot, 1)
    behind = pltpu.roll(values, half_rot, 1)
    return values * cosine + sign * (behind * sine_high - ahead * sine_low)


def dot(left, right, left_dim, right_dim):
    return lax.dot_general(
        left, right, (((left_dim,), (right_dim,)), ((), ())), preferred_element_type=jnp.float32
    )


def lane_tables(position):
    half_rot = ROT // 2
    feature = jnp.arange(LANES, dtype=jnp.int32) % HDIM
    frequency = 10000.0 ** (-(feature % half_rot).astype(jnp.float32) / half_rot)
    angles = position.astype(jnp.float32)[:, None] * frequency[None, :]
    cosine = jnp.where(feature < ROT, jnp.cos(angles), 1.0)
    sine = jnp.sin(angles)
    return (
        cosine,
        jnp.where(feature < half_rot, sine, 0.0),
        jnp.where((feature >= half_rot) & (feature < ROT), sine, 0.0),
    )


def seq_distance_order(block, seq_size):
    place = lax.axis_index("seq")
    return lax.rem(place + (seq_size - block), seq_size)


def part(kind, head):
    return slice(kind * LANES + head * HDIM, kind * LANES + (head + 1) * HDIM)


def self_forward(norms, qkv_cols, tables, segment):
    seq_size, (block, width) = len(norms), norms[0].shape
    length = block * seq_size
    group = 3 * LANES
    pairs = qkv_cols.shape[1] // group
    scale = HDIM ** (-0.5) * LOG2E

    def body(*refs):
        norm_refs = refs[:seq_size]
        cols_ref, cos_ref, low_ref, high_ref, seg_col, seg_row, qkv_out, mixed_ref, total_ref = refs[
            seq_size:
        ]
        for number in range(seq_size):
            rows = slice(number * block, (number + 1) * block)
            tables = cos_ref[rows], low_ref[rows], high_ref[rows]
            projected = dot(norm_refs[number][...], cols_ref[...], 1, 0)
            for kind in range(3):
                cols = slice(kind * LANES, (kind + 1) * LANES)
                values = projected[:, cols]
                if kind < 2:
                    values = turn(values, *tables, 1.0)
                qkv_out[rows, cols] = values.astype(jnp.bfloat16)
        for number in range(seq_size):
            rows = slice(number * block, (number + 1) * block)
            same = seg_col[...] == seg_row[:, rows]
            mixed = []
            for head in range(PAIR):
                scores = dot(qkv_out[:, part(1, head)], qkv_out[rows, part(0, head)], 1, 1)
                scores = jnp.where(same, scores, NEG_FILL)
                highest = jnp.max(scores, axis=0, keepdims=True)
                raised = jnp.exp2((scores - highest) * scale)
                total = jnp.sum(raised, axis=0, keepdims=True)
                mixed.append(dot(qkv_out[:, part(2, head)], raised.astype(jnp.bfloat16), 0, 0) / total)
                total_ref[0, head : head + 1, rows] = highest * scale + jnp.log2(total)
            place = seq_distance_order(number, seq_size)
            target = pl.ds(pl.multiple_of(place * block, block), block)
            mixed_ref[target, :] = jnp.concatenate(mixed).T.astype(jnp.bfloat16)

    whole = pl.BlockSpec((length, LANES), lambda p: (0, 0))
    return pl.pallas_call(
        body,
        grid=(pairs,),
        in_specs=[pl.BlockSpec((block, width), lambda p: (0, 0))] * seq_size
        + [pl.BlockSpec((width, group), lambda p: (0, p))]
        + [whole] * 3
        + [
            pl.BlockSpec((length, 1), lambda p: (0, 0)),
            pl.BlockSpec((1, length), lambda p: (0, 0)),
        ],
        out_specs=[
            pl.BlockSpec((length, group), lambda p: (0, p)),
            pl.BlockSpec((length, LANES), lambda p: (0, p)),
            pl.BlockSpec((1, PAIR, length), lambda p: (p, 0, 0)),
        ],
        out_shape=[
            jax.ShapeDtypeStruct((length, pairs * group), jnp.bfloat16),
            jax.ShapeDtypeStruct((length, pairs * LANES), jnp.bfloat16),
            jax.ShapeDtypeStruct((pairs, PAIR, length), jnp.float32),
        ],
        compiler_params=pltpu.CompilerParams(vmem_limit_bytes=40 << 20),
        cost_estimate=pl.CostEstimate(
            flops=8 * pairs * PAIR * length * length * HDIM,
            bytes_accessed=2 * (length + group * pairs) * width,
            transcendentals=pairs * PAIR * length * length,
        ),
    )(*norms, qkv_cols, *tables, segment[:, None], segment[None, :])


def self_backward(qkv, grad_out, log_total, tables, segment, seq_size):
    length = qkv.shape[0]
    group = 3 * LANES
    pairs = qkv.shape[1] // group
    block = length // seq_size
    scaling = HDIM ** (-0.5)
    scale = scaling * LOG2E

    def body(qkv_ref, grad_ref, total_ref, *rest):
        cos_ref, low_ref, high_ref, seg_col, seg_row, out_ref, dk_sum, dv_sum = rest
        for number in range(seq_size):
            rows = slice(number * block, (number + 1) * block)
            same = seg_col[...] == seg_row[:, rows]
            place = seq_distance_order(number, seq_size)
            grads = grad_ref[pl.ds(pl.multiple_of(place * block, block), block), :]
            grad_queries = []
            for head in range(PAIR):
                cols = slice(head * HDIM, (head + 1) * HDIM)
                grad_head = grads[:, cols]
                query_head = qkv_ref[rows, part(0, head)]
                key_head = qkv_ref[:, part(1, head)]
                scores = dot(key_head, query_head, 1, 1) * scale - total_ref[
                    0, head : head + 1, rows
                ]
                chance = jnp.exp2(jnp.where(same, scores, NEG_FILL))
                grad_chance = dot(qkv_ref[:, part(2, head)], grad_head, 1, 1)
                inner = jnp.sum(chance * grad_chance, axis=0, keepdims=True)
                grad_scores = (chance * (grad_chance - inner)).astype(jnp.bfloat16)
                grad_queries.append(dot(key_head, grad_scores, 0, 0))
                grad_keys = dot(grad_scores, query_head, 1, 0)
                grad_values = dot(chance.astype(jnp.bfloat16), grad_head, 1, 0)
                if number == 0:
                    dk_sum[:, cols] = grad_keys
                    dv_sum[:, cols] = grad_values
                else:
                    dk_sum[:, cols] += grad_keys
                    dv_sum[:, cols] += grad_values
            tables = cos_ref[rows], low_ref[rows], high_ref[rows]
            turned = turn(jnp.concatenate(grad_queries).T * scaling, *tables, -1.0)
            out_ref[rows, :LANES] = turned.astype(jnp.bfloat16)
        tables = cos_ref[...], low_ref[...], high_ref[...]
        turned = turn(dk_sum[...] * scaling, *tables, -1.0)
        out_ref[:, LANES : 2 * LANES] = turned.astype(jnp.bfloat16)
        out_ref[:, 2 * LANES :] = dv_sum[...].astype(jnp.bfloat16)

    whole = pl.BlockSpec((length, LANES), lambda p: (0, 0))
    return pl.pallas_call(
        body,
        grid=(pairs,),
        in_specs=[
            pl.BlockSpec((length, group), lambda p: (0, p)),
            pl.BlockSpec((length, LANES), lambda p: (0, p)),
            pl.BlockSpec((1, PAIR, length), lambda p: (p, 0, 0)),
        ]
        + [whole] * 3
        + [
            pl.BlockSpec((length, 1), lambda p: (0, 0)),
            pl.BlockSpec((1, length), lambda p: (0, 0)),
        ],
        out_specs=pl.BlockSpec((length, group), lambda p: (0, p)),
        out_shape=jax.ShapeDtypeStruct(qkv.shape, jnp.bfloat16),
        scratch_shapes=[pltpu.VMEM((length, LANES), jnp.float32)] * 2,
        compiler_params=pltpu.CompilerParams(vmem_limit_bytes=40 << 20),
        cost_estimate=pl.CostEstimate(
            flops=20 * pairs * PAIR * length * length * HDIM,
            bytes_accessed=20 * grad_out.size,
            transcendentals=pairs * PAIR * length * length,
        ),
    )(qkv, grad_out, log_total, *tables, segment[:, None], segment[None, :])


CROSS_HEADS = 8


def cross_softmax(queries, key_rows, item_row):
    scale = HDIM ** (-0.5) * LOG2E
    scores = dot(key_rows, queries, 1, 1)
    count = key_rows.shape[0]
    key_item = (lax.broadcasted_iota(jnp.int32, (count, 1), 0) >= count // 2).astype(jnp.int32)
    scores = jnp.where(key_item == item_row, scores, NEG_FILL)
    raised = jnp.exp2((scores - jnp.max(scores, axis=0, keepdims=True)) * scale)
    return raised / jnp.sum(raised, axis=0, keepdims=True)


def cross_call(body, arrays, item_row, out_rows, flops):
    width = arrays[0].shape[1]
    lanes = CROSS_HEADS * HDIM
    blocks = [pl.BlockSpec((a.shape[0], lanes), lambda p: (0, p)) for a in arrays]
    return pl.pallas_call(
        body,
        grid=(width // lanes,),
        in_specs=blocks + [pl.BlockSpec(item_row.shape, lambda p: (0, 0))],
        out_specs=[pl.BlockSpec((rows, lanes), lambda p: (0, p)) for rows in out_rows],
        out_shape=[jax.ShapeDtypeStruct((rows, width), jnp.bfloat16) for rows in out_rows],
        compiler_params=pltpu.CompilerParams(vmem_limit_bytes=32 << 20),
        cost_estimate=pl.CostEstimate(
            flops=flops * width * arrays[0].shape[0] * arrays[1].shape[0],
            bytes_accessed=2 * sum(a.size for a in arrays),
            transcendentals=HEADS * arrays[0].shape[0] * arrays[1].shape[0],
        ),
    )(*arrays, item_row)


def cross_forward(queries, key_rows, value_rows, item_row):
    def body(q_ref, k_ref, v_ref, item_ref, mixed_ref):
        mixed = []
        for head in range(CROSS_HEADS):
            cols = slice(head * HDIM, (head + 1) * HDIM)
            chance = cross_softmax(q_ref[:, cols], k_ref[:, cols], item_ref[...])
            mixed.append(dot(v_ref[:, cols], chance.astype(jnp.bfloat16), 0, 0))
        mixed_ref[...] = jnp.concatenate(mixed).T.astype(jnp.bfloat16)

    return cross_call(
        body, (queries, key_rows, value_rows), item_row, [queries.shape[0]], 4
    )[0]


def cross_backward(queries, key_rows, value_rows, grad_mixed, item_row):
    scaling = HDIM ** (-0.5)

    def body(q_ref, k_ref, v_ref, grad_ref, item_ref, dq_ref, dk_ref, dv_ref):
        grad_queries = []
        for head in range(CROSS_HEADS):
            cols = slice(head * HDIM, (head + 1) * HDIM)
            query_head, key_head, grad_head = q_ref[:, cols], k_ref[:, cols], grad_ref[:, cols]
            chance = cross_softmax(query_head, key_head, item_ref[...])
            grad_chance = dot(v_ref[:, cols], grad_head, 1, 1)
            inner = jnp.sum(chance * grad_chance, axis=0, keepdims=True)
            grad_scores = (chance * (grad_chance - inner)).astype(jnp.bfloat16)
            grad_queries.append(dot(key_head, grad_scores, 0, 0))
            dk_ref[:, cols] = (dot(grad_scores, query_head, 1, 0) * scaling).astype(jnp.bfloat16)
            dv_ref[:, cols] = dot(chance.astype(jnp.bfloat16), grad_head, 1, 0).astype(
                jnp.bfloat16
            )
        dq_ref[...] = (jnp.concatenate(grad_queries).T * scaling).astype(jnp.bfloat16)

    rows, keys = queries.shape[0], key_rows.shape[0]
    return cross_call(
        body, (queries, key_rows, value_rows, grad_mixed), item_row, [rows, keys, keys], 10
    )


def feed_block(normed, grads, gate_up, down, number, count, held):
    rows, width = normed.shape
    units = down.shape[0]
    steps = 3
    tile = units // steps

    def body(x_ref, g_ref, gate_ref, up_ref, down_ref, *rest):
        act_ref, dgate_ref, dup_ref, out_ref, dx_ref, out_sum, dx_sum = rest[-7:]
        step = pl.program_id(0)
        values, grad_rows = x_ref[...], g_ref[...]
        gate = dot(values, gate_ref[...], 1, 1)
        up = dot(values, up_ref[...], 1, 1)
        grad_act = dot(grad_rows, down_ref[...], 1, 1)
        chance = jax.nn.sigmoid(gate)
        silu = gate * chance
        act = (silu * up).astype(jnp.bfloat16)
        grad_gate = (grad_act * up * (chance + silu * (1.0 - chance))).astype(jnp.bfloat16)
        grad_up = (grad_act * silu).astype(jnp.bfloat16)
        act_ref[...] = act
        dgate_ref[...] = grad_gate
        dup_ref[...] = grad_up
        out_part = dot(act, down_ref[...], 1, 0)
        dx_part = dot(grad_gate, gate_ref[...], 1, 0) + dot(grad_up, up_ref[...], 1, 0)

        @pl.when(step == 0)
        def _():
            out_sum[...] = out_part
            dx_sum[...] = dx_part

        @pl.when(step > 0)
        def _():
            out_sum[...] += out_part
            dx_sum[...] += dx_part

        @pl.when(step == steps - 1)
        def _():
            out_ref[...] = out_sum[...].astype(jnp.bfloat16)
            dx_ref[...] = dx_sum[...].astype(jnp.bfloat16)

    full = pl.BlockSpec((rows, width), lambda t: (0, 0))
    block = pl.BlockSpec((rows, tile), lambda t: (number, t))
    unit_shape = jax.ShapeDtypeStruct((rows * count, units), jnp.bfloat16)
    row_shape = jax.ShapeDtypeStruct((rows, width), jnp.bfloat16)
    held = [] if held is None else list(held)
    return pl.pallas_call(
        body,
        grid=(steps,),
        in_specs=[
            full,
            full,
            pl.BlockSpec((tile, width), lambda t: (t, 0)),
            pl.BlockSpec((tile, width), lambda t: (steps + t, 0)),
            pl.BlockSpec((tile, width), lambda t: (t, 0)),
        ]
        + [pl.BlockSpec(memory_space=pl.ANY)] * len(held),
        out_specs=[block] * 3 + [full] * 2,
        out_shape=[unit_shape] * 3 + [row_shape] * 2,
        scratch_shapes=[pltpu.VMEM((rows, width), jnp.float32)] * 2,
        input_output_aliases={5 + n: n for n in range(len(held))},
        compiler_params=pltpu.CompilerParams(vmem_limit_bytes=40 << 20),
        cost_estimate=pl.CostEstimate(
            flops=12 * rows * width * units,
            bytes_accessed=6 * units * width + 10 * rows * width,
            transcendentals=rows * units,
        ),
    )(normed, grads, gate_up, gate_up, down, *held)


def unit_products(units, norms, grads, core, arrived=None):
    seq_size, (block, width) = len(norms), norms[0].shape
    length, count = units[0].shape
    steps = 3
    tile = count // (2 * steps)

    def body(*refs):
        unit_refs, refs = refs[:3], refs[3:]
        norm_refs, grad_refs, refs = refs[:seq_size], refs[seq_size : 2 * seq_size], refs[2 * seq_size :]
        out_ref, all_norms, all_grads = refs[-3:]

        @pl.when(pl.program_id(0) == 0)
        def _():
            for k in range(seq_size):
                rows = slice(k * block, (k + 1) * block)
                all_norms[rows, :] = norm_refs[k][...]
                all_grads[rows, :] = grad_refs[k][...]

        for kind in range(3):
            rows = (all_grads if kind == 2 else all_norms)[...]
            total = dot(unit_refs[kind][...], rows, 0, 0)
            if arrived is not None:
                total += refs[0][kind].astype(jnp.float32)
            out_ref[kind] = total.astype(jnp.bfloat16)

    out_block = pl.BlockSpec((3, tile, width), lambda t: (0, t, 0))
    extra = [] if arrived is None else [arrived]
    return pl.pallas_call(
        body,
        grid=(steps,),
        in_specs=[pl.BlockSpec((length, tile), lambda t: (0, core * steps + t))] * 3
        + [pl.BlockSpec((block, width), lambda t: (0, 0))] * (2 * seq_size)
        + [out_block] * len(extra),
        out_specs=out_block,
        out_shape=jax.ShapeDtypeStruct((3, count // 2, width), jnp.bfloat16),
        scratch_shapes=[pltpu.VMEM((length, width), jnp.bfloat16)] * 2,
        compiler_params=pltpu.CompilerParams(vmem_limit_bytes=56 << 20),
        cost_estimate=pl.CostEstimate(
            flops=3 * length * width * count,
            bytes_accessed=4 * length * width + 6 * count * width,
            transcendentals=0,
        ),
    )(*units, *norms, *grads, *extra)


def weight_products(lefts, rights, slot=0, slots=1, held=None):
    dp_size = lax.axis_size("dp")
    y_size = dp_size // 4
    rows, height = lefts[0].shape
    columns = rights[0].shape[1]
    tile = 3 * LANES
    place_rows = height // dp_size
    half_rows = place_rows * len(rights) // 2
    per_step = tile // place_rows

    def body(*refs):
        left_refs, refs = refs[: len(lefts)], refs[len(lefts) :]
        right_refs, (own_ref, other_ref, product) = refs[: len(rights)], refs[-3:]
        dp_place = lax.axis_index("dp")
        step = pl.program_id(0)
        for number, right_ref in enumerate(right_refs):
            total = None
            for k, left_ref in enumerate(left_refs):
                term = dot(left_ref[...], right_ref[k * rows : (k + 1) * rows, :], 0, 0)
                total = term if total is None else total + term
            product[...] = total.astype(jnp.bfloat16)
            for chip in range(per_step // 2):
                chip_place = step * (per_step // 2) + chip
                y_back = lax.rem((dp_place >> 2) + y_size - (chip_place >> 1), y_size)
                x_back = ((dp_place >> 1) ^ chip_place) & 1
                for target, core in ((own_ref, dp_place & 1), (other_ref, 1 - (dp_place & 1))):
                    first_row = (2 * chip + core) * place_rows
                    for half in range(2 // len(rights)):
                        begin = pl.multiple_of(first_row + half * half_rows, 16)
                        target[0, number + half, y_back, x_back] = product[
                            pl.ds(begin, half_rows), :
                        ]

    whole = (1, 2, y_size, 2, half_rows, columns)
    out_block = pl.BlockSpec(whole, lambda t: (slot, 0, 0, 0, 0, 0))
    out_shape = jax.ShapeDtypeStruct((slots,) + whole[1:], jnp.bfloat16)
    held = [] if held is None else list(held)
    return pl.pallas_call(
        body,
        grid=(height // tile,),
        in_specs=[pl.BlockSpec((rows, tile), lambda t: (0, t))] * len(lefts)
        + [pl.BlockSpec(r.shape, lambda t: (0, 0)) for r in rights]
        + [pl.BlockSpec(memory_space=pl.ANY)] * len(held),
        out_specs=[out_block] * 2,
        out_shape=[out_shape] * 2,
        scratch_shapes=[pltpu.VMEM((tile, columns), jnp.bfloat16)],
        input_output_aliases={len(lefts) + len(rights) + n: n for n in range(len(held))},
        compiler_params=pltpu.CompilerParams(vmem_limit_bytes=40 << 20),
        cost_estimate=pl.CostEstimate(
            flops=2 * rows * len(lefts) * height * columns * len(rights),
            bytes_accessed=4 * height * columns * len(rights),
            transcendentals=0,
        ),
    )(*lefts, *rights, *held)


def swap_core(values):
    return lax.ppermute(values, "dp", [(d, d ^ 1) for d in range(lax.axis_size("dp"))])


def shift_dp(values, y, x):
    size = lax.axis_size("dp")
    return lax.ppermute(values, "dp", [(d, ((d + 4 * y) % size) ^ (2 * x)) for d in range(size)])


def shift_seq(values, step=1):
    size = lax.axis_size("seq")
    return lax.ppermute(values, "seq", [(s, (s + step) % size) for s in range(size)])


def swap_seq(values):
    return lax.all_to_all(values, "seq", split_axis=0, concat_axis=0, tiled=True)


def gather_places(values):
    size = lax.axis_size("seq")
    return swap_seq(jnp.broadcast_to(values[None], (size,) + values.shape))


def add_wide(left, right):
    return left.astype(jnp.float32) + right.astype(jnp.float32)


def add_low(left, right):
    return add_wide(left, right).astype(jnp.bfloat16)


def stage(*values):
    return lax.optimization_barrier(values)


def spread_first(first, second):
    held = {(0, 0, 0): first, (1, 0, 0): second, (0, 0, 1): shift_dp(first, 0, 1)}
    for y in range(1, lax.axis_size("dp") // 4):
        held[1, y, 0] = shift_dp(held[1, y - 1, 0], 1, 0)
    return held


def spread_second(held):
    held = dict(held)
    for half, y, x in [(h, y, 0) for h, y, _ in held if h == 1]:
        held[half, y, 1] = shift_dp(held[half, y, x], 0, 1)
    for x in range(2):
        for y in range(1, lax.axis_size("dp") // 4):
            held[0, y, x] = shift_dp(held[0, y - 1, x], 1, 0)
    return held


def with_cores(plane):
    return {(core,) + p: swap_core(v) if core else v for core in range(2) for p, v in plane.items()}


def reduce_first(own, arrived=None):
    def terms(*index):
        index = (slice(None),) + index
        values = own[index].astype(jnp.float32)
        return values if arrived is None else values + arrived[index].astype(jnp.float32)

    y_size = own.shape[2]
    total = terms(0, y_size - 1).astype(jnp.bfloat16)
    for y in range(y_size - 2, -1, -1):
        total = (shift_dp(total, -1, 0).astype(jnp.float32) + terms(0, y)).astype(jnp.bfloat16)
    sent = shift_dp(terms(1, slice(None), 1).astype(jnp.bfloat16), 0, 1).astype(jnp.float32)
    return total, (sent + terms(1, slice(None), 0)).astype(jnp.bfloat16)


def reduce_second(first, second):
    first = add_wide(first[:, 0], shift_dp(first[:, 1], 0, 1))
    total = second[:, -1]
    for y in range(second.shape[1] - 2, -1, -1):
        total = add_wide(shift_dp(total.astype(jnp.bfloat16), -1, 0), second[:, y])
    return first, total


def dp_block(core, y, x, dp_place):
    size = lax.axis_size("dp")
    return lax.rem(dp_place + (size - 4 * y), size) ^ (core + 2 * x)


def assemble(pieces, out_shapes, copies):
    count = len(pieces)

    def body(*refs):
        sources, targets = refs[:count], refs[count : count + len(out_shapes)]
        held, loaded, stored = refs[count + len(out_shapes) : -2], refs[-2], refs[-1]
        dp_place = lax.axis_index("dp")
        loads = [pltpu.make_async_copy(sources[n], held[n], loaded.at[n]) for n in range(count)]
        for load in loads:
            load.start()
        stores = []
        for n in range(count):
            loads[n].wait()
            for number, (piece, source, out, target) in enumerate(copies):
                if piece == n:
                    stores.append(
                        pltpu.make_async_copy(
                            held[n].at[source],
                            targets[out].at[target(dp_place)],
                            stored.at[number],
                        )
                    )
                    stores[-1].start()
        for store in stores:
            store.wait()

    moved = sum(2 * p.size * p.dtype.itemsize for p in pieces)
    return pl.pallas_call(
        body,
        out_shape=[jax.ShapeDtypeStruct(s, jnp.bfloat16) for s in out_shapes],
        in_specs=[pl.BlockSpec(memory_space=pl.ANY)] * count,
        out_specs=[pl.BlockSpec(memory_space=pl.ANY)] * len(out_shapes),
        scratch_shapes=[pltpu.VMEM(p.shape, p.dtype) for p in pieces]
        + [pltpu.SemaphoreType.DMA((count,)), pltpu.SemaphoreType.DMA((len(copies),))],
        compiler_params=pltpu.CompilerParams(vmem_limit_bytes=32 << 20),
        cost_estimate=pl.CostEstimate(flops=0, bytes_accessed=moved, transcendentals=0),
    )(*pieces)


def in_place(plane):
    held = with_cores(plane)
    places = list(held)
    return assemble(
        [held[p] for p in places],
        [(lax.axis_size("dp"), 2) + held[places[0]].shape],
        [
            (n, (), 0, lambda d, p=p: (dp_block(p[0], p[2], p[3], d), p[1]))
            for n, p in enumerate(places)
        ],
    )[0]


def halves(values):
    middle = values.shape[0] // 2
    return values[:middle], values[middle:]


def local(
    tokens,
    context,
    item_lengths,
    gain_self,
    gain_cross,
    gain_feed,
    self_query,
    self_key,
    self_value,
    self_out,
    cross_query,
    cross_key,
    cross_value,
    cross_out,
    feed_gate,
    feed_up,
    feed_down,
    cotangent,
):
    rows_dev, width = tokens.shape
    dp_size, seq_size = lax.axis_size("dp"), lax.axis_size("seq")
    seq_place = lax.axis_index("seq")
    y_size = dp_size // 4
    head_width = HEADS // seq_size * HDIM
    pairs = -(-head_width // LANES)
    part_rows = self_query.shape[0]

    def whole_rows(rows):
        return lax.all_gather(rows, "dp", axis=0, tiled=False).reshape(width, width)

    qkv_parts = jnp.stack([self_query, self_key, self_value]).reshape(
        3, part_rows, seq_size, head_width
    )
    qkv_parts = jnp.pad(qkv_parts, ((0, 0),) * 3 + ((0, pairs * LANES - head_width),))
    qkv_parts = qkv_parts.reshape(3, part_rows, seq_size, pairs, LANES).transpose(2, 1, 3, 0, 4)
    qkv_rows = swap_seq(qkv_parts.reshape(seq_size, part_rows, pairs * 3 * LANES))
    full_cross_kv = lax.all_gather(
        jnp.stack([cross_key, cross_value]), ("dp", "seq"), axis=0, tiled=False
    )
    token_values = tokens.astype(jnp.float32)
    norm_one, norm_one_back = jax.vjp(layer_norm, token_values, gain_self.astype(jnp.float32))
    norm_one = norm_one.astype(jnp.bfloat16)
    norms_one = [norm_one, shift_seq(norm_one)]
    feed_parts = jnp.stack([feed_gate, feed_up, feed_down])
    half_units = feed_parts.shape[1] // 2
    feed_held = spread_first(feed_parts[:, :half_units], feed_parts[:, half_units:])
    row_ids = jnp.concatenate(
        [
            lax.rem(seq_place + (seq_size - k), seq_size) * rows_dev
            + jnp.arange(rows_dev, dtype=jnp.int32)
            for k in range(seq_size)
        ]
    )
    segment, position = layout(item_lengths[0], row_ids)
    row_segment = segment[:rows_dev]
    tables = lane_tables(position)
    valid_rows = (row_segment < 2).astype(jnp.float32)[:, None]
    grad_output_low = (cotangent.astype(jnp.float32) * valid_rows).astype(jnp.bfloat16)
    qkv_rows, norms_one[1], feed_held, tables, grad_output_low, self_out, cross_query, cross_out = (
        stage(
            qkv_rows,
            norms_one[1],
            feed_held,
            tables,
            grad_output_low,
            self_out,
            cross_query,
            cross_out,
        )
    )

    qkv_plane = spread_second(spread_first(*halves(qkv_rows)))
    norms_one.append(shift_seq(norms_one[-1]))
    out_rows = gather_places(self_out)
    qkv_plane, norms_one, out_rows, feed_held, cross_query, cross_out = stage(
        qkv_plane, norms_one, out_rows, feed_held, cross_query, cross_out
    )
    full_out = whole_rows(out_rows)

    for _ in range(seq_size - 3):
        norms_one.append(shift_seq(norms_one[-1]))
    cross_query_rows = gather_places(cross_query)
    for y in range(1, y_size):
        feed_held[0, y, 0] = shift_dp(feed_held[0, y - 1, 0], 1, 0)
    feed_held[1, 0, 1] = shift_dp(feed_held[1, 0, 0], 0, 1)
    qkv_cols = in_place(qkv_plane).reshape(width, pairs * 3 * LANES)
    norms_one, cross_query_rows, qkv_cols, feed_held, cross_out = stage(
        norms_one, cross_query_rows, qkv_cols, feed_held, cross_out
    )
    full_cross_query = whole_rows(cross_query_rows)

    cross_out_rows = gather_places(cross_out)
    for y in range(1, y_size):
        feed_held[0, y, 1] = shift_dp(feed_held[0, y - 1, 1], 1, 0)
        feed_held[1, y, 1] = shift_dp(feed_held[1, y, 0], 0, 1)
    qkv, head_attended, log_total = self_forward(norms_one, qkv_cols, tables, segment)
    cross_out_rows, feed_held, head_attended = stage(cross_out_rows, feed_held, head_attended)
    full_cross_out = whole_rows(cross_out_rows)

    attended = swap_seq(head_attended[:, :head_width].reshape(seq_size, rows_dev, head_width))
    feed_cores = with_cores(feed_held)
    places = [
        (core, half, y, x)
        for core in range(2)
        for half in range(2)
        for y in range(y_size)
        for x in range(2)
    ]
    unit_gate_up = jnp.concatenate(
        [feed_cores[p][kind] for kind in range(2) for p in places], axis=0
    )
    unit_down = jnp.concatenate([feed_cores[p][2] for p in places], axis=0)
    attended, unit_gate_up, unit_down, grad_output_low = stage(
        attended, unit_gate_up, unit_down, grad_output_low
    )

    all_grads = [grad_output_low, shift_seq(grad_output_low)]
    attended = jnp.concatenate([attended[s] for s in range(seq_size)], axis=1)
    first_sum = token_values + matmul(attended, full_out)
    norm_two, norm_two_back = jax.vjp(layer_norm, first_sum, gain_cross.astype(jnp.float32))
    norm_two = norm_two.astype(jnp.bfloat16)
    cross_queries = matmul(norm_two, full_cross_query).astype(jnp.bfloat16)
    all_grads, cross_queries = stage(all_grads, cross_queries)

    all_grads.append(shift_seq(all_grads[-1]))
    memory = context[0].reshape(-1, context.shape[3])
    full_cross_key = full_cross_kv[:, 0].reshape(-1, width)
    full_cross_value = full_cross_kv[:, 1].reshape(-1, width)
    memory_keys = matmul(memory, full_cross_key).astype(jnp.bfloat16)
    memory_values = matmul(memory, full_cross_value).astype(jnp.bfloat16)
    item_row = (row_segment == 1).astype(jnp.int32)[None, :]
    cross_mixed = cross_forward(cross_queries, memory_keys, memory_values, item_row)
    second_sum = first_sum + matmul(cross_mixed, full_cross_out)
    norm_three, norm_three_back = jax.vjp(layer_norm, second_sum, gain_feed.astype(jnp.float32))
    norm_three = norm_three.astype(jnp.bfloat16)
    all_grads, norm_three = stage(all_grads, norm_three)

    norms = [norm_three, shift_seq(norm_three)]
    for _ in range(seq_size - 3):
        all_grads.append(shift_seq(all_grads[-1]))
    norms, all_grads = stage(norms, all_grads)

    held, feed_out, feed_dx, moving, feed_moving = None, {}, {}, None, None

    def run_block(k, held):
        *held, feed_out[k], feed_dx[k] = feed_block(
            norms[k], all_grads[k], unit_gate_up, unit_down, k, seq_size, held
        )
        return held

    for k in range(1, seq_size):
        if k + 1 < seq_size:
            norms.append(shift_seq(norms[-1]))
        arrived = None if k == 1 else shift_seq(moving)
        held = run_block(k, held)
        if k == seq_size - 1:
            feed_moving = shift_seq(feed_out[1])
            held = run_block(0, held)
            activation, grad_gate, grad_up = held
            held = (grad_gate, grad_up, activation)
            other_units = unit_products(held, norms, all_grads, 1)
            arrived, feed_moving, held, other_units, feed_out, feed_dx = stage(
                arrived, feed_moving, held, other_units, feed_out, feed_dx
            )
        else:
            norms, arrived, held, feed_out, feed_dx = stage(norms, arrived, held, feed_out, feed_dx)
        moving = feed_dx[k] if k == 1 else add_low(arrived, feed_dx[k])
    arrived = shift_seq(moving)
    other_units = swap_core(other_units)
    arrived, other_units = stage(arrived, other_units)
    grad_norm_three = add_wide(arrived, feed_dx[0])

    def seq_blocks(first, second):
        blocks = jnp.concatenate([first.astype(jnp.bfloat16), second.astype(jnp.bfloat16)])
        return blocks.reshape(seq_size, part_rows, blocks.shape[1])

    if seq_size > 2:
        feed_moving = shift_seq(add_low(feed_moving, feed_out[2]))
    grad_output = cotangent.astype(jnp.float32) * valid_rows
    grad_second, grad_gain_feed = norm_three_back(grad_norm_three)
    grad_second = grad_second + grad_output
    second_low = grad_second.astype(jnp.bfloat16)
    grad_mixed = contract_cols(second_low, full_cross_out).astype(jnp.bfloat16)
    cross_out_own, cross_out_other = weight_products([cross_mixed], [second_low])
    cross_out_other = swap_core(cross_out_other)
    grad_cross_queries, grad_memory_keys, grad_memory_values = cross_backward(
        cross_queries, memory_keys, memory_values, grad_mixed, item_row
    )
    grad_norm_two = contract_cols(grad_cross_queries, full_cross_query)
    grad_first, grad_gain_cross = norm_two_back(grad_norm_two)
    grad_first = grad_first + grad_second
    first_low = grad_first.astype(jnp.bfloat16)
    grad_attended = contract_cols(first_low, full_out).astype(jnp.bfloat16)
    grad_attended = jnp.stack(
        [grad_attended[:, s * head_width : (s + 1) * head_width] for s in range(seq_size)]
    )
    feed_moving, cross_out_own, cross_out_other, grad_attended, first_low, grad_cross_queries = (
        stage(
            feed_moving,
            cross_out_own,
            cross_out_other,
            grad_attended,
            first_low,
            grad_cross_queries,
        )
    )

    head_grad = swap_seq(grad_attended).reshape(rows_dev * seq_size, head_width)
    head_grad = jnp.pad(head_grad, ((0, 0), (0, pairs * LANES - head_width)))
    for k in range(3, seq_size):
        feed_moving = shift_seq(add_low(feed_moving, feed_out[k]))
    cross_out_firsts = reduce_first(cross_out_own, cross_out_other)
    products = weight_products([norm_two], [grad_cross_queries], 0, 3)
    products = weight_products([attended], [first_low], 1, 3, products)
    weight_own, weight_other = weight_products(
        [memory], [grad_memory_keys, grad_memory_values], 2, 3, products
    )
    weight_other = swap_core(weight_other)
    head_grad, feed_moving, cross_out_firsts, weight_own, weight_other = stage(
        head_grad, feed_moving, cross_out_firsts, weight_own, weight_other
    )

    output = (second_sum + add_wide(feed_moving, feed_out[0])).astype(jnp.bfloat16)
    weight_firsts = reduce_first(weight_own, weight_other)
    turned = self_backward(qkv, head_grad, log_total, tables, segment, seq_size)
    norm_terms = contract_cols(turned, qkv_cols).astype(jnp.bfloat16)
    norm_terms = [norm_terms[k * rows_dev : (k + 1) * rows_dev] for k in range(seq_size)]
    weight_firsts, norm_terms, turned, cross_out_firsts = stage(
        weight_firsts, norm_terms, turned, cross_out_firsts
    )

    moving = shift_seq(norm_terms[1])
    cross_out_second = reduce_second(*cross_out_firsts)
    weight_seconds = reduce_second(*weight_firsts)
    own_units = unit_products(held, norms, all_grads, 0, other_units)
    qkv_own, qkv_other = weight_products(norms_one, [turned])
    moving, cross_out_second, weight_seconds, own_units, qkv_own, qkv_other = stage(
        moving, cross_out_second, weight_seconds, own_units, qkv_own, qkv_other
    )

    unit_firsts = reduce_first(own_units.reshape(3, 2, y_size, 2, half_units, width))
    placed = swap_seq(
        jnp.stack(
            [
                seq_blocks(*(s[0] for s in cross_out_second)),
                seq_blocks(*(s[0] for s in weight_seconds)),
            ],
            axis=1,
        )
    )
    if seq_size > 2:
        moving = shift_seq(add_low(moving, norm_terms[2]))
    qkv_other = swap_core(qkv_other)
    moving, placed, unit_firsts, qkv_other, weight_seconds = stage(
        moving, placed, unit_firsts, qkv_other, weight_seconds
    )

    for k in range(3, seq_size):
        moving = shift_seq(add_low(moving, norm_terms[k]))
    qkv_firsts = reduce_first(qkv_own, qkv_other)
    unit_grads = jnp.concatenate(reduce_second(*unit_firsts), axis=1)
    kv_blocks = jnp.stack(
        [s[2].astype(jnp.bfloat16).reshape(seq_size, -1, width) for s in weight_seconds], axis=1
    )
    later = swap_seq(
        jnp.stack(
            [
                seq_blocks(*(s[1] for s in weight_seconds)),
                kv_blocks.reshape(seq_size, part_rows, width),
            ],
            axis=1,
        )
    )
    moving, later, unit_grads, qkv_firsts = stage(moving, later, unit_grads, qkv_firsts)

    qkv_placed = swap_seq(seq_blocks(*(s[0] for s in reduce_second(*qkv_firsts))))
    grad_norm_one = add_wide(moving, norm_terms[0])
    grad_tokens_wide, grad_gain_self = norm_one_back(grad_norm_one)
    grad_tokens = (grad_tokens_wide + grad_first).astype(jnp.bfloat16)
    gains = jnp.stack([grad_gain_self, grad_gain_cross, grad_gain_feed])
    gains = gains.reshape(-1, dp_size * seq_size, part_rows).transpose(1, 0, 2)
    gains = jnp.sum(
        lax.all_to_all(gains, ("dp", "seq"), split_axis=0, concat_axis=0, tiled=True), axis=0
    )
    grad_cross_out, grad_cross_query, grad_cross_kv, grad_self_out = (
        jnp.sum(p[:, n].astype(jnp.float32), axis=0)
        for p, n in ((placed, 0), (placed, 1), (later, 1), (later, 0))
    )
    kv_rows = part_rows // 2
    grad_qkv = (
        qkv_placed
        .reshape(seq_size, part_rows, pairs, 3, LANES)
        .transpose(3, 1, 0, 2, 4)
        .reshape(3, part_rows, seq_size, pairs * LANES)[..., :head_width]
        .reshape(3, part_rows, width)
        .astype(jnp.float32)
    )
    return (
        output,
        grad_tokens,
        gains[0],
        gains[1],
        gains[2],
        grad_qkv[0],
        grad_qkv[1],
        grad_qkv[2],
        grad_self_out,
        grad_cross_query,
        grad_cross_kv[:kv_rows],
        grad_cross_kv[kv_rows:],
        grad_cross_out,
        unit_grads[0],
        unit_grads[1],
        unit_grads[2],
    )


def solution(mesh):
    placed = (
        P(("dp", "seq"), None),
        P("dp", None, None, None),
        P("dp", None),
        P(),
        P(),
        P(),
        P(("dp", "seq"), None),
        P(("dp", "seq"), None),
        P(("dp", "seq"), None),
        P(("dp", "seq"), None),
        P(("dp", "seq"), None),
        P(("dp", "seq"), None),
        P(("dp", "seq"), None),
        P(("dp", "seq"), None),
        P(("dp", "seq"), None),
        P(("dp", "seq"), None),
        P(("dp", "seq"), None),
        P(("dp", "seq"), None),
    )
    return jax.shard_map(
        local,
        mesh=mesh,
        in_specs=placed,
        out_specs=(
            P(("dp", "seq"), None),
            P(("dp", "seq"), None),
            P(("dp", "seq")),
            P(("dp", "seq")),
            P(("dp", "seq")),
            P(("dp", "seq"), None),
            P(("dp", "seq"), None),
            P(("dp", "seq"), None),
            P(("dp", "seq"), None),
            P(("dp", "seq"), None),
            P(("dp", "seq"), None),
            P(("dp", "seq"), None),
            P(("dp", "seq"), None),
            P(("dp", "seq"), None),
            P(("dp", "seq"), None),
            P(("dp", "seq"), None),
        ),
        check_vma=False,
    )
```

time: 2150 us -> 781 us (0.36)
  waiting for transfers between devices: 1620 us -> 260 us
  matrix products: 266 us -> 28.3 us
  Pallas kernels: 0 us -> 176 us
  starting transfers between devices: 14.2 us -> 96 us
  blocking collectives: 43.1 us -> 0 us
  local copies, waits for them, and re-layouts: 95.5 us -> 117 us
    all_gather x14 -> x4, waiting for transfers between devices: 710 us -> 0.05 us  [the longest x3 0.04 us: whole_rows(): return lax.all_gather(rows, 'dp', axis=0, tiled=False).reshape(width, width)]
    reduce_scatter x10 -> x0, waiting for transfers between devices: 633 us -> none  [the longest x1 142 us: local(): lax.psum_scatter(grad_self_out_full, ('dp', 'seq'), scatter_dimension=0,...]
    unnamed x28 -> x4, waiting for transfers between devices: 229 us -> 0.07 us
    ppermute x0 -> x66, waiting for transfers between devices: none -> 194 us  [the longest x18 123 us: shift_seq(): lax.ppermute(values, 'seq', [(s, (s + step) % size) for s in range(size)])]
    pallas_call x0 -> x16, Pallas kernels: none -> 176 us  [the longest x4 48.4 us: feed_block(): pl.pallas_call(body, grid=(steps,), in_specs=[full, full, pl.BlockSpec((t...]
    dot_general x30 -> x0, matrix products: 148 us -> none  [the longest x9 47.9 us: contract_rows(): lax.dot_general(left, right, (((0,), (0,)), ((), ())), preferred_element_...]
    ppermute x0 -> x66, starting transfers between devices: none -> 52.4 us  [the longest x28 31.2 us: shift_dp(): lax.ppermute(values, 'dp', [(d, (d + 4 * y) % size ^ 2 * x) for d in rang...]
    unnamed x128 -> x301, local copies, waits for them, and re-layouts: 31.5 us -> 80.9 us
  transfers between devices with their start and end apart: 29 -> 80, of which waited for: 26 -> 33; matrix products, arithmetic and copies ran while one was open for 11% -> 22% of each run, Pallas kernels for 0% -> 21%
where the time goes in v2:
time: 781 us; the launch traced here: 773 us
  waiting for transfers between devices  260 us (33%)
  Pallas kernels  176 us (23%)
  local copies, waits for them, and re-layouts  117 us (15%)
  starting transfers between devices  96 us (12%)
  other arithmetic  78 us (10%)
  matrix products  28.3 us (4%)
  between operations  17.6 us (2%)
    ppermute x18, waiting for transfers between devices, shift_seq(): lax.ppermute(values, 'seq', [(s, (s + step) % size) for s in range(size)])  123 us
    unnamed x301, local copies, waits for them, and re-layouts  80.9 us
    ppermute x28, waiting for transfers between devices, shift_dp(): lax.ppermute(values, 'dp', [(d, (d + 4 * y) % size ^ 2 * x) for d in rang...  67 us
    all_to_all x9, waiting for transfers between devices, swap_seq(): lax.all_to_all(values, 'seq', split_axis=0, concat_axis=0, tiled=True)  65 us
    pallas_call x4, Pallas kernels, feed_block(): pl.pallas_call(body, grid=(steps,), in_specs=[full, full, pl.BlockSpec((t...  48.4 us
    all_to_all x9, starting transfers between devices, swap_seq(): lax.all_to_all(values, 'seq', split_axis=0, concat_axis=0, tiled=True)  41 us
    ppermute x28, starting transfers between devices, shift_dp(): lax.ppermute(values, 'dp', [(d, (d + 4 * y) % size ^ 2 * x) for d in rang...  31.2 us
    pallas_call x2, Pallas kernels, unit_products(): pl.pallas_call(body, grid=(steps,), in_specs=[pl.BlockSpec((length, tile)...  27.7 us
  transfers between devices with their start and end apart: 80, of which 33 were waited for; matrix products, arithmetic and copies ran while one was open for 22% of the time, Pallas kernels for 21%

profile of v2, /device:TPU:0, one launch (start us, length us, event | category | flops | bytes accessed | tf_op | source)
XLA Modules:
  0.0 772.6 jit_solution(7227932669545206313)
XLA Ops:
  22.7 4.1 all-to-all-start
  32.8 15.0 %all-to-all-done = bf16[4,48,1152]{2,1,0:T(8,128)(2,1)} async-done(((bf16[4,48,1152]{2,1,0:T(8,128)(2,1)}), bf16[4,48,1152]{2,1,0:T(8,128)(2,1)}, u32[]{:S(2)}, u32[]{:S(2)}) %all-to-all-start) | async-done | bytes 442400 | tf_op jit(solution)/shard_map/all_to_all | solution.py:485
  49.7 5.1 all-to-all-start.1
  59.9 4.3 collective-permute-done.3.refs_1_
  75.9 14.1 %all-to-all-done.1 = bf16[4,48,1536]{2,1,0:T(8,128)(2,1)} async-done(((bf16[4,48,1536]{2,1,0:T(8,128)(2,1)}), bf16[4,48,1536]{2,1,0:T(8,128)(2,1)}, u32[]{:S(2)}, u32[]{:S(2)}) %all-to-all-start.1) | async-done | bytes 589856 | tf_op jit(solution)/shard_map/all_to_all | solution.py:485
  95.4 4.2 all-to-all-start.2
  110.7 8.9 %shard_map.297 = bf16[8,2,2,48,1152]{4,3,2,1,0:T(8,128)(2,1)S(1)} custom-call(bf16[2,48,1152]{2,1,0:T(8,128)(2,1)S(1)} %get-tuple-element.209.refs_0_, bf16[2,48,1152]{2,1,0:T(8,128)(2,1)S(1)} %collective-permute-done.3.refs_1_, bf16[2,48,1152]{2,1,0:T(8,128)(2,1)S(1)} %copy-done.48, bf16[2,48,1152]{2,1,0:T(8,128)(2,1)S(1)} %copy-done.52, ...), custom_call_target="tpu_custom_call" | custom-call | bytes 7077888 | tf_op jit(solution)/shard_map/pallas_call | solution.py:580
  121.4 12.7 %collective-permute-done.10.refs_3_ = bf16[256,1536]{1,0:T(8,128)(2,1)S(1)} collective-permute-done((bf16[256,1536]{1,0:T(8,128)(2,1)}, bf16[256,1536]{1,0:T(8,128)(2,1)S(1)}, u32[]{:S(2)}, u32[]{:S(2)}) %collective-permute-start.10) | collective-permute-done | bytes 786464 | tf_op jit(solution)/shard_map/ppermute | solution.py:481
  139.3 4.4 all-to-all-start.3
  152.6 24.9 %shard_map.298 = (bf16[1024,1152]{1,0:T(8,128)(2,1)S(1)}, bf16[1024,384]{1,0:T(8,128)(2,1)}, f32[3,2,1024]{2,1,0:T(2,128)S(1)}) custom-call(bf16[256,1536]{1,0:T(8,128)(2,1)S(1)} %fusion.14.refs_0_, bf16[256,1536]{1,0:T(8,128)(2,1)} %collective-permute-done.refs_1_, bf16[256,1536]{1,0:T(8,128)(2,1)} %collective-permute-done.9.refs_2_, ...), custom_call_target="tpu_custom_call" | custom-call | flops 3221225472 | bytes 6684672 | tf_op jit(solution)/shard_map/pallas_call | solution.py:130
  180.1 5.0 all-to-all-start.4
  241.9 4.2 fusion.84
  248.2 4.0 convolution_convert_fusion.5.q_ref
  252.2 4.0 collective-permute-done.31.g_ref.refs_8_
  256.3 8.9 %shard_map.299.refs_0_ = bf16[256,1536]{1,0:T(8,128)(2,1)S(1)} custom-call(bf16[256,1536]{1,0:T(8,128)(2,1)S(1)} %convolution_convert_fusion.5.q_ref, bf16[256,1536]{1,0:T(8,128)(2,1)S(1)} %fusion.4.k_ref, bf16[256,1536]{1,0:T(8,128)(2,1)S(1)} %fusion.5.v_ref, s32[1,256]{1,0:T(1,128)S(1)} %bitcast.358), custom_call_target="tpu_custom_call" | custom-call | flops 402653184 | bytes 2359296 | tf_op jit(solution)/shard_map/pallas_call | solution.py:247
  266.0 4.6 fusion.85
  271.3 6.3 collective-permute-done.32.g_ref.refs_9_
  278.4 21.4 %collective-permute-done.33.x_ref.refs_4_ = bf16[256,1536]{1,0:T(8,128)(2,1)S(1)} collective-permute-done((bf16[256,1536]{1,0:T(8,128)(2,1)S(1)}, bf16[256,1536]{1,0:T(8,128)(2,1)S(1)}, u32[]{:S(2)}, u32[]{:S(2)}) %collective-permute-start.33) | collective-permute-done | bytes 786464 | tf_op jit(solution)/shard_map/ppermute | solution.py:481
  299.8 14.8 %collective-permute-done.34.g_ref.refs_10_ = bf16[256,1536]{1,0:T(8,128)(2,1)S(1)} collective-permute-done((bf16[256,1536]{1,0:T(8,128)(2,1)S(1)}, bf16[256,1536]{1,0:T(8,128)(2,1)S(1)}, u32[]{:S(2)}, u32[]{:S(2)}) %collective-permute-start.34) | collective-permute-done | bytes 786464 | tf_op jit(solution)/shard_map/ppermute | solution.py:481
  314.7 12.7 %shard_map.300 = (bf16[1024,1536]{1,0:T(8,128)(2,1)S(1)}, bf16[1024,1536]{1,0:T(8,128)(2,1)S(1)}, bf16[1024,1536]{1,0:T(8,128)(2,1)S(1)}, bf16[256,1536]{1,0:T(8,128)(2,1)S(1)}, bf16[256,1536]{1,0:T(8,128)(2,1)S(1)}) custom-call(bf16[256,1536]{1,0:T(8,128)(2,1)S(1)} %collective-permute-done.33.x_ref.refs_4_, ...), custom_call_target="tpu_custom_call" | custom-call | flops 7247757312 | bytes 18087936 | tf_op jit(solution)/shard_map/pallas_call | solution.py:345
  327.4 6.5 collective-permute-done.35.x_ref.refs_5_
  334.1 11.9 %shard_map.301 = (bf16[1024,1536]{1,0:T(8,128)(2,1)S(1)}, bf16[1024,1536]{1,0:T(8,128)(2,1)S(1)}, bf16[1024,1536]{1,0:T(8,128)(2,1)S(1)}, bf16[256,1536]{1,0:T(8,128)(2,1)S(1)}, bf16[256,1536]{1,0:T(8,128)(2,1)S(1)}) custom-call(bf16[256,1536]{1,0:T(8,128)(2,1)S(1)} %collective-permute-done.35.x_ref.refs_5, ...), custom_call_target="tpu_custom_call", output_to_operand_aliasing={{0}: (5, {}), {1}: (6, {}), {2}: (7, {})} | custom-call | flops 7247757312 | bytes 18087936 | tf_op jit(solution)/shard_map/pallas_call | solution.py:345
  346.1 10.1 %collective-permute-done.36.x_ref.refs_6_ = bf16[256,1536]{1,0:T(8,128)(2,1)S(1)} collective-permute-done((bf16[256,1536]{1,0:T(8,128)(2,1)S(1)}, bf16[256,1536]{1,0:T(8,128)(2,1)S(1)}, u32[]{:S(2)}, u32[]{:S(2)}) %collective-permute-start.36) | collective-permute-done | bytes 786464 | tf_op jit(solution)/shard_map/ppermute | solution.py:481
  356.2 13.0 %collective-permute-done.37 = bf16[256,1536]{1,0:T(8,128)(2,1)S(1)} collective-permute-done((bf16[256,1536]{1,0:T(8,128)(2,1)S(1)}, bf16[256,1536]{1,0:T(8,128)(2,1)S(1)}, u32[]{:S(2)}, u32[]{:S(2)}) %collective-permute-start.37) | collective-permute-done | bytes 786464 | tf_op jit(solution)/shard_map/ppermute | solution.py:481
  369.6 11.9 %shard_map.302 = (bf16[1024,1536]{1,0:T(8,128)(2,1)S(1)}, bf16[1024,1536]{1,0:T(8,128)(2,1)S(1)}, bf16[1024,1536]{1,0:T(8,128)(2,1)S(1)}, bf16[256,1536]{1,0:T(8,128)(2,1)S(1)}, bf16[256,1536]{1,0:T(8,128)(2,1)S(1)}) custom-call(bf16[256,1536]{1,0:T(8,128)(2,1)S(1)} %collective-permute-done.36.x_ref.refs_6, ...), custom_call_target="tpu_custom_call", output_to_operand_aliasing={{0}: (5, {}), {1}: (6, {}), {2}: (7, {})} | custom-call | flops 7247757312 | bytes 18087936 | tf_op jit(solution)/shard_map/pallas_call | solution.py:345
  383.3 11.8 %shard_map.303 = (bf16[1024,1536]{1,0:T(8,128)(2,1)S(1)}, bf16[1024,1536]{1,0:T(8,128)(2,1)S(1)}, bf16[1024,1536]{1,0:T(8,128)(2,1)S(1)}, bf16[256,1536]{1,0:T(8,128)(2,1)S(1)}, bf16[256,1536]{1,0:T(8,128)(2,1)S(1)}) custom-call(bf16[256,1536]{1,0:T(8,128)(2,1)S(1)} %multiply_convert_fusion.x_ref.refs_3_, ...), custom_call_target="tpu_custom_call", output_to_operand_aliasing={{0}: (5, {}), {1}: (6, {}), {2}: (7, {})} | custom-call | flops 7247757312 | bytes 18087936 | tf_op jit(solution)/shard_map/pallas_call | solution.py:345
  401.8 13.4 %shard_map.304 = bf16[3,768,1536]{2,1,0:T(8,128)(2,1)} custom-call(bf16[1024,1536]{1,0:T(8,128)(2,1)} %copy-done.2, bf16[1024,1536]{1,0:T(8,128)(2,1)} %copy-done.3, bf16[1024,1536]{1,0:T(8,128)(2,1)} %copy-done.1, bf16[256,1536]{1,0:T(8,128)(2,1)} %copy-done.6, bf16[256,1536]{1,0:T(8,128)(2,1)} %copy-done.37, bf16[256,1536]{1,0:T(8,128)(2,1)} %copy-done.15, ...), custom_call_target="tpu_custom_call" | custom-call | flops 7247757312 | bytes 20447232 | tf_op jit(solution)/shard_map/pallas_call | solution.py:396
  416.9 4.3 collective-permute-start.40
  421.1 16.7 %collective-permute-done.41 = bf16[256,1536]{1,0:T(8,128)(2,1)S(1)} collective-permute-done((bf16[256,1536]{1,0:T(8,128)(2,1)S(1)}, bf16[256,1536]{1,0:T(8,128)(2,1)S(1)}, u32[]{:S(2)}, u32[]{:S(2)}) %collective-permute-start.41) | collective-permute-done | bytes 786464 | tf_op jit(solution)/shard_map/ppermute | solution.py:481
  448.0 10.8 %shard_map.306 = (bf16[256,1536]{1,0:T(8,128)(2,1)S(1)}, bf16[256,1536]{1,0:T(8,128)(2,1)S(1)}, bf16[256,1536]{1,0:T(8,128)(2,1)S(1)}) custom-call(bf16[256,1536]{1,0:T(8,128)(2,1)S(1)} %copy-done.26, bf16[256,1536]{1,0:T(8,128)(2,1)S(1)} %copy-done.22, bf16[256,1536]{1,0:T(8,128)(2,1)S(1)} %copy-done.24, ...), custom_call_target="tpu_custom_call" | custom-call | flops 1006632960 | bytes 3145728 | tf_op jit(solution)/shard_map/pallas_call | solution.py:247
  459.0 4.1 multiply_reduce_fusion.1
  488.5 4.9 all-to-all-start.5
  493.4 14.3 %shard_map.311 = bf16[3,768,1536]{2,1,0:T(8,128)(2,1)} custom-call(bf16[1024,1536]{1,0:T(8,128)(2,1)} %copy-done.2, bf16[1024,1536]{1,0:T(8,128)(2,1)} %copy-done.3, bf16[1024,1536]{1,0:T(8,128)(2,1)} %copy-done.1, bf16[256,1536]{1,0:T(8,128)(2,1)} %copy-done.6, bf16[256,1536]{1,0:T(8,128)(2,1)} %copy-done.37, bf16[256,1536]{1,0:T(8,128)(2,1)} %copy-done.15, ...), custom_call_target="tpu_custom_call" | custom-call | flops 7247757312 | bytes 20447232 | tf_op jit(solution)/shard_map/pallas_call | solution.py:396
  512.2 13.7 %all-to-all-done.5 = bf16[4,256,384]{2,1,0:T(8,128)(2,1)S(1)} async-done(((bf16[4,256,384]{2,1,0:T(8,128)(2,1)}), bf16[4,256,384]{2,1,0:T(8,128)(2,1)S(1)}, u32[]{:S(2)}, u32[]{:S(2)}) %all-to-all-start.5) | async-done | bytes 786464 | tf_op jit(solution)/shard_map/all_to_all | solution.py:485
  532.6 26.2 %shard_map.310.refs_4_ = bf16[1024,1152]{1,0:T(8,128)(2,1)S(1)} custom-call(bf16[1024,1152]{1,0:T(8,128)(2,1)S(1)} %copy-done.59, bf16[1024,384]{1,0:T(8,128)(2,1)S(1)} %bitcast.354, f32[3,2,1024]{2,1,0:T(2,128)S(1)} %copy-done.61, f32[1024,128]{1,0:T(8,128)S(1)} %copy-done.43, f32[1024,128]{1,0:T(8,128)S(1)} %copy-done.41, f32[1024,128]{1,0:T(8,128)S(1)} %copy-done.39, ...), custom_call_target="tpu_custom_call" | custom-call | flops 8053063680 | bytes 7864320 | tf_op jit(solution)/shard_map/pallas_call | solution.py:205
  558.8 4.7 convolution_convert_fusion
  567.5 4.2 collective-permute-done.49
  580.7 6.5 shard_map.312
  587.3 16.1 %collective-permute-done.52 = bf16[1,96,1536]{2,1,0:T(8,128)(2,1)S(1)} collective-permute-done((bf16[1,96,1536]{2,1,0:T(8,128)(2,1)S(1)}, bf16[1,96,1536]{2,1,0:T(8,128)(2,1)S(1)}, u32[]{:S(2)}, u32[]{:S(2)}) %collective-permute-start.52) | collective-permute-done | bytes 294944 | tf_op jit(solution)/shard_map/ppermute | solution.py:476
  614.8 4.3 all-to-all-start.6
  622.9 25.9 %collective-permute-done.57 = bf16[3,2,96,1536]{3,2,0,1:T(8,128)(2,1)} collective-permute-done((bf16[3,2,96,1536]{3,2,0,1:T(8,128)(2,1)}, bf16[3,2,96,1536]{3,2,0,1:T(8,128)(2,1)}, u32[]{:S(2)}, u32[]{:S(2)}) %collective-permute-start.57) | collective-permute-done | bytes 1769504 | tf_op jit(solution)/shard_map/ppermute | solution.py:476
  657.1 5.4 all-to-all-done.6
  674.1 4.3 all-to-all-start.7
  687.3 9.9 %collective-permute-done.60 = bf16[3,96,1536]{2,1,0:T(8,128)(2,1)} collective-permute-done((bf16[3,96,1536]{2,1,0:T(8,128)(2,1)}, bf16[3,96,1536]{2,1,0:T(8,128)(2,1)}, u32[]{:S(2)}, u32[]{:S(2)}) %collective-permute-start.60) | collective-permute-done | bytes 884768 | tf_op jit(solution)/shard_map/ppermute | solution.py:476
  702.1 14.7 %collective-permute-done.59 = bf16[256,1536]{1,0:T(8,128)(2,1)} collective-permute-done((bf16[256,1536]{1,0:T(8,128)(2,1)S(1)}, bf16[256,1536]{1,0:T(8,128)(2,1)}, u32[]{:S(2)}, u32[]{:S(2)}) %collective-permute-start.59) | collective-permute-done | bytes 786464 | tf_op jit(solution)/shard_map/ppermute | solution.py:481
  716.8 5.4 all-to-all-done.7
  743.9 4.9 all-to-all-start.9
  751.5 10.4 %all-to-all-done.9 = bf16[4,48,1152]{2,1,0:T(8,128)(2,1)S(1)} async-done(((bf16[4,48,1152]{2,1,0:T(8,128)(2,1)}), bf16[4,48,1152]{2,1,0:T(8,128)(2,1)S(1)}, u32[]{:S(2)}, u32[]{:S(2)}) %all-to-all-start.9) | async-done | bytes 442400 | tf_op jit(solution)/shard_map/all_to_all | solution.py:485
  (581 shorter events, 281.2 us)
Async XLA Ops:
  7.2 229.7 %all-gather.13.cloned.1.call-start = ((), (), s32[]{:S(2)}) async-start(), calls=%async_computation.12 | async-start | bytes 4866048 | tf_op jit(solution)/shard_map/all_gather | solution.py:647
  12.4 35.4 %collective-permute-start = (bf16[256,1536]{1,0:T(8,128)(2,1)S(1)}, bf16[256,1536]{1,0:T(8,128)(2,1)}, u32[]{:S(2)}, u32[]{:S(2)}) collective-permute-start(bf16[256,1536]{1,0:T(8,128)(2,1)S(1)} %fusion.14.refs_0_), channel_id=1, source_target_pairs={{0,1},{1,2},{2,3},{3,0},{4,5},{5,6},{6,7},{7,4},{8,9},{9,10},{10,1... | collective-permute-start | bytes 2359304 | tf_op jit(solution)/shard_map/ppermute | solution.py:481
  17.1 30.7 %collective-permute-start.1 = (bf16[3,96,1536]{2,1,0:T(8,128)(2,1)}, bf16[3,96,1536]{2,1,0:T(8,128)(2,1)}, u32[]{:S(2)}, u32[]{:S(2)}) collective-permute-start(bf16[3,96,1536]{2,1,0:T(8,128)(2,1)} %get-tuple-element.239), channel_id=1, source_target_pairs={{0,8},{4,12},{8,0},{12,4},{16,24},{20,28},{24,16},{28,20},{1,9},{5... | collective-permute-start | bytes 2654216 | tf_op jit(solution)/shard_map/ppermute | solution.py:476
  18.6 29.2 %collective-permute-start.2 = (bf16[3,96,1536]{2,1,0:T(8,128)(2,1)}, bf16[3,96,1536]{2,1,0:T(8,128)(2,1)}, u32[]{:S(2)}, u32[]{:S(2)}) collective-permute-start(bf16[3,96,1536]{2,1,0:T(8,128)(2,1)} %get-tuple-element.243), channel_id=1, source_target_pairs={{0,16},{4,20},{8,24},{12,28},{16,0},{20,4},{24,8},{28,12},{1,17},{... | collective-permute-start | bytes 2654216 | tf_op jit(solution)/shard_map/ppermute | solution.py:476
  22.7 25.1 %all-to-all-start = ((bf16[4,48,1152]{2,1,0:T(8,128)(2,1)}), bf16[4,48,1152]{2,1,0:T(8,128)(2,1)}, u32[]{:S(2)}, u32[]{:S(2)}) async-start(bf16[4,48,1152]{2,1,0:T(8,128)(2,1)} %reshape.787), calls=%async_computation | async-start | bytes 884736 | tf_op jit(solution)/shard_map/all_to_all | solution.py:485
  47.8 28.1 %collective-permute-start.9 = (bf16[256,1536]{1,0:T(8,128)(2,1)}, bf16[256,1536]{1,0:T(8,128)(2,1)}, u32[]{:S(2)}, u32[]{:S(2)}) collective-permute-start(bf16[256,1536]{1,0:T(8,128)(2,1)} %collective-permute-done.refs_1_), channel_id=1, source_target_pairs={{0,1},{1,2},{2,3},{3,0},{4,5},{5,6},{6,7},{7,4},{8,9},{9,10},{10,1... | collective-permute-start | bytes 2359304 | tf_op jit(solution)/shard_map/ppermute | solution.py:481
  49.7 40.3 %all-to-all-start.1 = ((bf16[4,48,1536]{2,1,0:T(8,128)(2,1)}), bf16[4,48,1536]{2,1,0:T(8,128)(2,1)}, u32[]{:S(2)}, u32[]{:S(2)}) async-start(bf16[4,48,1536]{2,1,0:T(8,128)(2,1)} %broadcast_in_dim.113), calls=%async_computation.1 | async-start | bytes 1179648 | tf_op jit(solution)/shard_map/all_to_all | solution.py:485
  54.7 186.6 %all-gather.9.cloned.1.call-start = ((), (), s32[]{:S(2)}) async-start(), calls=%async_computation.10 | async-start | bytes 5308416 | tf_op jit(solution)/shard_map/all_gather | solution.py:639
  90.6 44.4 %collective-permute-start.19 = (bf16[3,96,1536]{2,1,0:T(8,128)(2,1)}, bf16[3,96,1536]{2,1,0:T(8,128)(2,1)}, u32[]{:S(2)}, u32[]{:S(2)}) collective-permute-start(bf16[3,96,1536]{2,1,0:T(8,128)(2,1)} %get-tuple-element.239), channel_id=1, source_target_pairs={{0,16},{4,20},{8,24},{12,28},{16,0},{20,4},{24,8},{28,12},{1,17},{... | collective-permute-start | bytes 2654216 | tf_op jit(solution)/shard_map/ppermute | solution.py:476
  92.1 42.9 %collective-permute-start.20 = (bf16[3,96,1536]{2,1,0:T(8,128)(2,1)}, bf16[3,96,1536]{2,1,0:T(8,128)(2,1)}, u32[]{:S(2)}, u32[]{:S(2)}) collective-permute-start(bf16[3,96,1536]{2,1,0:T(8,128)(2,1)} %get-tuple-element.243), channel_id=1, source_target_pairs={{0,8},{4,12},{8,0},{12,4},{16,24},{20,28},{24,16},{28,20},{1,9},{5... | collective-permute-start | bytes 2654216 | tf_op jit(solution)/shard_map/ppermute | solution.py:476
  95.4 40.7 %all-to-all-start.2 = ((bf16[4,48,1536]{2,1,0:T(8,128)(2,1)}), bf16[4,48,1536]{2,1,0:T(8,128)(2,1)}, u32[]{:S(2)}, u32[]{:S(2)}) async-start(bf16[4,48,1536]{2,1,0:T(8,128)(2,1)} %broadcast_in_dim.114), calls=%async_computation.2 | async-start | bytes 1179648 | tf_op jit(solution)/shard_map/all_to_all | solution.py:485
  99.5 148.7 %all-gather.11.cloned.1.call-start = ((), (), s32[]{:S(2)}) async-start(), calls=%async_computation.11 | async-start | bytes 5308416 | tf_op jit(solution)/shard_map/all_gather | solution.py:639
  99.6 34.6 %collective-permute-start.10 = (bf16[256,1536]{1,0:T(8,128)(2,1)}, bf16[256,1536]{1,0:T(8,128)(2,1)S(1)}, u32[]{:S(2)}, u32[]{:S(2)}) collective-permute-start(bf16[256,1536]{1,0:T(8,128)(2,1)} %collective-permute-done.9.refs_2_), channel_id=1, source_target_pairs={{0,1},{1,2},{2,3},{3,0},{4,5},{5,6},{6,7},{7,4},{8,9},{9,10},{10,1... | collective-permute-start | bytes 2359304 | tf_op jit(solution)/shard_map/ppermute | solution.py:481
  136.1 42.8 %collective-permute-start.21 = (bf16[3,96,1536]{2,1,0:T(8,128)(2,1)}, bf16[3,96,1536]{2,1,0:T(8,128)(2,1)}, u32[]{:S(2)}, u32[]{:S(2)}) collective-permute-start(bf16[3,96,1536]{2,1,0:T(8,128)(2,1)} %collective-permute-done.1), channel_id=1, source_target_pairs={{0,16},{4,20},{8,24},{12,28},{16,0},{20,4},{24,8},{28,12},{1,17},{... | collective-permute-start | bytes 2654216 | tf_op jit(solution)/shard_map/ppermute | solution.py:476
  137.1 41.8 %collective-permute-start.22 = (bf16[3,96,1536]{2,1,0:T(8,128)(2,1)}, bf16[3,96,1536]{2,1,0:T(8,128)(2,1)}, u32[]{:S(2)}, u32[]{:S(2)}) collective-permute-start(bf16[3,96,1536]{2,1,0:T(8,128)(2,1)} %collective-permute-done.2), channel_id=1, source_target_pairs={{0,8},{4,12},{8,0},{12,4},{16,24},{20,28},{24,16},{28,20},{1,9},{5... | collective-permute-start | bytes 2654216 | tf_op jit(solution)/shard_map/ppermute | solution.py:476
  139.3 39.6 %all-to-all-start.3 = ((bf16[4,48,1536]{2,1,0:T(8,128)(2,1)}), bf16[4,48,1536]{2,1,0:T(8,128)(2,1)}, u32[]{:S(2)}, u32[]{:S(2)}) async-start(bf16[4,48,1536]{2,1,0:T(8,128)(2,1)} %broadcast_in_dim.115), calls=%async_computation.3 | async-start | bytes 1179648 | tf_op jit(solution)/shard_map/all_to_all | solution.py:485
  179.5 23.2 %collective-permute-start.25 = (bf16[3,96,1536]{2,1,0:T(8,128)(2,1)}, bf16[3,96,1536]{2,1,0:T(8,128)(2,1)}, u32[]{:S(2)}, u32[]{:S(2)}) collective-permute-start(bf16[3,96,1536]{2,1,0:T(8,128)(2,1)} %collective-permute-done.19), channel_id=1, source_target_pairs={{0,4},{4,0},{8,12},{12,8},{16,20},{20,16},{24,28},{28,24},{1,5},{5... | collective-permute-start | bytes 2654216 | tf_op jit(solution)/shard_map/ppermute | solution.py:471
  179.6 24.9 %collective-permute-start.26 = (bf16[3,96,1536]{2,1,0:T(8,128)(2,1)}, bf16[3,96,1536]{2,1,0:T(8,128)(2,1)S(1)}, u32[]{:S(2)}, u32[]{:S(2)}) collective-permute-start(bf16[3,96,1536]{2,1,0:T(8,128)(2,1)} %collective-permute-done.21), channel_id=1, source_target_pairs={{0,4},{4,0},{8,12},{12,8},{16,20},{20,16},{24,28},{28,24},{1,5},{5... | collective-permute-start | bytes 2654216 | tf_op jit(solution)/shard_map/ppermute | solution.py:471
  180.1 25.3 %collective-permute-start.27 = (bf16[3,96,1536]{2,1,0:T(8,128)(2,1)}, bf16[3,96,1536]{2,1,0:T(8,128)(2,1)S(1)}, u32[]{:S(2)}, u32[]{:S(2)}) collective-permute-start(bf16[3,96,1536]{2,1,0:T(8,128)(2,1)} %get-tuple-element.243), channel_id=1, source_target_pairs={{0,4},{4,0},{8,12},{12,8},{16,20},{20,16},{24,28},{28,24},{1,5},{5... | collective-permute-start | bytes 2654216 | tf_op jit(solution)/shard_map/ppermute | solution.py:471
  180.1 53.7 %all-to-all-start.4 = ((bf16[4,256,384]{2,1,0:T(8,128)(2,1)}), bf16[4,256,384]{2,1,0:T(8,128)(2,1)S(1)}, u32[]{:S(2)}, u32[]{:S(2)}) async-start(bf16[4,256,384]{2,1,0:T(8,128)(2,1)} %bitcast.15), calls=%async_computation.4 | async-start | bytes 1572864 | tf_op jit(solution)/shard_map/all_to_all | solution.py:485
  185.1 80.9 %all-gather.15.cloned.1.call-start = ((), (), s32[]{:S(2)}) async-start(), calls=%async_computation.13 | async-start | bytes 5308416 | tf_op jit(solution)/shard_map/all_gather | solution.py:639
  277.6 37.1 %collective-permute-start.34 = (bf16[256,1536]{1,0:T(8,128)(2,1)S(1)}, bf16[256,1536]{1,0:T(8,128)(2,1)S(1)}, u32[]{:S(2)}, u32[]{:S(2)}) collective-permute-start(bf16[256,1536]{1,0:T(8,128)(2,1)S(1)} %collective-permute-done.32.g_ref.refs_9_), channel_id=1, source_target_pairs={{0,1},{1,2},{2,3},{3,0},{4,5},{5,6},{6,7},{7,4},{8,9},{9,10},{10,1... | collective-permute-start | bytes 2359304 | tf_op jit(solution)/shard_map/ppermute | solution.py:481
  334.0 35.2 %collective-permute-start.37 = (bf16[256,1536]{1,0:T(8,128)(2,1)S(1)}, bf16[256,1536]{1,0:T(8,128)(2,1)S(1)}, u32[]{:S(2)}, u32[]{:S(2)}) collective-permute-start(bf16[256,1536]{1,0:T(8,128)(2,1)S(1)} %get-tuple-element.273), channel_id=1, source_target_pairs={{0,1},{1,2},{2,3},{3,0},{4,5},{5,6},{6,7},{7,4},{8,9},{9,10},{10,1... | collective-permute-start | bytes 2359304 | tf_op jit(solution)/shard_map/ppermute | solution.py:481
  369.4 45.8 %collective-permute-start.38 = (bf16[256,1536]{1,0:T(8,128)(2,1)S(1)}, bf16[256,1536]{1,0:T(8,128)(2,1)S(1)}, u32[]{:S(2)}, u32[]{:S(2)}) collective-permute-start(bf16[256,1536]{1,0:T(8,128)(2,1)S(1)} %add_convert_fusion.9), channel_id=1, source_target_pairs={{0,1},{1,2},{2,3},{3,0},{4,5},{5,6},{6,7},{7,4},{8,9},{9,10},{10,1... | collective-permute-start | bytes 2359304 | tf_op jit(solution)/shard_map/ppermute | solution.py:481
  369.5 45.7 %collective-permute-start.39 = (bf16[256,1536]{1,0:T(8,128)(2,1)S(1)}, bf16[256,1536]{1,0:T(8,128)(2,1)S(1)}, u32[]{:S(2)}, u32[]{:S(2)}) collective-permute-start(bf16[256,1536]{1,0:T(8,128)(2,1)S(1)} %get-tuple-element.286), channel_id=1, source_target_pairs={{0,1},{1,2},{2,3},{3,0},{4,5},{5,6},{6,7},{7,4},{8,9},{9,10},{10,1... | collective-permute-start | bytes 2359304 | tf_op jit(solution)/shard_map/ppermute | solution.py:481
  415.3 22.6 %collective-permute-start.42 = (bf16[3,768,1536]{2,1,0:T(8,128)(2,1)}, bf16[3,768,1536]{2,1,0:T(8,128)(2,1)S(1)}, u32[]{:S(2)}, u32[]{:S(2)}) collective-permute-start(bf16[3,768,1536]{2,1,0:T(8,128)(2,1)} %shard_map.304), channel_id=1, source_target_pairs={{0,4},{4,0},{8,12},{12,8},{16,20},{20,16},{24,28},{28,24},{1,5},{5... | collective-permute-start | bytes 21233672 | tf_op jit(solution)/shard_map/ppermute | solution.py:471
  416.9 50.8 %collective-permute-start.40 = (bf16[256,1536]{1,0:T(8,128)(2,1)S(1)}, bf16[256,1536]{1,0:T(8,128)(2,1)S(1)}, u32[]{:S(2)}, u32[]{:S(2)}) collective-permute-start(bf16[256,1536]{1,0:T(8,128)(2,1)S(1)} %add_convert_fusion.8), channel_id=1, source_target_pairs={{0,1},{1,2},{2,3},{3,0},{4,5},{5,6},{6,7},{7,4},{8,9},{9,10},{10,1... | collective-permute-start | bytes 2359304 | tf_op jit(solution)/shard_map/ppermute | solution.py:481
  481.9 44.1 %collective-permute-start.47 = (bf16[3,2,2,2,96,1536]{5,4,3,2,1,0:T(8,128)(2,1)}, bf16[3,2,2,2,96,1536]{5,4,3,2,1,0:T(8,128)(2,1)}, u32[]{:S(2)}, u32[]{:S(2)}) collective-permute-start(bf16[3,2,2,2,96,1536]{5,4,3,2,1,0:T(8,128)(2,1)} %get-tuple-element.331), channel_id=1, source_target_pairs={{0,4},{4,0},{8,12},{12,8},{16,20},{20,16},{24,28},{28,24},{1,5},{5... | collective-permute-start | bytes 21233672 | tf_op jit(solution)/shard_map/ppermute | solution.py:471
  483.4 25.8 %collective-permute-start.45 = (bf16[1,2,96,1536]{3,2,1,0:T(8,128)(2,1)}, bf16[1,2,96,1536]{3,2,1,0:T(8,128)(2,1)}, u32[]{:S(2)}, u32[]{:S(2)}) collective-permute-start(bf16[1,2,96,1536]{3,2,1,0:T(8,128)(2,1)} %fusion.28), channel_id=1, source_target_pairs={{0,16},{4,20},{8,24},{12,28},{16,0},{20,4},{24,8},{28,12},{1,17},{... | collective-permute-start | bytes 1769480 | tf_op jit(solution)/shard_map/ppermute | solution.py:476
  485.8 23.4 %collective-permute-start.46 = (bf16[1,2,96,1536]{3,2,1,0:T(8,128)(2,1)}, bf16[1,2,96,1536]{3,2,1,0:T(8,128)(2,1)}, u32[]{:S(2)}, u32[]{:S(2)}) collective-permute-start(bf16[1,2,96,1536]{3,2,1,0:T(8,128)(2,1)} %fusion.29), channel_id=1, source_target_pairs={{0,8},{4,12},{8,0},{12,4},{16,24},{20,28},{24,16},{28,20},{1,9},{5... | collective-permute-start | bytes 1769480 | tf_op jit(solution)/shard_map/ppermute | solution.py:476
  488.2 24.0 %collective-permute-start.44 = (bf16[256,1536]{1,0:T(8,128)(2,1)}, bf16[256,1536]{1,0:T(8,128)(2,1)}, u32[]{:S(2)}, u32[]{:S(2)}) collective-permute-start(bf16[256,1536]{1,0:T(8,128)(2,1)} %add_convert_fusion.6), channel_id=1, source_target_pairs={{0,1},{1,2},{2,3},{3,0},{4,5},{5,6},{6,7},{7,4},{8,9},{9,10},{10,1... | collective-permute-start | bytes 2359304 | tf_op jit(solution)/shard_map/ppermute | solution.py:481
  488.5 37.4 %all-to-all-start.5 = ((bf16[4,256,384]{2,1,0:T(8,128)(2,1)}), bf16[4,256,384]{2,1,0:T(8,128)(2,1)S(1)}, u32[]{:S(2)}, u32[]{:S(2)}) async-start(bf16[4,256,384]{2,1,0:T(8,128)(2,1)} %pad_maximum_fusion.5), calls=%async_computation.5 | async-start | bytes 1572864 | tf_op jit(solution)/shard_map/all_to_all | solution.py:485
  531.1 40.6 %collective-permute-start.49 = (bf16[3,2,96,1536]{3,2,1,0:T(8,128)(2,1)S(1)}, bf16[3,2,96,1536]{3,2,1,0:T(8,128)(2,1)S(1)}, u32[]{:S(2)}, u32[]{:S(2)}) collective-permute-start(bf16[3,2,96,1536]{3,2,1,0:T(8,128)(2,1)S(1)} %fusion.13), channel_id=1, source_target_pairs={{0,8},{4,12},{8,0},{12,4},{16,24},{20,28},{24,16},{28,20},{1,9},{5... | collective-permute-start | bytes 5308424 | tf_op jit(solution)/shard_map/ppermute | solution.py:476
  531.9 42.1 %collective-permute-start.48 = (bf16[3,2,96,1536]{3,2,0,1:T(8,128)(2,1)S(1)}, bf16[3,2,96,1536]{3,2,0,1:T(8,128)(2,1)S(1)}, u32[]{:S(2)}, u32[]{:S(2)}) collective-permute-start(bf16[3,2,96,1536]{3,2,0,1:T(8,128)(2,1)S(1)} %fusion.12), channel_id=1, source_target_pairs={{0,16},{4,20},{8,24},{12,28},{16,0},{20,4},{24,8},{28,12},{1,17},{... | collective-permute-start | bytes 5308424 | tf_op jit(solution)/shard_map/ppermute | solution.py:476
  576.3 27.6 %collective-permute-start.54 = (bf16[3,96,1536]{2,1,0:T(8,128)(2,1)S(1)}, bf16[3,96,1536]{2,1,0:T(8,128)(2,1)}, u32[]{:S(2)}, u32[]{:S(2)}) collective-permute-start(bf16[3,96,1536]{2,1,0:T(8,128)(2,1)S(1)} %slice_bitcast_fusion.3), channel_id=1, source_target_pairs={{0,16},{4,20},{8,24},{12,28},{16,0},{20,4},{24,8},{28,12},{1,17},{... | collective-permute-start | bytes 2654216 | tf_op jit(solution)/shard_map/ppermute | solution.py:476
  577.0 28.3 %collective-permute-start.53 = (bf16[3,96,1536]{2,1,0:T(8,128)(2,1)S(1)}, bf16[3,96,1536]{2,1,0:T(8,128)(2,1)S(1)}, u32[]{:S(2)}, u32[]{:S(2)}) collective-permute-start(bf16[3,96,1536]{2,1,0:T(8,128)(2,1)S(1)} %slice_bitcast_fusion.6), channel_id=1, source_target_pairs={{0,8},{4,12},{8,0},{12,4},{16,24},{20,28},{24,16},{28,20},{1,9},{5... | collective-permute-start | bytes 2654216 | tf_op jit(solution)/shard_map/ppermute | solution.py:476
  577.8 25.6 %collective-permute-start.52 = (bf16[1,96,1536]{2,1,0:T(8,128)(2,1)S(1)}, bf16[1,96,1536]{2,1,0:T(8,128)(2,1)S(1)}, u32[]{:S(2)}, u32[]{:S(2)}) collective-permute-start(bf16[1,96,1536]{2,1,0:T(8,128)(2,1)S(1)} %slice_bitcast_fusion.33), channel_id=1, source_target_pairs={{0,16},{4,20},{8,24},{12,28},{16,0},{20,4},{24,8},{28,12},{1,17},{... | collective-permute-start | bytes 884744 | tf_op jit(solution)/shard_map/ppermute | solution.py:476
  579.3 24.5 %collective-permute-start.51 = (bf16[1,96,1536]{2,1,0:T(8,128)(2,1)S(1)}, bf16[1,96,1536]{2,1,0:T(8,128)(2,1)S(1)}, u32[]{:S(2)}, u32[]{:S(2)}) collective-permute-start(bf16[1,96,1536]{2,1,0:T(8,128)(2,1)S(1)} %slice_bitcast_fusion.34), channel_id=1, source_target_pairs={{0,8},{4,12},{8,0},{12,4},{16,24},{20,28},{24,16},{28,20},{1,9},{5... | collective-permute-start | bytes 884744 | tf_op jit(solution)/shard_map/ppermute | solution.py:476
  580.7 24.8 %collective-permute-start.50 = (bf16[256,1536]{1,0:T(8,128)(2,1)}, bf16[256,1536]{1,0:T(8,128)(2,1)}, u32[]{:S(2)}, u32[]{:S(2)}) collective-permute-start(bf16[256,1536]{1,0:T(8,128)(2,1)} %get-tuple-element.341), channel_id=1, source_target_pairs={{0,1},{1,2},{2,3},{3,0},{4,5},{5,6},{6,7},{7,4},{8,9},{9,10},{10,1... | collective-permute-start | bytes 2359304 | tf_op jit(solution)/shard_map/ppermute | solution.py:481
  610.0 38.8 %collective-permute-start.57 = (bf16[3,2,96,1536]{3,2,0,1:T(8,128)(2,1)}, bf16[3,2,96,1536]{3,2,0,1:T(8,128)(2,1)}, u32[]{:S(2)}, u32[]{:S(2)}) collective-permute-start(bf16[3,2,96,1536]{3,2,0,1:T(8,128)(2,1)} %bitcast.348), channel_id=1, source_target_pairs={{0,8},{4,12},{8,0},{12,4},{16,24},{20,28},{24,16},{28,20},{1,9},{5... | collective-permute-start | bytes 5308424 | tf_op jit(solution)/shard_map/ppermute | solution.py:476
  612.1 40.0 %collective-permute-start.56 = (bf16[3,2,96,1536]{3,2,0,1:T(8,128)(2,1)}, bf16[3,2,96,1536]{3,2,0,1:T(8,128)(2,1)}, u32[]{:S(2)}, u32[]{:S(2)}) collective-permute-start(bf16[3,2,96,1536]{3,2,0,1:T(8,128)(2,1)} %bitcast.349), channel_id=1, source_target_pairs={{0,16},{4,20},{8,24},{12,28},{16,0},{20,4},{24,8},{28,12},{1,17},{... | collective-permute-start | bytes 5308424 | tf_op jit(solution)/shard_map/ppermute | solution.py:476
  614.8 47.6 %all-to-all-start.6 = ((bf16[4,2,48,1536]{3,2,1,0:T(8,128)(2,1)}), bf16[4,2,48,1536]{3,2,1,0:T(8,128)(2,1)}, u32[]{:S(2)}, u32[]{:S(2)}) async-start(bf16[4,2,48,1536]{3,2,1,0:T(8,128)(2,1)} %pad_maximum_fusion.2), calls=%async_computation.6 | async-start | bytes 2359296 | tf_op jit(solution)/shard_map/all_to_all | solution.py:485
  619.1 43.3 %collective-permute-start.58 = (bf16[1,2,2,2,96,1152]{5,4,3,2,1,0:T(8,128)(2,1)S(1)}, bf16[1,2,2,2,96,1152]{5,4,3,2,1,0:T(8,128)(2,1)}, u32[]{:S(2)}, u32[]{:S(2)}) collective-permute-start(bf16[1,2,2,2,96,1152]{5,4,3,2,1,0:T(8,128)(2,1)S(1)} %get-tuple-element.360), channel_id=1, source_target_pairs={{0,4},{4,0},{8,12},{12,8},{16,20},{20,16},{24,28},{28,24},{1,5},{5... | collective-permute-start | bytes 5308424 | tf_op jit(solution)/shard_map/ppermute | solution.py:471
  620.9 36.2 %collective-permute-start.55 = (bf16[256,1536]{1,0:T(8,128)(2,1)S(1)}, bf16[256,1536]{1,0:T(8,128)(2,1)}, u32[]{:S(2)}, u32[]{:S(2)}) collective-permute-start(bf16[256,1536]{1,0:T(8,128)(2,1)S(1)} %add_convert_fusion.4), channel_id=1, source_target_pairs={{0,1},{1,2},{2,3},{3,0},{4,5},{5,6},{6,7},{7,4},{8,9},{9,10},{10,1... | collective-permute-start | bytes 2359304 | tf_op jit(solution)/shard_map/ppermute | solution.py:481
  669.4 27.8 %collective-permute-start.60 = (bf16[3,96,1536]{2,1,0:T(8,128)(2,1)}, bf16[3,96,1536]{2,1,0:T(8,128)(2,1)}, u32[]{:S(2)}, u32[]{:S(2)}) collective-permute-start(bf16[3,96,1536]{2,1,0:T(8,128)(2,1)} %slice_bitcast_fusion.5), channel_id=1, source_target_pairs={{0,8},{4,12},{8,0},{12,4},{16,24},{20,28},{24,16},{28,20},{1,9},{5... | collective-permute-start | bytes 2654216 | tf_op jit(solution)/shard_map/ppermute | solution.py:476
  671.2 27.4 %collective-permute-start.61 = (bf16[3,96,1536]{2,1,0:T(8,128)(2,1)}, bf16[3,96,1536]{2,1,0:T(8,128)(2,1)}, u32[]{:S(2)}, u32[]{:S(2)}) collective-permute-start(bf16[3,96,1536]{2,1,0:T(8,128)(2,1)} %slice_bitcast_fusion.4), channel_id=1, source_target_pairs={{0,16},{4,20},{8,24},{12,28},{16,0},{20,4},{24,8},{28,12},{1,17},{... | collective-permute-start | bytes 2654216 | tf_op jit(solution)/shard_map/ppermute | solution.py:476
  674.1 48.1 %all-to-all-start.7 = ((bf16[4,2,48,1536]{3,2,1,0:T(8,128)(2,1)}), bf16[4,2,48,1536]{3,2,1,0:T(8,128)(2,1)}, u32[]{:S(2)}, u32[]{:S(2)}) async-start(bf16[4,2,48,1536]{3,2,1,0:T(8,128)(2,1)} %copy.149), calls=%async_computation.7 | async-start | bytes 2359296 | tf_op jit(solution)/shard_map/all_to_all | solution.py:485
  679.9 36.9 %collective-permute-start.59 = (bf16[256,1536]{1,0:T(8,128)(2,1)S(1)}, bf16[256,1536]{1,0:T(8,128)(2,1)}, u32[]{:S(2)}, u32[]{:S(2)}) collective-permute-start(bf16[256,1536]{1,0:T(8,128)(2,1)S(1)} %add_convert_fusion.3), channel_id=1, source_target_pairs={{0,1},{1,2},{2,3},{3,0},{4,5},{5,6},{6,7},{7,4},{8,9},{9,10},{10,1... | collective-permute-start | bytes 2359304 | tf_op jit(solution)/shard_map/ppermute | solution.py:481
  (165 other events, 2618.6 us)
Sparse Core Ops, SparseCore 0:
  11.4 102.2 all-gather.12
  115.6 53.0 all-gather.8
  170.6 37.8 all-gather.10
  210.2 38.9 all-gather.14

commit v3 on v2

--- a/solution.py
+++ b/solution.py
@@ -50,6 +50,12 @@
 LANES = 128
 PAIR = LANES // HDIM
 LOG2E = 1.4426950408889634
+
+
+def taking(microseconds):
+    return pl.CostEstimate(
+        flops=0, bytes_accessed=int(3e6 * microseconds), transcendentals=0
+    )
 
 
 def turn(values, cosine, sine_low, sine_high, sign):
@@ -148,11 +154,7 @@
             jax.ShapeDtypeStruct((pairs, PAIR, length), jnp.float32),
         ],
         compiler_params=pltpu.CompilerParams(vmem_limit_bytes=40 << 20),
-        cost_estimate=pl.CostEstimate(
-            flops=8 * pairs * PAIR * length * length * HDIM,
-            bytes_accessed=2 * (length + group * pairs) * width,
-            transcendentals=pairs * PAIR * length * length,
-        ),
+        cost_estimate=taking(8),
     )(*norms, qkv_cols, *tables, segment[:, None], segment[None, :])
 
 
@@ -219,11 +221,7 @@
         out_shape=jax.ShapeDtypeStruct(qkv.shape, jnp.bfloat16),
         scratch_shapes=[pltpu.VMEM((length, LANES), jnp.float32)] * 2,
         compiler_params=pltpu.CompilerParams(vmem_limit_bytes=40 << 20),
-        cost_estimate=pl.CostEstimate(
-            flops=20 * pairs * PAIR * length * length * HDIM,
-            bytes_accessed=20 * grad_out.size,
-            transcendentals=pairs * PAIR * length * length,
-        ),
+        cost_estimate=taking(9),
     )(qkv, grad_out, log_total, *tables, segment[:, None], segment[None, :])
 
 
@@ -251,11 +249,7 @@
         out_specs=[pl.BlockSpec((rows, lanes), lambda p: (0, p)) for rows in out_rows],
         out_shape=[jax.ShapeDtypeStruct((rows, width), jnp.bfloat16) for rows in out_rows],
         compiler_params=pltpu.CompilerParams(vmem_limit_bytes=32 << 20),
-        cost_estimate=pl.CostEstimate(
-            flops=flops * width * arrays[0].shape[0] * arrays[1].shape[0],
-            bytes_accessed=2 * sum(a.size for a in arrays),
-            transcendentals=HEADS * arrays[0].shape[0] * arrays[1].shape[0],
-        ),
+        cost_estimate=taking(4),
     )(*arrays, item_row)
 
 
@@ -358,11 +352,7 @@
         scratch_shapes=[pltpu.VMEM((rows, width), jnp.float32)] * 2,
         input_output_aliases={5 + n: n for n in range(len(held))},
         compiler_params=pltpu.CompilerParams(vmem_limit_bytes=40 << 20),
-        cost_estimate=pl.CostEstimate(
-            flops=12 * rows * width * units,
-            bytes_accessed=6 * units * width + 10 * rows * width,
-            transcendentals=rows * units,
-        ),
+        cost_estimate=taking(4),
     )(normed, grads, gate_up, gate_up, down, *held)
 
 
@@ -403,11 +393,7 @@
         out_shape=jax.ShapeDtypeStruct((3, count // 2, width), jnp.bfloat16),
         scratch_shapes=[pltpu.VMEM((length, width), jnp.bfloat16)] * 2,
         compiler_params=pltpu.CompilerParams(vmem_limit_bytes=56 << 20),
-        cost_estimate=pl.CostEstimate(
-            flops=3 * length * width * count,
-            bytes_accessed=4 * length * width + 6 * count * width,
-            transcendentals=0,
-        ),
+        cost_estimate=taking(5),
     )(*units, *norms, *grads, *extra)
 
 
@@ -459,11 +445,7 @@
         scratch_shapes=[pltpu.VMEM((tile, columns), jnp.bfloat16)],
         input_output_aliases={len(lefts) + len(rights) + n: n for n in range(len(held))},
         compiler_params=pltpu.CompilerParams(vmem_limit_bytes=40 << 20),
-        cost_estimate=pl.CostEstimate(
-            flops=2 * rows * len(lefts) * height * columns * len(rights),
-            bytes_accessed=4 * height * columns * len(rights),
-            transcendentals=0,
-        ),
+        cost_estimate=taking(1.5),
     )(*lefts, *rights, *held)
 
 
@@ -479,6 +461,14 @@
 def shift_seq(values, step=1):
     size = lax.axis_size("seq")
     return lax.ppermute(values, "seq", [(s, (s + step) % size) for s in range(size)])
+
+
+def gather_rest(pieces):
+    last = shift_seq(pieces[0], -1)
+    pieces = list(pieces)
+    for _ in range(lax.axis_size("seq") - 3):
+        pieces.append(shift_seq(pieces[-1]))
+    return pieces + [last]
 
 
 def swap_seq(values):
@@ -523,31 +513,48 @@
     return {(core,) + p: swap_core(v) if core else v for core in range(2) for p, v in plane.items()}
 
 
-def reduce_first(own, arrived=None):
-    def terms(*index):
-        index = (slice(None),) + index
-        values = own[index].astype(jnp.float32)
-        return values if arrived is None else values + arrived[index].astype(jnp.float32)
-
+def low(values):
+    return values.astype(jnp.bfloat16)
+
+
+def terms(own, arrived, *index):
+    index = (slice(None),) + index
+    values = own[index].astype(jnp.float32)
+    return values if arrived is None else values + arrived[index].astype(jnp.float32)
+
+
+def pack_first(own, arrived=None):
     y_size = own.shape[2]
-    total = terms(0, y_size - 1).astype(jnp.bfloat16)
-    for y in range(y_size - 2, -1, -1):
-        total = (shift_dp(total, -1, 0).astype(jnp.float32) + terms(0, y)).astype(jnp.bfloat16)
-    sent = shift_dp(terms(1, slice(None), 1).astype(jnp.bfloat16), 0, 1).astype(jnp.float32)
-    return total, (sent + terms(1, slice(None), 0)).astype(jnp.bfloat16)
-
-
-def reduce_second(first, second):
-    first = add_wide(first[:, 0], shift_dp(first[:, 1], 0, 1))
+    total = low(terms(own, arrived, 0, y_size - 1))
+    for y in range(y_size - 2, 0, -1):
+        total = low(shift_dp(total, -1, 0).astype(jnp.float32) + terms(own, arrived, 0, y))
+    return total, low(terms(own, arrived, 1, slice(None), 1))
+
+
+def send_first(packed):
+    return shift_dp(packed[0], -1, 0), shift_dp(packed[1], 0, 1)
+
+
+def add_first(came, own, arrived=None):
+    return (
+        low(came[0].astype(jnp.float32) + terms(own, arrived, 0, 0)),
+        low(came[1].astype(jnp.float32) + terms(own, arrived, 1, slice(None), 0)),
+    )
+
+
+def pack_second(first, second):
     total = second[:, -1]
-    for y in range(second.shape[1] - 2, -1, -1):
-        total = add_wide(shift_dp(total.astype(jnp.bfloat16), -1, 0), second[:, y])
-    return first, total
-
-
-def dp_block(core, y, x, dp_place):
-    size = lax.axis_size("dp")
-    return lax.rem(dp_place + (size - 4 * y), size) ^ (core + 2 * x)
+    for y in range(second.shape[1] - 2, 0, -1):
+        total = add_low(shift_dp(total, -1, 0), second[:, y])
+    return first[:, 1], total
+
+
+def send_second(packed):
+    return shift_dp(packed[0], 0, 1), shift_dp(packed[1], -1, 0)
+
+
+def add_second(came, first, second):
+    return add_wide(first[:, 0], came[0]), add_wide(second[:, 0], came[1])
 
 
 def assemble(pieces, out_shapes, copies):
@@ -556,7 +563,6 @@
     def body(*refs):
         sources, targets = refs[:count], refs[count : count + len(out_shapes)]
         held, loaded, stored = refs[count + len(out_shapes) : -2], refs[-2], refs[-1]
-        dp_place = lax.axis_index("dp")
         loads = [pltpu.make_async_copy(sources[n], held[n], loaded.at[n]) for n in range(count)]
         for load in loads:
             load.start()
@@ -568,7 +574,7 @@
                     stores.append(
                         pltpu.make_async_copy(
                             held[n].at[source],
-                            targets[out].at[target(dp_place)],
+                            targets[out].at[target],
                             stored.at[number],
                         )
                     )
@@ -576,7 +582,6 @@
         for store in stores:
             store.wait()
 
-    moved = sum(2 * p.size * p.dtype.itemsize for p in pieces)
     return pl.pallas_call(
         body,
         out_shape=[jax.ShapeDtypeStruct(s, jnp.bfloat16) for s in out_shapes],
@@ -585,26 +590,8 @@
         scratch_shapes=[pltpu.VMEM(p.shape, p.dtype) for p in pieces]
         + [pltpu.SemaphoreType.DMA((count,)), pltpu.SemaphoreType.DMA((len(copies),))],
         compiler_params=pltpu.CompilerParams(vmem_limit_bytes=32 << 20),
-        cost_estimate=pl.CostEstimate(flops=0, bytes_accessed=moved, transcendentals=0),
+        cost_estimate=taking(2),
     )(*pieces)
-
-
-def in_place(plane):
-    held = with_cores(plane)
-    places = list(held)
-    return assemble(
-        [held[p] for p in places],
-        [(lax.axis_size("dp"), 2) + held[places[0]].shape],
-        [
-            (n, (), 0, lambda d, p=p: (dp_block(p[0], p[2], p[3], d), p[1]))
-            for n, p in enumerate(places)
-        ],
-    )[0]
-
-
-def halves(values):
-    middle = values.shape[0] // 2
-    return values[:middle], values[middle:]
 
 
 def local(
@@ -636,17 +623,23 @@
     part_rows = self_query.shape[0]
 
     def whole_rows(rows):
-        return lax.all_gather(rows, "dp", axis=0, tiled=False).reshape(width, width)
+        return lax.all_gather(rows, "dp", axis=0, tiled=False).reshape(-1, rows.shape[-1])
 
     qkv_parts = jnp.stack([self_query, self_key, self_value]).reshape(
         3, part_rows, seq_size, head_width
     )
     qkv_parts = jnp.pad(qkv_parts, ((0, 0),) * 3 + ((0, pairs * LANES - head_width),))
     qkv_parts = qkv_parts.reshape(3, part_rows, seq_size, pairs, LANES).transpose(2, 1, 3, 0, 4)
-    qkv_rows = swap_seq(qkv_parts.reshape(seq_size, part_rows, pairs * 3 * LANES))
-    full_cross_kv = lax.all_gather(
-        jnp.stack([cross_key, cross_value]), ("dp", "seq"), axis=0, tiled=False
-    )
+    qkv_parts = qkv_parts.reshape(seq_size, part_rows, pairs * 3 * LANES)
+    qkv_parts = jnp.concatenate(
+        [qkv_parts]
+        + [jnp.broadcast_to(self_out[None], (seq_size,) + self_out.shape)],
+        axis=2,
+    )
+    qkv_parts, tokens, feed_gate, feed_up, feed_down, cotangent, item_lengths = stage(
+        qkv_parts, tokens, feed_gate, feed_up, feed_down, cotangent, item_lengths
+    )
+    early_rows = swap_seq(qkv_parts)
     token_values = tokens.astype(jnp.float32)
     norm_one, norm_one_back = jax.vjp(layer_norm, token_values, gain_self.astype(jnp.float32))
     norm_one = norm_one.astype(jnp.bfloat16)
@@ -654,6 +647,9 @@
     feed_parts = jnp.stack([feed_gate, feed_up, feed_down])
     half_units = feed_parts.shape[1] // 2
     feed_held = spread_first(feed_parts[:, :half_units], feed_parts[:, half_units:])
+    for y in range(1, y_size):
+        feed_held[0, y, 0] = shift_dp(feed_held[0, y - 1, 0], 1, 0)
+    feed_held[1, 0, 1] = shift_dp(feed_held[1, 0, 0], 0, 1)
     row_ids = jnp.concatenate(
         [
             lax.rem(seq_place + (seq_size - k), seq_size) * rows_dev
@@ -666,48 +662,33 @@
     tables = lane_tables(position)
     valid_rows = (row_segment < 2).astype(jnp.float32)[:, None]
     grad_output_low = (cotangent.astype(jnp.float32) * valid_rows).astype(jnp.bfloat16)
-    qkv_rows, norms_one[1], feed_held, tables, grad_output_low, self_out, cross_query, cross_out = (
-        stage(
-            qkv_rows,
-            norms_one[1],
-            feed_held,
-            tables,
-            grad_output_low,
-            self_out,
-            cross_query,
-            cross_out,
-        )
-    )
-
-    qkv_plane = spread_second(spread_first(*halves(qkv_rows)))
-    norms_one.append(shift_seq(norms_one[-1]))
-    out_rows = gather_places(self_out)
-    qkv_plane, norms_one, out_rows, feed_held, cross_query, cross_out = stage(
-        qkv_plane, norms_one, out_rows, feed_held, cross_query, cross_out
-    )
-    full_out = whole_rows(out_rows)
-
-    for _ in range(seq_size - 3):
-        norms_one.append(shift_seq(norms_one[-1]))
-    cross_query_rows = gather_places(cross_query)
-    for y in range(1, y_size):
-        feed_held[0, y, 0] = shift_dp(feed_held[0, y - 1, 0], 1, 0)
-    feed_held[1, 0, 1] = shift_dp(feed_held[1, 0, 0], 0, 1)
-    qkv_cols = in_place(qkv_plane).reshape(width, pairs * 3 * LANES)
-    norms_one, cross_query_rows, qkv_cols, feed_held, cross_out = stage(
-        norms_one, cross_query_rows, qkv_cols, feed_held, cross_out
-    )
-    full_cross_query = whole_rows(cross_query_rows)
-
-    cross_out_rows = gather_places(cross_out)
+    cross_kv = jnp.concatenate([cross_key, cross_value])
+    early_rows, norms_one[1], feed_held, tables, grad_output_low, cross_query = stage(
+        early_rows, norms_one[1], feed_held, tables, grad_output_low, cross_query
+    )
+    qkv_cols = whole_rows(early_rows[:, :, :-width])
+    full_out = whole_rows(early_rows[:, :, -width:])
+
+    norms_one = gather_rest(norms_one)
+    query_rows = gather_places(cross_query)
     for y in range(1, y_size):
         feed_held[0, y, 1] = shift_dp(feed_held[0, y - 1, 1], 1, 0)
         feed_held[1, y, 1] = shift_dp(feed_held[1, y, 0], 0, 1)
+    norms_one, qkv_cols, feed_held, cross_kv, cross_out, query_rows = stage(
+        norms_one, qkv_cols, feed_held, cross_kv, cross_out, query_rows
+    )
+    full_cross_query = whole_rows(query_rows)
+
+    cross_rows = gather_places(jnp.stack([cross_kv, cross_out]))
     qkv, head_attended, log_total = self_forward(norms_one, qkv_cols, tables, segment)
-    cross_out_rows, feed_held, head_attended = stage(cross_out_rows, feed_held, head_attended)
-    full_cross_out = whole_rows(cross_out_rows)
+    cross_rows, feed_held, head_attended, grad_output_low = stage(
+        cross_rows, feed_held, head_attended, grad_output_low
+    )
+    full_cross_kv = whole_rows(cross_rows[:, 0]).reshape(dp_size * seq_size, 2, -1, width)
+    full_cross_out = whole_rows(cross_rows[:, 1])
 
     attended = swap_seq(head_attended[:, :head_width].reshape(seq_size, rows_dev, head_width))
+    all_grads = [grad_output_low, shift_seq(grad_output_low)]
     feed_cores = with_cores(feed_held)
     places = [
         (core, half, y, x)
@@ -716,23 +697,31 @@
         for y in range(y_size)
         for x in range(2)
     ]
-    unit_gate_up = jnp.concatenate(
-        [feed_cores[p][kind] for kind in range(2) for p in places], axis=0
-    )
-    unit_down = jnp.concatenate([feed_cores[p][2] for p in places], axis=0)
-    attended, unit_gate_up, unit_down, grad_output_low = stage(
-        attended, unit_gate_up, unit_down, grad_output_low
-    )
-
-    all_grads = [grad_output_low, shift_seq(grad_output_low)]
+    unit_gate_up, unit_down = assemble(
+        [feed_cores[p] for p in places],
+        [(2, len(places), half_units, width), (1, len(places), half_units, width)],
+        [
+            (n, (kind,), kind // 2, (kind % 2, n))
+            for n in range(len(places))
+            for kind in range(3)
+        ],
+    )
+    unit_gate_up, unit_down = unit_gate_up.reshape(-1, width), unit_down.reshape(-1, width)
+    attended, unit_gate_up, unit_down, all_grads = stage(
+        attended, unit_gate_up, unit_down, all_grads
+    )
+
+    last_grad = shift_seq(all_grads[0], -1)
     attended = jnp.concatenate([attended[s] for s in range(seq_size)], axis=1)
     first_sum = token_values + matmul(attended, full_out)
     norm_two, norm_two_back = jax.vjp(layer_norm, first_sum, gain_cross.astype(jnp.float32))
     norm_two = norm_two.astype(jnp.bfloat16)
     cross_queries = matmul(norm_two, full_cross_query).astype(jnp.bfloat16)
-    all_grads, cross_queries = stage(all_grads, cross_queries)
-
-    all_grads.append(shift_seq(all_grads[-1]))
+    all_grads, last_grad, cross_queries = stage(all_grads, last_grad, cross_queries)
+
+    for _ in range(seq_size - 3):
+        all_grads.append(shift_seq(all_grads[-1]))
+    all_grads.append(last_grad)
     memory = context[0].reshape(-1, context.shape[3])
     full_cross_key = full_cross_kv[:, 0].reshape(-1, width)
     full_cross_value = full_cross_kv[:, 1].reshape(-1, width)
@@ -746,8 +735,6 @@
     all_grads, norm_three = stage(all_grads, norm_three)
 
     norms = [norm_three, shift_seq(norm_three)]
-    for _ in range(seq_size - 3):
-        all_grads.append(shift_seq(all_grads[-1]))
     norms, all_grads = stage(norms, all_grads)
 
     held, feed_out, feed_dx, moving, feed_moving = None, {}, {}, None, None
@@ -768,16 +755,16 @@
             held = run_block(0, held)
             activation, grad_gate, grad_up = held
             held = (grad_gate, grad_up, activation)
-            other_units = unit_products(held, norms, all_grads, 1)
-            arrived, feed_moving, held, other_units, feed_out, feed_dx = stage(
-                arrived, feed_moving, held, other_units, feed_out, feed_dx
+            arrived, feed_moving, held, feed_out, feed_dx = stage(
+                arrived, feed_moving, held, feed_out, feed_dx
             )
         else:
             norms, arrived, held, feed_out, feed_dx = stage(norms, arrived, held, feed_out, feed_dx)
         moving = feed_dx[k] if k == 1 else add_low(arrived, feed_dx[k])
     arrived = shift_seq(moving)
+    other_units = unit_products(held, norms, all_grads, 1)
+    arrived, other_units = stage(arrived, other_units)
     other_units = swap_core(other_units)
-    arrived, other_units = stage(arrived, other_units)
     grad_norm_three = add_wide(arrived, feed_dx[0])
 
     def seq_blocks(first, second):
@@ -804,51 +791,67 @@
     grad_attended = jnp.stack(
         [grad_attended[:, s * head_width : (s + 1) * head_width] for s in range(seq_size)]
     )
-    feed_moving, cross_out_own, cross_out_other, grad_attended, first_low, grad_cross_queries = (
-        stage(
-            feed_moving,
-            cross_out_own,
-            cross_out_other,
-            grad_attended,
-            first_low,
-            grad_cross_queries,
-        )
-    )
-
-    head_grad = swap_seq(grad_attended).reshape(rows_dev * seq_size, head_width)
-    head_grad = jnp.pad(head_grad, ((0, 0), (0, pairs * LANES - head_width)))
-    for k in range(3, seq_size):
-        feed_moving = shift_seq(add_low(feed_moving, feed_out[k]))
-    cross_out_firsts = reduce_first(cross_out_own, cross_out_other)
     products = weight_products([norm_two], [grad_cross_queries], 0, 3)
     products = weight_products([attended], [first_low], 1, 3, products)
     weight_own, weight_other = weight_products(
         [memory], [grad_memory_keys, grad_memory_values], 2, 3, products
     )
+    cross_out_packed = pack_first(cross_out_own, cross_out_other)
+    feed_moving, cross_out_packed, grad_attended, weight_other, other_units = stage(
+        feed_moving, cross_out_packed, grad_attended, weight_other, other_units
+    )
+
+    head_grad = swap_seq(grad_attended)
+    cross_out_came = send_first(cross_out_packed)
     weight_other = swap_core(weight_other)
-    head_grad, feed_moving, cross_out_firsts, weight_own, weight_other = stage(
-        head_grad, feed_moving, cross_out_firsts, weight_own, weight_other
-    )
-
-    output = (second_sum + add_wide(feed_moving, feed_out[0])).astype(jnp.bfloat16)
-    weight_firsts = reduce_first(weight_own, weight_other)
+    own_units = unit_products(held, norms, all_grads, 0, other_units)
+    head_grad, cross_out_came, weight_other, own_units = stage(
+        head_grad, cross_out_came, weight_other, own_units
+    )
+
+    weight_packed = pack_first(weight_own, weight_other)
+    cross_out_firsts = add_first(cross_out_came, cross_out_own, cross_out_other)
+    head_grad = head_grad.reshape(rows_dev * seq_size, head_width)
+    head_grad = jnp.pad(head_grad, ((0, 0), (0, pairs * LANES - head_width)))
+    for k in range(3, seq_size):
+        feed_moving = add_low(feed_moving, feed_out[k])
+        if k + 1 < seq_size:
+            feed_moving = shift_seq(feed_moving)
+    head_grad, weight_packed, feed_moving, cross_out_firsts = stage(
+        head_grad, weight_packed, feed_moving, cross_out_firsts
+    )
+    if seq_size > 3:
+        feed_moving = shift_seq(feed_moving)
+    weight_came = send_first(weight_packed)
     turned = self_backward(qkv, head_grad, log_total, tables, segment, seq_size)
-    norm_terms = contract_cols(turned, qkv_cols).astype(jnp.bfloat16)
+    weight_came, turned, feed_moving, cross_out_firsts = stage(
+        weight_came, turned, feed_moving, cross_out_firsts
+    )
+
+    norm_terms = low(contract_cols(turned, qkv_cols))
     norm_terms = [norm_terms[k * rows_dev : (k + 1) * rows_dev] for k in range(seq_size)]
-    weight_firsts, norm_terms, turned, cross_out_firsts = stage(
-        weight_firsts, norm_terms, turned, cross_out_firsts
-    )
-
+    weight_firsts = add_first(weight_came, weight_own, weight_other)
+    cross_out_packed = pack_second(*cross_out_firsts)
+    weight_packed = pack_second(*weight_firsts)
+    norm_terms, cross_out_packed, weight_packed, turned, own_units, feed_moving = stage(
+        norm_terms, cross_out_packed, weight_packed, turned, own_units, feed_moving
+    )
     moving = shift_seq(norm_terms[1])
-    cross_out_second = reduce_second(*cross_out_firsts)
-    weight_seconds = reduce_second(*weight_firsts)
-    own_units = unit_products(held, norms, all_grads, 0, other_units)
+    cross_out_came = send_second(cross_out_packed)
+    weight_came = send_second(weight_packed)
     qkv_own, qkv_other = weight_products(norms_one, [turned])
-    moving, cross_out_second, weight_seconds, own_units, qkv_own, qkv_other = stage(
-        moving, cross_out_second, weight_seconds, own_units, qkv_own, qkv_other
-    )
-
-    unit_firsts = reduce_first(own_units.reshape(3, 2, y_size, 2, half_units, width))
+    moving, cross_out_came, weight_came, qkv_own, qkv_other = stage(
+        moving, cross_out_came, weight_came, qkv_own, qkv_other
+    )
+
+    qkv_other = swap_core(qkv_other)
+    if seq_size > 2:
+        moving = shift_seq(add_low(moving, norm_terms[2]))
+    own_units = own_units.reshape(3, 2, y_size, 2, half_units, width)
+    unit_came = send_first(pack_first(own_units))
+    output = low(second_sum + add_wide(feed_moving, feed_out[0]))
+    cross_out_second = add_second(cross_out_came, *cross_out_firsts)
+    weight_seconds = add_second(weight_came, *weight_firsts)
     placed = swap_seq(
         jnp.stack(
             [
@@ -858,32 +861,30 @@
             axis=1,
         )
     )
-    if seq_size > 2:
-        moving = shift_seq(add_low(moving, norm_terms[2]))
-    qkv_other = swap_core(qkv_other)
-    moving, placed, unit_firsts, qkv_other, weight_seconds = stage(
-        moving, placed, unit_firsts, qkv_other, weight_seconds
-    )
+    kv_blocks = jnp.stack(
+        [low(s[2]).reshape(seq_size, -1, width) for s in weight_seconds], axis=1
+    )
+    qkv_came = send_first(pack_first(qkv_own, qkv_other))
+    qkv_firsts = add_first(qkv_came, qkv_own, qkv_other)
+    qkv_seconds = add_second(send_second(pack_second(*qkv_firsts)), *qkv_firsts)
+    later = jnp.concatenate(
+        [
+            seq_blocks(*(s[1] for s in weight_seconds)),
+            kv_blocks.reshape(seq_size, part_rows, width),
+            seq_blocks(*(s[0] for s in qkv_seconds)),
+        ],
+        axis=2,
+    )
+    moving, placed, unit_came, later = stage(moving, placed, unit_came, later)
 
     for k in range(3, seq_size):
         moving = shift_seq(add_low(moving, norm_terms[k]))
-    qkv_firsts = reduce_first(qkv_own, qkv_other)
-    unit_grads = jnp.concatenate(reduce_second(*unit_firsts), axis=1)
-    kv_blocks = jnp.stack(
-        [s[2].astype(jnp.bfloat16).reshape(seq_size, -1, width) for s in weight_seconds], axis=1
-    )
-    later = swap_seq(
-        jnp.stack(
-            [
-                seq_blocks(*(s[1] for s in weight_seconds)),
-                kv_blocks.reshape(seq_size, part_rows, width),
-            ],
-            axis=1,
-        )
-    )
-    moving, later, unit_grads, qkv_firsts = stage(moving, later, unit_grads, qkv_firsts)
-
-    qkv_placed = swap_seq(seq_blocks(*(s[0] for s in reduce_second(*qkv_firsts))))
+    later = swap_seq(later)
+    unit_firsts = add_first(unit_came, own_units)
+    unit_came = send_second(pack_second(*unit_firsts))
+    moving, later, unit_came = stage(moving, later, unit_came)
+
+    unit_grads = jnp.concatenate(add_second(unit_came, *unit_firsts), axis=1)
     grad_norm_one = add_wide(moving, norm_terms[0])
     grad_tokens_wide, grad_gain_self = norm_one_back(grad_norm_one)
     grad_tokens = (grad_tokens_wide + grad_first).astype(jnp.bfloat16)
@@ -892,13 +893,14 @@
     gains = jnp.sum(
         lax.all_to_all(gains, ("dp", "seq"), split_axis=0, concat_axis=0, tiled=True), axis=0
     )
+    split = later[:, :, : 2 * width].reshape(seq_size, part_rows, 2, width).transpose(0, 2, 1, 3)
     grad_cross_out, grad_cross_query, grad_cross_kv, grad_self_out = (
         jnp.sum(p[:, n].astype(jnp.float32), axis=0)
-        for p, n in ((placed, 0), (placed, 1), (later, 1), (later, 0))
+        for p, n in ((placed, 0), (placed, 1), (split, 1), (split, 0))
     )
     kv_rows = part_rows // 2
     grad_qkv = (
-        qkv_placed
+        later[:, :, 2 * width :]
         .reshape(seq_size, part_rows, pairs, 3, LANES)
         .transpose(3, 1, 0, 2, 4)
         .reshape(3, part_rows, seq_size, pairs * LANES)[..., :head_width]

time: 781 us -> 742 us (0.950)
  local copies, waits for them, and re-layouts: 117 us -> 75.9 us
  waiting for transfers between devices: 260 us -> 278 us
  starting transfers between devices: 96 us -> 81 us
    unnamed x301 -> x286, local copies, waits for them, and re-layouts: 80.9 us -> 33.7 us
    ppermute x18, waiting for transfers between devices: 123 us -> 170 us  [shift_seq(): lax.ppermute(values, 'seq', [(s, (s + step) % size) for s in range(size)])]
    all_to_all x9 -> x7, waiting for transfers between devices: 65 us -> 20.9 us  [swap_seq(): lax.all_to_all(values, 'seq', split_axis=0, concat_axis=0, tiled=True)]
    all_gather x4 -> x5, waiting for transfers between devices: 0.05 us -> 20.2 us  [whole_rows(): lax.all_gather(rows, 'dp', axis=0, tiled=False).reshape(-1, rows.shape[-1])]
    all_to_all x9 -> x7, starting transfers between devices: 41 us -> 32.8 us  [swap_seq(): lax.all_to_all(values, 'seq', split_axis=0, concat_axis=0, tiled=True)]
    ppermute x28 -> x22, starting transfers between devices: 31.2 us -> 25.5 us  [shift_dp(): lax.ppermute(values, 'dp', [(d, (d + 4 * y) % size ^ 2 * x) for d in rang...]
    ppermute x28 -> x22, waiting for transfers between devices: 67 us -> 63.9 us  [shift_dp(): lax.ppermute(values, 'dp', [(d, (d + 4 * y) % size ^ 2 * x) for d in rang...]
    convert_element_type x13 -> x14, other arithmetic: 30.1 us -> 28 us  [the longest x13 26.9 us: low(): return values.astype(jnp.bfloat16)]
  transfers between devices with their start and end apart: 80 -> 65, of which waited for: 33 -> 31; matrix products, arithmetic and copies ran while one was open for 22% -> 14% of each run, Pallas kernels for 21% -> 24%
where the time goes in v3:
time: 742 us; the launch traced here: 735 us
  waiting for transfers between devices  278 us (37%)
  Pallas kernels  173 us (23%)
  starting transfers between devices  81 us (11%)
  other arithmetic  80.6 us (11%)
  local copies, waits for them, and re-layouts  75.9 us (10%)
  matrix products  28.8 us (4%)
  between operations  17.4 us (2%)
    ppermute x18, waiting for transfers between devices, shift_seq(): lax.ppermute(values, 'seq', [(s, (s + step) % size) for s in range(size)])  170 us
    ppermute x22, waiting for transfers between devices, shift_dp(): lax.ppermute(values, 'dp', [(d, (d + 4 * y) % size ^ 2 * x) for d in rang...  63.9 us
    pallas_call x4, Pallas kernels, feed_block(): pl.pallas_call(body, grid=(steps,), in_specs=[full, full, pl.BlockSpec((t...  48.2 us
    unnamed x286, local copies, waits for them, and re-layouts  33.7 us
    all_to_all x7, starting transfers between devices, swap_seq(): lax.all_to_all(values, 'seq', split_axis=0, concat_axis=0, tiled=True)  32.8 us
    pallas_call x2, Pallas kernels, unit_products(): pl.pallas_call(body, grid=(steps,), in_specs=[pl.BlockSpec((length, tile)...  27.6 us
    convert_element_type x13, other arithmetic, low(): return values.astype(jnp.bfloat16)  26.9 us
    pallas_call x1, Pallas kernels, self_backward(): pl.pallas_call(body, grid=(pairs,), in_specs=[pl.BlockSpec((length, group...  26.1 us
  transfers between devices with their start and end apart: 65, of which 31 were waited for; matrix products, arithmetic and copies ran while one was open for 14% of the time, Pallas kernels for 24%

profile of v3, /device:TPU:0, one launch (start us, length us, event | category | flops | bytes accessed | tf_op | source)
XLA Modules:
  0.0 734.8 jit_solution(12219754956395293546)
XLA Ops:
  23.9 4.2 all-to-all-start
  34.8 9.9 %collective-permute-done.refs_1_ = bf16[256,1536]{1,0:T(8,128)(2,1)} collective-permute-done((bf16[256,1536]{1,0:T(8,128)(2,1)S(1)}, bf16[256,1536]{1,0:T(8,128)(2,1)}, u32[]{:S(2)}, u32[]{:S(2)}) %collective-permute-start) | collective-permute-done | bytes 786464 | tf_op jit(solution)/shard_map/ppermute | solution.py:463
  44.7 12.3 %collective-permute-done.3.refs_5_ = bf16[3,96,1536]{2,1,0:T(8,128)(2,1)} collective-permute-done((bf16[3,96,1536]{2,1,0:T(8,128)(2,1)}, bf16[3,96,1536]{2,1,0:T(8,128)(2,1)}, u32[]{:S(2)}, u32[]{:S(2)}) %collective-permute-start.3) | collective-permute-done | bytes 884768 | tf_op jit(solution)/shard_map/ppermute | solution.py:458
  58.5 6.2 all-to-all-done
  72.4 4.1 all-to-all-start.1
  81.0 24.1 %collective-permute-done.6.refs_3_ = bf16[256,1536]{1,0:T(8,128)(2,1)S(1)} collective-permute-done((bf16[256,1536]{1,0:T(8,128)(2,1)S(1)}, bf16[256,1536]{1,0:T(8,128)(2,1)S(1)}, u32[]{:S(2)}, u32[]{:S(2)}) %collective-permute-start.6) | collective-permute-done | bytes 786464 | tf_op jit(solution)/shard_map/ppermute | solution.py:463
  106.0 17.9 %collective-permute-done.5.refs_2_ = bf16[256,1536]{1,0:T(8,128)(2,1)S(1)} collective-permute-done((bf16[256,1536]{1,0:T(8,128)(2,1)}, bf16[256,1536]{1,0:T(8,128)(2,1)S(1)}, u32[]{:S(2)}, u32[]{:S(2)}) %collective-permute-start.5) | collective-permute-done | bytes 786464 | tf_op jit(solution)/shard_map/ppermute | solution.py:463
  127.0 4.8 all-to-all-start.2
  139.2 24.0 %shard_map.297 = (bf16[1024,1152]{1,0:T(8,128)(2,1)S(1)}, bf16[1024,384]{1,0:T(8,128)(2,1)S(1)}, f32[3,2,1024]{2,1,0:T(2,128)S(1)}) custom-call(bf16[256,1536]{1,0:T(8,128)(2,1)S(1)} %fusion.16.refs_0_, bf16[256,1536]{1,0:T(8,128)(2,1)} %collective-permute-done.refs_1_, bf16[256,1536]{1,0:T(8,128)(2,1)S(1)} %copy-done.41, bf16[256,1536]{1,0:T(8,128)(2,1)S(1)} %copy-done.38, ...), custom_call_target="tpu_custom_call" | custom-call | bytes 24000000 | tf_op jit(solution)/shard_map/pallas_call | solution.py:136
  171.0 5.0 all-to-all-start.3
  184.2 7.3 shard_map.298
  193.6 16.4 %collective-permute-done.17.g_ref.refs_8_ = bf16[256,1536]{1,0:T(8,128)(2,1)S(1)} collective-permute-done((bf16[256,1536]{1,0:T(8,128)(2,1)S(1)}, bf16[256,1536]{1,0:T(8,128)(2,1)S(1)}, u32[]{:S(2)}, u32[]{:S(2)}) %collective-permute-start.17) | collective-permute-done | bytes 786464 | tf_op jit(solution)/shard_map/ppermute | solution.py:463
  215.4 4.2 fusion.71
  221.2 4.9 convolution_convert_fusion.5.q_ref
  226.1 5.8 collective-permute-done.18.g_ref.refs_10_
  237.9 8.9 %shard_map.299.refs_0_ = bf16[256,1536]{1,0:T(8,128)(2,1)S(1)} custom-call(bf16[256,1536]{1,0:T(8,128)(2,1)S(1)} %copy-done.31, bf16[256,1536]{1,0:T(8,128)(2,1)S(1)} %fusion.4.k_ref, bf16[256,1536]{1,0:T(8,128)(2,1)S(1)} %fusion.5.v_ref, s32[1,256]{1,0:T(1,128)S(1)} %bitcast.242), custom_call_target="tpu_custom_call" | custom-call | bytes 12000000 | tf_op jit(solution)/shard_map/pallas_call | solution.py:245
  247.7 20.1 %all-gather.19.cloned.1.call-done = bf16[32,1,48,1536]{3,2,1,0:T(8,128)(2,1)} async-done(((bf16[4,1,48,1536]{3,2,1,0:T(8,128)(2,1)}), bf16[32,1,48,1536]{3,2,1,0:T(8,128)(2,1)}) %all-gather.19.cloned.1.call-update) | async-done | bytes 4718608 | tf_op jit(solution)/shard_map/all_gather | solution.py:626
  267.8 4.3 fusion.72
  275.5 20.0 %collective-permute-done.20.x_ref.refs_4_ = bf16[256,1536]{1,0:T(8,128)(2,1)S(1)} collective-permute-done((bf16[256,1536]{1,0:T(8,128)(2,1)S(1)}, bf16[256,1536]{1,0:T(8,128)(2,1)S(1)}, u32[]{:S(2)}, u32[]{:S(2)}) %collective-permute-start.20) | collective-permute-done | bytes 786464 | tf_op jit(solution)/shard_map/ppermute | solution.py:463
  295.5 12.1 %shard_map.300 = (bf16[1024,1536]{1,0:T(8,128)(2,1)S(1)}, bf16[1024,1536]{1,0:T(8,128)(2,1)S(1)}, bf16[1024,1536]{1,0:T(8,128)(2,1)S(1)}, bf16[256,1536]{1,0:T(8,128)(2,1)S(1)}, bf16[256,1536]{1,0:T(8,128)(2,1)S(1)}) custom-call(bf16[256,1536]{1,0:T(8,128)(2,1)S(1)} %collective-permute-done.20.x_ref.refs_4_, ...), custom_call_target="tpu_custom_call" | custom-call | bytes 12000000 | tf_op jit(solution)/shard_map/pallas_call | solution.py:339
  307.7 8.5 %collective-permute-done.21.x_ref.refs_5_ = bf16[256,1536]{1,0:T(8,128)(2,1)S(1)} collective-permute-done((bf16[256,1536]{1,0:T(8,128)(2,1)S(1)}, bf16[256,1536]{1,0:T(8,128)(2,1)S(1)}, u32[]{:S(2)}, u32[]{:S(2)}) %collective-permute-start.21) | collective-permute-done | bytes 786464 | tf_op jit(solution)/shard_map/ppermute | solution.py:463
  316.3 12.1 %shard_map.301 = (bf16[1024,1536]{1,0:T(8,128)(2,1)S(1)}, bf16[1024,1536]{1,0:T(8,128)(2,1)S(1)}, bf16[1024,1536]{1,0:T(8,128)(2,1)S(1)}, bf16[256,1536]{1,0:T(8,128)(2,1)S(1)}, bf16[256,1536]{1,0:T(8,128)(2,1)S(1)}) custom-call(bf16[256,1536]{1,0:T(8,128)(2,1)S(1)} %collective-permute-done.21.x_ref.refs_5, ...), custom_call_target="tpu_custom_call", output_to_operand_aliasing={{0}: (5, {}), {1}: (6, {}), {2}: (7, {})} | custom-call | bytes 12000000 | tf_op jit(solution)/shard_map/pallas_call | solution.py:339
  328.4 10.1 %collective-permute-done.22.x_ref.refs_6_ = bf16[256,1536]{1,0:T(8,128)(2,1)S(1)} collective-permute-done((bf16[256,1536]{1,0:T(8,128)(2,1)S(1)}, bf16[256,1536]{1,0:T(8,128)(2,1)S(1)}, u32[]{:S(2)}, u32[]{:S(2)}) %collective-permute-start.22) | collective-permute-done | bytes 786464 | tf_op jit(solution)/shard_map/ppermute | solution.py:463
  338.5 14.3 %collective-permute-done.23 = bf16[256,1536]{1,0:T(8,128)(2,1)S(1)} collective-permute-done((bf16[256,1536]{1,0:T(8,128)(2,1)S(1)}, bf16[256,1536]{1,0:T(8,128)(2,1)S(1)}, u32[]{:S(2)}, u32[]{:S(2)}) %collective-permute-start.23) | collective-permute-done | bytes 786464 | tf_op jit(solution)/shard_map/ppermute | solution.py:463
  353.4 11.9 %shard_map.302 = (bf16[1024,1536]{1,0:T(8,128)(2,1)S(1)}, bf16[1024,1536]{1,0:T(8,128)(2,1)S(1)}, bf16[1024,1536]{1,0:T(8,128)(2,1)S(1)}, bf16[256,1536]{1,0:T(8,128)(2,1)S(1)}, bf16[256,1536]{1,0:T(8,128)(2,1)S(1)}) custom-call(bf16[256,1536]{1,0:T(8,128)(2,1)S(1)} %collective-permute-done.22.x_ref.refs_6, ...), custom_call_target="tpu_custom_call", output_to_operand_aliasing={{0}: (5, {}), {1}: (6, {}), {2}: (7, {})} | custom-call | bytes 12000000 | tf_op jit(solution)/shard_map/pallas_call | solution.py:339
  365.3 12.1 %shard_map.303 = (bf16[1024,1536]{1,0:T(8,128)(2,1)S(1)}, bf16[1024,1536]{1,0:T(8,128)(2,1)S(1)}, bf16[1024,1536]{1,0:T(8,128)(2,1)S(1)}, bf16[256,1536]{1,0:T(8,128)(2,1)S(1)}, bf16[256,1536]{1,0:T(8,128)(2,1)S(1)}) custom-call(bf16[256,1536]{1,0:T(8,128)(2,1)S(1)} %multiply_convert_fusion.x_ref.refs_3_, ...), custom_call_target="tpu_custom_call", output_to_operand_aliasing={{0}: (5, {}), {1}: (6, {}), {2}: (7, {})} | custom-call | bytes 12000000 | tf_op jit(solution)/shard_map/pallas_call | solution.py:339
  382.4 6.4 collective-permute-done.25
  390.0 13.5 %shard_map.304 = bf16[3,768,1536]{2,1,0:T(8,128)(2,1)} custom-call(bf16[1024,1536]{1,0:T(8,128)(2,1)} %copy-done.1, bf16[1024,1536]{1,0:T(8,128)(2,1)} %copy-done.2, bf16[1024,1536]{1,0:T(8,128)(2,1)} %copy-done, bf16[256,1536]{1,0:T(8,128)(2,1)} %copy-done.6, bf16[256,1536]{1,0:T(8,128)(2,1)} %copy-done.8, bf16[256,1536]{1,0:T(8,128)(2,1)} %copy-done.13, ...), custom_call_target="tpu_custom_call" | custom-call | bytes 15000000 | tf_op jit(solution)/shard_map/pallas_call | solution.py:386
  403.5 4.4 collective-permute-done.27
  415.6 3.9 convolution_convert_fusion.4.grad_ref
  419.6 10.8 %shard_map.306 = (bf16[256,1536]{1,0:T(8,128)(2,1)S(1)}, bf16[256,1536]{1,0:T(8,128)(2,1)S(1)}, bf16[256,1536]{1,0:T(8,128)(2,1)S(1)}) custom-call(bf16[256,1536]{1,0:T(8,128)(2,1)S(1)} %copy-done.32, bf16[256,1536]{1,0:T(8,128)(2,1)S(1)} %copy-done.34, bf16[256,1536]{1,0:T(8,128)(2,1)S(1)} %copy-done.36, ...), custom_call_target="tpu_custom_call" | custom-call | bytes 12000000 | tf_op jit(solution)/shard_map/pallas_call | solution.py:245
  431.0 4.0 multiply_reduce_fusion.1
  435.1 3.9 shard_map.307
  441.1 3.9 shard_map.308
  456.7 5.2 all-to-all-start.4
  463.9 14.1 %shard_map.310 = bf16[3,768,1536]{2,1,0:T(8,128)(2,1)} custom-call(bf16[1024,1536]{1,0:T(8,128)(2,1)} %copy-done.1, bf16[1024,1536]{1,0:T(8,128)(2,1)} %copy-done.2, bf16[1024,1536]{1,0:T(8,128)(2,1)} %copy-done, bf16[256,1536]{1,0:T(8,128)(2,1)} %copy-done.6, bf16[256,1536]{1,0:T(8,128)(2,1)} %copy-done.8, bf16[256,1536]{1,0:T(8,128)(2,1)} %copy-done.13, ...), custom_call_target="tpu_custom_call" | custom-call | bytes 15000000 | tf_op jit(solution)/shard_map/pallas_call | solution.py:386
  484.9 3.9 fusion.12
  493.9 26.1 %shard_map.311.refs_4_ = bf16[1024,1152]{1,0:T(8,128)(2,1)S(1)} custom-call(bf16[1024,1152]{1,0:T(8,128)(2,1)S(1)} %copy-done.44, bf16[1024,384]{1,0:T(8,128)(2,1)S(1)} %bitcast.237, f32[3,2,1024]{2,1,0:T(2,128)S(1)} %copy-done.54, f32[1024,128]{1,0:T(8,128)S(1)} %copy-done.22, f32[1024,128]{1,0:T(8,128)S(1)} %copy-done.20, f32[1024,128]{1,0:T(8,128)S(1)} %copy-done.18, ...), custom_call_target="tpu_custom_call" | custom-call | bytes 27000000 | tf_op jit(solution)/shard_map/pallas_call | solution.py:207
  520.1 10.8 %collective-permute-done.33 = bf16[3,2,96,1536]{3,2,0,1:T(8,128)(2,1)S(1)} collective-permute-done((bf16[3,2,96,1536]{3,2,0,1:T(8,128)(2,1)}, bf16[3,2,96,1536]{3,2,0,1:T(8,128)(2,1)S(1)}, u32[]{:S(2)}, u32[]{:S(2)}) %collective-permute-start.33) | collective-permute-done | bytes 1769504 | tf_op jit(solution)/shard_map/ppermute | solution.py:458
  537.2 4.5 convolution_convert_fusion
  553.7 6.5 shard_map.312
  563.0 7.4 %collective-permute-done.37 = bf16[1,96,1536]{2,1,0:T(8,128)(2,1)S(1)} collective-permute-done((bf16[1,96,1536]{2,1,0:T(8,128)(2,1)}, bf16[1,96,1536]{2,1,0:T(8,128)(2,1)S(1)}, u32[]{:S(2)}, u32[]{:S(2)}) %collective-permute-start.37) | collective-permute-done | bytes 294944 | tf_op jit(solution)/shard_map/ppermute | solution.py:458
  580.2 5.0 all-to-all-start.5
  593.7 25.0 %collective-permute-done.47 = bf16[1,2,96,1152]{3,2,1,0:T(8,128)(2,1)S(1)} collective-permute-done((bf16[1,2,96,1152]{3,2,1,0:T(8,128)(2,1)S(1)}, bf16[1,2,96,1152]{3,2,1,0:T(8,128)(2,1)S(1)}, u32[]{:S(2)}, u32[]{:S(2)}) %collective-permute-start.47) | collective-permute-done | bytes 442400 | tf_op jit(solution)/shard_map/ppermute | solution.py:458
  622.5 3.9 collective-permute-done.46
  636.2 4.4 all-to-all-start.6
  655.9 31.7 %collective-permute-done.49 = bf16[256,1536]{1,0:T(8,128)(2,1)S(1)} collective-permute-done((bf16[256,1536]{1,0:T(8,128)(2,1)}, bf16[256,1536]{1,0:T(8,128)(2,1)S(1)}, u32[]{:S(2)}, u32[]{:S(2)}) %collective-permute-start.49) | collective-permute-done | bytes 786464 | tf_op jit(solution)/shard_map/ppermute | solution.py:463
  687.5 7.7 %all-to-all-done.6 = bf16[4,48,4224]{2,1,0:T(8,128)(2,1)} async-done(((bf16[4,48,4224]{2,1,0:T(8,128)(2,1)}), bf16[4,48,4224]{2,1,0:T(8,128)(2,1)}, u32[]{:S(2)}, u32[]{:S(2)}) %all-to-all-start.6) | async-done | bytes 1622048 | tf_op jit(solution)/shard_map/all_to_all | solution.py:475
  (539 shorter events, 224.6 us)
Async XLA Ops:
  15.1 29.6 %collective-permute-start.1 = (bf16[3,96,1536]{2,1,0:T(8,128)(2,1)}, bf16[3,96,1536]{2,1,0:T(8,128)(2,1)}, u32[]{:S(2)}, u32[]{:S(2)}) collective-permute-start(bf16[3,96,1536]{2,1,0:T(8,128)(2,1)} %get-tuple-element.239.refs_0_), channel_id=1, source_target_pairs={{0,8},{4,12},{8,0},{12,4},{16,24},{20,28},{24,16},{28,20},{1,9},{5... | collective-permute-start | bytes 2654216 | tf_op jit(solution)/shard_map/ppermute | solution.py:458
  18.1 26.6 %collective-permute-start.2 = (bf16[3,96,1536]{2,1,0:T(8,128)(2,1)}, bf16[3,96,1536]{2,1,0:T(8,128)(2,1)}, u32[]{:S(2)}, u32[]{:S(2)}) collective-permute-start(bf16[3,96,1536]{2,1,0:T(8,128)(2,1)} %get-tuple-element.239.refs_0_), channel_id=1, source_target_pairs={{0,16},{4,20},{8,24},{12,28},{16,0},{20,4},{24,8},{28,12},{1,17},{... | collective-permute-start | bytes 2654216 | tf_op jit(solution)/shard_map/ppermute | solution.py:458
  19.6 37.4 %collective-permute-start.3 = (bf16[3,96,1536]{2,1,0:T(8,128)(2,1)}, bf16[3,96,1536]{2,1,0:T(8,128)(2,1)}, u32[]{:S(2)}, u32[]{:S(2)}) collective-permute-start(bf16[3,96,1536]{2,1,0:T(8,128)(2,1)} %get-tuple-element.243.refs_4_), channel_id=1, source_target_pairs={{0,8},{4,12},{8,0},{12,4},{16,24},{20,28},{24,16},{28,20},{1,9},{5... | collective-permute-start | bytes 2654216 | tf_op jit(solution)/shard_map/ppermute | solution.py:458
  20.1 38.3 %collective-permute-start.4 = (bf16[3,96,1536]{2,1,0:T(8,128)(2,1)}, bf16[3,96,1536]{2,1,0:T(8,128)(2,1)}, u32[]{:S(2)}, u32[]{:S(2)}) collective-permute-start(bf16[3,96,1536]{2,1,0:T(8,128)(2,1)} %get-tuple-element.243.refs_4_), channel_id=1, source_target_pairs={{0,16},{4,20},{8,24},{12,28},{16,0},{20,4},{24,8},{28,12},{1,17},{... | collective-permute-start | bytes 2654216 | tf_op jit(solution)/shard_map/ppermute | solution.py:458
  21.9 22.8 %collective-permute-start = (bf16[256,1536]{1,0:T(8,128)(2,1)S(1)}, bf16[256,1536]{1,0:T(8,128)(2,1)}, u32[]{:S(2)}, u32[]{:S(2)}) collective-permute-start(bf16[256,1536]{1,0:T(8,128)(2,1)S(1)} %fusion.16.refs_0_), channel_id=1, source_target_pairs={{0,1},{1,2},{2,3},{3,0},{4,5},{5,6},{6,7},{7,4},{8,9},{9,10},{10,1... | collective-permute-start | bytes 2359304 | tf_op jit(solution)/shard_map/ppermute | solution.py:463
  23.9 40.7 %all-to-all-start = ((bf16[4,48,2688]{2,1,0:T(8,128)(2,1)}), bf16[4,48,2688]{2,1,0:T(8,128)(2,1)}, u32[]{:S(2)}, u32[]{:S(2)}) async-start(bf16[4,48,2688]{2,1,0:T(8,128)(2,1)} %pad_maximum_fusion.4), calls=%async_computation | async-start | bytes 2064384 | tf_op jit(solution)/shard_map/all_to_all | solution.py:475
  28.2 96.6 %all-gather.11.cloned.1.call-start = ((), (), s32[]{:S(2)}) async-start(), calls=%async_computation.8 | async-start | bytes 3981312 | tf_op jit(solution)/shard_map/all_gather | solution.py:626
  66.5 148.9 %all-gather.13.cloned.1.call-start = ((), (), s32[]{:S(2)}) async-start(), calls=%async_computation.9 | async-start | bytes 5308416 | tf_op jit(solution)/shard_map/all_gather | solution.py:626
  68.5 56.3 %collective-permute-start.7 = (bf16[3,96,1536]{2,1,0:T(8,128)(2,1)}, bf16[3,96,1536]{2,1,0:T(8,128)(2,1)}, u32[]{:S(2)}, u32[]{:S(2)}) collective-permute-start(bf16[3,96,1536]{2,1,0:T(8,128)(2,1)} %collective-permute-done.1.refs_1_), channel_id=1, source_target_pairs={{0,16},{4,20},{8,24},{12,28},{16,0},{20,4},{24,8},{28,12},{1,17},{... | collective-permute-start | bytes 2654216 | tf_op jit(solution)/shard_map/ppermute | solution.py:458
  70.0 54.7 %collective-permute-start.8 = (bf16[3,96,1536]{2,1,0:T(8,128)(2,1)}, bf16[3,96,1536]{2,1,0:T(8,128)(2,1)}, u32[]{:S(2)}, u32[]{:S(2)}) collective-permute-start(bf16[3,96,1536]{2,1,0:T(8,128)(2,1)} %collective-permute-done.4.refs_6_), channel_id=1, source_target_pairs={{0,8},{4,12},{8,0},{12,4},{16,24},{20,28},{24,16},{28,20},{1,9},{5... | collective-permute-start | bytes 2654216 | tf_op jit(solution)/shard_map/ppermute | solution.py:458
  72.4 52.4 %all-to-all-start.1 = ((bf16[4,48,1536]{2,1,0:T(8,128)(2,1)}), bf16[4,48,1536]{2,1,0:T(8,128)(2,1)}, u32[]{:S(2)}, u32[]{:S(2)}) async-start(bf16[4,48,1536]{2,1,0:T(8,128)(2,1)} %broadcast_in_dim.114), calls=%async_computation.1 | async-start | bytes 1179648 | tf_op jit(solution)/shard_map/all_to_all | solution.py:475
  76.6 144.6 %all-gather.15.cloned.1.call-start = ((), (), s32[]{:S(2)}) async-start(), calls=%async_computation.10 | async-start | bytes 5308416 | tf_op jit(solution)/shard_map/all_gather | solution.py:626
  76.6 28.5 %collective-permute-start.6 = (bf16[256,1536]{1,0:T(8,128)(2,1)S(1)}, bf16[256,1536]{1,0:T(8,128)(2,1)S(1)}, u32[]{:S(2)}, u32[]{:S(2)}) collective-permute-start(bf16[256,1536]{1,0:T(8,128)(2,1)S(1)} %fusion.16.refs_0_), channel_id=1, source_target_pairs={{0,3},{1,0},{2,1},{3,2},{4,7},{5,4},{6,5},{7,6},{8,11},{9,8},{10,9... | collective-permute-start | bytes 2359304 | tf_op jit(solution)/shard_map/ppermute | solution.py:463
  80.3 43.6 %collective-permute-start.5 = (bf16[256,1536]{1,0:T(8,128)(2,1)}, bf16[256,1536]{1,0:T(8,128)(2,1)S(1)}, u32[]{:S(2)}, u32[]{:S(2)}) collective-permute-start(bf16[256,1536]{1,0:T(8,128)(2,1)} %collective-permute-done.refs_1_), channel_id=1, source_target_pairs={{0,1},{1,2},{2,3},{3,0},{4,5},{5,6},{6,7},{7,4},{8,9},{9,10},{10,1... | collective-permute-start | bytes 2359304 | tf_op jit(solution)/shard_map/ppermute | solution.py:463
  127.0 39.9 %all-to-all-start.2 = ((bf16[4,2,48,1536]{3,2,1,0:T(8,128)(2,1)}), bf16[4,2,48,1536]{3,2,1,0:T(8,128)(2,1)}, u32[]{:S(2)}, u32[]{:S(2)}) async-start(bf16[4,2,48,1536]{3,2,1,0:T(8,128)(2,1)} %broadcast_in_dim.115), calls=%async_computation.2 | async-start | bytes 2359296 | tf_op jit(solution)/shard_map/all_to_all | solution.py:475
  131.8 101.0 %all-gather.17.cloned.1.call-start = ((), (), s32[]{:S(2)}) async-start(), calls=%async_computation.11 | async-start | bytes 5308416 | tf_op jit(solution)/shard_map/all_gather | solution.py:626
  169.3 98.4 %all-gather.19.cloned.1.call-start = ((), (), s32[]{:S(2)}) async-start(), calls=%async_computation.12 | async-start | bytes 5308416 | tf_op jit(solution)/shard_map/all_gather | solution.py:626
  171.0 42.3 %all-to-all-start.3 = ((bf16[4,256,384]{2,1,0:T(8,128)(2,1)}), bf16[4,256,384]{2,1,0:T(8,128)(2,1)}, u32[]{:S(2)}, u32[]{:S(2)}) async-start(bf16[4,256,384]{2,1,0:T(8,128)(2,1)} %bitcast.238), calls=%async_computation.3 | async-start | bytes 1572864 | tf_op jit(solution)/shard_map/all_to_all | solution.py:475
  178.3 31.7 %collective-permute-start.17 = (bf16[256,1536]{1,0:T(8,128)(2,1)S(1)}, bf16[256,1536]{1,0:T(8,128)(2,1)S(1)}, u32[]{:S(2)}, u32[]{:S(2)}) collective-permute-start(bf16[256,1536]{1,0:T(8,128)(2,1)S(1)} %fusion.20.g_ref.refs_7_), channel_id=1, source_target_pairs={{0,1},{1,2},{2,3},{3,0},{4,5},{5,6},{6,7},{7,4},{8,9},{9,10},{10,1... | collective-permute-start | bytes 2359304 | tf_op jit(solution)/shard_map/ppermute | solution.py:463
  231.9 41.2 %collective-permute-start.19 = (bf16[256,1536]{1,0:T(8,128)(2,1)S(1)}, bf16[256,1536]{1,0:T(8,128)(2,1)S(1)}, u32[]{:S(2)}, u32[]{:S(2)}) collective-permute-start(bf16[256,1536]{1,0:T(8,128)(2,1)S(1)} %collective-permute-done.17.g_ref.refs_8_), channel_id=1, source_target_pairs={{0,1},{1,2},{2,3},{3,0},{4,5},{5,6},{6,7},{7,4},{8,9},{9,10},{10,1... | collective-permute-start | bytes 2359304 | tf_op jit(solution)/shard_map/ppermute | solution.py:463
  274.0 21.5 %collective-permute-start.20 = (bf16[256,1536]{1,0:T(8,128)(2,1)S(1)}, bf16[256,1536]{1,0:T(8,128)(2,1)S(1)}, u32[]{:S(2)}, u32[]{:S(2)}) collective-permute-start(bf16[256,1536]{1,0:T(8,128)(2,1)S(1)} %multiply_convert_fusion.x_ref.refs_3_), channel_id=1, source_target_pairs={{0,1},{1,2},{2,3},{3,0},{4,5},{5,6},{6,7},{7,4},{8,9},{9,10},{10,1... | collective-permute-start | bytes 2359304 | tf_op jit(solution)/shard_map/ppermute | solution.py:463
  316.2 22.3 %collective-permute-start.22 = (bf16[256,1536]{1,0:T(8,128)(2,1)S(1)}, bf16[256,1536]{1,0:T(8,128)(2,1)S(1)}, u32[]{:S(2)}, u32[]{:S(2)}) collective-permute-start(bf16[256,1536]{1,0:T(8,128)(2,1)S(1)} %collective-permute-done.21.x_ref.refs_5_), channel_id=1, source_target_pairs={{0,1},{1,2},{2,3},{3,0},{4,5},{5,6},{6,7},{7,4},{8,9},{9,10},{10,1... | collective-permute-start | bytes 2359304 | tf_op jit(solution)/shard_map/ppermute | solution.py:463
  316.2 36.6 %collective-permute-start.23 = (bf16[256,1536]{1,0:T(8,128)(2,1)S(1)}, bf16[256,1536]{1,0:T(8,128)(2,1)S(1)}, u32[]{:S(2)}, u32[]{:S(2)}) collective-permute-start(bf16[256,1536]{1,0:T(8,128)(2,1)S(1)} %get-tuple-element.277), channel_id=1, source_target_pairs={{0,1},{1,2},{2,3},{3,0},{4,5},{5,6},{6,7},{7,4},{8,9},{9,10},{10,1... | collective-permute-start | bytes 2359304 | tf_op jit(solution)/shard_map/ppermute | solution.py:463
  353.0 29.3 %collective-permute-start.24 = (bf16[256,1536]{1,0:T(8,128)(2,1)S(1)}, bf16[256,1536]{1,0:T(8,128)(2,1)S(1)}, u32[]{:S(2)}, u32[]{:S(2)}) collective-permute-start(bf16[256,1536]{1,0:T(8,128)(2,1)S(1)} %add_convert_fusion.9), channel_id=1, source_target_pairs={{0,1},{1,2},{2,3},{3,0},{4,5},{5,6},{6,7},{7,4},{8,9},{9,10},{10,1... | collective-permute-start | bytes 2359304 | tf_op jit(solution)/shard_map/ppermute | solution.py:463
  353.1 35.7 %collective-permute-start.25 = (bf16[256,1536]{1,0:T(8,128)(2,1)S(1)}, bf16[256,1536]{1,0:T(8,128)(2,1)S(1)}, u32[]{:S(2)}, u32[]{:S(2)}) collective-permute-start(bf16[256,1536]{1,0:T(8,128)(2,1)S(1)} %get-tuple-element.290), channel_id=1, source_target_pairs={{0,1},{1,2},{2,3},{3,0},{4,5},{5,6},{6,7},{7,4},{8,9},{9,10},{10,1... | collective-permute-start | bytes 2359304 | tf_op jit(solution)/shard_map/ppermute | solution.py:463
  407.9 48.6 %collective-permute-start.29 = (bf16[3,768,1536]{2,1,0:T(8,128)(2,1)}, bf16[3,768,1536]{2,1,0:T(8,128)(2,1)}, u32[]{:S(2)}, u32[]{:S(2)}) collective-permute-start(bf16[3,768,1536]{2,1,0:T(8,128)(2,1)} %shard_map.304), channel_id=1, source_target_pairs={{0,4},{4,0},{8,12},{12,8},{16,20},{20,16},{24,28},{28,24},{1,5},{5... | collective-permute-start | bytes 21233672 | tf_op jit(solution)/shard_map/ppermute | solution.py:453
  409.2 47.4 %collective-permute-start.26 = (bf16[256,1536]{1,0:T(8,128)(2,1)}, bf16[256,1536]{1,0:T(8,128)(2,1)}, u32[]{:S(2)}, u32[]{:S(2)}) collective-permute-start(bf16[256,1536]{1,0:T(8,128)(2,1)} %add_convert_fusion.8), channel_id=1, source_target_pairs={{0,1},{1,2},{2,3},{3,0},{4,5},{5,6},{6,7},{7,4},{8,9},{9,10},{10,1... | collective-permute-start | bytes 2359304 | tf_op jit(solution)/shard_map/ppermute | solution.py:463
  430.4 22.1 %collective-permute-start.28 = (bf16[1,2,2,2,96,1536]{5,4,3,2,1,0:T(8,128)(2,1)S(1)}, bf16[1,2,2,2,96,1536]{5,4,3,2,1,0:T(8,128)(2,1)}, u32[]{:S(2)}, u32[]{:S(2)}) collective-permute-start(bf16[1,2,2,2,96,1536]{5,4,3,2,1,0:T(8,128)(2,1)S(1)} %get-tuple-element.321), channel_id=1, source_target_pairs={{0,4},{4,0},{8,12},{12,8},{16,20},{20,16},{24,28},{28,24},{1,5},{5... | collective-permute-start | bytes 7077896 | tf_op jit(solution)/shard_map/ppermute | solution.py:453
  456.5 25.7 %collective-permute-start.32 = (bf16[3,2,2,2,96,1536]{5,4,3,2,1,0:T(8,128)(2,1)}, bf16[3,2,2,2,96,1536]{5,4,3,2,1,0:T(8,128)(2,1)}, u32[]{:S(2)}, u32[]{:S(2)}) collective-permute-start(bf16[3,2,2,2,96,1536]{5,4,3,2,1,0:T(8,128)(2,1)} %get-tuple-element.334), channel_id=1, source_target_pairs={{0,4},{4,0},{8,12},{12,8},{16,20},{20,16},{24,28},{28,24},{1,5},{5... | collective-permute-start | bytes 21233672 | tf_op jit(solution)/shard_map/ppermute | solution.py:453
  456.7 25.6 %all-to-all-start.4 = ((bf16[4,256,384]{2,1,0:T(8,128)(2,1)}), bf16[4,256,384]{2,1,0:T(8,128)(2,1)S(1)}, u32[]{:S(2)}, u32[]{:S(2)}) async-start(bf16[4,256,384]{2,1,0:T(8,128)(2,1)} %pad_maximum_fusion.6), calls=%async_computation.4 | async-start | bytes 1572864 | tf_op jit(solution)/shard_map/all_to_all | solution.py:475
  490.9 39.9 %collective-permute-start.33 = (bf16[3,2,96,1536]{3,2,0,1:T(8,128)(2,1)}, bf16[3,2,96,1536]{3,2,0,1:T(8,128)(2,1)S(1)}, u32[]{:S(2)}, u32[]{:S(2)}) collective-permute-start(bf16[3,2,96,1536]{3,2,0,1:T(8,128)(2,1)} %fusion.12), channel_id=1, source_target_pairs={{0,16},{4,20},{8,24},{12,28},{16,0},{20,4},{24,8},{28,12},{1,17},{... | collective-permute-start | bytes 5308424 | tf_op jit(solution)/shard_map/ppermute | solution.py:458
  492.1 39.3 %collective-permute-start.34 = (bf16[3,2,96,1536]{3,2,1,0:T(8,128)(2,1)S(1)}, bf16[3,2,96,1536]{3,2,1,0:T(8,128)(2,1)S(1)}, u32[]{:S(2)}, u32[]{:S(2)}) collective-permute-start(bf16[3,2,96,1536]{3,2,1,0:T(8,128)(2,1)S(1)} %fusion.13), channel_id=1, source_target_pairs={{0,8},{4,12},{8,0},{12,4},{16,24},{20,28},{24,16},{28,20},{1,9},{5... | collective-permute-start | bytes 5308424 | tf_op jit(solution)/shard_map/ppermute | solution.py:458
  493.0 27.0 %collective-permute-start.35 = (bf16[256,1536]{1,0:T(8,128)(2,1)S(1)}, bf16[256,1536]{1,0:T(8,128)(2,1)S(1)}, u32[]{:S(2)}, u32[]{:S(2)}) collective-permute-start(bf16[256,1536]{1,0:T(8,128)(2,1)S(1)} %copy-done.91), channel_id=1, source_target_pairs={{0,1},{1,2},{2,3},{3,0},{4,5},{5,6},{6,7},{7,4},{8,9},{9,10},{10,1... | collective-permute-start | bytes 2359304 | tf_op jit(solution)/shard_map/ppermute | solution.py:463
  544.6 28.5 %collective-permute-start.39 = (bf16[3,96,1536]{2,1,0:T(8,128)(2,1)S(1)}, bf16[3,96,1536]{2,1,0:T(8,128)(2,1)}, u32[]{:S(2)}, u32[]{:S(2)}) collective-permute-start(bf16[3,96,1536]{2,1,0:T(8,128)(2,1)S(1)} %slice_bitcast_fusion.7), channel_id=1, source_target_pairs={{0,8},{4,12},{8,0},{12,4},{16,24},{20,28},{24,16},{28,20},{1,9},{5... | collective-permute-start | bytes 2654216 | tf_op jit(solution)/shard_map/ppermute | solution.py:458
  545.5 27.6 %collective-permute-start.40 = (bf16[3,96,1536]{2,1,0:T(8,128)(2,1)}, bf16[3,96,1536]{2,1,0:T(8,128)(2,1)}, u32[]{:S(2)}, u32[]{:S(2)}) collective-permute-start(bf16[3,96,1536]{2,1,0:T(8,128)(2,1)} %slice_bitcast_fusion.6), channel_id=1, source_target_pairs={{0,16},{4,20},{8,24},{12,28},{16,0},{20,4},{24,8},{28,12},{1,17},{... | collective-permute-start | bytes 2654216 | tf_op jit(solution)/shard_map/ppermute | solution.py:458
  547.0 26.1 %collective-permute-start.36 = (bf16[256,1536]{1,0:T(8,128)(2,1)S(1)}, bf16[256,1536]{1,0:T(8,128)(2,1)}, u32[]{:S(2)}, u32[]{:S(2)}) collective-permute-start(bf16[256,1536]{1,0:T(8,128)(2,1)S(1)} %get-tuple-element.360), channel_id=1, source_target_pairs={{0,1},{1,2},{2,3},{3,0},{4,5},{5,6},{6,7},{7,4},{8,9},{9,10},{10,1... | collective-permute-start | bytes 2359304 | tf_op jit(solution)/shard_map/ppermute | solution.py:463
  547.6 22.8 %collective-permute-start.37 = (bf16[1,96,1536]{2,1,0:T(8,128)(2,1)}, bf16[1,96,1536]{2,1,0:T(8,128)(2,1)S(1)}, u32[]{:S(2)}, u32[]{:S(2)}) collective-permute-start(bf16[1,96,1536]{2,1,0:T(8,128)(2,1)} %slice_bitcast_fusion.15), channel_id=1, source_target_pairs={{0,8},{4,12},{8,0},{12,4},{16,24},{20,28},{24,16},{28,20},{1,9},{5... | collective-permute-start | bytes 884744 | tf_op jit(solution)/shard_map/ppermute | solution.py:458
  548.5 24.1 %collective-permute-start.38 = (bf16[1,96,1536]{2,1,0:T(8,128)(2,1)}, bf16[1,96,1536]{2,1,0:T(8,128)(2,1)}, u32[]{:S(2)}, u32[]{:S(2)}) collective-permute-start(bf16[1,96,1536]{2,1,0:T(8,128)(2,1)} %slice_bitcast_fusion.14), channel_id=1, source_target_pairs={{0,16},{4,20},{8,24},{12,28},{16,0},{20,4},{24,8},{28,12},{1,17},{... | collective-permute-start | bytes 884744 | tf_op jit(solution)/shard_map/ppermute | solution.py:458
  570.4 58.3 %collective-permute-start.42 = (bf16[3,2,96,1536]{3,2,0,1:T(8,128)(2,1)}, bf16[3,2,96,1536]{3,2,0,1:T(8,128)(2,1)}, u32[]{:S(2)}, u32[]{:S(2)}) collective-permute-start(bf16[3,2,96,1536]{3,2,0,1:T(8,128)(2,1)} %bitcast.228), channel_id=1, source_target_pairs={{0,16},{4,20},{8,24},{12,28},{16,0},{20,4},{24,8},{28,12},{1,17},{... | collective-permute-start | bytes 5308424 | tf_op jit(solution)/shard_map/ppermute | solution.py:458
  572.6 56.1 %collective-permute-start.43 = (bf16[3,2,96,1536]{3,2,0,1:T(8,128)(2,1)}, bf16[3,2,96,1536]{3,2,0,1:T(8,128)(2,1)}, u32[]{:S(2)}, u32[]{:S(2)}) collective-permute-start(bf16[3,2,96,1536]{3,2,0,1:T(8,128)(2,1)} %bitcast.227), channel_id=1, source_target_pairs={{0,8},{4,12},{8,0},{12,4},{16,24},{20,28},{24,16},{28,20},{1,9},{5... | collective-permute-start | bytes 5308424 | tf_op jit(solution)/shard_map/ppermute | solution.py:458
  580.2 51.1 %all-to-all-start.5 = ((bf16[4,2,48,1536]{3,2,1,0:T(8,128)(2,1)}), bf16[4,2,48,1536]{3,2,1,0:T(8,128)(2,1)}, u32[]{:S(2)}, u32[]{:S(2)}) async-start(bf16[4,2,48,1536]{3,2,1,0:T(8,128)(2,1)} %pad_maximum_fusion.3), calls=%async_computation.5 | async-start | bytes 2359296 | tf_op jit(solution)/shard_map/all_to_all | solution.py:475
  586.7 42.0 %collective-permute-start.41 = (bf16[256,1536]{1,0:T(8,128)(2,1)S(1)}, bf16[256,1536]{1,0:T(8,128)(2,1)}, u32[]{:S(2)}, u32[]{:S(2)}) collective-permute-start(bf16[256,1536]{1,0:T(8,128)(2,1)S(1)} %add_convert_fusion.4), channel_id=1, source_target_pairs={{0,1},{1,2},{2,3},{3,0},{4,5},{5,6},{6,7},{7,4},{8,9},{9,10},{10,1... | collective-permute-start | bytes 2359304 | tf_op jit(solution)/shard_map/ppermute | solution.py:463
  590.0 28.8 %collective-permute-start.47 = (bf16[1,2,96,1152]{3,2,1,0:T(8,128)(2,1)S(1)}, bf16[1,2,96,1152]{3,2,1,0:T(8,128)(2,1)S(1)}, u32[]{:S(2)}, u32[]{:S(2)}) collective-permute-start(bf16[1,2,96,1152]{3,2,1,0:T(8,128)(2,1)S(1)} %fusion.43), channel_id=1, source_target_pairs={{0,8},{4,12},{8,0},{12,4},{16,24},{20,28},{24,16},{28,20},{1,9},{5... | collective-permute-start | bytes 1327112 | tf_op jit(solution)/shard_map/ppermute | solution.py:458
  591.9 26.9 %collective-permute-start.45 = (bf16[1,2,96,1152]{3,2,1,0:T(8,128)(2,1)S(1)}, bf16[1,2,96,1152]{3,2,1,0:T(8,128)(2,1)S(1)}, u32[]{:S(2)}, u32[]{:S(2)}) collective-permute-start(bf16[1,2,96,1152]{3,2,1,0:T(8,128)(2,1)S(1)} %fusion.42), channel_id=1, source_target_pairs={{0,16},{4,20},{8,24},{12,28},{16,0},{20,4},{24,8},{28,12},{1,17},{... | collective-permute-start | bytes 1327112 | tf_op jit(solution)/shard_map/ppermute | solution.py:458
  635.5 52.1 %collective-permute-start.51 = (bf16[3,96,1536]{2,1,0:T(8,128)(2,1)}, bf16[3,96,1536]{2,1,0:T(8,128)(2,1)}, u32[]{:S(2)}, u32[]{:S(2)}) collective-permute-start(bf16[3,96,1536]{2,1,0:T(8,128)(2,1)} %slice_bitcast_fusion.2), channel_id=1, source_target_pairs={{0,16},{4,20},{8,24},{12,28},{16,0},{20,4},{24,8},{28,12},{1,17},{... | collective-permute-start | bytes 2654216 | tf_op jit(solution)/shard_map/ppermute | solution.py:458
  636.2 59.1 %all-to-all-start.6 = ((bf16[4,48,4224]{2,1,0:T(8,128)(2,1)}), bf16[4,48,4224]{2,1,0:T(8,128)(2,1)}, u32[]{:S(2)}, u32[]{:S(2)}) async-start(bf16[4,48,4224]{2,1,0:T(8,128)(2,1)} %pad_maximum_fusion.1), calls=%async_computation.6 | async-start | bytes 3244032 | tf_op jit(solution)/shard_map/all_to_all | solution.py:475
  643.5 44.1 %collective-permute-start.50 = (bf16[3,96,1536]{2,1,0:T(8,128)(2,1)}, bf16[3,96,1536]{2,1,0:T(8,128)(2,1)}, u32[]{:S(2)}, u32[]{:S(2)}) collective-permute-start(bf16[3,96,1536]{2,1,0:T(8,128)(2,1)} %slice_bitcast_fusion.3), channel_id=1, source_target_pairs={{0,8},{4,12},{8,0},{12,4},{16,24},{20,28},{24,16},{28,20},{1,9},{5... | collective-permute-start | bytes 2654216 | tf_op jit(solution)/shard_map/ppermute | solution.py:458
  647.7 39.8 %collective-permute-start.49 = (bf16[256,1536]{1,0:T(8,128)(2,1)}, bf16[256,1536]{1,0:T(8,128)(2,1)S(1)}, u32[]{:S(2)}, u32[]{:S(2)}) collective-permute-start(bf16[256,1536]{1,0:T(8,128)(2,1)} %add_convert_fusion.3), channel_id=1, source_target_pairs={{0,1},{1,2},{2,3},{3,0},{4,5},{5,6},{6,7},{7,4},{8,9},{9,10},{10,1... | collective-permute-start | bytes 2359304 | tf_op jit(solution)/shard_map/ppermute | solution.py:463
  (158 other events, 2304.1 us)
Sparse Core Ops, SparseCore 0:
  66.6 40.7 all-gather.10
  109.2 36.2 all-gather.12
  147.4 38.9 all-gather.14
  188.1 38.9 all-gather.16
  228.8 38.9 all-gather.18

commit v4 on v3

--- a/solution.py
+++ b/solution.py
@@ -94,7 +94,7 @@
     return slice(kind * LANES + head * HDIM, kind * LANES + (head + 1) * HDIM)
 
 
-def self_forward(norms, qkv_cols, tables, segment):
+def self_forward(norms, qkv_cols, tables, segments):
     seq_size, (block, width) = len(norms), norms[0].shape
     length = block * seq_size
     group = 3 * LANES
@@ -155,10 +155,10 @@
         ],
         compiler_params=pltpu.CompilerParams(vmem_limit_bytes=40 << 20),
         cost_estimate=taking(8),
-    )(*norms, qkv_cols, *tables, segment[:, None], segment[None, :])
-
-
-def self_backward(qkv, grad_out, log_total, tables, segment, seq_size):
+    )(*norms, qkv_cols, *tables, *segments)
+
+
+def self_backward(qkv, grad_out, log_total, tables, segments, seq_size):
     length = qkv.shape[0]
     group = 3 * LANES
     pairs = qkv.shape[1] // group
@@ -222,7 +222,7 @@
         scratch_shapes=[pltpu.VMEM((length, LANES), jnp.float32)] * 2,
         compiler_params=pltpu.CompilerParams(vmem_limit_bytes=40 << 20),
         cost_estimate=taking(9),
-    )(qkv, grad_out, log_total, *tables, segment[:, None], segment[None, :])
+    )(qkv, grad_out, log_total, *tables, *segments)
 
 
 CROSS_HEADS = 8
@@ -469,6 +469,20 @@
     for _ in range(lax.axis_size("seq") - 3):
         pieces.append(shift_seq(pieces[-1]))
     return pieces + [last]
+
+
+def reduce_ahead(blocks):
+    size = lax.axis_size("seq")
+    total = blocks[size // 2 + 1]
+    for k in range(size // 2 + 2, size):
+        total = add_low(shift_seq(total), blocks[k])
+    return total
+
+
+def reduce_middle(total, blocks):
+    for k in range(lax.axis_size("seq") // 2 - 1, 1, -1):
+        total = shift_seq(add_low(total, blocks[k]), -1)
+    return add_low(total, blocks[1])
 
 
 def swap_seq(values):
@@ -631,25 +645,16 @@
     qkv_parts = jnp.pad(qkv_parts, ((0, 0),) * 3 + ((0, pairs * LANES - head_width),))
     qkv_parts = qkv_parts.reshape(3, part_rows, seq_size, pairs, LANES).transpose(2, 1, 3, 0, 4)
     qkv_parts = qkv_parts.reshape(seq_size, part_rows, pairs * 3 * LANES)
-    qkv_parts = jnp.concatenate(
-        [qkv_parts]
-        + [jnp.broadcast_to(self_out[None], (seq_size,) + self_out.shape)],
-        axis=2,
-    )
     qkv_parts, tokens, feed_gate, feed_up, feed_down, cotangent, item_lengths = stage(
         qkv_parts, tokens, feed_gate, feed_up, feed_down, cotangent, item_lengths
     )
-    early_rows = swap_seq(qkv_parts)
+    qkv_rows = swap_seq(qkv_parts)
     token_values = tokens.astype(jnp.float32)
     norm_one, norm_one_back = jax.vjp(layer_norm, token_values, gain_self.astype(jnp.float32))
     norm_one = norm_one.astype(jnp.bfloat16)
-    norms_one = [norm_one, shift_seq(norm_one)]
     feed_parts = jnp.stack([feed_gate, feed_up, feed_down])
     half_units = feed_parts.shape[1] // 2
-    feed_held = spread_first(feed_parts[:, :half_units], feed_parts[:, half_units:])
-    for y in range(1, y_size):
-        feed_held[0, y, 0] = shift_dp(feed_held[0, y - 1, 0], 1, 0)
-    feed_held[1, 0, 1] = shift_dp(feed_held[1, 0, 0], 0, 1)
+    feed_parts = feed_parts[:, :half_units], feed_parts[:, half_units:]
     row_ids = jnp.concatenate(
         [
             lax.rem(seq_place + (seq_size - k), seq_size) * rows_dev
@@ -662,33 +667,59 @@
     tables = lane_tables(position)
     valid_rows = (row_segment < 2).astype(jnp.float32)[:, None]
     grad_output_low = (cotangent.astype(jnp.float32) * valid_rows).astype(jnp.bfloat16)
-    cross_kv = jnp.concatenate([cross_key, cross_value])
-    early_rows, norms_one[1], feed_held, tables, grad_output_low, cross_query = stage(
-        early_rows, norms_one[1], feed_held, tables, grad_output_low, cross_query
-    )
-    qkv_cols = whole_rows(early_rows[:, :, :-width])
-    full_out = whole_rows(early_rows[:, :, -width:])
+    qkv_rows, norm_one, feed_parts, self_out, cross_query = stage(
+        qkv_rows, norm_one, feed_parts, self_out, cross_query
+    )
+    qkv_cols = whole_rows(qkv_rows)
+
+    norms_one = [norm_one, shift_seq(norm_one)]
+    out_rows = gather_places(self_out)
+    feed_held = spread_first(*feed_parts)
+    segments = segment[:, None], segment[None, :]
+    (
+        norms_one,
+        tables,
+        segments,
+        feed_held,
+        out_rows,
+        cross_query,
+        grad_output_low,
+        cross_rows,
+    ) = stage(
+        norms_one,
+        tables,
+        segments,
+        feed_held,
+        out_rows,
+        cross_query,
+        grad_output_low,
+        jnp.stack([jnp.concatenate([cross_key, cross_value]), cross_out]),
+    )
+    full_out = whole_rows(out_rows)
 
     norms_one = gather_rest(norms_one)
     query_rows = gather_places(cross_query)
     for y in range(1, y_size):
+        feed_held[0, y, 0] = shift_dp(feed_held[0, y - 1, 0], 1, 0)
+    feed_held[1, 0, 1] = shift_dp(feed_held[1, 0, 0], 0, 1)
+    norms_one, qkv_cols, feed_held, cross_rows, query_rows, grad_output_low = stage(
+        norms_one, qkv_cols, feed_held, cross_rows, query_rows, grad_output_low
+    )
+    full_cross_query = whole_rows(query_rows)
+
+    cross_rows = gather_places(cross_rows)
+    for y in range(1, y_size):
         feed_held[0, y, 1] = shift_dp(feed_held[0, y - 1, 1], 1, 0)
         feed_held[1, y, 1] = shift_dp(feed_held[1, y, 0], 0, 1)
-    norms_one, qkv_cols, feed_held, cross_kv, cross_out, query_rows = stage(
-        norms_one, qkv_cols, feed_held, cross_kv, cross_out, query_rows
-    )
-    full_cross_query = whole_rows(query_rows)
-
-    cross_rows = gather_places(jnp.stack([cross_kv, cross_out]))
-    qkv, head_attended, log_total = self_forward(norms_one, qkv_cols, tables, segment)
-    cross_rows, feed_held, head_attended, grad_output_low = stage(
-        cross_rows, feed_held, head_attended, grad_output_low
+    all_grads = [grad_output_low, shift_seq(grad_output_low)]
+    qkv, head_attended, log_total = self_forward(norms_one, qkv_cols, tables, segments)
+    cross_rows, feed_held, head_attended, all_grads = stage(
+        cross_rows, feed_held, head_attended, all_grads
     )
     full_cross_kv = whole_rows(cross_rows[:, 0]).reshape(dp_size * seq_size, 2, -1, width)
     full_cross_out = whole_rows(cross_rows[:, 1])
 
     attended = swap_seq(head_attended[:, :head_width].reshape(seq_size, rows_dev, head_width))
-    all_grads = [grad_output_low, shift_seq(grad_output_low)]
     feed_cores = with_cores(feed_held)
     places = [
         (core, half, y, x)
@@ -734,10 +765,7 @@
     norm_three = norm_three.astype(jnp.bfloat16)
     all_grads, norm_three = stage(all_grads, norm_three)
 
-    norms = [norm_three, shift_seq(norm_three)]
-    norms, all_grads = stage(norms, all_grads)
-
-    held, feed_out, feed_dx, moving, feed_moving = None, {}, {}, None, None
+    held, feed_out, feed_dx, moving = None, {}, {}, None
 
     def run_block(k, held):
         *held, feed_out[k], feed_dx[k] = feed_block(
@@ -745,25 +773,21 @@
         )
         return held
 
+    norms = [norm_three, shift_seq(norm_three)]
+    held = run_block(0, held)
+    norms, all_grads, held, feed_out, feed_dx = stage(norms, all_grads, held, feed_out, feed_dx)
     for k in range(1, seq_size):
         if k + 1 < seq_size:
             norms.append(shift_seq(norms[-1]))
         arrived = None if k == 1 else shift_seq(moving)
         held = run_block(k, held)
-        if k == seq_size - 1:
-            feed_moving = shift_seq(feed_out[1])
-            held = run_block(0, held)
-            activation, grad_gate, grad_up = held
-            held = (grad_gate, grad_up, activation)
-            arrived, feed_moving, held, feed_out, feed_dx = stage(
-                arrived, feed_moving, held, feed_out, feed_dx
-            )
-        else:
-            norms, arrived, held, feed_out, feed_dx = stage(norms, arrived, held, feed_out, feed_dx)
+        norms, arrived, held, feed_out, feed_dx = stage(norms, arrived, held, feed_out, feed_dx)
         moving = feed_dx[k] if k == 1 else add_low(arrived, feed_dx[k])
+    activation, grad_gate, grad_up = held
+    held = (grad_gate, grad_up, activation)
     arrived = shift_seq(moving)
     other_units = unit_products(held, norms, all_grads, 1)
-    arrived, other_units = stage(arrived, other_units)
+    arrived, other_units, feed_out = stage(arrived, other_units, feed_out)
     other_units = swap_core(other_units)
     grad_norm_three = add_wide(arrived, feed_dx[0])
 
@@ -771,8 +795,7 @@
         blocks = jnp.concatenate([first.astype(jnp.bfloat16), second.astype(jnp.bfloat16)])
         return blocks.reshape(seq_size, part_rows, blocks.shape[1])
 
-    if seq_size > 2:
-        feed_moving = shift_seq(add_low(feed_moving, feed_out[2]))
+    feed_came = shift_seq(feed_out[seq_size // 2], -1)
     grad_output = cotangent.astype(jnp.float32) * valid_rows
     grad_second, grad_gain_feed = norm_three_back(grad_norm_three)
     grad_second = grad_second + grad_output
@@ -797,8 +820,8 @@
         [memory], [grad_memory_keys, grad_memory_values], 2, 3, products
     )
     cross_out_packed = pack_first(cross_out_own, cross_out_other)
-    feed_moving, cross_out_packed, grad_attended, weight_other, other_units = stage(
-        feed_moving, cross_out_packed, grad_attended, weight_other, other_units
+    feed_came, cross_out_packed, grad_attended, weight_other, other_units = stage(
+        feed_came, cross_out_packed, grad_attended, weight_other, other_units
     )
 
     head_grad = swap_seq(grad_attended)
@@ -813,50 +836,48 @@
     cross_out_firsts = add_first(cross_out_came, cross_out_own, cross_out_other)
     head_grad = head_grad.reshape(rows_dev * seq_size, head_width)
     head_grad = jnp.pad(head_grad, ((0, 0), (0, pairs * LANES - head_width)))
-    for k in range(3, seq_size):
-        feed_moving = add_low(feed_moving, feed_out[k])
-        if k + 1 < seq_size:
-            feed_moving = shift_seq(feed_moving)
+    feed_moving = reduce_middle(feed_came, feed_out), reduce_ahead(feed_out)
     head_grad, weight_packed, feed_moving, cross_out_firsts = stage(
         head_grad, weight_packed, feed_moving, cross_out_firsts
     )
-    if seq_size > 3:
-        feed_moving = shift_seq(feed_moving)
+    feed_moving = shift_seq(feed_moving[0], -1), shift_seq(feed_moving[1])
     weight_came = send_first(weight_packed)
-    turned = self_backward(qkv, head_grad, log_total, tables, segment, seq_size)
+    turned = self_backward(qkv, head_grad, log_total, tables, segments, seq_size)
     weight_came, turned, feed_moving, cross_out_firsts = stage(
         weight_came, turned, feed_moving, cross_out_firsts
     )
 
     norm_terms = low(contract_cols(turned, qkv_cols))
     norm_terms = [norm_terms[k * rows_dev : (k + 1) * rows_dev] for k in range(seq_size)]
+    norm_terms, turned, own_units, feed_moving = stage(norm_terms, turned, own_units, feed_moving)
+    moving = shift_seq(norm_terms[seq_size // 2], -1), shift_seq(reduce_ahead(norm_terms))
     weight_firsts = add_first(weight_came, weight_own, weight_other)
-    cross_out_packed = pack_second(*cross_out_firsts)
+    weight_firsts = [jnp.concatenate(pair) for pair in zip(weight_firsts, cross_out_firsts)]
     weight_packed = pack_second(*weight_firsts)
-    norm_terms, cross_out_packed, weight_packed, turned, own_units, feed_moving = stage(
-        norm_terms, cross_out_packed, weight_packed, turned, own_units, feed_moving
-    )
-    moving = shift_seq(norm_terms[1])
-    cross_out_came = send_second(cross_out_packed)
     weight_came = send_second(weight_packed)
     qkv_own, qkv_other = weight_products(norms_one, [turned])
-    moving, cross_out_came, weight_came, qkv_own, qkv_other = stage(
-        moving, cross_out_came, weight_came, qkv_own, qkv_other
-    )
+    grad_gain_self = sum(
+        jnp.sum(term.astype(jnp.float32) * norm.astype(jnp.float32), axis=0)
+        for term, norm in zip(norm_terms, norms_one)
+    ) / gain_self.astype(jnp.float32)
+    gains = jnp.stack([grad_gain_self, grad_gain_cross, grad_gain_feed])
+    gains = gains.reshape(-1, dp_size * seq_size, part_rows).transpose(1, 0, 2)
+    gains = lax.all_to_all(gains, ("dp", "seq"), split_axis=0, concat_axis=0, tiled=True)
+    moving, weight_came, qkv_own, qkv_other, gains = stage(
+        moving, weight_came, qkv_own, qkv_other, gains
+    )
+    gains = jnp.sum(gains, axis=0)
 
     qkv_other = swap_core(qkv_other)
-    if seq_size > 2:
-        moving = shift_seq(add_low(moving, norm_terms[2]))
+    norm_came = shift_seq(reduce_middle(moving[0], norm_terms), -1)
     own_units = own_units.reshape(3, 2, y_size, 2, half_units, width)
     unit_came = send_first(pack_first(own_units))
-    output = low(second_sum + add_wide(feed_moving, feed_out[0]))
-    cross_out_second = add_second(cross_out_came, *cross_out_firsts)
     weight_seconds = add_second(weight_came, *weight_firsts)
     placed = swap_seq(
         jnp.stack(
             [
-                seq_blocks(*(s[0] for s in cross_out_second)),
-                seq_blocks(*(s[0] for s in weight_seconds)),
+                seq_blocks(*(s[n] for s in weight_seconds))
+                for n in (3, 0, 1)
             ],
             axis=1,
         )
@@ -869,38 +890,30 @@
     qkv_seconds = add_second(send_second(pack_second(*qkv_firsts)), *qkv_firsts)
     later = jnp.concatenate(
         [
-            seq_blocks(*(s[1] for s in weight_seconds)),
             kv_blocks.reshape(seq_size, part_rows, width),
             seq_blocks(*(s[0] for s in qkv_seconds)),
         ],
         axis=2,
     )
-    moving, placed, unit_came, later = stage(moving, placed, unit_came, later)
-
-    for k in range(3, seq_size):
-        moving = shift_seq(add_low(moving, norm_terms[k]))
+    output = low(
+        second_sum + add_wide(feed_moving[0], feed_out[0]) + feed_moving[1].astype(jnp.float32)
+    )
+    norm_came, placed, unit_came, later = stage(norm_came, placed, unit_came, later)
+
     later = swap_seq(later)
     unit_firsts = add_first(unit_came, own_units)
     unit_came = send_second(pack_second(*unit_firsts))
-    moving, later, unit_came = stage(moving, later, unit_came)
-
+    grad_norm_one = add_wide(norm_came, norm_terms[0]) + moving[1].astype(jnp.float32)
+    grad_tokens_wide = norm_one_back(grad_norm_one)[0]
+    grad_tokens = low(grad_tokens_wide + grad_first)
+    grad_cross_out, grad_cross_query, grad_self_out = (
+        jnp.sum(placed[:, n].astype(jnp.float32), axis=0) for n in range(3)
+    )
     unit_grads = jnp.concatenate(add_second(unit_came, *unit_firsts), axis=1)
-    grad_norm_one = add_wide(moving, norm_terms[0])
-    grad_tokens_wide, grad_gain_self = norm_one_back(grad_norm_one)
-    grad_tokens = (grad_tokens_wide + grad_first).astype(jnp.bfloat16)
-    gains = jnp.stack([grad_gain_self, grad_gain_cross, grad_gain_feed])
-    gains = gains.reshape(-1, dp_size * seq_size, part_rows).transpose(1, 0, 2)
-    gains = jnp.sum(
-        lax.all_to_all(gains, ("dp", "seq"), split_axis=0, concat_axis=0, tiled=True), axis=0
-    )
-    split = later[:, :, : 2 * width].reshape(seq_size, part_rows, 2, width).transpose(0, 2, 1, 3)
-    grad_cross_out, grad_cross_query, grad_cross_kv, grad_self_out = (
-        jnp.sum(p[:, n].astype(jnp.float32), axis=0)
-        for p, n in ((placed, 0), (placed, 1), (split, 1), (split, 0))
-    )
+    grad_cross_kv = jnp.sum(later[:, :, :width].astype(jnp.float32), axis=0)
     kv_rows = part_rows // 2
     grad_qkv = (
-        later[:, :, 2 * width :]
+        later[:, :, width:]
         .reshape(seq_size, part_rows, pairs, 3, LANES)
         .transpose(3, 1, 0, 2, 4)
         .reshape(3, part_rows, seq_size, pairs * LANES)[..., :head_width]

time: 742 us -> 696 us (0.938)
  waiting for transfers between devices: 278 us -> 214 us
  starting transfers between devices: 81 us -> 99.8 us
    ppermute x18, waiting for transfers between devices: 170 us -> 117 us  [shift_seq(): lax.ppermute(values, 'seq', [(s, (s + step) % size) for s in range(size)])]
    ppermute x22 -> x20, waiting for transfers between devices: 63.9 us -> 35.5 us  [shift_dp(): lax.ppermute(values, 'dp', [(d, (d + 4 * y) % size ^ 2 * x) for d in rang...]
    all_to_all x7 -> x8, waiting for transfers between devices: 20.9 us -> 35.5 us  [swap_seq(): lax.all_to_all(values, 'seq', split_axis=0, concat_axis=0, tiled=True)]
    all_to_all x7 -> x8, starting transfers between devices: 32.8 us -> 47.3 us  [swap_seq(): lax.all_to_all(values, 'seq', split_axis=0, concat_axis=0, tiled=True)]
    unnamed x286 -> x283, local copies, waits for them, and re-layouts: 33.7 us -> 41.4 us
    convert_element_type x13 -> x15, other arithmetic: 26.9 us -> 31.8 us  [low(): return values.astype(jnp.bfloat16)]
    ppermute x22 -> x20, starting transfers between devices: 25.5 us -> 23 us  [shift_dp(): lax.ppermute(values, 'dp', [(d, (d + 4 * y) % size ^ 2 * x) for d in rang...]
  transfers between devices with their start and end apart: 65 -> 64, of which waited for: 31 -> 29; matrix products, arithmetic and copies ran while one was open for 14% -> 16% of each run, Pallas kernels for 24% -> 25%
where the time goes in v4:
time: 696 us; the launch traced here: 688 us
  waiting for transfers between devices  214 us (31%)
  Pallas kernels  174 us (25%)
  starting transfers between devices  99.8 us (14%)
  other arithmetic  79.6 us (11%)
  local copies, waits for them, and re-layouts  73.4 us (11%)
  matrix products  30.7 us (4%)
  between operations  17.2 us (2%)
    ppermute x18, waiting for transfers between devices, shift_seq(): lax.ppermute(values, 'seq', [(s, (s + step) % size) for s in range(size)])  117 us
    pallas_call x4, Pallas kernels, feed_block(): pl.pallas_call(body, grid=(steps,), in_specs=[full, full, pl.BlockSpec((t...  49.4 us
    all_to_all x8, starting transfers between devices, swap_seq(): lax.all_to_all(values, 'seq', split_axis=0, concat_axis=0, tiled=True)  47.3 us
    unnamed x283, local copies, waits for them, and re-layouts  41.4 us
    ppermute x20, waiting for transfers between devices, shift_dp(): lax.ppermute(values, 'dp', [(d, (d + 4 * y) % size ^ 2 * x) for d in rang...  35.5 us
    all_to_all x8, waiting for transfers between devices, swap_seq(): lax.all_to_all(values, 'seq', split_axis=0, concat_axis=0, tiled=True)  35.5 us
    convert_element_type x15, other arithmetic, low(): return values.astype(jnp.bfloat16)  31.8 us
    pallas_call x2, Pallas kernels, unit_products(): pl.pallas_call(body, grid=(steps,), in_specs=[pl.BlockSpec((length, tile)...  27.4 us
  transfers between devices with their start and end apart: 64, of which 29 were waited for; matrix products, arithmetic and copies ran while one was open for 16% of the time, Pallas kernels for 25%

profile of v4, /device:TPU:0, one launch (start us, length us, event | category | flops | bytes accessed | tf_op | source)
XLA Modules:
  0.0 688.4 jit_solution(2763092174784982920)
XLA Ops:
  12.5 6.3 all-to-all-start
  22.3 9.3 %all-to-all-done = bf16[4,48,1152]{2,1,0:T(8,128)(2,1)S(1)} async-done(((bf16[4,48,1152]{2,1,0:T(8,128)(2,1)}), bf16[4,48,1152]{2,1,0:T(8,128)(2,1)S(1)}, u32[]{:S(2)}, u32[]{:S(2)}) %all-to-all-start) | async-done | bytes 442400 | tf_op jit(solution)/shard_map/all_to_all | solution.py:489
  41.6 4.2 all-to-all-start.1
  51.2 24.0 %collective-permute-done.refs_1_ = bf16[256,1536]{1,0:T(8,128)(2,1)S(1)} collective-permute-done((bf16[256,1536]{1,0:T(8,128)(2,1)S(1)}, bf16[256,1536]{1,0:T(8,128)(2,1)S(1)}, u32[]{:S(2)}, u32[]{:S(2)}) %collective-permute-start) | collective-permute-done | bytes 786464 | tf_op jit(solution)/shard_map/ppermute | solution.py:463
  80.5 4.2 all-to-all-start.2
  88.6 28.0 %collective-permute-done.3.refs_2_ = bf16[256,1536]{1,0:T(8,128)(2,1)S(1)} collective-permute-done((bf16[256,1536]{1,0:T(8,128)(2,1)S(1)}, bf16[256,1536]{1,0:T(8,128)(2,1)S(1)}, u32[]{:S(2)}, u32[]{:S(2)}) %collective-permute-start.3) | collective-permute-done | bytes 786464 | tf_op jit(solution)/shard_map/ppermute | solution.py:463
  117.5 11.6 %collective-permute-done.4.refs_3_ = bf16[256,1536]{1,0:T(8,128)(2,1)S(1)} collective-permute-done((bf16[256,1536]{1,0:T(8,128)(2,1)S(1)}, bf16[256,1536]{1,0:T(8,128)(2,1)S(1)}, u32[]{:S(2)}, u32[]{:S(2)}) %collective-permute-start.4) | collective-permute-done | bytes 786464 | tf_op jit(solution)/shard_map/ppermute | solution.py:463
  131.1 6.8 all-to-all-start.3
  151.8 23.0 %shard_map.297 = (bf16[1024,1152]{1,0:T(8,128)(2,1)S(1)}, bf16[1024,384]{1,0:T(8,128)(2,1)S(1)}, f32[3,2,1024]{2,1,0:T(2,128)S(1)}) custom-call(bf16[256,1536]{1,0:T(8,128)(2,1)S(1)} %fusion.21.refs_0_, bf16[256,1536]{1,0:T(8,128)(2,1)S(1)} %collective-permute-done.refs_1_, bf16[256,1536]{1,0:T(8,128)(2,1)S(1)} %copy-done.18, ...), custom_call_target="tpu_custom_call" | custom-call | bytes 24000000 | tf_op jit(solution)/shard_map/pallas_call | solution.py:136
  177.1 5.6 all-to-all-done.3
  186.3 4.2 all-to-all-start.4
  198.3 7.3 %shard_map.298 = (bf16[2,16,96,1536]{3,2,1,0:T(8,128)(2,1)}, bf16[1,16,96,1536]{3,2,1,0:T(8,128)(2,1)S(1)}) custom-call(bf16[3,96,1536]{2,1,0:T(8,128)(2,1)} %get-tuple-element.263.refs_0_, bf16[3,96,1536]{2,1,0:T(8,128)(2,1)} %collective-permute-done.1.refs_1_, bf16[3,96,1536]{2,1,0:T(8,128)(2,1)} %collective-permute-done.5.refs_2_, ...), custom_call_target="tpu_custom_call" | custom-call | bytes 6000000 | tf_op jit(solution)/shard_map/pallas_call | solution.py:599
  215.1 4.4 fusion.75
  221.8 4.9 convolution_convert_fusion.5.q_ref
  226.7 4.0 collective-permute-done.18.g_ref.refs_10_
  236.5 8.9 %shard_map.299.refs_0_ = bf16[256,1536]{1,0:T(8,128)(2,1)S(1)} custom-call(bf16[256,1536]{1,0:T(8,128)(2,1)S(1)} %copy-done.36, bf16[256,1536]{1,0:T(8,128)(2,1)S(1)} %fusion.4.k_ref, bf16[256,1536]{1,0:T(8,128)(2,1)S(1)} %fusion.5.v_ref, s32[1,256]{1,0:T(1,128)S(1)} %bitcast.235), custom_call_target="tpu_custom_call" | custom-call | bytes 12000000 | tf_op jit(solution)/shard_map/pallas_call | solution.py:245
  246.3 17.5 %all-gather.19.cloned.1.call-done = bf16[32,1,48,1536]{3,2,1,0:T(8,128)(2,1)} async-done(((bf16[4,1,48,1536]{3,2,1,0:T(8,128)(2,1)}), bf16[32,1,48,1536]{3,2,1,0:T(8,128)(2,1)}) %all-gather.19.cloned.1.call-update) | async-done | bytes 4718608 | tf_op jit(solution)/shard_map/all_gather | solution.py:640
  263.8 4.3 fusion.76
  270.8 11.8 %shard_map.300 = (bf16[1024,1536]{1,0:T(8,128)(2,1)S(1)}, bf16[1024,1536]{1,0:T(8,128)(2,1)S(1)}, bf16[1024,1536]{1,0:T(8,128)(2,1)S(1)}, bf16[256,1536]{1,0:T(8,128)(2,1)S(1)}, bf16[256,1536]{1,0:T(8,128)(2,1)S(1)}) custom-call(bf16[256,1536]{1,0:T(8,128)(2,1)S(1)} %multiply_convert_fusion.x_ref.refs_3_, bf16[256,1536]{1,0:T(8,128)(2,1)S(1)} %fusion.23.g_ref.refs_7_, ...), custom_call_target="tpu_custom_call" | custom-call | bytes 12000000 | tf_op jit(solution)/shard_map/pallas_call | solution.py:339
  282.7 8.1 %collective-permute-done.20.x_ref.refs_4_ = bf16[256,1536]{1,0:T(8,128)(2,1)S(1)} collective-permute-done((bf16[256,1536]{1,0:T(8,128)(2,1)S(1)}, bf16[256,1536]{1,0:T(8,128)(2,1)S(1)}, u32[]{:S(2)}, u32[]{:S(2)}) %collective-permute-start.20) | collective-permute-done | bytes 786464 | tf_op jit(solution)/shard_map/ppermute | solution.py:463
  290.8 12.1 %shard_map.301 = (bf16[1024,1536]{1,0:T(8,128)(2,1)S(1)}, bf16[1024,1536]{1,0:T(8,128)(2,1)S(1)}, bf16[1024,1536]{1,0:T(8,128)(2,1)S(1)}, bf16[256,1536]{1,0:T(8,128)(2,1)S(1)}, bf16[256,1536]{1,0:T(8,128)(2,1)S(1)}) custom-call(bf16[256,1536]{1,0:T(8,128)(2,1)S(1)} %collective-permute-done.20.x_ref.refs_4, ...), custom_call_target="tpu_custom_call", output_to_operand_aliasing={{0}: (5, {}), {1}: (6, {}), {2}: (7, {})} | custom-call | bytes 12000000 | tf_op jit(solution)/shard_map/pallas_call | solution.py:339
  303.9 7.6 %collective-permute-done.21.x_ref.refs_5_ = bf16[256,1536]{1,0:T(8,128)(2,1)S(1)} collective-permute-done((bf16[256,1536]{1,0:T(8,128)(2,1)S(1)}, bf16[256,1536]{1,0:T(8,128)(2,1)S(1)}, u32[]{:S(2)}, u32[]{:S(2)}) %collective-permute-start.21) | collective-permute-done | bytes 786464 | tf_op jit(solution)/shard_map/ppermute | solution.py:463
  311.5 12.7 %shard_map.302 = (bf16[1024,1536]{1,0:T(8,128)(2,1)S(1)}, bf16[1024,1536]{1,0:T(8,128)(2,1)S(1)}, bf16[1024,1536]{1,0:T(8,128)(2,1)S(1)}, bf16[256,1536]{1,0:T(8,128)(2,1)S(1)}, bf16[256,1536]{1,0:T(8,128)(2,1)S(1)}) custom-call(bf16[256,1536]{1,0:T(8,128)(2,1)S(1)} %collective-permute-done.21.x_ref.refs_5, ...), custom_call_target="tpu_custom_call", output_to_operand_aliasing={{0}: (5, {}), {1}: (6, {}), {2}: (7, {})} | custom-call | bytes 12000000 | tf_op jit(solution)/shard_map/pallas_call | solution.py:339
  324.3 9.5 %collective-permute-done.22.x_ref.refs_6_ = bf16[256,1536]{1,0:T(8,128)(2,1)S(1)} collective-permute-done((bf16[256,1536]{1,0:T(8,128)(2,1)S(1)}, bf16[256,1536]{1,0:T(8,128)(2,1)S(1)}, u32[]{:S(2)}, u32[]{:S(2)}) %collective-permute-start.22) | collective-permute-done | bytes 786464 | tf_op jit(solution)/shard_map/ppermute | solution.py:463
  333.8 14.3 %collective-permute-done.23 = bf16[256,1536]{1,0:T(8,128)(2,1)S(1)} collective-permute-done((bf16[256,1536]{1,0:T(8,128)(2,1)S(1)}, bf16[256,1536]{1,0:T(8,128)(2,1)S(1)}, u32[]{:S(2)}, u32[]{:S(2)}) %collective-permute-start.23) | collective-permute-done | bytes 786464 | tf_op jit(solution)/shard_map/ppermute | solution.py:463
  348.4 12.7 %shard_map.303 = (bf16[1024,1536]{1,0:T(8,128)(2,1)S(1)}, bf16[1024,1536]{1,0:T(8,128)(2,1)S(1)}, bf16[1024,1536]{1,0:T(8,128)(2,1)S(1)}, bf16[256,1536]{1,0:T(8,128)(2,1)}, bf16[256,1536]{1,0:T(8,128)(2,1)S(1)}) custom-call(bf16[256,1536]{1,0:T(8,128)(2,1)S(1)} %collective-permute-done.22.x_ref.refs_6_, ...), custom_call_target="tpu_custom_call", output_to_operand_aliasing={{0}: (5, {}), {1}: (6, {}), {2}: (7, {})} | custom-call | bytes 12000000 | tf_op jit(solution)/shard_map/pallas_call | solution.py:339
  367.7 13.3 %shard_map.304 = bf16[3,768,1536]{2,1,0:T(8,128)(2,1)} custom-call(bf16[1024,1536]{1,0:T(8,128)(2,1)} %copy-done.1, bf16[1024,1536]{1,0:T(8,128)(2,1)} %copy-done.2, bf16[1024,1536]{1,0:T(8,128)(2,1)} %copy-done, bf16[256,1536]{1,0:T(8,128)(2,1)} %copy-done.6, bf16[256,1536]{1,0:T(8,128)(2,1)} %copy-done.12, bf16[256,1536]{1,0:T(8,128)(2,1)} %copy-done.13, ...), custom_call_target="tpu_custom_call" | custom-call | bytes 15000000 | tf_op jit(solution)/shard_map/pallas_call | solution.py:386
  381.0 4.6 collective-permute-done.25
  391.0 4.6 convolution_convert_fusion.4.grad_ref
  395.7 10.8 %shard_map.306 = (bf16[256,1536]{1,0:T(8,128)(2,1)S(1)}, bf16[256,1536]{1,0:T(8,128)(2,1)S(1)}, bf16[256,1536]{1,0:T(8,128)(2,1)S(1)}) custom-call(bf16[256,1536]{1,0:T(8,128)(2,1)S(1)} %copy-done.37, bf16[256,1536]{1,0:T(8,128)(2,1)S(1)} %copy-done.39, bf16[256,1536]{1,0:T(8,128)(2,1)S(1)} %copy-done.41, ...), custom_call_target="tpu_custom_call" | custom-call | bytes 12000000 | tf_op jit(solution)/shard_map/pallas_call | solution.py:245
  407.1 5.1 multiply_reduce_fusion.1
  412.2 3.9 shard_map.307
  421.4 3.9 shard_map.308
  436.1 4.4 all-to-all-start.5
  442.5 14.1 %shard_map.310 = bf16[3,768,1536]{2,1,0:T(8,128)(2,1)} custom-call(bf16[1024,1536]{1,0:T(8,128)(2,1)} %copy-done.1, bf16[1024,1536]{1,0:T(8,128)(2,1)} %copy-done.2, bf16[1024,1536]{1,0:T(8,128)(2,1)} %copy-done, bf16[256,1536]{1,0:T(8,128)(2,1)} %copy-done.6, bf16[256,1536]{1,0:T(8,128)(2,1)} %copy-done.12, bf16[256,1536]{1,0:T(8,128)(2,1)} %copy-done.13, ...), custom_call_target="tpu_custom_call" | custom-call | bytes 15000000 | tf_op jit(solution)/shard_map/pallas_call | solution.py:386
  461.2 4.1 fusion.13
  465.3 3.9 fusion.12
  480.6 26.1 %shard_map.311.refs_4_ = bf16[1024,1152]{1,0:T(8,128)(2,1)S(1)} custom-call(bf16[1024,1152]{1,0:T(8,128)(2,1)S(1)} %copy-done.45, bf16[1024,384]{1,0:T(8,128)(2,1)S(1)} %bitcast.230, f32[3,2,1024]{2,1,0:T(2,128)S(1)} %copy-done.55, f32[1024,128]{1,0:T(8,128)S(1)} %copy-done.30, f32[1024,128]{1,0:T(8,128)S(1)} %copy-done.28, f32[1024,128]{1,0:T(8,128)S(1)} %copy-done.26, ...), custom_call_target="tpu_custom_call" | custom-call | bytes 27000000 | tf_op jit(solution)/shard_map/pallas_call | solution.py:207
  506.7 3.9 collective-permute-done.34
  514.3 4.5 convolution_convert_fusion
  542.5 4.2 all-to-all-start.6
  554.2 7.0 %shard_map.312 = (bf16[1,2,2,2,96,1152]{5,4,3,2,1,0:T(8,128)(2,1)S(1)}, bf16[1,2,2,2,96,1152]{5,4,3,2,1,0:T(8,128)(2,1)}) custom-call(bf16[256,1536]{1,0:T(8,128)(2,1)S(1)} %fusion.21.refs_0_, bf16[256,1536]{1,0:T(8,128)(2,1)S(1)} %copy-done.16, bf16[256,1536]{1,0:T(8,128)(2,1)S(1)} %copy-done.19, bf16[256,1536]{1,0:T(8,128)(2,1)S(1)} %copy-done.22, ...), custom_call_target="tpu_custom_call" | custom-call | bytes 4500000 | tf_op jit(solution)/shard_map/pallas_call | solution.py:437
  574.8 4.7 all-to-all-start.7
  581.8 3.8 collective-permute-start.40
  590.7 26.8 %collective-permute-done.46 = bf16[1,2,96,1152]{3,2,1,0:T(8,128)(2,1)S(1)} collective-permute-done((bf16[1,2,96,1152]{3,2,1,0:T(8,128)(2,1)S(1)}, bf16[1,2,96,1152]{3,2,1,0:T(8,128)(2,1)S(1)}, u32[]{:S(2)}, u32[]{:S(2)}) %collective-permute-start.46) | collective-permute-done | bytes 442400 | tf_op jit(solution)/shard_map/ppermute | solution.py:458
  621.7 3.6 collective-permute-done.45
  637.4 12.6 %all-to-all-start.8 = ((bf16[4,48,2688]{2,1,0:T(8,128)(2,1)}), bf16[4,48,2688]{2,1,0:T(8,128)(2,1)}, u32[]{:S(2)}, u32[]{:S(2)}) async-start(bf16[4,48,2688]{2,1,0:T(8,128)(2,1)} %pad_maximum_fusion.5), calls=%async_computation.8 | async-start | bytes 2064384 | tf_op jit(solution)/shard_map/all_to_all | solution.py:489
  662.8 12.1 %all-to-all-done.8 = bf16[4,48,2688]{2,1,0:T(8,128)(2,1)} async-done(((bf16[4,48,2688]{2,1,0:T(8,128)(2,1)}), bf16[4,48,2688]{2,1,0:T(8,128)(2,1)}, u32[]{:S(2)}, u32[]{:S(2)}) %all-to-all-start.8) | async-done | bytes 1032224 | tf_op jit(solution)/shard_map/all_to_all | solution.py:489
  (530 shorter events, 222.0 us)
Async XLA Ops:
  18.8 111.2 %all-gather.11.cloned.1.call-start = ((), (), s32[]{:S(2)}) async-start(), calls=%async_computation.9 | async-start | bytes 3981312 | tf_op jit(solution)/shard_map/all_gather | solution.py:640
  37.8 37.5 %collective-permute-start.1 = (bf16[3,96,1536]{2,1,0:T(8,128)(2,1)}, bf16[3,96,1536]{2,1,0:T(8,128)(2,1)}, u32[]{:S(2)}, u32[]{:S(2)}) collective-permute-start(bf16[3,96,1536]{2,1,0:T(8,128)(2,1)} %get-tuple-element.263.refs_0_), channel_id=1, source_target_pairs={{0,8},{4,12},{8,0},{12,4},{16,24},{20,28},{24,16},{28,20},{1,9},{5... | collective-permute-start | bytes 2654216 | tf_op jit(solution)/shard_map/ppermute | solution.py:458
  39.3 36.0 %collective-permute-start.2 = (bf16[3,96,1536]{2,1,0:T(8,128)(2,1)}, bf16[3,96,1536]{2,1,0:T(8,128)(2,1)}, u32[]{:S(2)}, u32[]{:S(2)}) collective-permute-start(bf16[3,96,1536]{2,1,0:T(8,128)(2,1)} %get-tuple-element.267.refs_4_), channel_id=1, source_target_pairs={{0,16},{4,20},{8,24},{12,28},{16,0},{20,4},{24,8},{28,12},{1,17},{... | collective-permute-start | bytes 2654216 | tf_op jit(solution)/shard_map/ppermute | solution.py:458
  41.6 35.9 %all-to-all-start.1 = ((bf16[4,48,1536]{2,1,0:T(8,128)(2,1)}), bf16[4,48,1536]{2,1,0:T(8,128)(2,1)}, u32[]{:S(2)}, u32[]{:S(2)}) async-start(bf16[4,48,1536]{2,1,0:T(8,128)(2,1)} %broadcast_in_dim.117), calls=%async_computation.1 | async-start | bytes 1179648 | tf_op jit(solution)/shard_map/all_to_all | solution.py:489
  45.8 169.2 %all-gather.13.cloned.1.call-start = ((), (), s32[]{:S(2)}) async-start(), calls=%async_computation.10 | async-start | bytes 5308416 | tf_op jit(solution)/shard_map/all_gather | solution.py:640
  45.9 29.4 %collective-permute-start = (bf16[256,1536]{1,0:T(8,128)(2,1)S(1)}, bf16[256,1536]{1,0:T(8,128)(2,1)S(1)}, u32[]{:S(2)}, u32[]{:S(2)}) collective-permute-start(bf16[256,1536]{1,0:T(8,128)(2,1)S(1)} %fusion.21.refs_0_), channel_id=1, source_target_pairs={{0,1},{1,2},{2,3},{3,0},{4,5},{5,6},{6,7},{7,4},{8,9},{9,10},{10,1... | collective-permute-start | bytes 2359304 | tf_op jit(solution)/shard_map/ppermute | solution.py:463
  77.6 52.4 %collective-permute-start.5 = (bf16[3,96,1536]{2,1,0:T(8,128)(2,1)}, bf16[3,96,1536]{2,1,0:T(8,128)(2,1)}, u32[]{:S(2)}, u32[]{:S(2)}) collective-permute-start(bf16[3,96,1536]{2,1,0:T(8,128)(2,1)} %get-tuple-element.263.refs_0_), channel_id=1, source_target_pairs={{0,16},{4,20},{8,24},{12,28},{16,0},{20,4},{24,8},{28,12},{1,17},{... | collective-permute-start | bytes 2654216 | tf_op jit(solution)/shard_map/ppermute | solution.py:458
  78.2 51.8 %collective-permute-start.6 = (bf16[3,96,1536]{2,1,0:T(8,128)(2,1)}, bf16[3,96,1536]{2,1,0:T(8,128)(2,1)}, u32[]{:S(2)}, u32[]{:S(2)}) collective-permute-start(bf16[3,96,1536]{2,1,0:T(8,128)(2,1)} %get-tuple-element.267.refs_4_), channel_id=1, source_target_pairs={{0,8},{4,12},{8,0},{12,4},{16,24},{20,28},{24,16},{28,20},{1,9},{5... | collective-permute-start | bytes 2654216 | tf_op jit(solution)/shard_map/ppermute | solution.py:458
  80.5 49.5 %all-to-all-start.2 = ((bf16[4,48,1536]{2,1,0:T(8,128)(2,1)}), bf16[4,48,1536]{2,1,0:T(8,128)(2,1)}, u32[]{:S(2)}, u32[]{:S(2)}) async-start(bf16[4,48,1536]{2,1,0:T(8,128)(2,1)} %broadcast_in_dim.118), calls=%async_computation.2 | async-start | bytes 1179648 | tf_op jit(solution)/shard_map/all_to_all | solution.py:489
  84.7 137.2 %all-gather.15.cloned.1.call-start = ((), (), s32[]{:S(2)}) async-start(), calls=%async_computation.11 | async-start | bytes 5308416 | tf_op jit(solution)/shard_map/all_gather | solution.py:640
  84.7 31.9 %collective-permute-start.3 = (bf16[256,1536]{1,0:T(8,128)(2,1)S(1)}, bf16[256,1536]{1,0:T(8,128)(2,1)S(1)}, u32[]{:S(2)}, u32[]{:S(2)}) collective-permute-start(bf16[256,1536]{1,0:T(8,128)(2,1)S(1)} %collective-permute-done.refs_1_), channel_id=1, source_target_pairs={{0,1},{1,2},{2,3},{3,0},{4,5},{5,6},{6,7},{7,4},{8,9},{9,10},{10,1... | collective-permute-start | bytes 2359304 | tf_op jit(solution)/shard_map/ppermute | solution.py:463
  86.6 42.4 %collective-permute-start.4 = (bf16[256,1536]{1,0:T(8,128)(2,1)S(1)}, bf16[256,1536]{1,0:T(8,128)(2,1)S(1)}, u32[]{:S(2)}, u32[]{:S(2)}) collective-permute-start(bf16[256,1536]{1,0:T(8,128)(2,1)S(1)} %fusion.21.refs_0_), channel_id=1, source_target_pairs={{0,3},{1,0},{2,1},{3,2},{4,7},{5,4},{6,5},{7,6},{8,11},{9,8},{10,9... | collective-permute-start | bytes 2359304 | tf_op jit(solution)/shard_map/ppermute | solution.py:463
  131.1 51.6 %all-to-all-start.3 = ((bf16[4,2,48,1536]{3,2,1,0:T(8,128)(2,1)}), bf16[4,2,48,1536]{3,2,1,0:T(8,128)(2,1)}, u32[]{:S(2)}, u32[]{:S(2)}) async-start(bf16[4,2,48,1536]{3,2,1,0:T(8,128)(2,1)} %broadcast_in_dim.119), calls=%async_computation.3 | async-start | bytes 2359296 | tf_op jit(solution)/shard_map/all_to_all | solution.py:489
  137.9 93.2 %all-gather.17.cloned.1.call-start = ((), (), s32[]{:S(2)}) async-start(), calls=%async_computation.12 | async-start | bytes 5308416 | tf_op jit(solution)/shard_map/all_gather | solution.py:640
  137.9 39.2 %collective-permute-start.7 = (bf16[3,96,1536]{2,1,0:T(8,128)(2,1)}, bf16[3,96,1536]{2,1,0:T(8,128)(2,1)}, u32[]{:S(2)}, u32[]{:S(2)}) collective-permute-start(bf16[3,96,1536]{2,1,0:T(8,128)(2,1)} %collective-permute-done.1.refs_1_), channel_id=1, source_target_pairs={{0,16},{4,20},{8,24},{12,28},{16,0},{20,4},{24,8},{28,12},{1,17},{... | collective-permute-start | bytes 2654216 | tf_op jit(solution)/shard_map/ppermute | solution.py:458
  139.4 37.7 %collective-permute-start.8 = (bf16[3,96,1536]{2,1,0:T(8,128)(2,1)}, bf16[3,96,1536]{2,1,0:T(8,128)(2,1)}, u32[]{:S(2)}, u32[]{:S(2)}) collective-permute-start(bf16[3,96,1536]{2,1,0:T(8,128)(2,1)} %collective-permute-done.2.refs_6_), channel_id=1, source_target_pairs={{0,8},{4,12},{8,0},{12,4},{16,24},{20,28},{24,16},{28,20},{1,9},{5... | collective-permute-start | bytes 2654216 | tf_op jit(solution)/shard_map/ppermute | solution.py:458
  140.9 36.2 %collective-permute-start.9 = (bf16[256,1536]{1,0:T(8,128)(2,1)S(1)}, bf16[256,1536]{1,0:T(8,128)(2,1)S(1)}, u32[]{:S(2)}, u32[]{:S(2)}) collective-permute-start(bf16[256,1536]{1,0:T(8,128)(2,1)S(1)} %fusion.23.g_ref.refs_7_), channel_id=1, source_target_pairs={{0,1},{1,2},{2,3},{3,0},{4,5},{5,6},{6,7},{7,4},{8,9},{9,10},{10,1... | collective-permute-start | bytes 2359304 | tf_op jit(solution)/shard_map/ppermute | solution.py:463
  185.0 78.8 %all-gather.19.cloned.1.call-start = ((), (), s32[]{:S(2)}) async-start(), calls=%async_computation.13 | async-start | bytes 5308416 | tf_op jit(solution)/shard_map/all_gather | solution.py:640
  186.3 25.3 %all-to-all-start.4 = ((bf16[4,256,384]{2,1,0:T(8,128)(2,1)}), bf16[4,256,384]{2,1,0:T(8,128)(2,1)}, u32[]{:S(2)}, u32[]{:S(2)}) async-start(bf16[4,256,384]{2,1,0:T(8,128)(2,1)} %bitcast.231), calls=%async_computation.4 | async-start | bytes 1572864 | tf_op jit(solution)/shard_map/all_to_all | solution.py:489
  211.5 19.1 %collective-permute-start.18 = (bf16[256,1536]{1,0:T(8,128)(2,1)S(1)}, bf16[256,1536]{1,0:T(8,128)(2,1)S(1)}, u32[]{:S(2)}, u32[]{:S(2)}) collective-permute-start(bf16[256,1536]{1,0:T(8,128)(2,1)S(1)} %fusion.23.g_ref.refs_7_), channel_id=1, source_target_pairs={{0,3},{1,0},{2,1},{3,2},{4,7},{5,4},{6,5},{7,6},{8,11},{9,8},{10,9... | collective-permute-start | bytes 2359304 | tf_op jit(solution)/shard_map/ppermute | solution.py:463
  230.7 38.6 %collective-permute-start.19 = (bf16[256,1536]{1,0:T(8,128)(2,1)S(1)}, bf16[256,1536]{1,0:T(8,128)(2,1)}, u32[]{:S(2)}, u32[]{:S(2)}) collective-permute-start(bf16[256,1536]{1,0:T(8,128)(2,1)S(1)} %collective-permute-done.9.g_ref.refs_8_), channel_id=1, source_target_pairs={{0,1},{1,2},{2,3},{3,0},{4,5},{5,6},{6,7},{7,4},{8,9},{9,10},{10,1... | collective-permute-start | bytes 2359304 | tf_op jit(solution)/shard_map/ppermute | solution.py:463
  269.3 21.6 %collective-permute-start.20 = (bf16[256,1536]{1,0:T(8,128)(2,1)S(1)}, bf16[256,1536]{1,0:T(8,128)(2,1)S(1)}, u32[]{:S(2)}, u32[]{:S(2)}) collective-permute-start(bf16[256,1536]{1,0:T(8,128)(2,1)S(1)} %multiply_convert_fusion.x_ref.refs_3_), channel_id=1, source_target_pairs={{0,1},{1,2},{2,3},{3,0},{4,5},{5,6},{6,7},{7,4},{8,9},{9,10},{10,1... | collective-permute-start | bytes 2359304 | tf_op jit(solution)/shard_map/ppermute | solution.py:463
  290.8 20.7 %collective-permute-start.21 = (bf16[256,1536]{1,0:T(8,128)(2,1)S(1)}, bf16[256,1536]{1,0:T(8,128)(2,1)S(1)}, u32[]{:S(2)}, u32[]{:S(2)}) collective-permute-start(bf16[256,1536]{1,0:T(8,128)(2,1)S(1)} %collective-permute-done.20.x_ref.refs_4_), channel_id=1, source_target_pairs={{0,1},{1,2},{2,3},{3,0},{4,5},{5,6},{6,7},{7,4},{8,9},{9,10},{10,1... | collective-permute-start | bytes 2359304 | tf_op jit(solution)/shard_map/ppermute | solution.py:463
  311.5 22.3 %collective-permute-start.22 = (bf16[256,1536]{1,0:T(8,128)(2,1)S(1)}, bf16[256,1536]{1,0:T(8,128)(2,1)S(1)}, u32[]{:S(2)}, u32[]{:S(2)}) collective-permute-start(bf16[256,1536]{1,0:T(8,128)(2,1)S(1)} %collective-permute-done.21.x_ref.refs_5_), channel_id=1, source_target_pairs={{0,1},{1,2},{2,3},{3,0},{4,5},{5,6},{6,7},{7,4},{8,9},{9,10},{10,1... | collective-permute-start | bytes 2359304 | tf_op jit(solution)/shard_map/ppermute | solution.py:463
  311.5 36.6 %collective-permute-start.23 = (bf16[256,1536]{1,0:T(8,128)(2,1)S(1)}, bf16[256,1536]{1,0:T(8,128)(2,1)S(1)}, u32[]{:S(2)}, u32[]{:S(2)}) collective-permute-start(bf16[256,1536]{1,0:T(8,128)(2,1)S(1)} %get-tuple-element.313), channel_id=1, source_target_pairs={{0,1},{1,2},{2,3},{3,0},{4,5},{5,6},{6,7},{7,4},{8,9},{9,10},{10,1... | collective-permute-start | bytes 2359304 | tf_op jit(solution)/shard_map/ppermute | solution.py:463
  385.6 50.4 %collective-permute-start.28 = (bf16[3,768,1536]{2,1,0:T(8,128)(2,1)}, bf16[3,768,1536]{2,1,0:T(8,128)(2,1)}, u32[]{:S(2)}, u32[]{:S(2)}) collective-permute-start(bf16[3,768,1536]{2,1,0:T(8,128)(2,1)} %shard_map.304), channel_id=1, source_target_pairs={{0,4},{4,0},{8,12},{12,8},{16,20},{20,16},{24,28},{28,24},{1,5},{5... | collective-permute-start | bytes 21233672 | tf_op jit(solution)/shard_map/ppermute | solution.py:453
  406.5 26.3 %collective-permute-start.27 = (bf16[1,2,2,2,96,1536]{5,4,3,2,1,0:T(8,128)(2,1)S(1)}, bf16[1,2,2,2,96,1536]{5,4,3,2,1,0:T(8,128)(2,1)}, u32[]{:S(2)}, u32[]{:S(2)}) collective-permute-start(bf16[1,2,2,2,96,1536]{5,4,3,2,1,0:T(8,128)(2,1)S(1)} %get-tuple-element.363), channel_id=1, source_target_pairs={{0,4},{4,0},{8,12},{12,8},{16,20},{20,16},{24,28},{28,24},{1,5},{5... | collective-permute-start | bytes 7077896 | tf_op jit(solution)/shard_map/ppermute | solution.py:453
  416.1 19.9 %collective-permute-start.26 = (bf16[256,1536]{1,0:T(8,128)(2,1)S(1)}, bf16[256,1536]{1,0:T(8,128)(2,1)S(1)}, u32[]{:S(2)}, u32[]{:S(2)}) collective-permute-start(bf16[256,1536]{1,0:T(8,128)(2,1)S(1)} %copy-done.57), channel_id=1, source_target_pairs={{0,3},{1,0},{2,1},{3,2},{4,7},{5,4},{6,5},{7,6},{8,11},{9,8},{10,9... | collective-permute-start | bytes 2359304 | tf_op jit(solution)/shard_map/ppermute | solution.py:463
  436.1 25.2 %collective-permute-start.31 = (bf16[3,2,2,2,96,1536]{5,4,3,2,1,0:T(8,128)(2,1)}, bf16[3,2,2,2,96,1536]{5,4,3,2,1,0:T(8,128)(2,1)}, u32[]{:S(2)}, u32[]{:S(2)}) collective-permute-start(bf16[3,2,2,2,96,1536]{5,4,3,2,1,0:T(8,128)(2,1)} %get-tuple-element.376), channel_id=1, source_target_pairs={{0,4},{4,0},{8,12},{12,8},{16,20},{20,16},{24,28},{28,24},{1,5},{5... | collective-permute-start | bytes 21233672 | tf_op jit(solution)/shard_map/ppermute | solution.py:453
  436.1 25.2 %all-to-all-start.5 = ((bf16[4,256,384]{2,1,0:T(8,128)(2,1)}), bf16[4,256,384]{2,1,0:T(8,128)(2,1)S(1)}, u32[]{:S(2)}, u32[]{:S(2)}) async-start(bf16[4,256,384]{2,1,0:T(8,128)(2,1)} %pad_maximum_fusion.7), calls=%async_computation.5 | async-start | bytes 1572864 | tf_op jit(solution)/shard_map/all_to_all | solution.py:489
  473.2 40.2 %collective-permute-start.32 = (bf16[3,2,96,1536]{3,2,0,1:T(8,128)(2,1)}, bf16[3,2,96,1536]{3,2,0,1:T(8,128)(2,1)}, u32[]{:S(2)}, u32[]{:S(2)}) collective-permute-start(bf16[3,2,96,1536]{3,2,0,1:T(8,128)(2,1)} %fusion.12), channel_id=1, source_target_pairs={{0,16},{4,20},{8,24},{12,28},{16,0},{20,4},{24,8},{28,12},{1,17},{... | collective-permute-start | bytes 5308424 | tf_op jit(solution)/shard_map/ppermute | solution.py:458
  474.3 40.0 %collective-permute-start.33 = (bf16[3,2,96,1536]{3,2,1,0:T(8,128)(2,1)}, bf16[3,2,96,1536]{3,2,1,0:T(8,128)(2,1)}, u32[]{:S(2)}, u32[]{:S(2)}) collective-permute-start(bf16[3,2,96,1536]{3,2,1,0:T(8,128)(2,1)} %fusion.13), channel_id=1, source_target_pairs={{0,8},{4,12},{8,0},{12,4},{16,24},{20,28},{24,16},{28,20},{1,9},{5... | collective-permute-start | bytes 5308424 | tf_op jit(solution)/shard_map/ppermute | solution.py:458
  475.2 35.5 %collective-permute-start.34 = (bf16[256,1536]{1,0:T(8,128)(2,1)}, bf16[256,1536]{1,0:T(8,128)(2,1)}, u32[]{:S(2)}, u32[]{:S(2)}) collective-permute-start(bf16[256,1536]{1,0:T(8,128)(2,1)} %add_convert_fusion.4), channel_id=1, source_target_pairs={{0,3},{1,0},{2,1},{3,2},{4,7},{5,4},{6,5},{7,6},{8,11},{9,8},{10,9... | collective-permute-start | bytes 2359304 | tf_op jit(solution)/shard_map/ppermute | solution.py:463
  476.6 34.0 %collective-permute-start.35 = (bf16[256,1536]{1,0:T(8,128)(2,1)}, bf16[256,1536]{1,0:T(8,128)(2,1)}, u32[]{:S(2)}, u32[]{:S(2)}) collective-permute-start(bf16[256,1536]{1,0:T(8,128)(2,1)} %get-tuple-element.392), channel_id=1, source_target_pairs={{0,1},{1,2},{2,3},{3,0},{4,5},{5,6},{6,7},{7,4},{8,9},{9,10},{10,1... | collective-permute-start | bytes 2359304 | tf_op jit(solution)/shard_map/ppermute | solution.py:463
  522.1 45.3 %collective-permute-start.36 = (bf16[256,1536]{1,0:T(8,128)(2,1)}, bf16[256,1536]{1,0:T(8,128)(2,1)}, u32[]{:S(2)}, u32[]{:S(2)}) collective-permute-start(bf16[256,1536]{1,0:T(8,128)(2,1)} %get-tuple-element.402), channel_id=1, source_target_pairs={{0,3},{1,0},{2,1},{3,2},{4,7},{5,4},{6,5},{7,6},{8,11},{9,8},{10,9... | collective-permute-start | bytes 2359304 | tf_op jit(solution)/shard_map/ppermute | solution.py:463
  525.1 43.2 %collective-permute-start.37 = (bf16[256,1536]{1,0:T(8,128)(2,1)}, bf16[256,1536]{1,0:T(8,128)(2,1)}, u32[]{:S(2)}, u32[]{:S(2)}) collective-permute-start(bf16[256,1536]{1,0:T(8,128)(2,1)} %get-tuple-element.403), channel_id=1, source_target_pairs={{0,1},{1,2},{2,3},{3,0},{4,5},{5,6},{6,7},{7,4},{8,9},{9,10},{10,1... | collective-permute-start | bytes 2359304 | tf_op jit(solution)/shard_map/ppermute | solution.py:463
  534.4 34.0 %collective-permute-start.39 = (bf16[4,96,1536]{2,1,0:T(8,128)(2,1)}, bf16[4,96,1536]{2,1,0:T(8,128)(2,1)}, u32[]{:S(2)}, u32[]{:S(2)}) collective-permute-start(bf16[4,96,1536]{2,1,0:T(8,128)(2,1)} %fusion.26), channel_id=1, source_target_pairs={{0,16},{4,20},{8,24},{12,28},{16,0},{20,4},{24,8},{28,12},{1,17},{... | collective-permute-start | bytes 3538952 | tf_op jit(solution)/shard_map/ppermute | solution.py:458
  539.6 28.8 %collective-permute-start.38 = (bf16[4,96,1536]{2,1,0:T(8,128)(2,1)}, bf16[4,96,1536]{2,1,0:T(8,128)(2,1)}, u32[]{:S(2)}, u32[]{:S(2)}) collective-permute-start(bf16[4,96,1536]{2,1,0:T(8,128)(2,1)} %fusion.28), channel_id=1, source_target_pairs={{0,8},{4,12},{8,0},{12,4},{16,24},{20,28},{24,16},{28,20},{1,9},{5... | collective-permute-start | bytes 3538952 | tf_op jit(solution)/shard_map/ppermute | solution.py:458
  542.5 23.7 %all-to-all-start.6 = ((f32[32,1,144]{2,1,0:T(1,128)}), f32[32,1,144]{2,1,0:T(1,128)S(1)}, u32[]{:S(2)}, u32[]{:S(2)}) async-start(f32[32,1,144]{2,1,0:T(1,128)} %reshape.796), calls=%async_computation.6 | async-start | bytes 65536 | tf_op jit(solution)/shard_map/all_to_all | solution.py:865
  549.8 78.3 %collective-permute-start.41 = (bf16[3,2,96,1536]{3,2,0,1:T(8,128)(2,1)}, bf16[3,2,96,1536]{3,2,0,1:T(8,128)(2,1)}, u32[]{:S(2)}, u32[]{:S(2)}) collective-permute-start(bf16[3,2,96,1536]{3,2,0,1:T(8,128)(2,1)} %bitcast.221), channel_id=1, source_target_pairs={{0,16},{4,20},{8,24},{12,28},{16,0},{20,4},{24,8},{28,12},{1,17},{... | collective-permute-start | bytes 5308424 | tf_op jit(solution)/shard_map/ppermute | solution.py:458
  567.5 60.6 %collective-permute-start.42 = (bf16[3,2,96,1536]{3,2,0,1:T(8,128)(2,1)}, bf16[3,2,96,1536]{3,2,0,1:T(8,128)(2,1)}, u32[]{:S(2)}, u32[]{:S(2)}) collective-permute-start(bf16[3,2,96,1536]{3,2,0,1:T(8,128)(2,1)} %bitcast.257), channel_id=1, source_target_pairs={{0,8},{4,12},{8,0},{12,4},{16,24},{20,28},{24,16},{28,20},{1,9},{5... | collective-permute-start | bytes 5308424 | tf_op jit(solution)/shard_map/ppermute | solution.py:458
  574.8 53.3 %all-to-all-start.7 = ((bf16[4,3,48,1536]{3,2,1,0:T(8,128)(2,1)}), bf16[4,3,48,1536]{3,2,1,0:T(8,128)(2,1)}, u32[]{:S(2)}, u32[]{:S(2)}) async-start(bf16[4,3,48,1536]{3,2,1,0:T(8,128)(2,1)} %pad_maximum_fusion.1), calls=%async_computation.7 | async-start | bytes 3538944 | tf_op jit(solution)/shard_map/all_to_all | solution.py:489
  581.8 46.3 %collective-permute-start.40 = (bf16[256,1536]{1,0:T(8,128)(2,1)}, bf16[256,1536]{1,0:T(8,128)(2,1)S(1)}, u32[]{:S(2)}, u32[]{:S(2)}) collective-permute-start(bf16[256,1536]{1,0:T(8,128)(2,1)} %fusion.18), channel_id=1, source_target_pairs={{0,3},{1,0},{2,1},{3,2},{4,7},{5,4},{6,5},{7,6},{8,11},{9,8},{10,9... | collective-permute-start | bytes 2359304 | tf_op jit(solution)/shard_map/ppermute | solution.py:463
  586.8 30.6 %collective-permute-start.46 = (bf16[1,2,96,1152]{3,2,1,0:T(8,128)(2,1)S(1)}, bf16[1,2,96,1152]{3,2,1,0:T(8,128)(2,1)S(1)}, u32[]{:S(2)}, u32[]{:S(2)}) collective-permute-start(bf16[1,2,96,1152]{3,2,1,0:T(8,128)(2,1)S(1)} %fusion.47), channel_id=1, source_target_pairs={{0,8},{4,12},{8,0},{12,4},{16,24},{20,28},{24,16},{28,20},{1,9},{5... | collective-permute-start | bytes 1327112 | tf_op jit(solution)/shard_map/ppermute | solution.py:458
  589.2 28.3 %collective-permute-start.44 = (bf16[1,2,96,1152]{3,2,1,0:T(8,128)(2,1)S(1)}, bf16[1,2,96,1152]{3,2,1,0:T(8,128)(2,1)S(1)}, u32[]{:S(2)}, u32[]{:S(2)}) collective-permute-start(bf16[1,2,96,1152]{3,2,1,0:T(8,128)(2,1)S(1)} %fusion.46), channel_id=1, source_target_pairs={{0,16},{4,20},{8,24},{12,28},{16,0},{20,4},{24,8},{28,12},{1,17},{... | collective-permute-start | bytes 1327112 | tf_op jit(solution)/shard_map/ppermute | solution.py:458
  631.6 26.5 %collective-permute-start.48 = (bf16[3,96,1536]{2,1,0:T(8,128)(2,1)}, bf16[3,96,1536]{2,1,0:T(8,128)(2,1)}, u32[]{:S(2)}, u32[]{:S(2)}) collective-permute-start(bf16[3,96,1536]{2,1,0:T(8,128)(2,1)} %slice_bitcast_fusion.2), channel_id=1, source_target_pairs={{0,8},{4,12},{8,0},{12,4},{16,24},{20,28},{24,16},{28,20},{1,9},{5... | collective-permute-start | bytes 2654216 | tf_op jit(solution)/shard_map/ppermute | solution.py:458
  636.1 23.4 %collective-permute-start.49 = (bf16[3,96,1536]{2,1,0:T(8,128)(2,1)}, bf16[3,96,1536]{2,1,0:T(8,128)(2,1)}, u32[]{:S(2)}, u32[]{:S(2)}) collective-permute-start(bf16[3,96,1536]{2,1,0:T(8,128)(2,1)} %slice_bitcast_fusion), channel_id=1, source_target_pairs={{0,16},{4,20},{8,24},{12,28},{16,0},{20,4},{24,8},{28,12},{1,17},{... | collective-permute-start | bytes 2654216 | tf_op jit(solution)/shard_map/ppermute | solution.py:458
  637.4 37.5 %all-to-all-start.8 = ((bf16[4,48,2688]{2,1,0:T(8,128)(2,1)}), bf16[4,48,2688]{2,1,0:T(8,128)(2,1)}, u32[]{:S(2)}, u32[]{:S(2)}) async-start(bf16[4,48,2688]{2,1,0:T(8,128)(2,1)} %pad_maximum_fusion.5), calls=%async_computation.8 | async-start | bytes 2064384 | tf_op jit(solution)/shard_map/all_to_all | solution.py:489
  (156 other events, 1616.6 us)
Sparse Core Ops, SparseCore 0:
  32.4 43.2 all-gather.10
  77.7 42.0 all-gather.12
  130.1 49.4 all-gather.14
  185.2 37.8 all-gather.16
  224.8 38.9 all-gather.18

commit v5 on v4

--- a/solution.py
+++ b/solution.py
@@ -103,9 +103,8 @@
 
     def body(*refs):
         norm_refs = refs[:seq_size]
-        cols_ref, cos_ref, low_ref, high_ref, seg_col, seg_row, qkv_out, mixed_ref, total_ref = refs[
-            seq_size:
-        ]
+        cols_ref, cos_ref, low_ref, high_ref, seg_col, seg_row, *outs = refs[seq_size:]
+        qkv_out, mixed_ref, total_ref, exact_ref = outs
         for number in range(seq_size):
             rows = slice(number * block, (number + 1) * block)
             tables = cos_ref[rows], low_ref[rows], high_ref[rows]
@@ -130,7 +129,9 @@
                 total_ref[0, head : head + 1, rows] = highest * scale + jnp.log2(total)
             place = seq_distance_order(number, seq_size)
             target = pl.ds(pl.multiple_of(place * block, block), block)
-            mixed_ref[target, :] = jnp.concatenate(mixed).T.astype(jnp.bfloat16)
+            mixed = jnp.concatenate(mixed)
+            exact_ref[0, :, rows] = mixed
+            mixed_ref[target, :] = mixed.T.astype(jnp.bfloat16)
 
     whole = pl.BlockSpec((length, LANES), lambda p: (0, 0))
     return pl.pallas_call(
@@ -147,18 +148,20 @@
             pl.BlockSpec((length, group), lambda p: (0, p)),
             pl.BlockSpec((length, LANES), lambda p: (0, p)),
             pl.BlockSpec((1, PAIR, length), lambda p: (p, 0, 0)),
+            pl.BlockSpec((1, LANES, length), lambda p: (p, 0, 0)),
         ],
         out_shape=[
             jax.ShapeDtypeStruct((length, pairs * group), jnp.bfloat16),
             jax.ShapeDtypeStruct((length, pairs * LANES), jnp.bfloat16),
             jax.ShapeDtypeStruct((pairs, PAIR, length), jnp.float32),
+            jax.ShapeDtypeStruct((pairs, LANES, length), jnp.float32),
         ],
         compiler_params=pltpu.CompilerParams(vmem_limit_bytes=40 << 20),
         cost_estimate=taking(8),
     )(*norms, qkv_cols, *tables, *segments)
 
 
-def self_backward(qkv, grad_out, log_total, tables, segments, seq_size):
+def self_backward(qkv, grad_out, log_total, exact, tables, segments, seq_size):
     length = qkv.shape[0]
     group = 3 * LANES
     pairs = qkv.shape[1] // group
@@ -166,16 +169,18 @@
     scaling = HDIM ** (-0.5)
     scale = scaling * LOG2E
 
-    def body(qkv_ref, grad_ref, total_ref, *rest):
+    def body(qkv_ref, grad_ref, total_ref, exact_ref, *rest):
         cos_ref, low_ref, high_ref, seg_col, seg_row, out_ref, dk_sum, dv_sum = rest
         for number in range(seq_size):
             rows = slice(number * block, (number + 1) * block)
             same = seg_col[...] == seg_row[:, rows]
             place = seq_distance_order(number, seq_size)
             grads = grad_ref[pl.ds(pl.multiple_of(place * block, block), block), :]
+            inner = grads.astype(jnp.float32).T * exact_ref[0, :, rows]
             grad_queries = []
             for head in range(PAIR):
                 cols = slice(head * HDIM, (head + 1) * HDIM)
+                head_inner = jnp.sum(inner[cols, :], axis=0, keepdims=True)
                 grad_head = grads[:, cols]
                 query_head = qkv_ref[rows, part(0, head)]
                 key_head = qkv_ref[:, part(1, head)]
@@ -184,24 +189,23 @@
                 ]
                 chance = jnp.exp2(jnp.where(same, scores, NEG_FILL))
                 grad_chance = dot(qkv_ref[:, part(2, head)], grad_head, 1, 1)
-                inner = jnp.sum(chance * grad_chance, axis=0, keepdims=True)
-                grad_scores = (chance * (grad_chance - inner)).astype(jnp.bfloat16)
+                grad_scores = (chance * (grad_chance - head_inner)).astype(jnp.bfloat16)
                 grad_queries.append(dot(key_head, grad_scores, 0, 0))
-                grad_keys = dot(grad_scores, query_head, 1, 0)
-                grad_values = dot(chance.astype(jnp.bfloat16), grad_head, 1, 0)
+                grad_keys = dot(query_head, grad_scores, 0, 1)
+                grad_values = dot(grad_head, chance.astype(jnp.bfloat16), 0, 1)
                 if number == 0:
-                    dk_sum[:, cols] = grad_keys
-                    dv_sum[:, cols] = grad_values
+                    dk_sum[cols, :] = grad_keys
+                    dv_sum[cols, :] = grad_values
                 else:
-                    dk_sum[:, cols] += grad_keys
-                    dv_sum[:, cols] += grad_values
+                    dk_sum[cols, :] += grad_keys
+                    dv_sum[cols, :] += grad_values
             tables = cos_ref[rows], low_ref[rows], high_ref[rows]
             turned = turn(jnp.concatenate(grad_queries).T * scaling, *tables, -1.0)
             out_ref[rows, :LANES] = turned.astype(jnp.bfloat16)
         tables = cos_ref[...], low_ref[...], high_ref[...]
-        turned = turn(dk_sum[...] * scaling, *tables, -1.0)
+        turned = turn(dk_sum[...].T * scaling, *tables, -1.0)
         out_ref[:, LANES : 2 * LANES] = turned.astype(jnp.bfloat16)
-        out_ref[:, 2 * LANES :] = dv_sum[...].astype(jnp.bfloat16)
+        out_ref[:, 2 * LANES :] = dv_sum[...].T.astype(jnp.bfloat16)
 
     whole = pl.BlockSpec((length, LANES), lambda p: (0, 0))
     return pl.pallas_call(
@@ -211,6 +215,7 @@
             pl.BlockSpec((length, group), lambda p: (0, p)),
             pl.BlockSpec((length, LANES), lambda p: (0, p)),
             pl.BlockSpec((1, PAIR, length), lambda p: (p, 0, 0)),
+            pl.BlockSpec((1, LANES, length), lambda p: (p, 0, 0)),
         ]
         + [whole] * 3
         + [
@@ -219,10 +224,10 @@
         ],
         out_specs=pl.BlockSpec((length, group), lambda p: (0, p)),
         out_shape=jax.ShapeDtypeStruct(qkv.shape, jnp.bfloat16),
-        scratch_shapes=[pltpu.VMEM((length, LANES), jnp.float32)] * 2,
+        scratch_shapes=[pltpu.VMEM((LANES, length), jnp.float32)] * 2,
         compiler_params=pltpu.CompilerParams(vmem_limit_bytes=40 << 20),
-        cost_estimate=taking(9),
-    )(qkv, grad_out, log_total, *tables, *segments)
+        cost_estimate=taking(7),
+    )(qkv, grad_out, log_total, exact, *tables, *segments)
 
 
 CROSS_HEADS = 8
@@ -712,7 +717,7 @@
         feed_held[0, y, 1] = shift_dp(feed_held[0, y - 1, 1], 1, 0)
         feed_held[1, y, 1] = shift_dp(feed_held[1, y, 0], 0, 1)
     all_grads = [grad_output_low, shift_seq(grad_output_low)]
-    qkv, head_attended, log_total = self_forward(norms_one, qkv_cols, tables, segments)
+    qkv, head_attended, log_total, exact = self_forward(norms_one, qkv_cols, tables, segments)
     cross_rows, feed_held, head_attended, all_grads = stage(
         cross_rows, feed_held, head_attended, all_grads
     )
@@ -833,29 +838,27 @@
     )
 
     weight_packed = pack_first(weight_own, weight_other)
-    cross_out_firsts = add_first(cross_out_came, cross_out_own, cross_out_other)
     head_grad = head_grad.reshape(rows_dev * seq_size, head_width)
     head_grad = jnp.pad(head_grad, ((0, 0), (0, pairs * LANES - head_width)))
     feed_moving = reduce_middle(feed_came, feed_out), reduce_ahead(feed_out)
-    head_grad, weight_packed, feed_moving, cross_out_firsts = stage(
-        head_grad, weight_packed, feed_moving, cross_out_firsts
-    )
+    head_grad, weight_packed, feed_moving = stage(head_grad, weight_packed, feed_moving)
     feed_moving = shift_seq(feed_moving[0], -1), shift_seq(feed_moving[1])
     weight_came = send_first(weight_packed)
-    turned = self_backward(qkv, head_grad, log_total, tables, segments, seq_size)
-    weight_came, turned, feed_moving, cross_out_firsts = stage(
-        weight_came, turned, feed_moving, cross_out_firsts
-    )
-
+    turned = self_backward(qkv, head_grad, log_total, exact, tables, segments, seq_size)
     norm_terms = low(contract_cols(turned, qkv_cols))
     norm_terms = [norm_terms[k * rows_dev : (k + 1) * rows_dev] for k in range(seq_size)]
-    norm_terms, turned, own_units, feed_moving = stage(norm_terms, turned, own_units, feed_moving)
+    qkv_own, qkv_other = weight_products(norms_one, [turned])
+    weight_came, norm_terms, qkv_own, qkv_other, feed_moving, cross_out_came, own_units = stage(
+        weight_came, norm_terms, qkv_own, qkv_other, feed_moving, cross_out_came, own_units
+    )
+    cross_out_firsts = add_first(cross_out_came, cross_out_own, cross_out_other)
+
     moving = shift_seq(norm_terms[seq_size // 2], -1), shift_seq(reduce_ahead(norm_terms))
     weight_firsts = add_first(weight_came, weight_own, weight_other)
     weight_firsts = [jnp.concatenate(pair) for pair in zip(weight_firsts, cross_out_firsts)]
     weight_packed = pack_second(*weight_firsts)
     weight_came = send_second(weight_packed)
-    qkv_own, qkv_other = weight_products(norms_one, [turned])
+    qkv_other = swap_core(qkv_other)
     grad_gain_self = sum(
         jnp.sum(term.astype(jnp.float32) * norm.astype(jnp.float32), axis=0)
         for term, norm in zip(norm_terms, norms_one)
@@ -868,7 +871,6 @@
     )
     gains = jnp.sum(gains, axis=0)
 
-    qkv_other = swap_core(qkv_other)
     norm_came = shift_seq(reduce_middle(moving[0], norm_terms), -1)
     own_units = own_units.reshape(3, 2, y_size, 2, half_units, width)
     unit_came = send_first(pack_first(own_units))

time: 696 us -> 692 us (level)
  Pallas kernels: 174 us -> 165 us
    pallas_call x1, Pallas kernels: 26.1 us -> 18.6 us  [self_backward(): pl.pallas_call(body, grid=(pairs,), in_specs=[pl.BlockSpec((length, group...]
    unnamed x283 -> x265, local copies, waits for them, and re-layouts: 41.4 us -> 41.4 us
  transfers between devices with their start and end apart: 64 -> 64, of which waited for: 29 -> 29; matrix products, arithmetic and copies ran while one was open for 16% -> 18% of each run, Pallas kernels for 25% -> 24%
where the time goes in v5:
time: 692 us; the launch traced here: 685 us
  waiting for transfers between devices  216 us (31%)
  Pallas kernels  165 us (24%)
  starting transfers between devices  100 us (14%)
  other arithmetic  82.2 us (12%)
  local copies, waits for them, and re-layouts  75 us (11%)
  matrix products  29.7 us (4%)
  between operations  17.1 us (2%)
    ppermute x18, waiting for transfers between devices, shift_seq(): lax.ppermute(values, 'seq', [(s, (s + step) % size) for s in range(size)])  122 us
    pallas_call x4, Pallas kernels, feed_block(): pl.pallas_call(body, grid=(steps,), in_specs=[full, full, pl.BlockSpec((t...  48.6 us
    all_to_all x8, starting transfers between devices, swap_seq(): lax.all_to_all(values, 'seq', split_axis=0, concat_axis=0, tiled=True)  46.7 us
    unnamed x265, local copies, waits for them, and re-layouts  41.4 us
    convert_element_type x15, other arithmetic, low(): return values.astype(jnp.bfloat16)  33.2 us
    all_to_all x8, waiting for transfers between devices, swap_seq(): lax.all_to_all(values, 'seq', split_axis=0, concat_axis=0, tiled=True)  33.1 us
    ppermute x20, waiting for transfers between devices, shift_dp(): lax.ppermute(values, 'dp', [(d, (d + 4 * y) % size ^ 2 * x) for d in rang...  28.6 us
    pallas_call x2, Pallas kernels, unit_products(): pl.pallas_call(body, grid=(steps,), in_specs=[pl.BlockSpec((length, tile)...  27.4 us
  transfers between devices with their start and end apart: 64, of which 29 were waited for; matrix products, arithmetic and copies ran while one was open for 18% of the time, Pallas kernels for 24%

profile of v5, /device:TPU:0, one launch (start us, length us, event | category | flops | bytes accessed | tf_op | source)
XLA Modules:
  0.0 685.2 jit_solution(1193462395774843751)
XLA Ops:
  12.5 6.3 all-to-all-start
  22.2 9.3 %all-to-all-done = bf16[4,48,1152]{2,1,0:T(8,128)(2,1)S(1)} async-done(((bf16[4,48,1152]{2,1,0:T(8,128)(2,1)}), bf16[4,48,1152]{2,1,0:T(8,128)(2,1)S(1)}, u32[]{:S(2)}, u32[]{:S(2)}) %all-to-all-start) | async-done | bytes 442400 | tf_op jit(solution)/shard_map/all_to_all | solution.py:494
  41.7 4.2 all-to-all-start.1
  51.3 24.0 %collective-permute-done.refs_1_ = bf16[256,1536]{1,0:T(8,128)(2,1)S(1)} collective-permute-done((bf16[256,1536]{1,0:T(8,128)(2,1)S(1)}, bf16[256,1536]{1,0:T(8,128)(2,1)S(1)}, u32[]{:S(2)}, u32[]{:S(2)}) %collective-permute-start) | collective-permute-done | bytes 786464 | tf_op jit(solution)/shard_map/ppermute | solution.py:468
  80.5 4.2 all-to-all-start.2
  88.6 28.0 %collective-permute-done.3.refs_2_ = bf16[256,1536]{1,0:T(8,128)(2,1)S(1)} collective-permute-done((bf16[256,1536]{1,0:T(8,128)(2,1)S(1)}, bf16[256,1536]{1,0:T(8,128)(2,1)S(1)}, u32[]{:S(2)}, u32[]{:S(2)}) %collective-permute-start.3) | collective-permute-done | bytes 786464 | tf_op jit(solution)/shard_map/ppermute | solution.py:468
  117.5 11.6 %collective-permute-done.4.refs_3_ = bf16[256,1536]{1,0:T(8,128)(2,1)S(1)} collective-permute-done((bf16[256,1536]{1,0:T(8,128)(2,1)S(1)}, bf16[256,1536]{1,0:T(8,128)(2,1)S(1)}, u32[]{:S(2)}, u32[]{:S(2)}) %collective-permute-start.4) | collective-permute-done | bytes 786464 | tf_op jit(solution)/shard_map/ppermute | solution.py:468
  131.2 6.8 all-to-all-start.3
  151.8 23.0 %shard_map.297 = (bf16[1024,1152]{1,0:T(8,128)(2,1)S(1)}, bf16[1024,384]{1,0:T(8,128)(2,1)S(1)}, f32[3,2,1024]{2,1,0:T(2,128)S(1)}, f32[3,128,1024]{2,1,0:T(8,128)S(1)}) custom-call(bf16[256,1536]{1,0:T(8,128)(2,1)S(1)} %fusion.21.refs_0_, bf16[256,1536]{1,0:T(8,128)(2,1)S(1)} %collective-permute-done.refs_1_, bf16[256,1536]{1,0:T(8,128)(2,1)S(1)} %copy-done.19, ...), custom_call_target="tpu_custom_call" | custom-call | bytes 24000000 | tf_op jit(solution)/shard_map/pallas_call | solution.py:137
  178.3 4.4 all-to-all-done.3
  186.4 4.2 all-to-all-start.4
  198.4 7.3 %shard_map.298 = (bf16[2,16,96,1536]{3,2,1,0:T(8,128)(2,1)}, bf16[1,16,96,1536]{3,2,1,0:T(8,128)(2,1)S(1)}) custom-call(bf16[3,96,1536]{2,1,0:T(8,128)(2,1)} %get-tuple-element.260.refs_0_, bf16[3,96,1536]{2,1,0:T(8,128)(2,1)} %collective-permute-done.1.refs_1_, bf16[3,96,1536]{2,1,0:T(8,128)(2,1)} %collective-permute-done.5.refs_2_, ...), custom_call_target="tpu_custom_call" | custom-call | bytes 6000000 | tf_op jit(solution)/shard_map/pallas_call | solution.py:604
  215.1 4.4 fusion.75
  221.9 4.9 convolution_convert_fusion.5.q_ref
  226.8 3.9 collective-permute-done.18.g_ref.refs_10_
  236.5 8.9 %shard_map.299.refs_0_ = bf16[256,1536]{1,0:T(8,128)(2,1)S(1)} custom-call(bf16[256,1536]{1,0:T(8,128)(2,1)S(1)} %copy-done.34, bf16[256,1536]{1,0:T(8,128)(2,1)S(1)} %fusion.4.k_ref, bf16[256,1536]{1,0:T(8,128)(2,1)S(1)} %fusion.5.v_ref, s32[1,256]{1,0:T(1,128)S(1)} %bitcast.231), custom_call_target="tpu_custom_call" | custom-call | bytes 12000000 | tf_op jit(solution)/shard_map/pallas_call | solution.py:250
  246.3 17.6 %all-gather.19.cloned.1.call-done = bf16[32,1,48,1536]{3,2,1,0:T(8,128)(2,1)} async-done(((bf16[4,1,48,1536]{3,2,1,0:T(8,128)(2,1)}), bf16[32,1,48,1536]{3,2,1,0:T(8,128)(2,1)}) %all-gather.19.cloned.1.call-update) | async-done | bytes 4718608 | tf_op jit(solution)/shard_map/all_gather | solution.py:645
  263.9 4.3 fusion.76
  270.8 11.8 %shard_map.300 = (bf16[1024,1536]{1,0:T(8,128)(2,1)S(1)}, bf16[1024,1536]{1,0:T(8,128)(2,1)S(1)}, bf16[1024,1536]{1,0:T(8,128)(2,1)S(1)}, bf16[256,1536]{1,0:T(8,128)(2,1)S(1)}, bf16[256,1536]{1,0:T(8,128)(2,1)S(1)}) custom-call(bf16[256,1536]{1,0:T(8,128)(2,1)S(1)} %multiply_convert_fusion.x_ref.refs_3_, bf16[256,1536]{1,0:T(8,128)(2,1)S(1)} %fusion.23.g_ref.refs_7_, ...), custom_call_target="tpu_custom_call" | custom-call | bytes 12000000 | tf_op jit(solution)/shard_map/pallas_call | solution.py:344
  282.7 8.2 %collective-permute-done.20.x_ref.refs_4_ = bf16[256,1536]{1,0:T(8,128)(2,1)S(1)} collective-permute-done((bf16[256,1536]{1,0:T(8,128)(2,1)S(1)}, bf16[256,1536]{1,0:T(8,128)(2,1)S(1)}, u32[]{:S(2)}, u32[]{:S(2)}) %collective-permute-start.20) | collective-permute-done | bytes 786464 | tf_op jit(solution)/shard_map/ppermute | solution.py:468
  290.8 12.1 %shard_map.301 = (bf16[1024,1536]{1,0:T(8,128)(2,1)S(1)}, bf16[1024,1536]{1,0:T(8,128)(2,1)S(1)}, bf16[1024,1536]{1,0:T(8,128)(2,1)S(1)}, bf16[256,1536]{1,0:T(8,128)(2,1)S(1)}, bf16[256,1536]{1,0:T(8,128)(2,1)S(1)}) custom-call(bf16[256,1536]{1,0:T(8,128)(2,1)S(1)} %collective-permute-done.20.x_ref.refs_4, ...), custom_call_target="tpu_custom_call", output_to_operand_aliasing={{0}: (5, {}), {1}: (6, {}), {2}: (7, {})} | custom-call | bytes 12000000 | tf_op jit(solution)/shard_map/pallas_call | solution.py:344
  303.9 7.6 %collective-permute-done.21.x_ref.refs_5_ = bf16[256,1536]{1,0:T(8,128)(2,1)S(1)} collective-permute-done((bf16[256,1536]{1,0:T(8,128)(2,1)S(1)}, bf16[256,1536]{1,0:T(8,128)(2,1)S(1)}, u32[]{:S(2)}, u32[]{:S(2)}) %collective-permute-start.21) | collective-permute-done | bytes 786464 | tf_op jit(solution)/shard_map/ppermute | solution.py:468
  311.5 12.7 %shard_map.302 = (bf16[1024,1536]{1,0:T(8,128)(2,1)S(1)}, bf16[1024,1536]{1,0:T(8,128)(2,1)S(1)}, bf16[1024,1536]{1,0:T(8,128)(2,1)S(1)}, bf16[256,1536]{1,0:T(8,128)(2,1)S(1)}, bf16[256,1536]{1,0:T(8,128)(2,1)S(1)}) custom-call(bf16[256,1536]{1,0:T(8,128)(2,1)S(1)} %collective-permute-done.21.x_ref.refs_5, ...), custom_call_target="tpu_custom_call", output_to_operand_aliasing={{0}: (5, {}), {1}: (6, {}), {2}: (7, {})} | custom-call | bytes 12000000 | tf_op jit(solution)/shard_map/pallas_call | solution.py:344
  324.3 9.5 %collective-permute-done.22.x_ref.refs_6_ = bf16[256,1536]{1,0:T(8,128)(2,1)S(1)} collective-permute-done((bf16[256,1536]{1,0:T(8,128)(2,1)S(1)}, bf16[256,1536]{1,0:T(8,128)(2,1)S(1)}, u32[]{:S(2)}, u32[]{:S(2)}) %collective-permute-start.22) | collective-permute-done | bytes 786464 | tf_op jit(solution)/shard_map/ppermute | solution.py:468
  333.8 14.3 %collective-permute-done.23 = bf16[256,1536]{1,0:T(8,128)(2,1)S(1)} collective-permute-done((bf16[256,1536]{1,0:T(8,128)(2,1)S(1)}, bf16[256,1536]{1,0:T(8,128)(2,1)S(1)}, u32[]{:S(2)}, u32[]{:S(2)}) %collective-permute-start.23) | collective-permute-done | bytes 786464 | tf_op jit(solution)/shard_map/ppermute | solution.py:468
  348.4 11.9 %shard_map.303 = (bf16[1024,1536]{1,0:T(8,128)(2,1)S(1)}, bf16[1024,1536]{1,0:T(8,128)(2,1)S(1)}, bf16[1024,1536]{1,0:T(8,128)(2,1)S(1)}, bf16[256,1536]{1,0:T(8,128)(2,1)S(1)}, bf16[256,1536]{1,0:T(8,128)(2,1)S(1)}) custom-call(bf16[256,1536]{1,0:T(8,128)(2,1)S(1)} %collective-permute-done.22.x_ref.refs_6, ...), custom_call_target="tpu_custom_call", output_to_operand_aliasing={{0}: (5, {}), {1}: (6, {}), {2}: (7, {})} | custom-call | bytes 12000000 | tf_op jit(solution)/shard_map/pallas_call | solution.py:344
  367.7 13.3 %shard_map.304 = bf16[3,768,1536]{2,1,0:T(8,128)(2,1)} custom-call(bf16[1024,1536]{1,0:T(8,128)(2,1)} %copy-done.1, bf16[1024,1536]{1,0:T(8,128)(2,1)} %copy-done.2, bf16[1024,1536]{1,0:T(8,128)(2,1)} %copy-done, bf16[256,1536]{1,0:T(8,128)(2,1)} %copy-done.6, bf16[256,1536]{1,0:T(8,128)(2,1)} %copy-done.10, bf16[256,1536]{1,0:T(8,128)(2,1)} %copy-done.11, ...), custom_call_target="tpu_custom_call" | custom-call | bytes 15000000 | tf_op jit(solution)/shard_map/pallas_call | solution.py:391
  381.1 4.6 collective-permute-done.25
  390.9 4.6 convolution_convert_fusion.4.grad_ref
  395.7 10.8 %shard_map.306 = (bf16[256,1536]{1,0:T(8,128)(2,1)S(1)}, bf16[256,1536]{1,0:T(8,128)(2,1)S(1)}, bf16[256,1536]{1,0:T(8,128)(2,1)S(1)}) custom-call(bf16[256,1536]{1,0:T(8,128)(2,1)S(1)} %copy-done.35, bf16[256,1536]{1,0:T(8,128)(2,1)S(1)} %copy-done.37, bf16[256,1536]{1,0:T(8,128)(2,1)S(1)} %copy-done.39, ...), custom_call_target="tpu_custom_call" | custom-call | bytes 12000000 | tf_op jit(solution)/shard_map/pallas_call | solution.py:250
  407.1 4.0 multiply_reduce_fusion.1
  411.2 3.9 shard_map.307
  418.0 3.9 shard_map.308
  434.9 3.7 all-to-all-start.5
  440.6 14.1 %shard_map.310 = bf16[3,768,1536]{2,1,0:T(8,128)(2,1)} custom-call(bf16[1024,1536]{1,0:T(8,128)(2,1)} %copy-done.1, bf16[1024,1536]{1,0:T(8,128)(2,1)} %copy-done.2, bf16[1024,1536]{1,0:T(8,128)(2,1)} %copy-done, bf16[256,1536]{1,0:T(8,128)(2,1)} %copy-done.6, bf16[256,1536]{1,0:T(8,128)(2,1)} %copy-done.10, bf16[256,1536]{1,0:T(8,128)(2,1)} %copy-done.11, ...), custom_call_target="tpu_custom_call" | custom-call | bytes 15000000 | tf_op jit(solution)/shard_map/pallas_call | solution.py:391
  460.3 3.8 fusion.13
  464.1 3.9 fusion.12
  476.9 18.6 %shard_map.311.refs_4_ = bf16[1024,1152]{1,0:T(8,128)(2,1)S(1)} custom-call(bf16[1024,1152]{1,0:T(8,128)(2,1)S(1)} %copy-done.41, bf16[1024,384]{1,0:T(8,128)(2,1)S(1)} %bitcast.226, f32[3,2,1024]{2,1,0:T(2,128)S(1)} %copy-done.53, f32[3,128,1024]{2,1,0:T(8,128)S(1)} %copy-done.45, f32[1024,128]{1,0:T(8,128)S(1)} %copy-done.28, f32[1024,128]{1,0:T(8,128)S(1)} %copy-done.26, ...), custom_call_target="tpu_custom_call" | custom-call | bytes 21000000 | tf_op jit(solution)/shard_map/pallas_call | solution.py:211
  495.5 4.5 convolution_convert_fusion
  500.1 7.0 %shard_map.312 = (bf16[1,2,2,2,96,1152]{5,4,3,2,1,0:T(8,128)(2,1)S(1)}, bf16[1,2,2,2,96,1152]{5,4,3,2,1,0:T(8,128)(2,1)}) custom-call(bf16[256,1536]{1,0:T(8,128)(2,1)S(1)} %fusion.21.refs_0_, bf16[256,1536]{1,0:T(8,128)(2,1)S(1)} %copy-done.14, bf16[256,1536]{1,0:T(8,128)(2,1)S(1)} %copy-done.20, bf16[256,1536]{1,0:T(8,128)(2,1)S(1)} %copy-done.17, ...), custom_call_target="tpu_custom_call" | custom-call | bytes 4500000 | tf_op jit(solution)/shard_map/pallas_call | solution.py:442
  536.9 5.0 all-to-all-start.6
  548.7 8.1 %all-to-all-done.6 = f32[32,1,144]{2,1,0:T(1,128)S(1)} async-done(((f32[32,1,144]{2,1,0:T(1,128)}), f32[32,1,144]{2,1,0:T(1,128)S(1)}, u32[]{:S(2)}, u32[]{:S(2)}) %all-to-all-start.6) | async-done | bytes 18464 | tf_op jit(solution)/shard_map/all_to_all | solution.py:868
  573.5 4.8 all-to-all-start.7
  580.5 3.8 collective-permute-start.41
  586.0 23.0 %collective-permute-done.46 = bf16[1,2,96,1152]{3,2,1,0:T(8,128)(2,1)} collective-permute-done((bf16[1,2,96,1152]{3,2,1,0:T(8,128)(2,1)}, bf16[1,2,96,1152]{3,2,1,0:T(8,128)(2,1)}, u32[]{:S(2)}, u32[]{:S(2)}) %collective-permute-start.46) | collective-permute-done | bytes 442400 | tf_op jit(solution)/shard_map/ppermute | solution.py:463
  619.4 5.3 collective-permute-done.41
  635.0 12.6 %all-to-all-start.8 = ((bf16[4,48,2688]{2,1,0:T(8,128)(2,1)}), bf16[4,48,2688]{2,1,0:T(8,128)(2,1)}, u32[]{:S(2)}, u32[]{:S(2)}) async-start(bf16[4,48,2688]{2,1,0:T(8,128)(2,1)} %pad_maximum_fusion.5), calls=%async_computation.8 | async-start | bytes 2064384 | tf_op jit(solution)/shard_map/all_to_all | solution.py:494
  660.6 11.1 %all-to-all-done.8 = bf16[4,48,2688]{2,1,0:T(8,128)(2,1)} async-done(((bf16[4,48,2688]{2,1,0:T(8,128)(2,1)}), bf16[4,48,2688]{2,1,0:T(8,128)(2,1)}, u32[]{:S(2)}, u32[]{:S(2)}) %all-to-all-start.8) | async-done | bytes 1032224 | tf_op jit(solution)/shard_map/all_to_all | solution.py:494
  (512 shorter events, 228.3 us)
Async XLA Ops:
  18.8 111.2 %all-gather.11.cloned.1.call-start = ((), (), s32[]{:S(2)}) async-start(), calls=%async_computation.9 | async-start | bytes 3981312 | tf_op jit(solution)/shard_map/all_gather | solution.py:645
  37.8 37.5 %collective-permute-start.1 = (bf16[3,96,1536]{2,1,0:T(8,128)(2,1)}, bf16[3,96,1536]{2,1,0:T(8,128)(2,1)}, u32[]{:S(2)}, u32[]{:S(2)}) collective-permute-start(bf16[3,96,1536]{2,1,0:T(8,128)(2,1)} %get-tuple-element.260.refs_0_), channel_id=1, source_target_pairs={{0,8},{4,12},{8,0},{12,4},{16,24},{20,28},{24,16},{28,20},{1,9},{5... | collective-permute-start | bytes 2654216 | tf_op jit(solution)/shard_map/ppermute | solution.py:463
  39.3 36.0 %collective-permute-start.2 = (bf16[3,96,1536]{2,1,0:T(8,128)(2,1)}, bf16[3,96,1536]{2,1,0:T(8,128)(2,1)}, u32[]{:S(2)}, u32[]{:S(2)}) collective-permute-start(bf16[3,96,1536]{2,1,0:T(8,128)(2,1)} %get-tuple-element.264.refs_4_), channel_id=1, source_target_pairs={{0,16},{4,20},{8,24},{12,28},{16,0},{20,4},{24,8},{28,12},{1,17},{... | collective-permute-start | bytes 2654216 | tf_op jit(solution)/shard_map/ppermute | solution.py:463
  41.7 35.9 %all-to-all-start.1 = ((bf16[4,48,1536]{2,1,0:T(8,128)(2,1)}), bf16[4,48,1536]{2,1,0:T(8,128)(2,1)}, u32[]{:S(2)}, u32[]{:S(2)}) async-start(bf16[4,48,1536]{2,1,0:T(8,128)(2,1)} %broadcast_in_dim.117), calls=%async_computation.1 | async-start | bytes 1179648 | tf_op jit(solution)/shard_map/all_to_all | solution.py:494
  45.8 169.3 %all-gather.13.cloned.1.call-start = ((), (), s32[]{:S(2)}) async-start(), calls=%async_computation.10 | async-start | bytes 5308416 | tf_op jit(solution)/shard_map/all_gather | solution.py:645
  45.9 29.4 %collective-permute-start = (bf16[256,1536]{1,0:T(8,128)(2,1)S(1)}, bf16[256,1536]{1,0:T(8,128)(2,1)S(1)}, u32[]{:S(2)}, u32[]{:S(2)}) collective-permute-start(bf16[256,1536]{1,0:T(8,128)(2,1)S(1)} %fusion.21.refs_0_), channel_id=1, source_target_pairs={{0,1},{1,2},{2,3},{3,0},{4,5},{5,6},{6,7},{7,4},{8,9},{9,10},{10,1... | collective-permute-start | bytes 2359304 | tf_op jit(solution)/shard_map/ppermute | solution.py:468
  77.6 52.4 %collective-permute-start.5 = (bf16[3,96,1536]{2,1,0:T(8,128)(2,1)}, bf16[3,96,1536]{2,1,0:T(8,128)(2,1)}, u32[]{:S(2)}, u32[]{:S(2)}) collective-permute-start(bf16[3,96,1536]{2,1,0:T(8,128)(2,1)} %get-tuple-element.260.refs_0_), channel_id=1, source_target_pairs={{0,16},{4,20},{8,24},{12,28},{16,0},{20,4},{24,8},{28,12},{1,17},{... | collective-permute-start | bytes 2654216 | tf_op jit(solution)/shard_map/ppermute | solution.py:463
  78.2 51.8 %collective-permute-start.6 = (bf16[3,96,1536]{2,1,0:T(8,128)(2,1)}, bf16[3,96,1536]{2,1,0:T(8,128)(2,1)}, u32[]{:S(2)}, u32[]{:S(2)}) collective-permute-start(bf16[3,96,1536]{2,1,0:T(8,128)(2,1)} %get-tuple-element.264.refs_4_), channel_id=1, source_target_pairs={{0,8},{4,12},{8,0},{12,4},{16,24},{20,28},{24,16},{28,20},{1,9},{5... | collective-permute-start | bytes 2654216 | tf_op jit(solution)/shard_map/ppermute | solution.py:463
  80.5 49.5 %all-to-all-start.2 = ((bf16[4,48,1536]{2,1,0:T(8,128)(2,1)}), bf16[4,48,1536]{2,1,0:T(8,128)(2,1)}, u32[]{:S(2)}, u32[]{:S(2)}) async-start(bf16[4,48,1536]{2,1,0:T(8,128)(2,1)} %broadcast_in_dim.118), calls=%async_computation.2 | async-start | bytes 1179648 | tf_op jit(solution)/shard_map/all_to_all | solution.py:494
  84.7 137.2 %all-gather.15.cloned.1.call-start = ((), (), s32[]{:S(2)}) async-start(), calls=%async_computation.11 | async-start | bytes 5308416 | tf_op jit(solution)/shard_map/all_gather | solution.py:645
  84.7 31.9 %collective-permute-start.3 = (bf16[256,1536]{1,0:T(8,128)(2,1)S(1)}, bf16[256,1536]{1,0:T(8,128)(2,1)S(1)}, u32[]{:S(2)}, u32[]{:S(2)}) collective-permute-start(bf16[256,1536]{1,0:T(8,128)(2,1)S(1)} %collective-permute-done.refs_1_), channel_id=1, source_target_pairs={{0,1},{1,2},{2,3},{3,0},{4,5},{5,6},{6,7},{7,4},{8,9},{9,10},{10,1... | collective-permute-start | bytes 2359304 | tf_op jit(solution)/shard_map/ppermute | solution.py:468
  86.7 42.4 %collective-permute-start.4 = (bf16[256,1536]{1,0:T(8,128)(2,1)S(1)}, bf16[256,1536]{1,0:T(8,128)(2,1)S(1)}, u32[]{:S(2)}, u32[]{:S(2)}) collective-permute-start(bf16[256,1536]{1,0:T(8,128)(2,1)S(1)} %fusion.21.refs_0_), channel_id=1, source_target_pairs={{0,3},{1,0},{2,1},{3,2},{4,7},{5,4},{6,5},{7,6},{8,11},{9,8},{10,9... | collective-permute-start | bytes 2359304 | tf_op jit(solution)/shard_map/ppermute | solution.py:468
  131.2 51.6 %all-to-all-start.3 = ((bf16[4,2,48,1536]{3,2,1,0:T(8,128)(2,1)}), bf16[4,2,48,1536]{3,2,1,0:T(8,128)(2,1)}, u32[]{:S(2)}, u32[]{:S(2)}) async-start(bf16[4,2,48,1536]{3,2,1,0:T(8,128)(2,1)} %broadcast_in_dim.119), calls=%async_computation.3 | async-start | bytes 2359296 | tf_op jit(solution)/shard_map/all_to_all | solution.py:494
  137.9 93.2 %all-gather.17.cloned.1.call-start = ((), (), s32[]{:S(2)}) async-start(), calls=%async_computation.12 | async-start | bytes 5308416 | tf_op jit(solution)/shard_map/all_gather | solution.py:645
  137.9 40.3 %collective-permute-start.7 = (bf16[3,96,1536]{2,1,0:T(8,128)(2,1)}, bf16[3,96,1536]{2,1,0:T(8,128)(2,1)}, u32[]{:S(2)}, u32[]{:S(2)}) collective-permute-start(bf16[3,96,1536]{2,1,0:T(8,128)(2,1)} %collective-permute-done.1.refs_1_), channel_id=1, source_target_pairs={{0,16},{4,20},{8,24},{12,28},{16,0},{20,4},{24,8},{28,12},{1,17},{... | collective-permute-start | bytes 2654216 | tf_op jit(solution)/shard_map/ppermute | solution.py:463
  139.4 38.8 %collective-permute-start.8 = (bf16[3,96,1536]{2,1,0:T(8,128)(2,1)}, bf16[3,96,1536]{2,1,0:T(8,128)(2,1)}, u32[]{:S(2)}, u32[]{:S(2)}) collective-permute-start(bf16[3,96,1536]{2,1,0:T(8,128)(2,1)} %collective-permute-done.2.refs_6_), channel_id=1, source_target_pairs={{0,8},{4,12},{8,0},{12,4},{16,24},{20,28},{24,16},{28,20},{1,9},{5... | collective-permute-start | bytes 2654216 | tf_op jit(solution)/shard_map/ppermute | solution.py:463
  140.9 37.3 %collective-permute-start.9 = (bf16[256,1536]{1,0:T(8,128)(2,1)S(1)}, bf16[256,1536]{1,0:T(8,128)(2,1)S(1)}, u32[]{:S(2)}, u32[]{:S(2)}) collective-permute-start(bf16[256,1536]{1,0:T(8,128)(2,1)S(1)} %fusion.23.g_ref.refs_7_), channel_id=1, source_target_pairs={{0,1},{1,2},{2,3},{3,0},{4,5},{5,6},{6,7},{7,4},{8,9},{9,10},{10,1... | collective-permute-start | bytes 2359304 | tf_op jit(solution)/shard_map/ppermute | solution.py:468
  185.1 78.7 %all-gather.19.cloned.1.call-start = ((), (), s32[]{:S(2)}) async-start(), calls=%async_computation.13 | async-start | bytes 5308416 | tf_op jit(solution)/shard_map/all_gather | solution.py:645
  186.4 25.3 %all-to-all-start.4 = ((bf16[4,256,384]{2,1,0:T(8,128)(2,1)}), bf16[4,256,384]{2,1,0:T(8,128)(2,1)}, u32[]{:S(2)}, u32[]{:S(2)}) async-start(bf16[4,256,384]{2,1,0:T(8,128)(2,1)} %bitcast.227), calls=%async_computation.4 | async-start | bytes 1572864 | tf_op jit(solution)/shard_map/all_to_all | solution.py:494
  230.7 38.6 %collective-permute-start.19 = (bf16[256,1536]{1,0:T(8,128)(2,1)S(1)}, bf16[256,1536]{1,0:T(8,128)(2,1)}, u32[]{:S(2)}, u32[]{:S(2)}) collective-permute-start(bf16[256,1536]{1,0:T(8,128)(2,1)S(1)} %collective-permute-done.9.g_ref.refs_8_), channel_id=1, source_target_pairs={{0,1},{1,2},{2,3},{3,0},{4,5},{5,6},{6,7},{7,4},{8,9},{9,10},{10,1... | collective-permute-start | bytes 2359304 | tf_op jit(solution)/shard_map/ppermute | solution.py:468
  269.3 21.5 %collective-permute-start.20 = (bf16[256,1536]{1,0:T(8,128)(2,1)S(1)}, bf16[256,1536]{1,0:T(8,128)(2,1)S(1)}, u32[]{:S(2)}, u32[]{:S(2)}) collective-permute-start(bf16[256,1536]{1,0:T(8,128)(2,1)S(1)} %multiply_convert_fusion.x_ref.refs_3_), channel_id=1, source_target_pairs={{0,1},{1,2},{2,3},{3,0},{4,5},{5,6},{6,7},{7,4},{8,9},{9,10},{10,1... | collective-permute-start | bytes 2359304 | tf_op jit(solution)/shard_map/ppermute | solution.py:468
  290.8 20.7 %collective-permute-start.21 = (bf16[256,1536]{1,0:T(8,128)(2,1)S(1)}, bf16[256,1536]{1,0:T(8,128)(2,1)S(1)}, u32[]{:S(2)}, u32[]{:S(2)}) collective-permute-start(bf16[256,1536]{1,0:T(8,128)(2,1)S(1)} %collective-permute-done.20.x_ref.refs_4_), channel_id=1, source_target_pairs={{0,1},{1,2},{2,3},{3,0},{4,5},{5,6},{6,7},{7,4},{8,9},{9,10},{10,1... | collective-permute-start | bytes 2359304 | tf_op jit(solution)/shard_map/ppermute | solution.py:468
  311.5 22.3 %collective-permute-start.22 = (bf16[256,1536]{1,0:T(8,128)(2,1)S(1)}, bf16[256,1536]{1,0:T(8,128)(2,1)S(1)}, u32[]{:S(2)}, u32[]{:S(2)}) collective-permute-start(bf16[256,1536]{1,0:T(8,128)(2,1)S(1)} %collective-permute-done.21.x_ref.refs_5_), channel_id=1, source_target_pairs={{0,1},{1,2},{2,3},{3,0},{4,5},{5,6},{6,7},{7,4},{8,9},{9,10},{10,1... | collective-permute-start | bytes 2359304 | tf_op jit(solution)/shard_map/ppermute | solution.py:468
  311.5 36.6 %collective-permute-start.23 = (bf16[256,1536]{1,0:T(8,128)(2,1)S(1)}, bf16[256,1536]{1,0:T(8,128)(2,1)S(1)}, u32[]{:S(2)}, u32[]{:S(2)}) collective-permute-start(bf16[256,1536]{1,0:T(8,128)(2,1)S(1)} %get-tuple-element.310), channel_id=1, source_target_pairs={{0,1},{1,2},{2,3},{3,0},{4,5},{5,6},{6,7},{7,4},{8,9},{9,10},{10,1... | collective-permute-start | bytes 2359304 | tf_op jit(solution)/shard_map/ppermute | solution.py:468
  385.6 49.2 %collective-permute-start.28 = (bf16[3,768,1536]{2,1,0:T(8,128)(2,1)}, bf16[3,768,1536]{2,1,0:T(8,128)(2,1)}, u32[]{:S(2)}, u32[]{:S(2)}) collective-permute-start(bf16[3,768,1536]{2,1,0:T(8,128)(2,1)} %shard_map.304), channel_id=1, source_target_pairs={{0,4},{4,0},{8,12},{12,8},{16,20},{20,16},{24,28},{28,24},{1,5},{5... | collective-permute-start | bytes 21233672 | tf_op jit(solution)/shard_map/ppermute | solution.py:458
  406.5 22.9 %collective-permute-start.27 = (bf16[1,2,2,2,96,1536]{5,4,3,2,1,0:T(8,128)(2,1)S(1)}, bf16[1,2,2,2,96,1536]{5,4,3,2,1,0:T(8,128)(2,1)}, u32[]{:S(2)}, u32[]{:S(2)}) collective-permute-start(bf16[1,2,2,2,96,1536]{5,4,3,2,1,0:T(8,128)(2,1)S(1)} %get-tuple-element.360), channel_id=1, source_target_pairs={{0,4},{4,0},{8,12},{12,8},{16,20},{20,16},{24,28},{28,24},{1,5},{5... | collective-permute-start | bytes 7077896 | tf_op jit(solution)/shard_map/ppermute | solution.py:458
  415.0 19.8 %collective-permute-start.26 = (bf16[256,1536]{1,0:T(8,128)(2,1)S(1)}, bf16[256,1536]{1,0:T(8,128)(2,1)}, u32[]{:S(2)}, u32[]{:S(2)}) collective-permute-start(bf16[256,1536]{1,0:T(8,128)(2,1)S(1)} %copy-done.56), channel_id=1, source_target_pairs={{0,3},{1,0},{2,1},{3,2},{4,7},{5,4},{6,5},{7,6},{8,11},{9,8},{10,9... | collective-permute-start | bytes 2359304 | tf_op jit(solution)/shard_map/ppermute | solution.py:468
  434.9 25.4 %collective-permute-start.31 = (bf16[3,2,2,2,96,1536]{5,4,3,2,1,0:T(8,128)(2,1)}, bf16[3,2,2,2,96,1536]{5,4,3,2,1,0:T(8,128)(2,1)}, u32[]{:S(2)}, u32[]{:S(2)}) collective-permute-start(bf16[3,2,2,2,96,1536]{5,4,3,2,1,0:T(8,128)(2,1)} %get-tuple-element.373), channel_id=1, source_target_pairs={{0,4},{4,0},{8,12},{12,8},{16,20},{20,16},{24,28},{28,24},{1,5},{5... | collective-permute-start | bytes 21233672 | tf_op jit(solution)/shard_map/ppermute | solution.py:458
  434.9 24.5 %all-to-all-start.5 = ((bf16[4,256,384]{2,1,0:T(8,128)(2,1)}), bf16[4,256,384]{2,1,0:T(8,128)(2,1)S(1)}, u32[]{:S(2)}, u32[]{:S(2)}) async-start(bf16[4,256,384]{2,1,0:T(8,128)(2,1)} %pad_maximum_fusion.7), calls=%async_computation.5 | async-start | bytes 1572864 | tf_op jit(solution)/shard_map/all_to_all | solution.py:494
  467.9 40.5 %collective-permute-start.32 = (bf16[3,2,96,1536]{3,2,0,1:T(8,128)(2,1)}, bf16[3,2,96,1536]{3,2,0,1:T(8,128)(2,1)}, u32[]{:S(2)}, u32[]{:S(2)}) collective-permute-start(bf16[3,2,96,1536]{3,2,0,1:T(8,128)(2,1)} %fusion.12), channel_id=1, source_target_pairs={{0,16},{4,20},{8,24},{12,28},{16,0},{20,4},{24,8},{28,12},{1,17},{... | collective-permute-start | bytes 5308424 | tf_op jit(solution)/shard_map/ppermute | solution.py:463
  469.1 40.0 %collective-permute-start.33 = (bf16[3,2,96,1536]{3,2,1,0:T(8,128)(2,1)}, bf16[3,2,96,1536]{3,2,1,0:T(8,128)(2,1)}, u32[]{:S(2)}, u32[]{:S(2)}) collective-permute-start(bf16[3,2,96,1536]{3,2,1,0:T(8,128)(2,1)} %fusion.13), channel_id=1, source_target_pairs={{0,8},{4,12},{8,0},{12,4},{16,24},{20,28},{24,16},{28,20},{1,9},{5... | collective-permute-start | bytes 5308424 | tf_op jit(solution)/shard_map/ppermute | solution.py:463
  470.2 38.3 %collective-permute-start.34 = (bf16[256,1536]{1,0:T(8,128)(2,1)}, bf16[256,1536]{1,0:T(8,128)(2,1)S(1)}, u32[]{:S(2)}, u32[]{:S(2)}) collective-permute-start(bf16[256,1536]{1,0:T(8,128)(2,1)} %add_convert_fusion.4), channel_id=1, source_target_pairs={{0,3},{1,0},{2,1},{3,2},{4,7},{5,4},{6,5},{7,6},{8,11},{9,8},{10,9... | collective-permute-start | bytes 2359304 | tf_op jit(solution)/shard_map/ppermute | solution.py:468
  471.7 36.8 %collective-permute-start.35 = (bf16[256,1536]{1,0:T(8,128)(2,1)}, bf16[256,1536]{1,0:T(8,128)(2,1)S(1)}, u32[]{:S(2)}, u32[]{:S(2)}) collective-permute-start(bf16[256,1536]{1,0:T(8,128)(2,1)} %copy-done.54), channel_id=1, source_target_pairs={{0,1},{1,2},{2,3},{3,0},{4,5},{5,6},{6,7},{7,4},{8,9},{9,10},{10,1... | collective-permute-start | bytes 2359304 | tf_op jit(solution)/shard_map/ppermute | solution.py:468
  511.4 46.7 %collective-permute-start.36 = (bf16[256,1536]{1,0:T(8,128)(2,1)}, bf16[256,1536]{1,0:T(8,128)(2,1)}, u32[]{:S(2)}, u32[]{:S(2)}) collective-permute-start(bf16[256,1536]{1,0:T(8,128)(2,1)} %get-tuple-element.397), channel_id=1, source_target_pairs={{0,3},{1,0},{2,1},{3,2},{4,7},{5,4},{6,5},{7,6},{8,11},{9,8},{10,9... | collective-permute-start | bytes 2359304 | tf_op jit(solution)/shard_map/ppermute | solution.py:468
  516.1 43.1 %collective-permute-start.37 = (bf16[256,1536]{1,0:T(8,128)(2,1)}, bf16[256,1536]{1,0:T(8,128)(2,1)}, u32[]{:S(2)}, u32[]{:S(2)}) collective-permute-start(bf16[256,1536]{1,0:T(8,128)(2,1)} %get-tuple-element.398), channel_id=1, source_target_pairs={{0,1},{1,2},{2,3},{3,0},{4,5},{5,6},{6,7},{7,4},{8,9},{9,10},{10,1... | collective-permute-start | bytes 2359304 | tf_op jit(solution)/shard_map/ppermute | solution.py:468
  522.6 37.6 %collective-permute-start.39 = (bf16[4,96,1536]{2,1,0:T(8,128)(2,1)}, bf16[4,96,1536]{2,1,0:T(8,128)(2,1)}, u32[]{:S(2)}, u32[]{:S(2)}) collective-permute-start(bf16[4,96,1536]{2,1,0:T(8,128)(2,1)} %fusion.26), channel_id=1, source_target_pairs={{0,16},{4,20},{8,24},{12,28},{16,0},{20,4},{24,8},{28,12},{1,17},{... | collective-permute-start | bytes 3538952 | tf_op jit(solution)/shard_map/ppermute | solution.py:463
  529.8 30.4 %collective-permute-start.38 = (bf16[4,96,1536]{2,1,0:T(8,128)(2,1)}, bf16[4,96,1536]{2,1,0:T(8,128)(2,1)}, u32[]{:S(2)}, u32[]{:S(2)}) collective-permute-start(bf16[4,96,1536]{2,1,0:T(8,128)(2,1)} %fusion.28), channel_id=1, source_target_pairs={{0,8},{4,12},{8,0},{12,4},{16,24},{20,28},{24,16},{28,20},{1,9},{5... | collective-permute-start | bytes 3538952 | tf_op jit(solution)/shard_map/ppermute | solution.py:463
  531.1 29.1 %collective-permute-start.40 = (bf16[1,2,2,2,96,1152]{5,4,3,2,1,0:T(8,128)(2,1)}, bf16[1,2,2,2,96,1152]{5,4,3,2,1,0:T(8,128)(2,1)}, u32[]{:S(2)}, u32[]{:S(2)}) collective-permute-start(bf16[1,2,2,2,96,1152]{5,4,3,2,1,0:T(8,128)(2,1)} %get-tuple-element.404), channel_id=1, source_target_pairs={{0,4},{4,0},{8,12},{12,8},{16,20},{20,16},{24,28},{28,24},{1,5},{5... | collective-permute-start | bytes 5308424 | tf_op jit(solution)/shard_map/ppermute | solution.py:458
  536.9 19.9 %all-to-all-start.6 = ((f32[32,1,144]{2,1,0:T(1,128)}), f32[32,1,144]{2,1,0:T(1,128)S(1)}, u32[]{:S(2)}, u32[]{:S(2)}) async-start(f32[32,1,144]{2,1,0:T(1,128)} %reshape.796), calls=%async_computation.6 | async-start | bytes 65536 | tf_op jit(solution)/shard_map/all_to_all | solution.py:868
  558.1 61.3 %collective-permute-start.42 = (bf16[3,2,96,1536]{3,2,0,1:T(8,128)(2,1)}, bf16[3,2,96,1536]{3,2,0,1:T(8,128)(2,1)}, u32[]{:S(2)}, u32[]{:S(2)}) collective-permute-start(bf16[3,2,96,1536]{3,2,0,1:T(8,128)(2,1)} %bitcast.254), channel_id=1, source_target_pairs={{0,16},{4,20},{8,24},{12,28},{16,0},{20,4},{24,8},{28,12},{1,17},{... | collective-permute-start | bytes 5308424 | tf_op jit(solution)/shard_map/ppermute | solution.py:463
  559.2 60.2 %collective-permute-start.43 = (bf16[3,2,96,1536]{3,2,0,1:T(8,128)(2,1)}, bf16[3,2,96,1536]{3,2,0,1:T(8,128)(2,1)}, u32[]{:S(2)}, u32[]{:S(2)}) collective-permute-start(bf16[3,2,96,1536]{3,2,0,1:T(8,128)(2,1)} %bitcast.253), channel_id=1, source_target_pairs={{0,8},{4,12},{8,0},{12,4},{16,24},{20,28},{24,16},{28,20},{1,9},{5... | collective-permute-start | bytes 5308424 | tf_op jit(solution)/shard_map/ppermute | solution.py:463
  569.8 39.2 %collective-permute-start.46 = (bf16[1,2,96,1152]{3,2,1,0:T(8,128)(2,1)}, bf16[1,2,96,1152]{3,2,1,0:T(8,128)(2,1)}, u32[]{:S(2)}, u32[]{:S(2)}) collective-permute-start(bf16[1,2,96,1152]{3,2,1,0:T(8,128)(2,1)} %fusion.47), channel_id=1, source_target_pairs={{0,8},{4,12},{8,0},{12,4},{16,24},{20,28},{24,16},{28,20},{1,9},{5... | collective-permute-start | bytes 1327112 | tf_op jit(solution)/shard_map/ppermute | solution.py:463
  570.9 38.2 %collective-permute-start.44 = (bf16[1,2,96,1152]{3,2,1,0:T(8,128)(2,1)}, bf16[1,2,96,1152]{3,2,1,0:T(8,128)(2,1)}, u32[]{:S(2)}, u32[]{:S(2)}) collective-permute-start(bf16[1,2,96,1152]{3,2,1,0:T(8,128)(2,1)} %fusion.46), channel_id=1, source_target_pairs={{0,16},{4,20},{8,24},{12,28},{16,0},{20,4},{24,8},{28,12},{1,17},{... | collective-permute-start | bytes 1327112 | tf_op jit(solution)/shard_map/ppermute | solution.py:463
  573.5 51.3 %all-to-all-start.7 = ((bf16[4,3,48,1536]{3,2,1,0:T(8,128)(2,1)}), bf16[4,3,48,1536]{3,2,1,0:T(8,128)(2,1)}, u32[]{:S(2)}, u32[]{:S(2)}) async-start(bf16[4,3,48,1536]{3,2,1,0:T(8,128)(2,1)} %pad_maximum_fusion.1), calls=%async_computation.7 | async-start | bytes 3538944 | tf_op jit(solution)/shard_map/all_to_all | solution.py:494
  580.5 44.3 %collective-permute-start.41 = (bf16[256,1536]{1,0:T(8,128)(2,1)}, bf16[256,1536]{1,0:T(8,128)(2,1)S(1)}, u32[]{:S(2)}, u32[]{:S(2)}) collective-permute-start(bf16[256,1536]{1,0:T(8,128)(2,1)} %fusion.18), channel_id=1, source_target_pairs={{0,3},{1,0},{2,1},{3,2},{4,7},{5,4},{6,5},{7,6},{8,11},{9,8},{10,9... | collective-permute-start | bytes 2359304 | tf_op jit(solution)/shard_map/ppermute | solution.py:468
  628.6 27.0 %collective-permute-start.48 = (bf16[3,96,1536]{2,1,0:T(8,128)(2,1)}, bf16[3,96,1536]{2,1,0:T(8,128)(2,1)}, u32[]{:S(2)}, u32[]{:S(2)}) collective-permute-start(bf16[3,96,1536]{2,1,0:T(8,128)(2,1)} %slice_bitcast_fusion.2), channel_id=1, source_target_pairs={{0,8},{4,12},{8,0},{12,4},{16,24},{20,28},{24,16},{28,20},{1,9},{5... | collective-permute-start | bytes 2654216 | tf_op jit(solution)/shard_map/ppermute | solution.py:463
  634.0 23.1 %collective-permute-start.49 = (bf16[3,96,1536]{2,1,0:T(8,128)(2,1)}, bf16[3,96,1536]{2,1,0:T(8,128)(2,1)}, u32[]{:S(2)}, u32[]{:S(2)}) collective-permute-start(bf16[3,96,1536]{2,1,0:T(8,128)(2,1)} %slice_bitcast_fusion), channel_id=1, source_target_pairs={{0,16},{4,20},{8,24},{12,28},{16,0},{20,4},{24,8},{28,12},{1,17},{... | collective-permute-start | bytes 2654216 | tf_op jit(solution)/shard_map/ppermute | solution.py:463
  635.0 36.6 %all-to-all-start.8 = ((bf16[4,48,2688]{2,1,0:T(8,128)(2,1)}), bf16[4,48,2688]{2,1,0:T(8,128)(2,1)}, u32[]{:S(2)}, u32[]{:S(2)}) async-start(bf16[4,48,2688]{2,1,0:T(8,128)(2,1)} %pad_maximum_fusion.5), calls=%async_computation.8 | async-start | bytes 2064384 | tf_op jit(solution)/shard_map/all_to_all | solution.py:494
  (147 other events, 1461.3 us)
Sparse Core Ops, SparseCore 0:
  32.5 43.2 all-gather.10
  77.7 42.0 all-gather.12
  130.2 49.4 all-gather.14
  185.2 37.8 all-gather.16
  224.9 38.9 all-gather.18

commit v6 on v5

--- a/solution.py
+++ b/solution.py
@@ -233,57 +233,68 @@
 CROSS_HEADS = 8
 
 
-def cross_softmax(queries, key_rows, item_row):
-    scale = HDIM ** (-0.5) * LOG2E
+def cross_scores(queries, key_rows, item_row):
     scores = dot(key_rows, queries, 1, 1)
     count = key_rows.shape[0]
     key_item = (lax.broadcasted_iota(jnp.int32, (count, 1), 0) >= count // 2).astype(jnp.int32)
-    scores = jnp.where(key_item == item_row, scores, NEG_FILL)
-    raised = jnp.exp2((scores - jnp.max(scores, axis=0, keepdims=True)) * scale)
-    return raised / jnp.sum(raised, axis=0, keepdims=True)
-
-
-def cross_call(body, arrays, item_row, out_rows, flops):
-    width = arrays[0].shape[1]
-    lanes = CROSS_HEADS * HDIM
-    blocks = [pl.BlockSpec((a.shape[0], lanes), lambda p: (0, p)) for a in arrays]
-    return pl.pallas_call(
-        body,
-        grid=(width // lanes,),
-        in_specs=blocks + [pl.BlockSpec(item_row.shape, lambda p: (0, 0))],
-        out_specs=[pl.BlockSpec((rows, lanes), lambda p: (0, p)) for rows in out_rows],
-        out_shape=[jax.ShapeDtypeStruct((rows, width), jnp.bfloat16) for rows in out_rows],
-        compiler_params=pltpu.CompilerParams(vmem_limit_bytes=32 << 20),
-        cost_estimate=taking(4),
-    )(*arrays, item_row)
+    return jnp.where(key_item == item_row, scores, NEG_FILL)
 
 
 def cross_forward(queries, key_rows, value_rows, item_row):
-    def body(q_ref, k_ref, v_ref, item_ref, mixed_ref):
+    scale = HDIM ** (-0.5) * LOG2E
+
+    def body(q_ref, k_ref, v_ref, item_ref, mixed_ref, total_ref, exact_ref):
         mixed = []
         for head in range(CROSS_HEADS):
             cols = slice(head * HDIM, (head + 1) * HDIM)
-            chance = cross_softmax(q_ref[:, cols], k_ref[:, cols], item_ref[...])
-            mixed.append(dot(v_ref[:, cols], chance.astype(jnp.bfloat16), 0, 0))
-        mixed_ref[...] = jnp.concatenate(mixed).T.astype(jnp.bfloat16)
-
-    return cross_call(
-        body, (queries, key_rows, value_rows), item_row, [queries.shape[0]], 4
-    )[0]
-
-
-def cross_backward(queries, key_rows, value_rows, grad_mixed, item_row):
+            scores = cross_scores(q_ref[:, cols], k_ref[:, cols], item_ref[...])
+            highest = jnp.max(scores, axis=0, keepdims=True)
+            raised = jnp.exp2((scores - highest) * scale)
+            total = jnp.sum(raised, axis=0, keepdims=True)
+            mixed.append(dot(v_ref[:, cols], raised.astype(jnp.bfloat16), 0, 0) / total)
+            total_ref[0, head : head + 1, :] = highest * scale + jnp.log2(total)
+        mixed = jnp.concatenate(mixed)
+        exact_ref[...] = mixed
+        mixed_ref[...] = mixed.T.astype(jnp.bfloat16)
+
+    (rows, width), keys = queries.shape, key_rows.shape[0]
+    lanes = CROSS_HEADS * HDIM
+    steps = width // lanes
+    return pl.pallas_call(
+        body,
+        grid=(steps,),
+        in_specs=[pl.BlockSpec((n, lanes), lambda p: (0, p)) for n in (rows, keys, keys)]
+        + [pl.BlockSpec(item_row.shape, lambda p: (0, 0))],
+        out_specs=[
+            pl.BlockSpec((rows, lanes), lambda p: (0, p)),
+            pl.BlockSpec((1, CROSS_HEADS, rows), lambda p: (p, 0, 0)),
+            pl.BlockSpec((lanes, rows), lambda p: (p, 0)),
+        ],
+        out_shape=[
+            jax.ShapeDtypeStruct((rows, width), jnp.bfloat16),
+            jax.ShapeDtypeStruct((steps, CROSS_HEADS, rows), jnp.float32),
+            jax.ShapeDtypeStruct((width, rows), jnp.float32),
+        ],
+        compiler_params=pltpu.CompilerParams(vmem_limit_bytes=32 << 20),
+        cost_estimate=taking(4),
+    )(queries, key_rows, value_rows, item_row)
+
+
+def cross_backward(queries, key_rows, value_rows, grad_mixed, item_row, log_total, exact):
     scaling = HDIM ** (-0.5)
-
-    def body(q_ref, k_ref, v_ref, grad_ref, item_ref, dq_ref, dk_ref, dv_ref):
+    scale = scaling * LOG2E
+
+    def body(q_ref, k_ref, v_ref, grad_ref, item_ref, total_ref, exact_ref, dq_ref, dk_ref, dv_ref):
         grad_queries = []
+        inner = grad_ref[...].astype(jnp.float32).T * exact_ref[...]
         for head in range(CROSS_HEADS):
             cols = slice(head * HDIM, (head + 1) * HDIM)
             query_head, key_head, grad_head = q_ref[:, cols], k_ref[:, cols], grad_ref[:, cols]
-            chance = cross_softmax(query_head, key_head, item_ref[...])
+            scores = cross_scores(query_head, key_head, item_ref[...])
+            chance = jnp.exp2(scores * scale - total_ref[0, head : head + 1, :])
             grad_chance = dot(v_ref[:, cols], grad_head, 1, 1)
-            inner = jnp.sum(chance * grad_chance, axis=0, keepdims=True)
-            grad_scores = (chance * (grad_chance - inner)).astype(jnp.bfloat16)
+            head_inner = jnp.sum(inner[cols, :], axis=0, keepdims=True)
+            grad_scores = (chance * (grad_chance - head_inner)).astype(jnp.bfloat16)
             grad_queries.append(dot(key_head, grad_scores, 0, 0))
             dk_ref[:, cols] = (dot(grad_scores, query_head, 1, 0) * scaling).astype(jnp.bfloat16)
             dv_ref[:, cols] = dot(chance.astype(jnp.bfloat16), grad_head, 1, 0).astype(
@@ -291,10 +302,23 @@
             )
         dq_ref[...] = (jnp.concatenate(grad_queries).T * scaling).astype(jnp.bfloat16)
 
-    rows, keys = queries.shape[0], key_rows.shape[0]
-    return cross_call(
-        body, (queries, key_rows, value_rows, grad_mixed), item_row, [rows, keys, keys], 10
-    )
+    (rows, width), keys = queries.shape, key_rows.shape[0]
+    lanes = CROSS_HEADS * HDIM
+    sizes = (rows, keys, keys)
+    return pl.pallas_call(
+        body,
+        grid=(width // lanes,),
+        in_specs=[pl.BlockSpec((n, lanes), lambda p: (0, p)) for n in sizes + (rows,)]
+        + [
+            pl.BlockSpec(item_row.shape, lambda p: (0, 0)),
+            pl.BlockSpec((1, CROSS_HEADS, rows), lambda p: (p, 0, 0)),
+            pl.BlockSpec((lanes, rows), lambda p: (p, 0)),
+        ],
+        out_specs=[pl.BlockSpec((n, lanes), lambda p: (0, p)) for n in sizes],
+        out_shape=[jax.ShapeDtypeStruct((n, width), jnp.bfloat16) for n in sizes],
+        compiler_params=pltpu.CompilerParams(vmem_limit_bytes=32 << 20),
+        cost_estimate=taking(4),
+    )(queries, key_rows, value_rows, grad_mixed, item_row, log_total, exact)
 
 
 def feed_block(normed, grads, gate_up, down, number, count, held):
@@ -764,7 +788,9 @@
     memory_keys = matmul(memory, full_cross_key).astype(jnp.bfloat16)
     memory_values = matmul(memory, full_cross_value).astype(jnp.bfloat16)
     item_row = (row_segment == 1).astype(jnp.int32)[None, :]
-    cross_mixed = cross_forward(cross_queries, memory_keys, memory_values, item_row)
+    cross_mixed, cross_total, cross_exact = cross_forward(
+        cross_queries, memory_keys, memory_values, item_row
+    )
     second_sum = first_sum + matmul(cross_mixed, full_cross_out)
     norm_three, norm_three_back = jax.vjp(layer_norm, second_sum, gain_feed.astype(jnp.float32))
     norm_three = norm_three.astype(jnp.bfloat16)
@@ -809,7 +835,13 @@
     cross_out_own, cross_out_other = weight_products([cross_mixed], [second_low])
     cross_out_other = swap_core(cross_out_other)
     grad_cross_queries, grad_memory_keys, grad_memory_values = cross_backward(
-        cross_queries, memory_keys, memory_values, grad_mixed, item_row
+        cross_queries,
+        memory_keys,
+        memory_values,
+        grad_mixed,
+        item_row,
+        cross_total,
+        cross_exact,
     )
     grad_norm_two = contract_cols(grad_cross_queries, full_cross_query)
     grad_first, grad_gain_cross = norm_two_back(grad_norm_two)

time: 692 us -> 687 us (level)
    unnamed x265 -> x299, local copies, waits for them, and re-layouts: 41.4 us -> 43.7 us
where the time goes in v6:
time: 687 us; the launch traced here: 680 us
  waiting for transfers between devices  213 us (31%)
  Pallas kernels  161 us (23%)
  starting transfers between devices  99.9 us (15%)
  other arithmetic  82.5 us (12%)
  local copies, waits for them, and re-layouts  77.3 us (11%)
  matrix products  27.8 us (4%)
  between operations  17.4 us (3%)
    ppermute x18, waiting for transfers between devices, shift_seq(): lax.ppermute(values, 'seq', [(s, (s + step) % size) for s in range(size)])  121 us
    pallas_call x4, Pallas kernels, feed_block(): pl.pallas_call(body, grid=(steps,), in_specs=[full, full, pl.BlockSpec((t...  48.4 us
    all_to_all x8, starting transfers between devices, swap_seq(): lax.all_to_all(values, 'seq', split_axis=0, concat_axis=0, tiled=True)  46.6 us
    unnamed x299, local copies, waits for them, and re-layouts  43.7 us
    convert_element_type x15, other arithmetic, low(): return values.astype(jnp.bfloat16)  33.6 us
    all_to_all x8, waiting for transfers between devices, swap_seq(): lax.all_to_all(values, 'seq', split_axis=0, concat_axis=0, tiled=True)  33 us
    ppermute x20, waiting for transfers between devices, shift_dp(): lax.ppermute(values, 'dp', [(d, (d + 4 * y) % size ^ 2 * x) for d in rang...  28.5 us
    pallas_call x2, Pallas kernels, unit_products(): pl.pallas_call(body, grid=(steps,), in_specs=[pl.BlockSpec((length, tile)...  27.4 us
  transfers between devices with their start and end apart: 64, of which 29 were waited for; matrix products, arithmetic and copies ran while one was open for 18% of the time, Pallas kernels for 24%

profile of v6, /device:TPU:0, one launch (start us, length us, event | category | flops | bytes accessed | tf_op | source)
XLA Modules:
  0.0 679.8 jit_solution(6014815250097478757)
XLA Ops:
  12.5 6.3 all-to-all-start
  22.3 9.3 %all-to-all-done = bf16[4,48,1152]{2,1,0:T(8,128)(2,1)S(1)} async-done(((bf16[4,48,1152]{2,1,0:T(8,128)(2,1)}), bf16[4,48,1152]{2,1,0:T(8,128)(2,1)S(1)}, u32[]{:S(2)}, u32[]{:S(2)}) %all-to-all-start) | async-done | bytes 442400 | tf_op jit(solution)/shard_map/all_to_all | solution.py:518
  41.7 4.1 all-to-all-start.1
  51.3 24.0 %collective-permute-done.refs_1_ = bf16[256,1536]{1,0:T(8,128)(2,1)S(1)} collective-permute-done((bf16[256,1536]{1,0:T(8,128)(2,1)S(1)}, bf16[256,1536]{1,0:T(8,128)(2,1)S(1)}, u32[]{:S(2)}, u32[]{:S(2)}) %collective-permute-start) | collective-permute-done | bytes 786464 | tf_op jit(solution)/shard_map/ppermute | solution.py:492
  87.9 28.1 %collective-permute-done.3.refs_2_ = bf16[256,1536]{1,0:T(8,128)(2,1)S(1)} collective-permute-done((bf16[256,1536]{1,0:T(8,128)(2,1)S(1)}, bf16[256,1536]{1,0:T(8,128)(2,1)S(1)}, u32[]{:S(2)}, u32[]{:S(2)}) %collective-permute-start.3) | collective-permute-done | bytes 786464 | tf_op jit(solution)/shard_map/ppermute | solution.py:492
  116.9 11.6 %collective-permute-done.4.refs_3_ = bf16[256,1536]{1,0:T(8,128)(2,1)S(1)} collective-permute-done((bf16[256,1536]{1,0:T(8,128)(2,1)S(1)}, bf16[256,1536]{1,0:T(8,128)(2,1)S(1)}, u32[]{:S(2)}, u32[]{:S(2)}) %collective-permute-start.4) | collective-permute-done | bytes 786464 | tf_op jit(solution)/shard_map/ppermute | solution.py:492
  131.3 6.8 all-to-all-start.3
  151.9 23.0 %shard_map.297 = (bf16[1024,1152]{1,0:T(8,128)(2,1)S(1)}, bf16[1024,384]{1,0:T(8,128)(2,1)S(1)}, f32[3,2,1024]{2,1,0:T(2,128)S(1)}, f32[3,128,1024]{2,1,0:T(8,128)S(1)}) custom-call(bf16[256,1536]{1,0:T(8,128)(2,1)S(1)} %fusion.21.refs_0_, bf16[256,1536]{1,0:T(8,128)(2,1)S(1)} %collective-permute-done.refs_1_, bf16[256,1536]{1,0:T(8,128)(2,1)S(1)} %copy-done.19, ...), custom_call_target="tpu_custom_call" | custom-call | bytes 24000000 | tf_op jit(solution)/shard_map/pallas_call | solution.py:137
  178.4 4.4 all-to-all-done.3
  186.5 4.2 all-to-all-start.4
  198.5 7.3 %shard_map.298 = (bf16[2,16,96,1536]{3,2,1,0:T(8,128)(2,1)}, bf16[1,16,96,1536]{3,2,1,0:T(8,128)(2,1)S(1)}) custom-call(bf16[3,96,1536]{2,1,0:T(8,128)(2,1)} %get-tuple-element.263.refs_0_, bf16[3,96,1536]{2,1,0:T(8,128)(2,1)} %collective-permute-done.1.refs_1_, bf16[3,96,1536]{2,1,0:T(8,128)(2,1)} %collective-permute-done.5.refs_2_, ...), custom_call_target="tpu_custom_call" | custom-call | bytes 6000000 | tf_op jit(solution)/shard_map/pallas_call | solution.py:628
  208.2 3.6 all-to-all-done.4
  215.3 4.4 fusion.75
  222.0 4.9 convolution_convert_fusion.5.q_ref
  226.9 4.0 collective-permute-done.18.g_ref.refs_10_
  236.5 7.9 %shard_map.299 = (bf16[256,1536]{1,0:T(8,128)(2,1)S(1)}, f32[3,8,256]{2,1,0:T(8,128)S(1)}, f32[1536,256]{1,0:T(8,128)S(1)}) custom-call(bf16[256,1536]{1,0:T(8,128)(2,1)S(1)} %copy-done.34, bf16[256,1536]{1,0:T(8,128)(2,1)S(1)} %fusion.4.k_ref, bf16[256,1536]{1,0:T(8,128)(2,1)S(1)} %fusion.5.v_ref, s32[1,256]{1,0:T(1,128)S(1)} %bitcast.231), custom_call_target="tpu_custom_call" | custom-call | bytes 12000000 | tf_op jit(solution)/shard_map/pallas_call | solution.py:263
  248.0 16.0 %all-gather.19.cloned.1.call-done = bf16[32,1,48,1536]{3,2,1,0:T(8,128)(2,1)} async-done(((bf16[4,1,48,1536]{3,2,1,0:T(8,128)(2,1)}), bf16[32,1,48,1536]{3,2,1,0:T(8,128)(2,1)}) %all-gather.19.cloned.1.call-update) | async-done | bytes 4718608 | tf_op jit(solution)/shard_map/all_gather | solution.py:669
  264.0 4.5 fusion.76
  271.2 11.8 %shard_map.300 = (bf16[1024,1536]{1,0:T(8,128)(2,1)S(1)}, bf16[1024,1536]{1,0:T(8,128)(2,1)S(1)}, bf16[1024,1536]{1,0:T(8,128)(2,1)S(1)}, bf16[256,1536]{1,0:T(8,128)(2,1)S(1)}, bf16[256,1536]{1,0:T(8,128)(2,1)S(1)}) custom-call(bf16[256,1536]{1,0:T(8,128)(2,1)S(1)} %multiply_convert_fusion.x_ref.refs_3_, bf16[256,1536]{1,0:T(8,128)(2,1)S(1)} %fusion.23.g_ref.refs_7_, ...), custom_call_target="tpu_custom_call" | custom-call | bytes 12000000 | tf_op jit(solution)/shard_map/pallas_call | solution.py:368
  283.1 8.1 %collective-permute-done.20.x_ref.refs_4_ = bf16[256,1536]{1,0:T(8,128)(2,1)S(1)} collective-permute-done((bf16[256,1536]{1,0:T(8,128)(2,1)S(1)}, bf16[256,1536]{1,0:T(8,128)(2,1)S(1)}, u32[]{:S(2)}, u32[]{:S(2)}) %collective-permute-start.20) | collective-permute-done | bytes 786464 | tf_op jit(solution)/shard_map/ppermute | solution.py:492
  291.3 12.1 %shard_map.301 = (bf16[1024,1536]{1,0:T(8,128)(2,1)S(1)}, bf16[1024,1536]{1,0:T(8,128)(2,1)S(1)}, bf16[1024,1536]{1,0:T(8,128)(2,1)S(1)}, bf16[256,1536]{1,0:T(8,128)(2,1)S(1)}, bf16[256,1536]{1,0:T(8,128)(2,1)S(1)}) custom-call(bf16[256,1536]{1,0:T(8,128)(2,1)S(1)} %collective-permute-done.20.x_ref.refs_4, ...), custom_call_target="tpu_custom_call", output_to_operand_aliasing={{0}: (5, {}), {1}: (6, {}), {2}: (7, {})} | custom-call | bytes 12000000 | tf_op jit(solution)/shard_map/pallas_call | solution.py:368
  304.4 7.6 %collective-permute-done.21.x_ref.refs_5_ = bf16[256,1536]{1,0:T(8,128)(2,1)S(1)} collective-permute-done((bf16[256,1536]{1,0:T(8,128)(2,1)S(1)}, bf16[256,1536]{1,0:T(8,128)(2,1)S(1)}, u32[]{:S(2)}, u32[]{:S(2)}) %collective-permute-start.21) | collective-permute-done | bytes 786464 | tf_op jit(solution)/shard_map/ppermute | solution.py:492
  312.4 12.6 %shard_map.302 = (bf16[1024,1536]{1,0:T(8,128)(2,1)S(1)}, bf16[1024,1536]{1,0:T(8,128)(2,1)S(1)}, bf16[1024,1536]{1,0:T(8,128)(2,1)S(1)}, bf16[256,1536]{1,0:T(8,128)(2,1)S(1)}, bf16[256,1536]{1,0:T(8,128)(2,1)S(1)}) custom-call(bf16[256,1536]{1,0:T(8,128)(2,1)S(1)} %collective-permute-done.21.x_ref.refs_5, ...), custom_call_target="tpu_custom_call", output_to_operand_aliasing={{0}: (5, {}), {1}: (6, {}), {2}: (7, {})} | custom-call | bytes 12000000 | tf_op jit(solution)/shard_map/pallas_call | solution.py:368
  325.0 9.2 %collective-permute-done.22.x_ref.refs_6_ = bf16[256,1536]{1,0:T(8,128)(2,1)S(1)} collective-permute-done((bf16[256,1536]{1,0:T(8,128)(2,1)S(1)}, bf16[256,1536]{1,0:T(8,128)(2,1)S(1)}, u32[]{:S(2)}, u32[]{:S(2)}) %collective-permute-start.22) | collective-permute-done | bytes 786464 | tf_op jit(solution)/shard_map/ppermute | solution.py:492
  334.2 14.3 %collective-permute-done.23 = bf16[256,1536]{1,0:T(8,128)(2,1)S(1)} collective-permute-done((bf16[256,1536]{1,0:T(8,128)(2,1)S(1)}, bf16[256,1536]{1,0:T(8,128)(2,1)S(1)}, u32[]{:S(2)}, u32[]{:S(2)}) %collective-permute-start.23) | collective-permute-done | bytes 786464 | tf_op jit(solution)/shard_map/ppermute | solution.py:492
  348.9 11.8 %shard_map.303 = (bf16[1024,1536]{1,0:T(8,128)(2,1)S(1)}, bf16[1024,1536]{1,0:T(8,128)(2,1)S(1)}, bf16[1024,1536]{1,0:T(8,128)(2,1)S(1)}, bf16[256,1536]{1,0:T(8,128)(2,1)S(1)}, bf16[256,1536]{1,0:T(8,128)(2,1)S(1)}) custom-call(bf16[256,1536]{1,0:T(8,128)(2,1)S(1)} %collective-permute-done.22.x_ref.refs_6, ...), custom_call_target="tpu_custom_call", output_to_operand_aliasing={{0}: (5, {}), {1}: (6, {}), {2}: (7, {})} | custom-call | bytes 12000000 | tf_op jit(solution)/shard_map/pallas_call | solution.py:368
  368.2 13.3 %shard_map.304 = bf16[3,768,1536]{2,1,0:T(8,128)(2,1)} custom-call(bf16[1024,1536]{1,0:T(8,128)(2,1)} %copy-done.1, bf16[1024,1536]{1,0:T(8,128)(2,1)} %copy-done.2, bf16[1024,1536]{1,0:T(8,128)(2,1)} %copy-done, bf16[256,1536]{1,0:T(8,128)(2,1)} %copy-done.6, bf16[256,1536]{1,0:T(8,128)(2,1)} %copy-done.10, bf16[256,1536]{1,0:T(8,128)(2,1)} %copy-done.11, ...), custom_call_target="tpu_custom_call" | custom-call | bytes 15000000 | tf_op jit(solution)/shard_map/pallas_call | solution.py:415
  381.5 4.5 collective-permute-done.25
  392.8 4.9 convolution_convert_fusion.4.grad_ref
  397.8 7.9 %shard_map.306 = (bf16[256,1536]{1,0:T(8,128)(2,1)S(1)}, bf16[256,1536]{1,0:T(8,128)(2,1)S(1)}, bf16[256,1536]{1,0:T(8,128)(2,1)S(1)}) custom-call(bf16[256,1536]{1,0:T(8,128)(2,1)S(1)} %copy-done.34, bf16[256,1536]{1,0:T(8,128)(2,1)S(1)} %copy-done.36, bf16[256,1536]{1,0:T(8,128)(2,1)S(1)} %copy-done.38, ...), custom_call_target="tpu_custom_call" | custom-call | bytes 12000000 | tf_op jit(solution)/shard_map/pallas_call | solution.py:308
  407.5 3.9 shard_map.307
  414.5 3.9 shard_map.308
  418.4 3.5 shard_map.309
  431.0 3.7 all-to-all-start.5
  436.7 14.1 %shard_map.310 = bf16[3,768,1536]{2,1,0:T(8,128)(2,1)} custom-call(bf16[1024,1536]{1,0:T(8,128)(2,1)} %copy-done.1, bf16[1024,1536]{1,0:T(8,128)(2,1)} %copy-done.2, bf16[1024,1536]{1,0:T(8,128)(2,1)} %copy-done, bf16[256,1536]{1,0:T(8,128)(2,1)} %copy-done.6, bf16[256,1536]{1,0:T(8,128)(2,1)} %copy-done.10, bf16[256,1536]{1,0:T(8,128)(2,1)} %copy-done.11, ...), custom_call_target="tpu_custom_call" | custom-call | bytes 15000000 | tf_op jit(solution)/shard_map/pallas_call | solution.py:415
  456.4 3.8 fusion.13
  460.2 3.9 fusion.12
  472.9 18.6 %shard_map.311.refs_4_ = bf16[1024,1152]{1,0:T(8,128)(2,1)S(1)} custom-call(bf16[1024,1152]{1,0:T(8,128)(2,1)S(1)} %copy-done.40, bf16[1024,384]{1,0:T(8,128)(2,1)S(1)} %bitcast.226, f32[3,2,1024]{2,1,0:T(2,128)S(1)} %copy-done.56, f32[3,128,1024]{2,1,0:T(8,128)S(1)} %copy-done.44, f32[1024,128]{1,0:T(8,128)S(1)} %copy-done.28, f32[1024,128]{1,0:T(8,128)S(1)} %copy-done.26, ...), custom_call_target="tpu_custom_call" | custom-call | bytes 21000000 | tf_op jit(solution)/shard_map/pallas_call | solution.py:211
  491.6 4.5 convolution_convert_fusion
  496.2 7.0 %shard_map.312 = (bf16[1,2,2,2,96,1152]{5,4,3,2,1,0:T(8,128)(2,1)S(1)}, bf16[1,2,2,2,96,1152]{5,4,3,2,1,0:T(8,128)(2,1)}) custom-call(bf16[256,1536]{1,0:T(8,128)(2,1)S(1)} %fusion.21.refs_0_, bf16[256,1536]{1,0:T(8,128)(2,1)S(1)} %copy-done.14, bf16[256,1536]{1,0:T(8,128)(2,1)S(1)} %copy-done.20, bf16[256,1536]{1,0:T(8,128)(2,1)S(1)} %copy-done.17, ...), custom_call_target="tpu_custom_call" | custom-call | bytes 4500000 | tf_op jit(solution)/shard_map/pallas_call | solution.py:466
  532.8 5.0 all-to-all-start.6
  544.6 8.2 %all-to-all-done.6 = f32[32,1,144]{2,1,0:T(1,128)S(1)} async-done(((f32[32,1,144]{2,1,0:T(1,128)}), f32[32,1,144]{2,1,0:T(1,128)S(1)}, u32[]{:S(2)}, u32[]{:S(2)}) %all-to-all-start.6) | async-done | bytes 18464 | tf_op jit(solution)/shard_map/all_to_all | solution.py:900
  569.5 4.8 all-to-all-start.7
  576.5 3.8 collective-permute-start.41
  582.0 23.0 %collective-permute-done.46 = bf16[1,2,96,1152]{3,2,1,0:T(8,128)(2,1)} collective-permute-done((bf16[1,2,96,1152]{3,2,1,0:T(8,128)(2,1)}, bf16[1,2,96,1152]{3,2,1,0:T(8,128)(2,1)}, u32[]{:S(2)}, u32[]{:S(2)}) %collective-permute-start.46) | collective-permute-done | bytes 442400 | tf_op jit(solution)/shard_map/ppermute | solution.py:487
  615.5 5.3 collective-permute-done.41
  629.4 13.1 %all-to-all-start.8 = ((bf16[4,48,2688]{2,1,0:T(8,128)(2,1)}), bf16[4,48,2688]{2,1,0:T(8,128)(2,1)}, u32[]{:S(2)}, u32[]{:S(2)}) async-start(bf16[4,48,2688]{2,1,0:T(8,128)(2,1)} %pad_maximum_fusion.5), calls=%async_computation.8 | async-start | bytes 2064384 | tf_op jit(solution)/shard_map/all_to_all | solution.py:518
  655.4 10.9 %all-to-all-done.8 = bf16[4,48,2688]{2,1,0:T(8,128)(2,1)} async-done(((bf16[4,48,2688]{2,1,0:T(8,128)(2,1)}), bf16[4,48,2688]{2,1,0:T(8,128)(2,1)}, u32[]{:S(2)}, u32[]{:S(2)}) %all-to-all-start.8) | async-done | bytes 1032224 | tf_op jit(solution)/shard_map/all_to_all | solution.py:518
  (547 shorter events, 228.6 us)
Async XLA Ops:
  18.8 110.5 %all-gather.11.cloned.1.call-start = ((), (), s32[]{:S(2)}) async-start(), calls=%async_computation.9 | async-start | bytes 3981312 | tf_op jit(solution)/shard_map/all_gather | solution.py:669
  37.8 37.5 %collective-permute-start.1 = (bf16[3,96,1536]{2,1,0:T(8,128)(2,1)}, bf16[3,96,1536]{2,1,0:T(8,128)(2,1)}, u32[]{:S(2)}, u32[]{:S(2)}) collective-permute-start(bf16[3,96,1536]{2,1,0:T(8,128)(2,1)} %get-tuple-element.263.refs_0_), channel_id=1, source_target_pairs={{0,8},{4,12},{8,0},{12,4},{16,24},{20,28},{24,16},{28,20},{1,9},{5... | collective-permute-start | bytes 2654216 | tf_op jit(solution)/shard_map/ppermute | solution.py:487
  39.3 36.0 %collective-permute-start.2 = (bf16[3,96,1536]{2,1,0:T(8,128)(2,1)}, bf16[3,96,1536]{2,1,0:T(8,128)(2,1)}, u32[]{:S(2)}, u32[]{:S(2)}) collective-permute-start(bf16[3,96,1536]{2,1,0:T(8,128)(2,1)} %get-tuple-element.267.refs_4_), channel_id=1, source_target_pairs={{0,16},{4,20},{8,24},{12,28},{16,0},{20,4},{24,8},{28,12},{1,17},{... | collective-permute-start | bytes 2654216 | tf_op jit(solution)/shard_map/ppermute | solution.py:487
  41.7 35.9 %all-to-all-start.1 = ((bf16[4,48,1536]{2,1,0:T(8,128)(2,1)}), bf16[4,48,1536]{2,1,0:T(8,128)(2,1)}, u32[]{:S(2)}, u32[]{:S(2)}) async-start(bf16[4,48,1536]{2,1,0:T(8,128)(2,1)} %broadcast_in_dim.117), calls=%async_computation.1 | async-start | bytes 1179648 | tf_op jit(solution)/shard_map/all_to_all | solution.py:518
  45.8 169.4 %all-gather.13.cloned.1.call-start = ((), (), s32[]{:S(2)}) async-start(), calls=%async_computation.10 | async-start | bytes 5308416 | tf_op jit(solution)/shard_map/all_gather | solution.py:669
  45.9 29.4 %collective-permute-start = (bf16[256,1536]{1,0:T(8,128)(2,1)S(1)}, bf16[256,1536]{1,0:T(8,128)(2,1)S(1)}, u32[]{:S(2)}, u32[]{:S(2)}) collective-permute-start(bf16[256,1536]{1,0:T(8,128)(2,1)S(1)} %fusion.21.refs_0_), channel_id=1, source_target_pairs={{0,1},{1,2},{2,3},{3,0},{4,5},{5,6},{6,7},{7,4},{8,9},{9,10},{10,1... | collective-permute-start | bytes 2359304 | tf_op jit(solution)/shard_map/ppermute | solution.py:492
  77.6 51.7 %collective-permute-start.5 = (bf16[3,96,1536]{2,1,0:T(8,128)(2,1)}, bf16[3,96,1536]{2,1,0:T(8,128)(2,1)}, u32[]{:S(2)}, u32[]{:S(2)}) collective-permute-start(bf16[3,96,1536]{2,1,0:T(8,128)(2,1)} %get-tuple-element.263.refs_0_), channel_id=1, source_target_pairs={{0,16},{4,20},{8,24},{12,28},{16,0},{20,4},{24,8},{28,12},{1,17},{... | collective-permute-start | bytes 2654216 | tf_op jit(solution)/shard_map/ppermute | solution.py:487
  78.2 51.1 %collective-permute-start.6 = (bf16[3,96,1536]{2,1,0:T(8,128)(2,1)}, bf16[3,96,1536]{2,1,0:T(8,128)(2,1)}, u32[]{:S(2)}, u32[]{:S(2)}) collective-permute-start(bf16[3,96,1536]{2,1,0:T(8,128)(2,1)} %get-tuple-element.267.refs_4_), channel_id=1, source_target_pairs={{0,8},{4,12},{8,0},{12,4},{16,24},{20,28},{24,16},{28,20},{1,9},{5... | collective-permute-start | bytes 2654216 | tf_op jit(solution)/shard_map/ppermute | solution.py:487
  80.5 48.8 %all-to-all-start.2 = ((bf16[4,48,1536]{2,1,0:T(8,128)(2,1)}), bf16[4,48,1536]{2,1,0:T(8,128)(2,1)S(1)}, u32[]{:S(2)}, u32[]{:S(2)}) async-start(bf16[4,48,1536]{2,1,0:T(8,128)(2,1)} %broadcast_in_dim.118), calls=%async_computation.2 | async-start | bytes 1179648 | tf_op jit(solution)/shard_map/all_to_all | solution.py:518
  84.0 138.0 %all-gather.15.cloned.1.call-start = ((), (), s32[]{:S(2)}) async-start(), calls=%async_computation.11 | async-start | bytes 5308416 | tf_op jit(solution)/shard_map/all_gather | solution.py:669
  84.1 31.9 %collective-permute-start.3 = (bf16[256,1536]{1,0:T(8,128)(2,1)S(1)}, bf16[256,1536]{1,0:T(8,128)(2,1)S(1)}, u32[]{:S(2)}, u32[]{:S(2)}) collective-permute-start(bf16[256,1536]{1,0:T(8,128)(2,1)S(1)} %collective-permute-done.refs_1_), channel_id=1, source_target_pairs={{0,1},{1,2},{2,3},{3,0},{4,5},{5,6},{6,7},{7,4},{8,9},{9,10},{10,1... | collective-permute-start | bytes 2359304 | tf_op jit(solution)/shard_map/ppermute | solution.py:492
  86.0 42.4 %collective-permute-start.4 = (bf16[256,1536]{1,0:T(8,128)(2,1)S(1)}, bf16[256,1536]{1,0:T(8,128)(2,1)S(1)}, u32[]{:S(2)}, u32[]{:S(2)}) collective-permute-start(bf16[256,1536]{1,0:T(8,128)(2,1)S(1)} %fusion.21.refs_0_), channel_id=1, source_target_pairs={{0,3},{1,0},{2,1},{3,2},{4,7},{5,4},{6,5},{7,6},{8,11},{9,8},{10,9... | collective-permute-start | bytes 2359304 | tf_op jit(solution)/shard_map/ppermute | solution.py:492
  131.3 51.5 %all-to-all-start.3 = ((bf16[4,2,48,1536]{3,2,1,0:T(8,128)(2,1)}), bf16[4,2,48,1536]{3,2,1,0:T(8,128)(2,1)}, u32[]{:S(2)}, u32[]{:S(2)}) async-start(bf16[4,2,48,1536]{3,2,1,0:T(8,128)(2,1)} %broadcast_in_dim.119), calls=%async_computation.3 | async-start | bytes 2359296 | tf_op jit(solution)/shard_map/all_to_all | solution.py:518
  138.1 93.0 %all-gather.17.cloned.1.call-start = ((), (), s32[]{:S(2)}) async-start(), calls=%async_computation.12 | async-start | bytes 5308416 | tf_op jit(solution)/shard_map/all_gather | solution.py:669
  138.1 40.3 %collective-permute-start.7 = (bf16[3,96,1536]{2,1,0:T(8,128)(2,1)}, bf16[3,96,1536]{2,1,0:T(8,128)(2,1)}, u32[]{:S(2)}, u32[]{:S(2)}) collective-permute-start(bf16[3,96,1536]{2,1,0:T(8,128)(2,1)} %collective-permute-done.1.refs_1_), channel_id=1, source_target_pairs={{0,16},{4,20},{8,24},{12,28},{16,0},{20,4},{24,8},{28,12},{1,17},{... | collective-permute-start | bytes 2654216 | tf_op jit(solution)/shard_map/ppermute | solution.py:487
  139.6 38.8 %collective-permute-start.8 = (bf16[3,96,1536]{2,1,0:T(8,128)(2,1)}, bf16[3,96,1536]{2,1,0:T(8,128)(2,1)}, u32[]{:S(2)}, u32[]{:S(2)}) collective-permute-start(bf16[3,96,1536]{2,1,0:T(8,128)(2,1)} %collective-permute-done.2.refs_6_), channel_id=1, source_target_pairs={{0,8},{4,12},{8,0},{12,4},{16,24},{20,28},{24,16},{28,20},{1,9},{5... | collective-permute-start | bytes 2654216 | tf_op jit(solution)/shard_map/ppermute | solution.py:487
  141.1 37.3 %collective-permute-start.9 = (bf16[256,1536]{1,0:T(8,128)(2,1)S(1)}, bf16[256,1536]{1,0:T(8,128)(2,1)S(1)}, u32[]{:S(2)}, u32[]{:S(2)}) collective-permute-start(bf16[256,1536]{1,0:T(8,128)(2,1)S(1)} %fusion.23.g_ref.refs_7_), channel_id=1, source_target_pairs={{0,1},{1,2},{2,3},{3,0},{4,5},{5,6},{6,7},{7,4},{8,9},{9,10},{10,1... | collective-permute-start | bytes 2359304 | tf_op jit(solution)/shard_map/ppermute | solution.py:492
  185.2 78.8 %all-gather.19.cloned.1.call-start = ((), (), s32[]{:S(2)}) async-start(), calls=%async_computation.13 | async-start | bytes 5308416 | tf_op jit(solution)/shard_map/all_gather | solution.py:669
  186.5 25.3 %all-to-all-start.4 = ((bf16[4,256,384]{2,1,0:T(8,128)(2,1)}), bf16[4,256,384]{2,1,0:T(8,128)(2,1)}, u32[]{:S(2)}, u32[]{:S(2)}) async-start(bf16[4,256,384]{2,1,0:T(8,128)(2,1)} %bitcast.227), calls=%async_computation.4 | async-start | bytes 1572864 | tf_op jit(solution)/shard_map/all_to_all | solution.py:518
  230.9 38.8 %collective-permute-start.19 = (bf16[256,1536]{1,0:T(8,128)(2,1)S(1)}, bf16[256,1536]{1,0:T(8,128)(2,1)}, u32[]{:S(2)}, u32[]{:S(2)}) collective-permute-start(bf16[256,1536]{1,0:T(8,128)(2,1)S(1)} %collective-permute-done.9.g_ref.refs_8_), channel_id=1, source_target_pairs={{0,1},{1,2},{2,3},{3,0},{4,5},{5,6},{6,7},{7,4},{8,9},{9,10},{10,1... | collective-permute-start | bytes 2359304 | tf_op jit(solution)/shard_map/ppermute | solution.py:492
  269.7 21.6 %collective-permute-start.20 = (bf16[256,1536]{1,0:T(8,128)(2,1)S(1)}, bf16[256,1536]{1,0:T(8,128)(2,1)S(1)}, u32[]{:S(2)}, u32[]{:S(2)}) collective-permute-start(bf16[256,1536]{1,0:T(8,128)(2,1)S(1)} %multiply_convert_fusion.x_ref.refs_3_), channel_id=1, source_target_pairs={{0,1},{1,2},{2,3},{3,0},{4,5},{5,6},{6,7},{7,4},{8,9},{9,10},{10,1... | collective-permute-start | bytes 2359304 | tf_op jit(solution)/shard_map/ppermute | solution.py:492
  291.3 20.7 %collective-permute-start.21 = (bf16[256,1536]{1,0:T(8,128)(2,1)S(1)}, bf16[256,1536]{1,0:T(8,128)(2,1)S(1)}, u32[]{:S(2)}, u32[]{:S(2)}) collective-permute-start(bf16[256,1536]{1,0:T(8,128)(2,1)S(1)} %collective-permute-done.20.x_ref.refs_4_), channel_id=1, source_target_pairs={{0,1},{1,2},{2,3},{3,0},{4,5},{5,6},{6,7},{7,4},{8,9},{9,10},{10,1... | collective-permute-start | bytes 2359304 | tf_op jit(solution)/shard_map/ppermute | solution.py:492
  312.0 22.3 %collective-permute-start.22 = (bf16[256,1536]{1,0:T(8,128)(2,1)S(1)}, bf16[256,1536]{1,0:T(8,128)(2,1)S(1)}, u32[]{:S(2)}, u32[]{:S(2)}) collective-permute-start(bf16[256,1536]{1,0:T(8,128)(2,1)S(1)} %collective-permute-done.21.x_ref.refs_5_), channel_id=1, source_target_pairs={{0,1},{1,2},{2,3},{3,0},{4,5},{5,6},{6,7},{7,4},{8,9},{9,10},{10,1... | collective-permute-start | bytes 2359304 | tf_op jit(solution)/shard_map/ppermute | solution.py:492
  312.0 36.6 %collective-permute-start.23 = (bf16[256,1536]{1,0:T(8,128)(2,1)S(1)}, bf16[256,1536]{1,0:T(8,128)(2,1)S(1)}, u32[]{:S(2)}, u32[]{:S(2)}) collective-permute-start(bf16[256,1536]{1,0:T(8,128)(2,1)S(1)} %get-tuple-element.314), channel_id=1, source_target_pairs={{0,1},{1,2},{2,3},{3,0},{4,5},{5,6},{6,7},{7,4},{8,9},{9,10},{10,1... | collective-permute-start | bytes 2359304 | tf_op jit(solution)/shard_map/ppermute | solution.py:492
  386.1 44.9 %collective-permute-start.28 = (bf16[3,768,1536]{2,1,0:T(8,128)(2,1)}, bf16[3,768,1536]{2,1,0:T(8,128)(2,1)}, u32[]{:S(2)}, u32[]{:S(2)}) collective-permute-start(bf16[3,768,1536]{2,1,0:T(8,128)(2,1)} %shard_map.304), channel_id=1, source_target_pairs={{0,4},{4,0},{8,12},{12,8},{16,20},{20,16},{24,28},{28,24},{1,5},{5... | collective-permute-start | bytes 21233672 | tf_op jit(solution)/shard_map/ppermute | solution.py:482
  392.2 33.6 %collective-permute-start.27 = (bf16[1,2,2,2,96,1536]{5,4,3,2,1,0:T(8,128)(2,1)S(1)}, bf16[1,2,2,2,96,1536]{5,4,3,2,1,0:T(8,128)(2,1)}, u32[]{:S(2)}, u32[]{:S(2)}) collective-permute-start(bf16[1,2,2,2,96,1536]{5,4,3,2,1,0:T(8,128)(2,1)S(1)} %get-tuple-element.364), channel_id=1, source_target_pairs={{0,4},{4,0},{8,12},{12,8},{16,20},{20,16},{24,28},{28,24},{1,5},{5... | collective-permute-start | bytes 7077896 | tf_op jit(solution)/shard_map/ppermute | solution.py:482
  411.4 19.5 %collective-permute-start.26 = (bf16[256,1536]{1,0:T(8,128)(2,1)S(1)}, bf16[256,1536]{1,0:T(8,128)(2,1)}, u32[]{:S(2)}, u32[]{:S(2)}) collective-permute-start(bf16[256,1536]{1,0:T(8,128)(2,1)S(1)} %copy-done.61), channel_id=1, source_target_pairs={{0,3},{1,0},{2,1},{3,2},{4,7},{5,4},{6,5},{7,6},{8,11},{9,8},{10,9... | collective-permute-start | bytes 2359304 | tf_op jit(solution)/shard_map/ppermute | solution.py:492
  431.0 25.4 %collective-permute-start.31 = (bf16[3,2,2,2,96,1536]{5,4,3,2,1,0:T(8,128)(2,1)}, bf16[3,2,2,2,96,1536]{5,4,3,2,1,0:T(8,128)(2,1)}, u32[]{:S(2)}, u32[]{:S(2)}) collective-permute-start(bf16[3,2,2,2,96,1536]{5,4,3,2,1,0:T(8,128)(2,1)} %get-tuple-element.379), channel_id=1, source_target_pairs={{0,4},{4,0},{8,12},{12,8},{16,20},{20,16},{24,28},{28,24},{1,5},{5... | collective-permute-start | bytes 21233672 | tf_op jit(solution)/shard_map/ppermute | solution.py:482
  431.0 24.5 %all-to-all-start.5 = ((bf16[4,256,384]{2,1,0:T(8,128)(2,1)}), bf16[4,256,384]{2,1,0:T(8,128)(2,1)S(1)}, u32[]{:S(2)}, u32[]{:S(2)}) async-start(bf16[4,256,384]{2,1,0:T(8,128)(2,1)} %pad_maximum_fusion.7), calls=%async_computation.5 | async-start | bytes 1572864 | tf_op jit(solution)/shard_map/all_to_all | solution.py:518
  464.0 40.6 %collective-permute-start.32 = (bf16[3,2,96,1536]{3,2,0,1:T(8,128)(2,1)}, bf16[3,2,96,1536]{3,2,0,1:T(8,128)(2,1)}, u32[]{:S(2)}, u32[]{:S(2)}) collective-permute-start(bf16[3,2,96,1536]{3,2,0,1:T(8,128)(2,1)} %fusion.12), channel_id=1, source_target_pairs={{0,16},{4,20},{8,24},{12,28},{16,0},{20,4},{24,8},{28,12},{1,17},{... | collective-permute-start | bytes 5308424 | tf_op jit(solution)/shard_map/ppermute | solution.py:487
  465.2 40.0 %collective-permute-start.33 = (bf16[3,2,96,1536]{3,2,1,0:T(8,128)(2,1)}, bf16[3,2,96,1536]{3,2,1,0:T(8,128)(2,1)}, u32[]{:S(2)}, u32[]{:S(2)}) collective-permute-start(bf16[3,2,96,1536]{3,2,1,0:T(8,128)(2,1)} %fusion.13), channel_id=1, source_target_pairs={{0,8},{4,12},{8,0},{12,4},{16,24},{20,28},{24,16},{28,20},{1,9},{5... | collective-permute-start | bytes 5308424 | tf_op jit(solution)/shard_map/ppermute | solution.py:487
  466.2 38.3 %collective-permute-start.34 = (bf16[256,1536]{1,0:T(8,128)(2,1)}, bf16[256,1536]{1,0:T(8,128)(2,1)S(1)}, u32[]{:S(2)}, u32[]{:S(2)}) collective-permute-start(bf16[256,1536]{1,0:T(8,128)(2,1)} %add_convert_fusion.4), channel_id=1, source_target_pairs={{0,3},{1,0},{2,1},{3,2},{4,7},{5,4},{6,5},{7,6},{8,11},{9,8},{10,9... | collective-permute-start | bytes 2359304 | tf_op jit(solution)/shard_map/ppermute | solution.py:492
  467.8 36.8 %collective-permute-start.35 = (bf16[256,1536]{1,0:T(8,128)(2,1)}, bf16[256,1536]{1,0:T(8,128)(2,1)S(1)}, u32[]{:S(2)}, u32[]{:S(2)}) collective-permute-start(bf16[256,1536]{1,0:T(8,128)(2,1)} %copy-done.59), channel_id=1, source_target_pairs={{0,1},{1,2},{2,3},{3,0},{4,5},{5,6},{6,7},{7,4},{8,9},{9,10},{10,1... | collective-permute-start | bytes 2359304 | tf_op jit(solution)/shard_map/ppermute | solution.py:492
  507.5 46.6 %collective-permute-start.36 = (bf16[256,1536]{1,0:T(8,128)(2,1)}, bf16[256,1536]{1,0:T(8,128)(2,1)}, u32[]{:S(2)}, u32[]{:S(2)}) collective-permute-start(bf16[256,1536]{1,0:T(8,128)(2,1)} %get-tuple-element.403), channel_id=1, source_target_pairs={{0,3},{1,0},{2,1},{3,2},{4,7},{5,4},{6,5},{7,6},{8,11},{9,8},{10,9... | collective-permute-start | bytes 2359304 | tf_op jit(solution)/shard_map/ppermute | solution.py:492
  512.3 42.9 %collective-permute-start.37 = (bf16[256,1536]{1,0:T(8,128)(2,1)}, bf16[256,1536]{1,0:T(8,128)(2,1)}, u32[]{:S(2)}, u32[]{:S(2)}) collective-permute-start(bf16[256,1536]{1,0:T(8,128)(2,1)} %get-tuple-element.404), channel_id=1, source_target_pairs={{0,1},{1,2},{2,3},{3,0},{4,5},{5,6},{6,7},{7,4},{8,9},{9,10},{10,1... | collective-permute-start | bytes 2359304 | tf_op jit(solution)/shard_map/ppermute | solution.py:492
  518.8 37.5 %collective-permute-start.39 = (bf16[4,96,1536]{2,1,0:T(8,128)(2,1)}, bf16[4,96,1536]{2,1,0:T(8,128)(2,1)}, u32[]{:S(2)}, u32[]{:S(2)}) collective-permute-start(bf16[4,96,1536]{2,1,0:T(8,128)(2,1)} %fusion.26), channel_id=1, source_target_pairs={{0,16},{4,20},{8,24},{12,28},{16,0},{20,4},{24,8},{28,12},{1,17},{... | collective-permute-start | bytes 3538952 | tf_op jit(solution)/shard_map/ppermute | solution.py:487
  526.1 30.1 %collective-permute-start.38 = (bf16[4,96,1536]{2,1,0:T(8,128)(2,1)}, bf16[4,96,1536]{2,1,0:T(8,128)(2,1)}, u32[]{:S(2)}, u32[]{:S(2)}) collective-permute-start(bf16[4,96,1536]{2,1,0:T(8,128)(2,1)} %fusion.28), channel_id=1, source_target_pairs={{0,8},{4,12},{8,0},{12,4},{16,24},{20,28},{24,16},{28,20},{1,9},{5... | collective-permute-start | bytes 3538952 | tf_op jit(solution)/shard_map/ppermute | solution.py:487
  527.1 29.2 %collective-permute-start.40 = (bf16[1,2,2,2,96,1152]{5,4,3,2,1,0:T(8,128)(2,1)}, bf16[1,2,2,2,96,1152]{5,4,3,2,1,0:T(8,128)(2,1)}, u32[]{:S(2)}, u32[]{:S(2)}) collective-permute-start(bf16[1,2,2,2,96,1152]{5,4,3,2,1,0:T(8,128)(2,1)} %get-tuple-element.410), channel_id=1, source_target_pairs={{0,4},{4,0},{8,12},{12,8},{16,20},{20,16},{24,28},{28,24},{1,5},{5... | collective-permute-start | bytes 5308424 | tf_op jit(solution)/shard_map/ppermute | solution.py:482
  532.8 20.0 %all-to-all-start.6 = ((f32[32,1,144]{2,1,0:T(1,128)}), f32[32,1,144]{2,1,0:T(1,128)S(1)}, u32[]{:S(2)}, u32[]{:S(2)}) async-start(f32[32,1,144]{2,1,0:T(1,128)} %reshape.796), calls=%async_computation.6 | async-start | bytes 65536 | tf_op jit(solution)/shard_map/all_to_all | solution.py:900
  554.1 61.3 %collective-permute-start.42 = (bf16[3,2,96,1536]{3,2,0,1:T(8,128)(2,1)}, bf16[3,2,96,1536]{3,2,0,1:T(8,128)(2,1)}, u32[]{:S(2)}, u32[]{:S(2)}) collective-permute-start(bf16[3,2,96,1536]{3,2,0,1:T(8,128)(2,1)} %bitcast.254), channel_id=1, source_target_pairs={{0,16},{4,20},{8,24},{12,28},{16,0},{20,4},{24,8},{28,12},{1,17},{... | collective-permute-start | bytes 5308424 | tf_op jit(solution)/shard_map/ppermute | solution.py:487
  555.2 60.3 %collective-permute-start.43 = (bf16[3,2,96,1536]{3,2,0,1:T(8,128)(2,1)}, bf16[3,2,96,1536]{3,2,0,1:T(8,128)(2,1)}, u32[]{:S(2)}, u32[]{:S(2)}) collective-permute-start(bf16[3,2,96,1536]{3,2,0,1:T(8,128)(2,1)} %bitcast.253), channel_id=1, source_target_pairs={{0,8},{4,12},{8,0},{12,4},{16,24},{20,28},{24,16},{28,20},{1,9},{5... | collective-permute-start | bytes 5308424 | tf_op jit(solution)/shard_map/ppermute | solution.py:487
  565.9 39.1 %collective-permute-start.46 = (bf16[1,2,96,1152]{3,2,1,0:T(8,128)(2,1)}, bf16[1,2,96,1152]{3,2,1,0:T(8,128)(2,1)}, u32[]{:S(2)}, u32[]{:S(2)}) collective-permute-start(bf16[1,2,96,1152]{3,2,1,0:T(8,128)(2,1)} %fusion.47), channel_id=1, source_target_pairs={{0,8},{4,12},{8,0},{12,4},{16,24},{20,28},{24,16},{28,20},{1,9},{5... | collective-permute-start | bytes 1327112 | tf_op jit(solution)/shard_map/ppermute | solution.py:487
  566.8 38.2 %collective-permute-start.44 = (bf16[1,2,96,1152]{3,2,1,0:T(8,128)(2,1)}, bf16[1,2,96,1152]{3,2,1,0:T(8,128)(2,1)}, u32[]{:S(2)}, u32[]{:S(2)}) collective-permute-start(bf16[1,2,96,1152]{3,2,1,0:T(8,128)(2,1)} %fusion.46), channel_id=1, source_target_pairs={{0,16},{4,20},{8,24},{12,28},{16,0},{20,4},{24,8},{28,12},{1,17},{... | collective-permute-start | bytes 1327112 | tf_op jit(solution)/shard_map/ppermute | solution.py:487
  569.5 51.3 %all-to-all-start.7 = ((bf16[4,3,48,1536]{3,2,1,0:T(8,128)(2,1)}), bf16[4,3,48,1536]{3,2,1,0:T(8,128)(2,1)}, u32[]{:S(2)}, u32[]{:S(2)}) async-start(bf16[4,3,48,1536]{3,2,1,0:T(8,128)(2,1)} %pad_maximum_fusion.1), calls=%async_computation.7 | async-start | bytes 3538944 | tf_op jit(solution)/shard_map/all_to_all | solution.py:518
  576.5 44.3 %collective-permute-start.41 = (bf16[256,1536]{1,0:T(8,128)(2,1)}, bf16[256,1536]{1,0:T(8,128)(2,1)S(1)}, u32[]{:S(2)}, u32[]{:S(2)}) collective-permute-start(bf16[256,1536]{1,0:T(8,128)(2,1)} %fusion.18), channel_id=1, source_target_pairs={{0,3},{1,0},{2,1},{3,2},{4,7},{5,4},{6,5},{7,6},{8,11},{9,8},{10,9... | collective-permute-start | bytes 2359304 | tf_op jit(solution)/shard_map/ppermute | solution.py:492
  624.0 26.6 %collective-permute-start.48 = (bf16[3,96,1536]{2,1,0:T(8,128)(2,1)}, bf16[3,96,1536]{2,1,0:T(8,128)(2,1)}, u32[]{:S(2)}, u32[]{:S(2)}) collective-permute-start(bf16[3,96,1536]{2,1,0:T(8,128)(2,1)} %slice_bitcast_fusion.2), channel_id=1, source_target_pairs={{0,8},{4,12},{8,0},{12,4},{16,24},{20,28},{24,16},{28,20},{1,9},{5... | collective-permute-start | bytes 2654216 | tf_op jit(solution)/shard_map/ppermute | solution.py:487
  628.5 23.6 %collective-permute-start.49 = (bf16[3,96,1536]{2,1,0:T(8,128)(2,1)}, bf16[3,96,1536]{2,1,0:T(8,128)(2,1)}, u32[]{:S(2)}, u32[]{:S(2)}) collective-permute-start(bf16[3,96,1536]{2,1,0:T(8,128)(2,1)} %slice_bitcast_fusion), channel_id=1, source_target_pairs={{0,16},{4,20},{8,24},{12,28},{16,0},{20,4},{24,8},{28,12},{1,17},{... | collective-permute-start | bytes 2654216 | tf_op jit(solution)/shard_map/ppermute | solution.py:487
  629.4 36.9 %all-to-all-start.8 = ((bf16[4,48,2688]{2,1,0:T(8,128)(2,1)}), bf16[4,48,2688]{2,1,0:T(8,128)(2,1)}, u32[]{:S(2)}, u32[]{:S(2)}) async-start(bf16[4,48,2688]{2,1,0:T(8,128)(2,1)} %pad_maximum_fusion.5), calls=%async_computation.8 | async-start | bytes 2064384 | tf_op jit(solution)/shard_map/all_to_all | solution.py:518
  (164 other events, 1567.4 us)
Sparse Core Ops, SparseCore 0:
  32.5 43.2 all-gather.10
  77.7 42.0 all-gather.12
  130.3 49.4 all-gather.14
  185.3 37.9 all-gather.16
  225.0 38.9 all-gather.18

commit v7 on v6

--- a/solution.py
+++ b/solution.py
@@ -230,7 +230,7 @@
     )(qkv, grad_out, log_total, exact, *tables, *segments)
 
 
-CROSS_HEADS = 8
+CROSS_HEADS = 12
 
 
 def cross_scores(queries, key_rows, item_row):

time: 687 us -> 687 us (level)
  no operation moved by 1% of the time
where the time goes in v7:
time: 687 us; the launch traced here: 679 us
  waiting for transfers between devices  213 us (31%)
  Pallas kernels  161 us (23%)
  starting transfers between devices  99.8 us (15%)
  other arithmetic  82.6 us (12%)
  local copies, waits for them, and re-layouts  77.3 us (11%)
  matrix products  27.8 us (4%)
  between operations  17.4 us (3%)
    ppermute x18, waiting for transfers between devices, shift_seq(): lax.ppermute(values, 'seq', [(s, (s + step) % size) for s in range(size)])  122 us
    pallas_call x4, Pallas kernels, feed_block(): pl.pallas_call(body, grid=(steps,), in_specs=[full, full, pl.BlockSpec((t...  48.4 us
    all_to_all x8, starting transfers between devices, swap_seq(): lax.all_to_all(values, 'seq', split_axis=0, concat_axis=0, tiled=True)  46.6 us
    unnamed x299, local copies, waits for them, and re-layouts  43.7 us
    convert_element_type x15, other arithmetic, low(): return values.astype(jnp.bfloat16)  33.6 us
    all_to_all x8, waiting for transfers between devices, swap_seq(): lax.all_to_all(values, 'seq', split_axis=0, concat_axis=0, tiled=True)  32.9 us
    ppermute x20, waiting for transfers between devices, shift_dp(): lax.ppermute(values, 'dp', [(d, (d + 4 * y) % size ^ 2 * x) for d in rang...  28.5 us
    pallas_call x2, Pallas kernels, unit_products(): pl.pallas_call(body, grid=(steps,), in_specs=[pl.BlockSpec((length, tile)...  27.6 us
  transfers between devices with their start and end apart: 64, of which 29 were waited for; matrix products, arithmetic and copies ran while one was open for 18% of the time, Pallas kernels for 24%

profile of v7, /device:TPU:0, one launch (start us, length us, event | category | flops | bytes accessed | tf_op | source)
XLA Modules:
  0.0 679.4 jit_solution(506908884582867404)
XLA Ops:
  12.5 6.3 all-to-all-start
  22.3 9.3 %all-to-all-done = bf16[4,48,1152]{2,1,0:T(8,128)(2,1)S(1)} async-done(((bf16[4,48,1152]{2,1,0:T(8,128)(2,1)}), bf16[4,48,1152]{2,1,0:T(8,128)(2,1)S(1)}, u32[]{:S(2)}, u32[]{:S(2)}) %all-to-all-start) | async-done | bytes 442400 | tf_op jit(solution)/shard_map/all_to_all | solution.py:518
  41.7 4.1 all-to-all-start.1
  51.3 24.0 %collective-permute-done.refs_1_ = bf16[256,1536]{1,0:T(8,128)(2,1)S(1)} collective-permute-done((bf16[256,1536]{1,0:T(8,128)(2,1)S(1)}, bf16[256,1536]{1,0:T(8,128)(2,1)S(1)}, u32[]{:S(2)}, u32[]{:S(2)}) %collective-permute-start) | collective-permute-done | bytes 786464 | tf_op jit(solution)/shard_map/ppermute | solution.py:492
  87.9 28.1 %collective-permute-done.3.refs_2_ = bf16[256,1536]{1,0:T(8,128)(2,1)S(1)} collective-permute-done((bf16[256,1536]{1,0:T(8,128)(2,1)S(1)}, bf16[256,1536]{1,0:T(8,128)(2,1)S(1)}, u32[]{:S(2)}, u32[]{:S(2)}) %collective-permute-start.3) | collective-permute-done | bytes 786464 | tf_op jit(solution)/shard_map/ppermute | solution.py:492
  116.9 11.6 %collective-permute-done.4.refs_3_ = bf16[256,1536]{1,0:T(8,128)(2,1)S(1)} collective-permute-done((bf16[256,1536]{1,0:T(8,128)(2,1)S(1)}, bf16[256,1536]{1,0:T(8,128)(2,1)S(1)}, u32[]{:S(2)}, u32[]{:S(2)}) %collective-permute-start.4) | collective-permute-done | bytes 786464 | tf_op jit(solution)/shard_map/ppermute | solution.py:492
  131.3 6.8 all-to-all-start.3
  151.9 23.0 %shard_map.297 = (bf16[1024,1152]{1,0:T(8,128)(2,1)S(1)}, bf16[1024,384]{1,0:T(8,128)(2,1)S(1)}, f32[3,2,1024]{2,1,0:T(2,128)S(1)}, f32[3,128,1024]{2,1,0:T(8,128)S(1)}) custom-call(bf16[256,1536]{1,0:T(8,128)(2,1)S(1)} %fusion.21.refs_0_, bf16[256,1536]{1,0:T(8,128)(2,1)S(1)} %collective-permute-done.refs_1_, bf16[256,1536]{1,0:T(8,128)(2,1)S(1)} %copy-done.19, ...), custom_call_target="tpu_custom_call" | custom-call | bytes 24000000 | tf_op jit(solution)/shard_map/pallas_call | solution.py:137
  178.4 4.4 all-to-all-done.3
  186.5 4.2 all-to-all-start.4
  198.5 7.3 %shard_map.298 = (bf16[2,16,96,1536]{3,2,1,0:T(8,128)(2,1)}, bf16[1,16,96,1536]{3,2,1,0:T(8,128)(2,1)S(1)}) custom-call(bf16[3,96,1536]{2,1,0:T(8,128)(2,1)} %get-tuple-element.263.refs_0_, bf16[3,96,1536]{2,1,0:T(8,128)(2,1)} %collective-permute-done.1.refs_1_, bf16[3,96,1536]{2,1,0:T(8,128)(2,1)} %collective-permute-done.5.refs_2_, ...), custom_call_target="tpu_custom_call" | custom-call | bytes 6000000 | tf_op jit(solution)/shard_map/pallas_call | solution.py:628
  208.2 3.6 all-to-all-done.4
  215.3 4.4 fusion.75
  222.0 4.9 convolution_convert_fusion.5.q_ref
  226.9 4.0 collective-permute-done.18.g_ref.refs_10_
  236.7 7.7 %shard_map.299 = (bf16[256,1536]{1,0:T(8,128)(2,1)S(1)}, f32[2,12,256]{2,1,0:T(8,128)S(1)}, f32[1536,256]{1,0:T(8,128)S(1)}) custom-call(bf16[256,1536]{1,0:T(8,128)(2,1)S(1)} %copy-done.34, bf16[256,1536]{1,0:T(8,128)(2,1)S(1)} %fusion.4.k_ref, bf16[256,1536]{1,0:T(8,128)(2,1)S(1)} %fusion.5.v_ref, s32[1,256]{1,0:T(1,128)S(1)} %bitcast.231), custom_call_target="tpu_custom_call" | custom-call | bytes 12000000 | tf_op jit(solution)/shard_map/pallas_call | solution.py:263
  248.0 16.0 %all-gather.19.cloned.1.call-done = bf16[32,1,48,1536]{3,2,1,0:T(8,128)(2,1)} async-done(((bf16[4,1,48,1536]{3,2,1,0:T(8,128)(2,1)}), bf16[32,1,48,1536]{3,2,1,0:T(8,128)(2,1)}) %all-gather.19.cloned.1.call-update) | async-done | bytes 4718608 | tf_op jit(solution)/shard_map/all_gather | solution.py:669
  264.0 4.5 fusion.76
  271.2 11.8 %shard_map.300 = (bf16[1024,1536]{1,0:T(8,128)(2,1)S(1)}, bf16[1024,1536]{1,0:T(8,128)(2,1)S(1)}, bf16[1024,1536]{1,0:T(8,128)(2,1)S(1)}, bf16[256,1536]{1,0:T(8,128)(2,1)S(1)}, bf16[256,1536]{1,0:T(8,128)(2,1)S(1)}) custom-call(bf16[256,1536]{1,0:T(8,128)(2,1)S(1)} %multiply_convert_fusion.x_ref.refs_3_, bf16[256,1536]{1,0:T(8,128)(2,1)S(1)} %fusion.23.g_ref.refs_7_, ...), custom_call_target="tpu_custom_call" | custom-call | bytes 12000000 | tf_op jit(solution)/shard_map/pallas_call | solution.py:368
  283.1 8.1 %collective-permute-done.20.x_ref.refs_4_ = bf16[256,1536]{1,0:T(8,128)(2,1)S(1)} collective-permute-done((bf16[256,1536]{1,0:T(8,128)(2,1)S(1)}, bf16[256,1536]{1,0:T(8,128)(2,1)S(1)}, u32[]{:S(2)}, u32[]{:S(2)}) %collective-permute-start.20) | collective-permute-done | bytes 786464 | tf_op jit(solution)/shard_map/ppermute | solution.py:492
  291.3 12.1 %shard_map.301 = (bf16[1024,1536]{1,0:T(8,128)(2,1)S(1)}, bf16[1024,1536]{1,0:T(8,128)(2,1)S(1)}, bf16[1024,1536]{1,0:T(8,128)(2,1)S(1)}, bf16[256,1536]{1,0:T(8,128)(2,1)S(1)}, bf16[256,1536]{1,0:T(8,128)(2,1)S(1)}) custom-call(bf16[256,1536]{1,0:T(8,128)(2,1)S(1)} %collective-permute-done.20.x_ref.refs_4, ...), custom_call_target="tpu_custom_call", output_to_operand_aliasing={{0}: (5, {}), {1}: (6, {}), {2}: (7, {})} | custom-call | bytes 12000000 | tf_op jit(solution)/shard_map/pallas_call | solution.py:368
  304.4 7.6 %collective-permute-done.21.x_ref.refs_5_ = bf16[256,1536]{1,0:T(8,128)(2,1)S(1)} collective-permute-done((bf16[256,1536]{1,0:T(8,128)(2,1)S(1)}, bf16[256,1536]{1,0:T(8,128)(2,1)S(1)}, u32[]{:S(2)}, u32[]{:S(2)}) %collective-permute-start.21) | collective-permute-done | bytes 786464 | tf_op jit(solution)/shard_map/ppermute | solution.py:492
  312.1 12.6 %shard_map.302 = (bf16[1024,1536]{1,0:T(8,128)(2,1)S(1)}, bf16[1024,1536]{1,0:T(8,128)(2,1)S(1)}, bf16[1024,1536]{1,0:T(8,128)(2,1)S(1)}, bf16[256,1536]{1,0:T(8,128)(2,1)S(1)}, bf16[256,1536]{1,0:T(8,128)(2,1)S(1)}) custom-call(bf16[256,1536]{1,0:T(8,128)(2,1)S(1)} %collective-permute-done.21.x_ref.refs_5, ...), custom_call_target="tpu_custom_call", output_to_operand_aliasing={{0}: (5, {}), {1}: (6, {}), {2}: (7, {})} | custom-call | bytes 12000000 | tf_op jit(solution)/shard_map/pallas_call | solution.py:368
  324.8 9.4 %collective-permute-done.22.x_ref.refs_6_ = bf16[256,1536]{1,0:T(8,128)(2,1)S(1)} collective-permute-done((bf16[256,1536]{1,0:T(8,128)(2,1)S(1)}, bf16[256,1536]{1,0:T(8,128)(2,1)S(1)}, u32[]{:S(2)}, u32[]{:S(2)}) %collective-permute-start.22) | collective-permute-done | bytes 786464 | tf_op jit(solution)/shard_map/ppermute | solution.py:492
  334.2 14.3 %collective-permute-done.23 = bf16[256,1536]{1,0:T(8,128)(2,1)S(1)} collective-permute-done((bf16[256,1536]{1,0:T(8,128)(2,1)S(1)}, bf16[256,1536]{1,0:T(8,128)(2,1)S(1)}, u32[]{:S(2)}, u32[]{:S(2)}) %collective-permute-start.23) | collective-permute-done | bytes 786464 | tf_op jit(solution)/shard_map/ppermute | solution.py:492
  348.9 11.8 %shard_map.303 = (bf16[1024,1536]{1,0:T(8,128)(2,1)S(1)}, bf16[1024,1536]{1,0:T(8,128)(2,1)S(1)}, bf16[1024,1536]{1,0:T(8,128)(2,1)S(1)}, bf16[256,1536]{1,0:T(8,128)(2,1)S(1)}, bf16[256,1536]{1,0:T(8,128)(2,1)S(1)}) custom-call(bf16[256,1536]{1,0:T(8,128)(2,1)S(1)} %collective-permute-done.22.x_ref.refs_6, ...), custom_call_target="tpu_custom_call", output_to_operand_aliasing={{0}: (5, {}), {1}: (6, {}), {2}: (7, {})} | custom-call | bytes 12000000 | tf_op jit(solution)/shard_map/pallas_call | solution.py:368
  368.0 13.5 %shard_map.304 = bf16[3,768,1536]{2,1,0:T(8,128)(2,1)} custom-call(bf16[1024,1536]{1,0:T(8,128)(2,1)} %copy-done.1, bf16[1024,1536]{1,0:T(8,128)(2,1)} %copy-done.2, bf16[1024,1536]{1,0:T(8,128)(2,1)} %copy-done, bf16[256,1536]{1,0:T(8,128)(2,1)} %copy-done.6, bf16[256,1536]{1,0:T(8,128)(2,1)} %copy-done.10, bf16[256,1536]{1,0:T(8,128)(2,1)} %copy-done.11, ...), custom_call_target="tpu_custom_call" | custom-call | bytes 15000000 | tf_op jit(solution)/shard_map/pallas_call | solution.py:415
  381.5 4.4 collective-permute-done.25
  392.7 4.9 convolution_convert_fusion.4.grad_ref
  397.7 7.6 %shard_map.306 = (bf16[256,1536]{1,0:T(8,128)(2,1)S(1)}, bf16[256,1536]{1,0:T(8,128)(2,1)S(1)}, bf16[256,1536]{1,0:T(8,128)(2,1)S(1)}) custom-call(bf16[256,1536]{1,0:T(8,128)(2,1)S(1)} %copy-done.34, bf16[256,1536]{1,0:T(8,128)(2,1)S(1)} %copy-done.36, bf16[256,1536]{1,0:T(8,128)(2,1)S(1)} %copy-done.38, ...), custom_call_target="tpu_custom_call" | custom-call | bytes 12000000 | tf_op jit(solution)/shard_map/pallas_call | solution.py:308
  407.0 3.9 shard_map.307
  414.0 3.9 shard_map.308
  417.9 3.5 shard_map.309
  430.5 3.7 all-to-all-start.5
  436.2 14.1 %shard_map.310 = bf16[3,768,1536]{2,1,0:T(8,128)(2,1)} custom-call(bf16[1024,1536]{1,0:T(8,128)(2,1)} %copy-done.1, bf16[1024,1536]{1,0:T(8,128)(2,1)} %copy-done.2, bf16[1024,1536]{1,0:T(8,128)(2,1)} %copy-done, bf16[256,1536]{1,0:T(8,128)(2,1)} %copy-done.6, bf16[256,1536]{1,0:T(8,128)(2,1)} %copy-done.10, bf16[256,1536]{1,0:T(8,128)(2,1)} %copy-done.11, ...), custom_call_target="tpu_custom_call" | custom-call | bytes 15000000 | tf_op jit(solution)/shard_map/pallas_call | solution.py:415
  455.9 3.8 fusion.13
  459.7 3.9 fusion.12
  472.5 18.6 %shard_map.311.refs_4_ = bf16[1024,1152]{1,0:T(8,128)(2,1)S(1)} custom-call(bf16[1024,1152]{1,0:T(8,128)(2,1)S(1)} %copy-done.40, bf16[1024,384]{1,0:T(8,128)(2,1)S(1)} %bitcast.226, f32[3,2,1024]{2,1,0:T(2,128)S(1)} %copy-done.58, f32[3,128,1024]{2,1,0:T(8,128)S(1)} %copy-done.44, f32[1024,128]{1,0:T(8,128)S(1)} %copy-done.28, f32[1024,128]{1,0:T(8,128)S(1)} %copy-done.26, ...), custom_call_target="tpu_custom_call" | custom-call | bytes 21000000 | tf_op jit(solution)/shard_map/pallas_call | solution.py:211
  491.1 4.5 convolution_convert_fusion
  495.7 7.0 %shard_map.312 = (bf16[1,2,2,2,96,1152]{5,4,3,2,1,0:T(8,128)(2,1)S(1)}, bf16[1,2,2,2,96,1152]{5,4,3,2,1,0:T(8,128)(2,1)}) custom-call(bf16[256,1536]{1,0:T(8,128)(2,1)S(1)} %fusion.21.refs_0_, bf16[256,1536]{1,0:T(8,128)(2,1)S(1)} %copy-done.14, bf16[256,1536]{1,0:T(8,128)(2,1)S(1)} %copy-done.20, bf16[256,1536]{1,0:T(8,128)(2,1)S(1)} %copy-done.17, ...), custom_call_target="tpu_custom_call" | custom-call | bytes 4500000 | tf_op jit(solution)/shard_map/pallas_call | solution.py:466
  532.4 5.0 all-to-all-start.6
  544.2 8.2 %all-to-all-done.6 = f32[32,1,144]{2,1,0:T(1,128)S(1)} async-done(((f32[32,1,144]{2,1,0:T(1,128)}), f32[32,1,144]{2,1,0:T(1,128)S(1)}, u32[]{:S(2)}, u32[]{:S(2)}) %all-to-all-start.6) | async-done | bytes 18464 | tf_op jit(solution)/shard_map/all_to_all | solution.py:900
  569.1 4.8 all-to-all-start.7
  576.0 3.8 collective-permute-start.41
  581.5 23.0 %collective-permute-done.46 = bf16[1,2,96,1152]{3,2,1,0:T(8,128)(2,1)} collective-permute-done((bf16[1,2,96,1152]{3,2,1,0:T(8,128)(2,1)}, bf16[1,2,96,1152]{3,2,1,0:T(8,128)(2,1)}, u32[]{:S(2)}, u32[]{:S(2)}) %collective-permute-start.46) | collective-permute-done | bytes 442400 | tf_op jit(solution)/shard_map/ppermute | solution.py:487
  615.0 5.3 collective-permute-done.41
  628.9 13.1 %all-to-all-start.8 = ((bf16[4,48,2688]{2,1,0:T(8,128)(2,1)}), bf16[4,48,2688]{2,1,0:T(8,128)(2,1)}, u32[]{:S(2)}, u32[]{:S(2)}) async-start(bf16[4,48,2688]{2,1,0:T(8,128)(2,1)} %pad_maximum_fusion.5), calls=%async_computation.8 | async-start | bytes 2064384 | tf_op jit(solution)/shard_map/all_to_all | solution.py:518
  654.9 10.9 %all-to-all-done.8 = bf16[4,48,2688]{2,1,0:T(8,128)(2,1)} async-done(((bf16[4,48,2688]{2,1,0:T(8,128)(2,1)}), bf16[4,48,2688]{2,1,0:T(8,128)(2,1)}, u32[]{:S(2)}, u32[]{:S(2)}) %all-to-all-start.8) | async-done | bytes 1032224 | tf_op jit(solution)/shard_map/all_to_all | solution.py:518
  (547 shorter events, 228.5 us)
Async XLA Ops:
  18.8 110.5 %all-gather.11.cloned.1.call-start = ((), (), s32[]{:S(2)}) async-start(), calls=%async_computation.9 | async-start | bytes 3981312 | tf_op jit(solution)/shard_map/all_gather | solution.py:669
  37.8 37.5 %collective-permute-start.1 = (bf16[3,96,1536]{2,1,0:T(8,128)(2,1)}, bf16[3,96,1536]{2,1,0:T(8,128)(2,1)}, u32[]{:S(2)}, u32[]{:S(2)}) collective-permute-start(bf16[3,96,1536]{2,1,0:T(8,128)(2,1)} %get-tuple-element.263.refs_0_), channel_id=1, source_target_pairs={{0,8},{4,12},{8,0},{12,4},{16,24},{20,28},{24,16},{28,20},{1,9},{5... | collective-permute-start | bytes 2654216 | tf_op jit(solution)/shard_map/ppermute | solution.py:487
  39.3 36.0 %collective-permute-start.2 = (bf16[3,96,1536]{2,1,0:T(8,128)(2,1)}, bf16[3,96,1536]{2,1,0:T(8,128)(2,1)}, u32[]{:S(2)}, u32[]{:S(2)}) collective-permute-start(bf16[3,96,1536]{2,1,0:T(8,128)(2,1)} %get-tuple-element.267.refs_4_), channel_id=1, source_target_pairs={{0,16},{4,20},{8,24},{12,28},{16,0},{20,4},{24,8},{28,12},{1,17},{... | collective-permute-start | bytes 2654216 | tf_op jit(solution)/shard_map/ppermute | solution.py:487
  41.7 35.9 %all-to-all-start.1 = ((bf16[4,48,1536]{2,1,0:T(8,128)(2,1)}), bf16[4,48,1536]{2,1,0:T(8,128)(2,1)}, u32[]{:S(2)}, u32[]{:S(2)}) async-start(bf16[4,48,1536]{2,1,0:T(8,128)(2,1)} %broadcast_in_dim.117), calls=%async_computation.1 | async-start | bytes 1179648 | tf_op jit(solution)/shard_map/all_to_all | solution.py:518
  45.8 169.4 %all-gather.13.cloned.1.call-start = ((), (), s32[]{:S(2)}) async-start(), calls=%async_computation.10 | async-start | bytes 5308416 | tf_op jit(solution)/shard_map/all_gather | solution.py:669
  45.9 29.4 %collective-permute-start = (bf16[256,1536]{1,0:T(8,128)(2,1)S(1)}, bf16[256,1536]{1,0:T(8,128)(2,1)S(1)}, u32[]{:S(2)}, u32[]{:S(2)}) collective-permute-start(bf16[256,1536]{1,0:T(8,128)(2,1)S(1)} %fusion.21.refs_0_), channel_id=1, source_target_pairs={{0,1},{1,2},{2,3},{3,0},{4,5},{5,6},{6,7},{7,4},{8,9},{9,10},{10,1... | collective-permute-start | bytes 2359304 | tf_op jit(solution)/shard_map/ppermute | solution.py:492
  77.6 51.7 %collective-permute-start.5 = (bf16[3,96,1536]{2,1,0:T(8,128)(2,1)}, bf16[3,96,1536]{2,1,0:T(8,128)(2,1)}, u32[]{:S(2)}, u32[]{:S(2)}) collective-permute-start(bf16[3,96,1536]{2,1,0:T(8,128)(2,1)} %get-tuple-element.263.refs_0_), channel_id=1, source_target_pairs={{0,16},{4,20},{8,24},{12,28},{16,0},{20,4},{24,8},{28,12},{1,17},{... | collective-permute-start | bytes 2654216 | tf_op jit(solution)/shard_map/ppermute | solution.py:487
  78.2 51.1 %collective-permute-start.6 = (bf16[3,96,1536]{2,1,0:T(8,128)(2,1)}, bf16[3,96,1536]{2,1,0:T(8,128)(2,1)}, u32[]{:S(2)}, u32[]{:S(2)}) collective-permute-start(bf16[3,96,1536]{2,1,0:T(8,128)(2,1)} %get-tuple-element.267.refs_4_), channel_id=1, source_target_pairs={{0,8},{4,12},{8,0},{12,4},{16,24},{20,28},{24,16},{28,20},{1,9},{5... | collective-permute-start | bytes 2654216 | tf_op jit(solution)/shard_map/ppermute | solution.py:487
  80.5 48.8 %all-to-all-start.2 = ((bf16[4,48,1536]{2,1,0:T(8,128)(2,1)}), bf16[4,48,1536]{2,1,0:T(8,128)(2,1)S(1)}, u32[]{:S(2)}, u32[]{:S(2)}) async-start(bf16[4,48,1536]{2,1,0:T(8,128)(2,1)} %broadcast_in_dim.118), calls=%async_computation.2 | async-start | bytes 1179648 | tf_op jit(solution)/shard_map/all_to_all | solution.py:518
  84.0 138.0 %all-gather.15.cloned.1.call-start = ((), (), s32[]{:S(2)}) async-start(), calls=%async_computation.11 | async-start | bytes 5308416 | tf_op jit(solution)/shard_map/all_gather | solution.py:669
  84.1 31.9 %collective-permute-start.3 = (bf16[256,1536]{1,0:T(8,128)(2,1)S(1)}, bf16[256,1536]{1,0:T(8,128)(2,1)S(1)}, u32[]{:S(2)}, u32[]{:S(2)}) collective-permute-start(bf16[256,1536]{1,0:T(8,128)(2,1)S(1)} %collective-permute-done.refs_1_), channel_id=1, source_target_pairs={{0,1},{1,2},{2,3},{3,0},{4,5},{5,6},{6,7},{7,4},{8,9},{9,10},{10,1... | collective-permute-start | bytes 2359304 | tf_op jit(solution)/shard_map/ppermute | solution.py:492
  86.0 42.4 %collective-permute-start.4 = (bf16[256,1536]{1,0:T(8,128)(2,1)S(1)}, bf16[256,1536]{1,0:T(8,128)(2,1)S(1)}, u32[]{:S(2)}, u32[]{:S(2)}) collective-permute-start(bf16[256,1536]{1,0:T(8,128)(2,1)S(1)} %fusion.21.refs_0_), channel_id=1, source_target_pairs={{0,3},{1,0},{2,1},{3,2},{4,7},{5,4},{6,5},{7,6},{8,11},{9,8},{10,9... | collective-permute-start | bytes 2359304 | tf_op jit(solution)/shard_map/ppermute | solution.py:492
  131.3 51.5 %all-to-all-start.3 = ((bf16[4,2,48,1536]{3,2,1,0:T(8,128)(2,1)}), bf16[4,2,48,1536]{3,2,1,0:T(8,128)(2,1)}, u32[]{:S(2)}, u32[]{:S(2)}) async-start(bf16[4,2,48,1536]{3,2,1,0:T(8,128)(2,1)} %broadcast_in_dim.119), calls=%async_computation.3 | async-start | bytes 2359296 | tf_op jit(solution)/shard_map/all_to_all | solution.py:518
  138.1 93.3 %all-gather.17.cloned.1.call-start = ((), (), s32[]{:S(2)}) async-start(), calls=%async_computation.12 | async-start | bytes 5308416 | tf_op jit(solution)/shard_map/all_gather | solution.py:669
  138.1 40.4 %collective-permute-start.7 = (bf16[3,96,1536]{2,1,0:T(8,128)(2,1)}, bf16[3,96,1536]{2,1,0:T(8,128)(2,1)}, u32[]{:S(2)}, u32[]{:S(2)}) collective-permute-start(bf16[3,96,1536]{2,1,0:T(8,128)(2,1)} %collective-permute-done.1.refs_1_), channel_id=1, source_target_pairs={{0,16},{4,20},{8,24},{12,28},{16,0},{20,4},{24,8},{28,12},{1,17},{... | collective-permute-start | bytes 2654216 | tf_op jit(solution)/shard_map/ppermute | solution.py:487
  139.6 38.9 %collective-permute-start.8 = (bf16[3,96,1536]{2,1,0:T(8,128)(2,1)}, bf16[3,96,1536]{2,1,0:T(8,128)(2,1)}, u32[]{:S(2)}, u32[]{:S(2)}) collective-permute-start(bf16[3,96,1536]{2,1,0:T(8,128)(2,1)} %collective-permute-done.2.refs_6_), channel_id=1, source_target_pairs={{0,8},{4,12},{8,0},{12,4},{16,24},{20,28},{24,16},{28,20},{1,9},{5... | collective-permute-start | bytes 2654216 | tf_op jit(solution)/shard_map/ppermute | solution.py:487
  141.1 37.4 %collective-permute-start.9 = (bf16[256,1536]{1,0:T(8,128)(2,1)S(1)}, bf16[256,1536]{1,0:T(8,128)(2,1)S(1)}, u32[]{:S(2)}, u32[]{:S(2)}) collective-permute-start(bf16[256,1536]{1,0:T(8,128)(2,1)S(1)} %fusion.23.g_ref.refs_7_), channel_id=1, source_target_pairs={{0,1},{1,2},{2,3},{3,0},{4,5},{5,6},{6,7},{7,4},{8,9},{9,10},{10,1... | collective-permute-start | bytes 2359304 | tf_op jit(solution)/shard_map/ppermute | solution.py:492
  185.2 78.8 %all-gather.19.cloned.1.call-start = ((), (), s32[]{:S(2)}) async-start(), calls=%async_computation.13 | async-start | bytes 5308416 | tf_op jit(solution)/shard_map/all_gather | solution.py:669
  186.5 25.3 %all-to-all-start.4 = ((bf16[4,256,384]{2,1,0:T(8,128)(2,1)}), bf16[4,256,384]{2,1,0:T(8,128)(2,1)}, u32[]{:S(2)}, u32[]{:S(2)}) async-start(bf16[4,256,384]{2,1,0:T(8,128)(2,1)} %bitcast.227), calls=%async_computation.4 | async-start | bytes 1572864 | tf_op jit(solution)/shard_map/all_to_all | solution.py:518
  230.9 38.8 %collective-permute-start.19 = (bf16[256,1536]{1,0:T(8,128)(2,1)S(1)}, bf16[256,1536]{1,0:T(8,128)(2,1)}, u32[]{:S(2)}, u32[]{:S(2)}) collective-permute-start(bf16[256,1536]{1,0:T(8,128)(2,1)S(1)} %collective-permute-done.9.g_ref.refs_8_), channel_id=1, source_target_pairs={{0,1},{1,2},{2,3},{3,0},{4,5},{5,6},{6,7},{7,4},{8,9},{9,10},{10,1... | collective-permute-start | bytes 2359304 | tf_op jit(solution)/shard_map/ppermute | solution.py:492
  269.7 21.6 %collective-permute-start.20 = (bf16[256,1536]{1,0:T(8,128)(2,1)S(1)}, bf16[256,1536]{1,0:T(8,128)(2,1)S(1)}, u32[]{:S(2)}, u32[]{:S(2)}) collective-permute-start(bf16[256,1536]{1,0:T(8,128)(2,1)S(1)} %multiply_convert_fusion.x_ref.refs_3_), channel_id=1, source_target_pairs={{0,1},{1,2},{2,3},{3,0},{4,5},{5,6},{6,7},{7,4},{8,9},{9,10},{10,1... | collective-permute-start | bytes 2359304 | tf_op jit(solution)/shard_map/ppermute | solution.py:492
  291.3 20.7 %collective-permute-start.21 = (bf16[256,1536]{1,0:T(8,128)(2,1)S(1)}, bf16[256,1536]{1,0:T(8,128)(2,1)S(1)}, u32[]{:S(2)}, u32[]{:S(2)}) collective-permute-start(bf16[256,1536]{1,0:T(8,128)(2,1)S(1)} %collective-permute-done.20.x_ref.refs_4_), channel_id=1, source_target_pairs={{0,1},{1,2},{2,3},{3,0},{4,5},{5,6},{6,7},{7,4},{8,9},{9,10},{10,1... | collective-permute-start | bytes 2359304 | tf_op jit(solution)/shard_map/ppermute | solution.py:492
  312.0 22.3 %collective-permute-start.22 = (bf16[256,1536]{1,0:T(8,128)(2,1)S(1)}, bf16[256,1536]{1,0:T(8,128)(2,1)S(1)}, u32[]{:S(2)}, u32[]{:S(2)}) collective-permute-start(bf16[256,1536]{1,0:T(8,128)(2,1)S(1)} %collective-permute-done.21.x_ref.refs_5_), channel_id=1, source_target_pairs={{0,1},{1,2},{2,3},{3,0},{4,5},{5,6},{6,7},{7,4},{8,9},{9,10},{10,1... | collective-permute-start | bytes 2359304 | tf_op jit(solution)/shard_map/ppermute | solution.py:492
  312.0 36.6 %collective-permute-start.23 = (bf16[256,1536]{1,0:T(8,128)(2,1)S(1)}, bf16[256,1536]{1,0:T(8,128)(2,1)S(1)}, u32[]{:S(2)}, u32[]{:S(2)}) collective-permute-start(bf16[256,1536]{1,0:T(8,128)(2,1)S(1)} %get-tuple-element.314), channel_id=1, source_target_pairs={{0,1},{1,2},{2,3},{3,0},{4,5},{5,6},{6,7},{7,4},{8,9},{9,10},{10,1... | collective-permute-start | bytes 2359304 | tf_op jit(solution)/shard_map/ppermute | solution.py:492
  385.9 44.6 %collective-permute-start.28 = (bf16[3,768,1536]{2,1,0:T(8,128)(2,1)}, bf16[3,768,1536]{2,1,0:T(8,128)(2,1)}, u32[]{:S(2)}, u32[]{:S(2)}) collective-permute-start(bf16[3,768,1536]{2,1,0:T(8,128)(2,1)} %shard_map.304), channel_id=1, source_target_pairs={{0,4},{4,0},{8,12},{12,8},{16,20},{20,16},{24,28},{28,24},{1,5},{5... | collective-permute-start | bytes 21233672 | tf_op jit(solution)/shard_map/ppermute | solution.py:482
  392.1 33.3 %collective-permute-start.27 = (bf16[1,2,2,2,96,1536]{5,4,3,2,1,0:T(8,128)(2,1)S(1)}, bf16[1,2,2,2,96,1536]{5,4,3,2,1,0:T(8,128)(2,1)}, u32[]{:S(2)}, u32[]{:S(2)}) collective-permute-start(bf16[1,2,2,2,96,1536]{5,4,3,2,1,0:T(8,128)(2,1)S(1)} %get-tuple-element.364), channel_id=1, source_target_pairs={{0,4},{4,0},{8,12},{12,8},{16,20},{20,16},{24,28},{28,24},{1,5},{5... | collective-permute-start | bytes 7077896 | tf_op jit(solution)/shard_map/ppermute | solution.py:482
  410.9 19.6 %collective-permute-start.26 = (bf16[256,1536]{1,0:T(8,128)(2,1)S(1)}, bf16[256,1536]{1,0:T(8,128)(2,1)}, u32[]{:S(2)}, u32[]{:S(2)}) collective-permute-start(bf16[256,1536]{1,0:T(8,128)(2,1)S(1)} %copy-done.61), channel_id=1, source_target_pairs={{0,3},{1,0},{2,1},{3,2},{4,7},{5,4},{6,5},{7,6},{8,11},{9,8},{10,9... | collective-permute-start | bytes 2359304 | tf_op jit(solution)/shard_map/ppermute | solution.py:492
  430.5 25.4 %collective-permute-start.31 = (bf16[3,2,2,2,96,1536]{5,4,3,2,1,0:T(8,128)(2,1)}, bf16[3,2,2,2,96,1536]{5,4,3,2,1,0:T(8,128)(2,1)}, u32[]{:S(2)}, u32[]{:S(2)}) collective-permute-start(bf16[3,2,2,2,96,1536]{5,4,3,2,1,0:T(8,128)(2,1)} %get-tuple-element.379), channel_id=1, source_target_pairs={{0,4},{4,0},{8,12},{12,8},{16,20},{20,16},{24,28},{28,24},{1,5},{5... | collective-permute-start | bytes 21233672 | tf_op jit(solution)/shard_map/ppermute | solution.py:482
  430.5 24.5 %all-to-all-start.5 = ((bf16[4,256,384]{2,1,0:T(8,128)(2,1)}), bf16[4,256,384]{2,1,0:T(8,128)(2,1)S(1)}, u32[]{:S(2)}, u32[]{:S(2)}) async-start(bf16[4,256,384]{2,1,0:T(8,128)(2,1)} %pad_maximum_fusion.7), calls=%async_computation.5 | async-start | bytes 1572864 | tf_op jit(solution)/shard_map/all_to_all | solution.py:518
  463.6 40.6 %collective-permute-start.32 = (bf16[3,2,96,1536]{3,2,0,1:T(8,128)(2,1)}, bf16[3,2,96,1536]{3,2,0,1:T(8,128)(2,1)}, u32[]{:S(2)}, u32[]{:S(2)}) collective-permute-start(bf16[3,2,96,1536]{3,2,0,1:T(8,128)(2,1)} %fusion.12), channel_id=1, source_target_pairs={{0,16},{4,20},{8,24},{12,28},{16,0},{20,4},{24,8},{28,12},{1,17},{... | collective-permute-start | bytes 5308424 | tf_op jit(solution)/shard_map/ppermute | solution.py:487
  464.7 40.0 %collective-permute-start.33 = (bf16[3,2,96,1536]{3,2,1,0:T(8,128)(2,1)}, bf16[3,2,96,1536]{3,2,1,0:T(8,128)(2,1)}, u32[]{:S(2)}, u32[]{:S(2)}) collective-permute-start(bf16[3,2,96,1536]{3,2,1,0:T(8,128)(2,1)} %fusion.13), channel_id=1, source_target_pairs={{0,8},{4,12},{8,0},{12,4},{16,24},{20,28},{24,16},{28,20},{1,9},{5... | collective-permute-start | bytes 5308424 | tf_op jit(solution)/shard_map/ppermute | solution.py:487
  465.8 38.3 %collective-permute-start.34 = (bf16[256,1536]{1,0:T(8,128)(2,1)}, bf16[256,1536]{1,0:T(8,128)(2,1)S(1)}, u32[]{:S(2)}, u32[]{:S(2)}) collective-permute-start(bf16[256,1536]{1,0:T(8,128)(2,1)} %add_convert_fusion.4), channel_id=1, source_target_pairs={{0,3},{1,0},{2,1},{3,2},{4,7},{5,4},{6,5},{7,6},{8,11},{9,8},{10,9... | collective-permute-start | bytes 2359304 | tf_op jit(solution)/shard_map/ppermute | solution.py:492
  467.4 36.8 %collective-permute-start.35 = (bf16[256,1536]{1,0:T(8,128)(2,1)}, bf16[256,1536]{1,0:T(8,128)(2,1)S(1)}, u32[]{:S(2)}, u32[]{:S(2)}) collective-permute-start(bf16[256,1536]{1,0:T(8,128)(2,1)} %copy-done.59), channel_id=1, source_target_pairs={{0,1},{1,2},{2,3},{3,0},{4,5},{5,6},{6,7},{7,4},{8,9},{9,10},{10,1... | collective-permute-start | bytes 2359304 | tf_op jit(solution)/shard_map/ppermute | solution.py:492
  507.0 46.6 %collective-permute-start.36 = (bf16[256,1536]{1,0:T(8,128)(2,1)}, bf16[256,1536]{1,0:T(8,128)(2,1)}, u32[]{:S(2)}, u32[]{:S(2)}) collective-permute-start(bf16[256,1536]{1,0:T(8,128)(2,1)} %get-tuple-element.403), channel_id=1, source_target_pairs={{0,3},{1,0},{2,1},{3,2},{4,7},{5,4},{6,5},{7,6},{8,11},{9,8},{10,9... | collective-permute-start | bytes 2359304 | tf_op jit(solution)/shard_map/ppermute | solution.py:492
  511.8 42.9 %collective-permute-start.37 = (bf16[256,1536]{1,0:T(8,128)(2,1)}, bf16[256,1536]{1,0:T(8,128)(2,1)}, u32[]{:S(2)}, u32[]{:S(2)}) collective-permute-start(bf16[256,1536]{1,0:T(8,128)(2,1)} %get-tuple-element.404), channel_id=1, source_target_pairs={{0,1},{1,2},{2,3},{3,0},{4,5},{5,6},{6,7},{7,4},{8,9},{9,10},{10,1... | collective-permute-start | bytes 2359304 | tf_op jit(solution)/shard_map/ppermute | solution.py:492
  518.3 37.5 %collective-permute-start.39 = (bf16[4,96,1536]{2,1,0:T(8,128)(2,1)}, bf16[4,96,1536]{2,1,0:T(8,128)(2,1)}, u32[]{:S(2)}, u32[]{:S(2)}) collective-permute-start(bf16[4,96,1536]{2,1,0:T(8,128)(2,1)} %fusion.26), channel_id=1, source_target_pairs={{0,16},{4,20},{8,24},{12,28},{16,0},{20,4},{24,8},{28,12},{1,17},{... | collective-permute-start | bytes 3538952 | tf_op jit(solution)/shard_map/ppermute | solution.py:487
  525.6 30.1 %collective-permute-start.38 = (bf16[4,96,1536]{2,1,0:T(8,128)(2,1)}, bf16[4,96,1536]{2,1,0:T(8,128)(2,1)}, u32[]{:S(2)}, u32[]{:S(2)}) collective-permute-start(bf16[4,96,1536]{2,1,0:T(8,128)(2,1)} %fusion.28), channel_id=1, source_target_pairs={{0,8},{4,12},{8,0},{12,4},{16,24},{20,28},{24,16},{28,20},{1,9},{5... | collective-permute-start | bytes 3538952 | tf_op jit(solution)/shard_map/ppermute | solution.py:487
  526.6 29.2 %collective-permute-start.40 = (bf16[1,2,2,2,96,1152]{5,4,3,2,1,0:T(8,128)(2,1)}, bf16[1,2,2,2,96,1152]{5,4,3,2,1,0:T(8,128)(2,1)}, u32[]{:S(2)}, u32[]{:S(2)}) collective-permute-start(bf16[1,2,2,2,96,1152]{5,4,3,2,1,0:T(8,128)(2,1)} %get-tuple-element.410), channel_id=1, source_target_pairs={{0,4},{4,0},{8,12},{12,8},{16,20},{20,16},{24,28},{28,24},{1,5},{5... | collective-permute-start | bytes 5308424 | tf_op jit(solution)/shard_map/ppermute | solution.py:482
  532.4 19.9 %all-to-all-start.6 = ((f32[32,1,144]{2,1,0:T(1,128)}), f32[32,1,144]{2,1,0:T(1,128)S(1)}, u32[]{:S(2)}, u32[]{:S(2)}) async-start(f32[32,1,144]{2,1,0:T(1,128)} %reshape.796), calls=%async_computation.6 | async-start | bytes 65536 | tf_op jit(solution)/shard_map/all_to_all | solution.py:900
  553.7 61.3 %collective-permute-start.42 = (bf16[3,2,96,1536]{3,2,0,1:T(8,128)(2,1)}, bf16[3,2,96,1536]{3,2,0,1:T(8,128)(2,1)}, u32[]{:S(2)}, u32[]{:S(2)}) collective-permute-start(bf16[3,2,96,1536]{3,2,0,1:T(8,128)(2,1)} %bitcast.254), channel_id=1, source_target_pairs={{0,16},{4,20},{8,24},{12,28},{16,0},{20,4},{24,8},{28,12},{1,17},{... | collective-permute-start | bytes 5308424 | tf_op jit(solution)/shard_map/ppermute | solution.py:487
  554.7 60.3 %collective-permute-start.43 = (bf16[3,2,96,1536]{3,2,0,1:T(8,128)(2,1)}, bf16[3,2,96,1536]{3,2,0,1:T(8,128)(2,1)}, u32[]{:S(2)}, u32[]{:S(2)}) collective-permute-start(bf16[3,2,96,1536]{3,2,0,1:T(8,128)(2,1)} %bitcast.253), channel_id=1, source_target_pairs={{0,8},{4,12},{8,0},{12,4},{16,24},{20,28},{24,16},{28,20},{1,9},{5... | collective-permute-start | bytes 5308424 | tf_op jit(solution)/shard_map/ppermute | solution.py:487
  565.4 39.1 %collective-permute-start.46 = (bf16[1,2,96,1152]{3,2,1,0:T(8,128)(2,1)}, bf16[1,2,96,1152]{3,2,1,0:T(8,128)(2,1)}, u32[]{:S(2)}, u32[]{:S(2)}) collective-permute-start(bf16[1,2,96,1152]{3,2,1,0:T(8,128)(2,1)} %fusion.47), channel_id=1, source_target_pairs={{0,8},{4,12},{8,0},{12,4},{16,24},{20,28},{24,16},{28,20},{1,9},{5... | collective-permute-start | bytes 1327112 | tf_op jit(solution)/shard_map/ppermute | solution.py:487
  566.4 38.2 %collective-permute-start.44 = (bf16[1,2,96,1152]{3,2,1,0:T(8,128)(2,1)}, bf16[1,2,96,1152]{3,2,1,0:T(8,128)(2,1)}, u32[]{:S(2)}, u32[]{:S(2)}) collective-permute-start(bf16[1,2,96,1152]{3,2,1,0:T(8,128)(2,1)} %fusion.46), channel_id=1, source_target_pairs={{0,16},{4,20},{8,24},{12,28},{16,0},{20,4},{24,8},{28,12},{1,17},{... | collective-permute-start | bytes 1327112 | tf_op jit(solution)/shard_map/ppermute | solution.py:487
  569.1 51.3 %all-to-all-start.7 = ((bf16[4,3,48,1536]{3,2,1,0:T(8,128)(2,1)}), bf16[4,3,48,1536]{3,2,1,0:T(8,128)(2,1)}, u32[]{:S(2)}, u32[]{:S(2)}) async-start(bf16[4,3,48,1536]{3,2,1,0:T(8,128)(2,1)} %pad_maximum_fusion.1), calls=%async_computation.7 | async-start | bytes 3538944 | tf_op jit(solution)/shard_map/all_to_all | solution.py:518
  576.0 44.3 %collective-permute-start.41 = (bf16[256,1536]{1,0:T(8,128)(2,1)}, bf16[256,1536]{1,0:T(8,128)(2,1)S(1)}, u32[]{:S(2)}, u32[]{:S(2)}) collective-permute-start(bf16[256,1536]{1,0:T(8,128)(2,1)} %fusion.18), channel_id=1, source_target_pairs={{0,3},{1,0},{2,1},{3,2},{4,7},{5,4},{6,5},{7,6},{8,11},{9,8},{10,9... | collective-permute-start | bytes 2359304 | tf_op jit(solution)/shard_map/ppermute | solution.py:492
  623.5 26.6 %collective-permute-start.48 = (bf16[3,96,1536]{2,1,0:T(8,128)(2,1)}, bf16[3,96,1536]{2,1,0:T(8,128)(2,1)}, u32[]{:S(2)}, u32[]{:S(2)}) collective-permute-start(bf16[3,96,1536]{2,1,0:T(8,128)(2,1)} %slice_bitcast_fusion.2), channel_id=1, source_target_pairs={{0,8},{4,12},{8,0},{12,4},{16,24},{20,28},{24,16},{28,20},{1,9},{5... | collective-permute-start | bytes 2654216 | tf_op jit(solution)/shard_map/ppermute | solution.py:487
  628.0 23.6 %collective-permute-start.49 = (bf16[3,96,1536]{2,1,0:T(8,128)(2,1)}, bf16[3,96,1536]{2,1,0:T(8,128)(2,1)}, u32[]{:S(2)}, u32[]{:S(2)}) collective-permute-start(bf16[3,96,1536]{2,1,0:T(8,128)(2,1)} %slice_bitcast_fusion), channel_id=1, source_target_pairs={{0,16},{4,20},{8,24},{12,28},{16,0},{20,4},{24,8},{28,12},{1,17},{... | collective-permute-start | bytes 2654216 | tf_op jit(solution)/shard_map/ppermute | solution.py:487
  628.9 36.9 %all-to-all-start.8 = ((bf16[4,48,2688]{2,1,0:T(8,128)(2,1)}), bf16[4,48,2688]{2,1,0:T(8,128)(2,1)}, u32[]{:S(2)}, u32[]{:S(2)}) async-start(bf16[4,48,2688]{2,1,0:T(8,128)(2,1)} %pad_maximum_fusion.5), calls=%async_computation.8 | async-start | bytes 2064384 | tf_op jit(solution)/shard_map/all_to_all | solution.py:518
  (164 other events, 1564.5 us)
Sparse Core Ops, SparseCore 0:
  32.5 43.2 all-gather.10
  77.7 42.0 all-gather.12
  130.3 49.4 all-gather.14
  185.3 37.9 all-gather.16
  225.0 38.9 all-gather.18
